TPU v7x, 32 devices: a whole 2x2x4 slice. The times are simulated.
32 devices in a mesh: sim: 8 (over z, x), grp: 4 (over y, core).
Axes of the slice: x: 2, y: 2, z: 4, core: 2. Of those that a mesh axis runs over, the one named last changes fastest.
Arguments:
- velocity: float32 [8, 4, 3, 256, 512], P('sim', 'grp'), may hold values from -6 to 6
- slot_of: int32 [8, 4, 256], P('sim', 'grp'), may hold values from 0 to 255, each once within a row
- w_encode: bfloat16 [1024, 256], replicated, may hold values from -0.1875 to 0.1875
- w_conv: bfloat16 [27, 256, 256], replicated, may hold values from -0.078125 to 0.078125
- w_head: bfloat16 [256, 128], replicated, may hold values from -0.375 to 0.375
Outputs:
- velocity_next: float32 [8, 4, 3, 256, 512], P('sim', 'grp')
- grad_encode: float32 [1024, 256], P(None, 'grp')
- grad_conv: float32 [27, 256, 256], P(None, None, 'grp')
- grad_head: float32 [256, 128], P('grp')
Inputs may be any that keep to these rules, and one draw needn't show every extreme that they name: `slot_of`: each block's row of 256 entries names every slot once.
All inputs are finite; a program needn't handle non-finite values.
Results may differ from a plain program's by a relative error of at most 0.0085.
Values may be sent and summed in bfloat16 or wider, within the bound.
No kernel may reach another device: no remote copies, remote signals or barrier semaphores. Data moves between devices by JAX's collectives and lax.ppermute only.
A program may use at most 128 MiB of HBM per device.

v0:
```python
import jax
import jax.numpy as jnp
import numpy as np
from jax import lax
from jax.sharding import PartitionSpec as P

NP = 8
EX = 2
EY = 4
EZ = 32
STEPS = 2


VISCOSITY = 0.2
TIME_STEP = 0.005
PENALTY = 100.0
LOSS_WEIGHT = 64.0


def as_sent(value):

    def short(part):
        return part.astype(jnp.bfloat16) if part.dtype == jnp.float32 else part

    return jax.tree.map(short, value)


def passed_along(value, axis, steps):
    count = lax.axis_size(axis)
    pairs = [(source, (source + steps) % count) for source in range(count)]
    return lax.ppermute(value, axis, pairs)


def from_behind(block, axis, distance):
    devices = range(lax.axis_size(axis))
    route = [(i - distance, i) for i in devices if i - distance in devices]
    return lax.ppermute(block, axis, route)


def derivative_matrix(count):
    places = np.arange(count)
    points = -np.cos(np.pi * places / (count - 1))
    weights = np.where(places % 2 == 0, 1.0, -1.0)
    weights[0] = weights[0] * 0.5
    weights[count - 1] = weights[count - 1] * 0.5
    identity = np.eye(count)
    spread = points[:, None] - points[None, :] + identity
    deriv = weights[None, :] / weights[:, None] / spread
    deriv = deriv * (1.0 - identity)
    return deriv - identity * deriv.sum(axis=1)[:, None]


def element_tables(count):
    deriv = derivative_matrix(count)
    single = np.eye(count)
    square = np.eye(count * count)
    along_x = np.kron(deriv, square)
    along_y = np.kron(single, np.kron(deriv, single))
    along_z = np.kron(square, deriv)
    laplace = along_x @ along_x + along_y @ along_y + along_z @ along_z
    stencil = np.concatenate([along_x.T, along_y.T, along_z.T, laplace.T], axis=1)
    grid = np.arange(count**3).reshape(count, count, count)
    final = count - 1
    chosen = np.concatenate(
        [
            grid[0].ravel(),
            grid[final].ravel(),
            grid[:, 0].ravel(),
            grid[:, final].ravel(),
            grid[:, :, 0].ravel(),
            grid[:, :, final].ravel(),
        ]
    )
    select = np.zeros((count**3, chosen.size))
    select[chosen, np.arange(chosen.size)] = 1.0
    bottom = np.zeros((count**3, count * count))
    for first in range(count):
        for middle in range(count):
            for inner in range(count):
                bottom[grid[first, middle, inner], first * count + inner] = (
                    VISCOSITY * deriv[0, middle]
                )
    return (
        jnp.asarray(stencil, jnp.float32),
        jnp.asarray(select, jnp.float32),
        jnp.asarray(bottom, jnp.float32),
    )


def silu_grad(value):
    sigma = jax.nn.sigmoid(value)
    return sigma * (1.0 + value * (1.0 - sigma))


def advance(field, faces, beside, stencil, select):
    points = field.shape[-1]
    derived = jnp.einsum("cxyzp,pq->cxyzq", field, stencil, precision=lax.Precision.HIGHEST)
    advect = field[0][None] * derived[..., 0:points]
    advect = advect + field[1][None] * derived[..., points : 2 * points]
    advect = advect + field[2][None] * derived[..., 2 * points : 3 * points]
    laplace = derived[..., 3 * points :]
    penalty = jnp.einsum("cxyzq,pq->cxyzp", beside - faces, select, precision=lax.Precision.HIGHEST)
    return field + TIME_STEP * (VISCOSITY * (laplace + PENALTY * penalty) - advect)


def face_part(faces, which):
    width = faces.shape[-1] // 6
    return faces[..., which * width : (which + 1) * width]


def local_beside(faces):
    last_x = face_part(faces, 1)[:, -1]
    from_left = passed_along(as_sent(last_x.reshape(3, -1)), "sim", 1).reshape(last_x.shape)
    first_x = face_part(faces, 0)[:, 0]
    from_right = passed_along(as_sent(first_x.reshape(3, -1)), "sim", -1).reshape(first_x.shape)
    before_x = jnp.concatenate([from_left[:, None], face_part(faces, 1)[:, :-1]], axis=1)
    after_x = jnp.concatenate([face_part(faces, 0)[:, 1:], from_right[:, None]], axis=1)
    top_y = face_part(faces, 3)[:, :, -1]
    from_below = from_behind(as_sent(top_y.reshape(3, -1)), "grp", 1).reshape(top_y.shape)
    base_y = face_part(faces, 2)[:, :, 0]
    from_above = from_behind(as_sent(base_y.reshape(3, -1)), "grp", -1).reshape(base_y.shape)
    below = jnp.concatenate([from_below[:, :, None], face_part(faces, 3)[:, :, :-1]], axis=2)
    above = jnp.concatenate([face_part(faces, 2)[:, :, 1:], from_above[:, :, None]], axis=2)
    before_z = jnp.roll(face_part(faces, 5), 1, axis=3)
    after_z = jnp.roll(face_part(faces, 4), -1, axis=3)
    return jnp.concatenate([before_x, after_x, below, above, before_z, after_z], axis=-1)


def crop_windows(grid, sign):
    padded = jnp.pad(grid, ((1, 1), (1, 1), (1, 1), (0, 0)))
    lengths = grid.shape[:3]
    pieces = []
    for shift_x in (-1, 0, 1):
        for shift_y in (-1, 0, 1):
            for shift_z in (-1, 0, 1):
                start_x = 1 + sign * shift_x
                start_y = 1 + sign * shift_y
                start_z = 1 + sign * shift_z
                pieces.append(
                    padded[
                        start_x : start_x + lengths[0],
                        start_y : start_y + lengths[1],
                        start_z : start_z + lengths[2],
                    ]
                )
    return jnp.concatenate(pieces, axis=-1).reshape(-1, 27 * grid.shape[-1])


def train_core(h1_grid, target_rows, w_conv, w_head, total):
    channels = h1_grid.shape[-1]
    patches = crop_windows(h1_grid, 1)
    z2 = jnp.dot(
        patches, w_conv.reshape(27 * channels, channels), preferred_element_type=jnp.float32
    )
    h2 = jax.nn.silu(z2).astype(jnp.bfloat16)
    output = jnp.dot(h2, w_head, preferred_element_type=jnp.float32)
    resid = (LOSS_WEIGHT * (output - target_rows.astype(jnp.float32)) / total).astype(jnp.bfloat16)
    grad_head = jnp.einsum("nc,no->co", h2, resid, preferred_element_type=jnp.float32)
    dh2 = jnp.dot(resid, w_head.T, preferred_element_type=jnp.float32)
    dz2 = (dh2 * silu_grad(z2)).astype(jnp.bfloat16)
    grad_conv = jnp.einsum("nk,nc->kc", patches, dz2, preferred_element_type=jnp.float32).reshape(
        27, channels, channels
    )
    back_patches = crop_windows(dz2.reshape(h1_grid.shape), -1)
    flipped = jnp.transpose(w_conv, (0, 2, 1)).reshape(27 * channels, channels)
    dh1 = jnp.dot(back_patches, flipped, preferred_element_type=jnp.float32)
    return (dh1, grad_conv, grad_head)


def body(velocity, slot_of, w_encode, w_conv, w_head):
    stencil, select, bottom = element_tables(NP)
    block = velocity[0, 0]
    slots = slot_of[0, 0]
    points = block.shape[-1]
    field = block[:, slots].reshape(3, EX, EY, EZ, points)
    for step in range(STEPS):
        faces = jnp.einsum("cxyzp,pq->cxyzq", field, select, precision=lax.Precision.HIGHEST)
        beside = local_beside(faces)
        field = advance(field, faces, beside, stencil, select)
    inverse = jnp.argsort(slots)
    velocity_next = field.reshape(3, EX * EY * EZ, points)[:, inverse][None, None]
    snapshot = jnp.concatenate([field[0], field[2]], axis=-1).astype(jnp.bfloat16)
    wall_low = jnp.einsum("xyzp,pq->xyzq", field[0], bottom, precision=lax.Precision.HIGHEST)
    wall_side = jnp.einsum("xyzp,pq->xyzq", field[2], bottom, precision=lax.Precision.HIGHEST)
    target = jnp.concatenate([wall_low, wall_side], axis=-1).astype(jnp.bfloat16)
    groups = lax.axis_size("grp")
    total = EX * EY * EZ * lax.axis_size("sim") * groups
    crop_x, crop_t = (
        lax.all_to_all(snapshot, "grp", split_axis=2, concat_axis=1, tiled=True),
        lax.all_to_all(target, "grp", split_axis=2, concat_axis=1, tiled=True),
    )
    rows = crop_x.reshape(-1, crop_x.shape[-1])
    z1 = jnp.dot(rows, w_encode, preferred_element_type=jnp.float32)
    h1 = jax.nn.silu(z1).astype(jnp.bfloat16)
    dh1, grad_conv, grad_head = train_core(
        h1.reshape(crop_x.shape[:3] + (h1.shape[-1],)),
        crop_t.reshape(-1, crop_t.shape[-1]),
        w_conv,
        w_head,
        total,
    )
    dz1 = (dh1 * silu_grad(z1)).astype(jnp.bfloat16)
    grad_encode = jnp.einsum("nf,nc->fc", rows, dz1, preferred_element_type=jnp.float32)
    total_encode, total_conv, total_head = lax.psum(
        (grad_encode, grad_conv, grad_head), ("sim", "grp")
    )
    quarter = w_encode.shape[1] // groups
    start = lax.axis_index("grp") * quarter
    out_encode = lax.dynamic_slice_in_dim(total_encode, start, quarter, 1)
    out_conv = lax.dynamic_slice_in_dim(total_conv, start, quarter, 2)
    out_head = lax.dynamic_slice_in_dim(total_head, start, quarter, 0)
    return (velocity_next, out_encode, out_conv, out_head)


def solution(mesh):
    placed = (P("sim", "grp", None, None, None), P("sim", "grp", None), P(), P(), P())
    return jax.shard_map(
        body,
        mesh=mesh,
        in_specs=placed,
        out_specs=(
            P("sim", "grp", None, None, None),
            P(None, "grp"),
            P(None, None, "grp"),
            P("grp", None),
        ),
        check_vma=False,
    )
```

profile of v0, /device:TPU:0, one launch (start us, length us, event | category | flops | bytes accessed | tf_op | source)
XLA Modules:
  0.0 395.0 jit_solution(4314997208378536792)
XLA Ops:
  9.8 3.2 sort.17
  13.0 3.1 gather_fusion
  18.1 4.3 %fusion.42 = (bf16[3,2,4,32,384]{4,3,2,1,0:T(8,128)(2,1)S(1)}, f32[3,2,4,32,384]{4,3,2,1,0:T(8,128)S(1)}) fusion(f32[3,2,4,32,512]{4,3,2,1,0:T(8,128)S(1)} %bitcast.157, f32[512,384,1,1,1]{1,0,4,3,2:T(8,128)} %constant.46), kind=kOutput, calls=%fused_computation.195 | convolution fusion | flops 1812234240 | bytes 4128768 | tf_op jit(solution)/shard_map/cxyzp,pq->cxyzq/dot_general | solution.py:177
  24.1 2.9 collective-permute-start
  27.2 3.1 collective-permute-start.1
  38.4 4.4 %fusion.29 = (f32[1,256,512]{2,0,1:T(1,128)S(1)}, f32[1,256,512]{2,0,1:T(1,128)S(1)}, f32[1,256,512]{2,0,1:T(1,128)S(1)}) fusion(f32[3,256,512]{2,0,1:T(4,128)} %bitcast.163), kind=kLoop, calls=%fused_computation.182 | loop fusion | bytes 3145728 | tf_op jit(solution)/shard_map/slice | solution.py:98
  42.8 12.2 %fusion.44 = f32[3,2,4,32,2048]{4,3,2,1,0:T(8,128)} fusion(f32[3,2,4,32,512]{4,3,2,1,0:T(8,128)S(1)} %bitcast.158, f32[512,2048,1,1,1]{1,0,4,3,2:T(8,128)S(1)} %copy-done.2), kind=kOutput, calls=%fused_computation.197 | convolution fusion | flops 9663676416 | bytes 12058624 | tf_op jit(solution)/shard_map/cxyzp,pq->cxyzq/dot_general | solution.py:97
  70.3 7.5 %fusion.9 = f32[3,2,4,32,512]{4,3,2,1,0:T(8,128)S(1)} fusion(f32[3,2,4,32,512]{4,3,2,1,0:T(8,128)} %bitcast.159, f32[3,2,4,32,2048]{4,3,2,1,0:T(8,128)} %fusion.44, f32[512,384,1,1,1]{1,0,4,3,2:T(8,128)} %constant.46, f32[3,2,4,32,384]{4,3,2,1,0:T(8,128)} %concatenate.170, f32[3,2,4,32,384]{4,3,2,1,0:T(8,128)S(1)} %get-tuple-element.106, ...), kind=kOutput, calls=%fused_computation.69 | convolution fusion | flops 1816559616 | bytes 14155776 | tf_op jit(solution)/shard_map/cxyzq,pq->cxyzp/dot_general | solution.py:102
  77.8 12.3 %fusion.45 = f32[3,2,4,32,2048]{4,3,2,1,0:T(8,128)} fusion(f32[3,2,4,32,512]{4,3,2,1,0:T(8,128)S(1)} %fusion.9, f32[512,2048,1,1,1]{1,0,4,3,2:T(8,128)S(1)} %copy-done.3), kind=kOutput, calls=%fused_computation.198 | convolution fusion | flops 9663676416 | bytes 12058624 | tf_op jit(solution)/shard_map/cxyzp,pq->cxyzq/dot_general | solution.py:97
  101.6 4.7 %collective-permute-start.5 = (bf16[3,8192]{1,0:T(4,128)(2,1)}, bf16[3,8192]{1,0:T(4,128)(2,1)}, u32[]{:S(2)}, u32[]{:S(2)}) collective-permute-start(bf16[3,8192]{1,0:T(4,128)(2,1)} %convert_element_type.191), channel_id=1, source_target_pairs={{0,28},{4,0},{8,4},{12,8},{16,12},{20,16},{24,20},{28,24},{1,29},{... | collective-permute-start | bytes 147464 | tf_op jit(solution)/shard_map/ppermute | solution.py:31
  107.8 4.2 %collective-permute-start.6 = (bf16[3,4096]{1,0:T(4,128)(2,1)}, bf16[3,4096]{1,0:T(4,128)(2,1)}, u32[]{:S(2)}, u32[]{:S(2)}) collective-permute-start(bf16[3,4096]{1,0:T(4,128)(2,1)} %convert_element_type.194), channel_id=1, source_target_pairs={{0,1},{1,2},{2,3},{4,5},{5,6},{6,7},{8,9},{9,10},{10,11},{12,13},{... | collective-permute-start | bytes 73736 | tf_op jit(solution)/shard_map/ppermute | solution.py:37
  133.2 7.0 %fusion.3 = f32[3,2,4,32,512]{4,3,2,1,0:T(8,128)S(1)} fusion(f32[3,2,4,32,512]{4,3,2,1,0:T(8,128)S(1)} %fusion.9, f32[3,2,4,32,2048]{4,3,2,1,0:T(8,128)} %fusion.45, f32[512,384,1,1,1]{1,0,4,3,2:T(8,128)} %constant.46, f32[3,2,4,32,384]{4,3,2,1,0:T(8,128)} %concatenate.177, f32[3,2,4,32,384]{4,3,2,1,0:T(8,128)S(1)} %get-tuple-element.108, ...), kind=kOutput, calls=%fused_computation.59 | convolution fusion | flops 1816559616 | bytes 14155776 | tf_op jit(solution)/shard_map/cxyzq,pq->cxyzp/dot_general | solution.py:102
  142.7 5.2 %all-to-all-start.1 = ((bf16[2,4,32,128]{3,1,0,2:T(4,128)(2,1)}), bf16[2,4,32,128]{3,1,0,2:T(4,128)(2,1)S(1)}, u32[]{:S(2)}, u32[]{:S(2)}) async-start(bf16[2,4,32,128]{3,1,0,2:T(4,128)(2,1)} %copy.40), calls=%async_computation.1 | async-start | bytes 131072 | tf_op jit(solution)/shard_map/all_to_all | solution.py:190
  149.2 2.9 all-to-all-done.1
  152.0 3.5 all-to-all-start
  155.5 6.0 %copy.42 = bf16[27,256,256]{1,2,0:T(8,128)(2,1)} copy(bf16[27,256,256]{2,1,0:T(8,128)(2,1)} %param.11) | data formatting | bytes 7077888 | tf_op args[3]
  161.5 2.7 all-to-all-done
  165.8 2.7 copy-done.8
  180.8 6.0 %copy.43 = bf16[6912,256]{1,0:T(8,128)(2,1)} copy(bf16[6912,256]{0,1:T(8,128)(2,1)} %bitcast.169) | data formatting | bytes 7077888 | tf_op jit(solution)/shard_map/nk,nc->kc/dot_general | solution.py:161
  186.8 6.0 %fusion.25 = f32[27,256,256]{1,2,0:T(8,128)} fusion(bf16[27,256,256]{2,1,0:T(8,128)(2,1)} %bitcast.161, bf16[256,256]{1,0:T(8,128)(2,1)S(1)} %fusion.14), kind=kOutput, calls=%fused_computation.116 | convolution fusion | flops 905969664 | bytes 10747904 | tf_op jit(solution)/shard_map/nk,nc->kc/dot_general | solution.py:161
  201.7 5.7 %fusion.16 = f32[1024,256]{0,1:T(8,128)} fusion(bf16[256,1024]{1,0:T(8,128)(2,1)S(1)} %bitcast.217, bf16[256,6912]{1,0:T(8,128)(2,1)} %constant_dynamic-update-slice_fusion.27, bf16[6912,256]{1,0:T(8,128)(2,1)} %bitcast.171, f32[256,256]{1,0:T(8,128)S(1)} %get-tuple-element.110), kind=kOutput, calls=%fused_computation.81 | convolution fusion | flops 1040777216 | bytes 8912896 | tf_op jit(solution)/shard_map/nf,nc->fc/dot_general | solution.py:203
  211.2 3.5 gather_fusion.1
  216.2 165.6 %all-reduce.5.cloned.1.call-done = (f32[1024,256]{0,1:T(8,128)}, f32[27,256,256]{1,2,0:T(8,128)}, f32[256,128]{1,0:T(8,128)}) async-done(((f32[1024,256]{0,1:T(8,128)}, f32[27,256,256]{1,2,0:T(8,128)}, f32[256,128]{1,0:T(8,128)}), (f32[1024,256]{0,1:T(8,128)}, f32[27,256,256]{1,2,0:T(8,128)}, f32[256,128]{1,0:T(8,128)})) %all-reduce.5.cloned.1.call-update) | async-done | bytes 8257552 | tf_op jit(solution)/shard_map/psum | solution.py:204
  383.5 2.9 constant_dynamic-slice_fusion.1
  (171 shorter events, 98.4 us)
Async XLA Ops:
  7.2 157.5 %copy-start = (bf16[1024,256]{1,0:T(8,128)(2,1)S(1)}, bf16[1024,256]{1,0:T(8,128)(2,1)}, u32[]{:S(2)}) copy-start(bf16[1024,256]{1,0:T(8,128)(2,1)} %param.10) | copy-start | bytes 1572868
  7.2 2.6 copy-start.13
  18.1 24.7 %copy-start.1 = (f32[3,256,512]{2,1,0:T(8,128)}, f32[3,256,512]{2,1,0:T(8,128)S(1)}, u32[]{:S(2)}) copy-start(f32[3,256,512]{2,1,0:T(8,128)S(1)} %copy.35) | copy-start | bytes 4718596
  24.1 37.0 %collective-permute-start = (bf16[3,8192]{1,0:T(4,128)(2,1)}, bf16[3,8192]{1,0:T(4,128)(2,1)}, u32[]{:S(2)}, u32[]{:S(2)}) collective-permute-start(bf16[3,8192]{1,0:T(4,128)(2,1)} %convert_element_type.176), channel_id=1, source_target_pairs={{0,4},{4,8},{8,12},{12,16},{16,20},{20,24},{24,28},{28,0},{1,5},{5... | collective-permute-start | bytes 147464 | tf_op jit(solution)/shard_map/ppermute | solution.py:31
  27.2 37.4 %collective-permute-start.1 = (bf16[3,8192]{1,0:T(4,128)(2,1)S(1)}, bf16[3,8192]{1,0:T(4,128)(2,1)}, u32[]{:S(2)}, u32[]{:S(2)}) collective-permute-start(bf16[3,8192]{1,0:T(4,128)(2,1)S(1)} %convert_element_type.179), channel_id=1, source_target_pairs={{0,28},{4,0},{8,4},{12,8},{16,12},{20,16},{24,20},{28,24},{1,29},{... | collective-permute-start | bytes 147464 | tf_op jit(solution)/shard_map/ppermute | solution.py:31
  31.9 25.7 %collective-permute-start.2 = (bf16[3,4096]{1,0:T(4,128)(2,1)}, bf16[3,4096]{1,0:T(4,128)(2,1)}, u32[]{:S(2)}, u32[]{:S(2)}) collective-permute-start(bf16[3,4096]{1,0:T(4,128)(2,1)} %convert_element_type.182), channel_id=1, source_target_pairs={{0,1},{1,2},{2,3},{4,5},{5,6},{6,7},{8,9},{9,10},{10,11},{12,13},{... | collective-permute-start | bytes 73736 | tf_op jit(solution)/shard_map/ppermute | solution.py:37
  34.7 8.1 %copy-start.2 = (f32[512,2048,1,1,1]{1,0,4,3,2:T(8,128)S(1)}, f32[512,2048,1,1,1]{1,0,4,3,2:T(8,128)}, u32[]{:S(2)}) copy-start(f32[512,2048,1,1,1]{1,0,4,3,2:T(8,128)} %constant.45) | copy-start | bytes 12582916
  34.7 23.8 %collective-permute-start.3 = (bf16[3,4096]{1,0:T(4,128)(2,1)}, bf16[3,4096]{1,0:T(4,128)(2,1)}, u32[]{:S(2)}, u32[]{:S(2)}) collective-permute-start(bf16[3,4096]{1,0:T(4,128)(2,1)} %convert_element_type.185), channel_id=1, source_target_pairs={{1,0},{2,1},{3,2},{5,4},{6,5},{7,6},{9,8},{10,9},{11,10},{13,12},{... | collective-permute-start | bytes 73736 | tf_op jit(solution)/shard_map/ppermute | solution.py:37
  55.0 3.5 copy-start.10
  70.3 7.5 %copy-start.3 = (f32[512,2048,1,1,1]{1,0,4,3,2:T(8,128)S(1)}, f32[512,2048,1,1,1]{1,0,4,3,2:T(8,128)}, u32[]{:S(2)}) copy-start(f32[512,2048,1,1,1]{1,0,4,3,2:T(8,128)} %constant.45) | copy-start | bytes 12582916
  77.8 12.4 %copy-start.6 = (f32[512,384,1,1,1]{1,0,4,3,2:T(8,128)S(1)}, f32[512,384,1,1,1]{1,0,4,3,2:T(8,128)}, u32[]{:S(2)}) copy-start(f32[512,384,1,1,1]{1,0,4,3,2:T(8,128)} %constant.46) | copy-start | bytes 2359300
  99.9 23.8 %collective-permute-start.4 = (bf16[3,8192]{1,0:T(4,128)(2,1)}, bf16[3,8192]{1,0:T(4,128)(2,1)}, u32[]{:S(2)}, u32[]{:S(2)}) collective-permute-start(bf16[3,8192]{1,0:T(4,128)(2,1)} %convert_element_type.188), channel_id=1, source_target_pairs={{0,4},{4,8},{8,12},{12,16},{16,20},{20,24},{24,28},{28,0},{1,5},{5... | collective-permute-start | bytes 147464 | tf_op jit(solution)/shard_map/ppermute | solution.py:31
  101.6 25.6 %collective-permute-start.5 = (bf16[3,8192]{1,0:T(4,128)(2,1)}, bf16[3,8192]{1,0:T(4,128)(2,1)}, u32[]{:S(2)}, u32[]{:S(2)}) collective-permute-start(bf16[3,8192]{1,0:T(4,128)(2,1)} %convert_element_type.191), channel_id=1, source_target_pairs={{0,28},{4,0},{8,4},{12,8},{16,12},{20,16},{24,20},{28,24},{1,29},{... | collective-permute-start | bytes 147464 | tf_op jit(solution)/shard_map/ppermute | solution.py:31
  107.8 10.0 %collective-permute-start.6 = (bf16[3,4096]{1,0:T(4,128)(2,1)}, bf16[3,4096]{1,0:T(4,128)(2,1)}, u32[]{:S(2)}, u32[]{:S(2)}) collective-permute-start(bf16[3,4096]{1,0:T(4,128)(2,1)} %convert_element_type.194), channel_id=1, source_target_pairs={{0,1},{1,2},{2,3},{4,5},{5,6},{6,7},{8,9},{9,10},{10,11},{12,13},{... | collective-permute-start | bytes 73736 | tf_op jit(solution)/shard_map/ppermute | solution.py:37
  112.8 8.4 %collective-permute-start.7 = (bf16[3,4096]{1,0:T(4,128)(2,1)}, bf16[3,4096]{1,0:T(4,128)(2,1)S(1)}, u32[]{:S(2)}, u32[]{:S(2)}) collective-permute-start(bf16[3,4096]{1,0:T(4,128)(2,1)} %convert_element_type.197), channel_id=1, source_target_pairs={{1,0},{2,1},{3,2},{5,4},{6,5},{7,6},{9,8},{10,9},{11,10},{13,12},{... | collective-permute-start | bytes 73736 | tf_op jit(solution)/shard_map/ppermute | solution.py:37
  133.2 7.1 %copy-start.11 = (f32[512,64,1,1]{0,1,3,2:T(8,128)S(1)}, f32[512,64,1,1]{0,1,3,2:T(8,128)}, u32[]{:S(2)}) copy-start(f32[512,64,1,1]{0,1,3,2:T(8,128)} %constant.47) | copy-start | bytes 393220
  140.2 1.1 copy-start.4
  142.7 9.3 %all-to-all-start.1 = ((bf16[2,4,32,128]{3,1,0,2:T(4,128)(2,1)}), bf16[2,4,32,128]{3,1,0,2:T(4,128)(2,1)S(1)}, u32[]{:S(2)}, u32[]{:S(2)}) async-start(bf16[2,4,32,128]{3,1,0,2:T(4,128)(2,1)} %copy.40), calls=%async_computation.1 | async-start | bytes 131072 | tf_op jit(solution)/shard_map/all_to_all | solution.py:190
  152.0 12.3 %all-to-all-start = ((bf16[2,4,32,1024]{3,1,0,2:T(4,128)(2,1)}), bf16[2,4,32,1024]{3,1,0,2:T(4,128)(2,1)S(1)}, u32[]{:S(2)}, u32[]{:S(2)}) async-start(bf16[2,4,32,1024]{3,1,0,2:T(4,128)(2,1)} %copy.37), calls=%async_computation | async-start | bytes 1048576 | tf_op jit(solution)/shard_map/all_to_all | solution.py:189
  155.5 226.3 %all-reduce.5.cloned.1.call-start = ((), (), s32[]{:S(2)}) async-start(), calls=%async_computation.2 | async-start | bytes 16515072 | tf_op jit(solution)/shard_map/psum | solution.py:204
  165.3 3.3 copy-start.8
  165.8 3.9 copy-start.7
  168.6 1.1 copy-start.12
  207.4 1.4 copy-start.5
  (1 other events, 0.8 us)
Sparse Core Ops, SparseCore 0:
  207.5 174.2 all-reduce.4
where the time goes:
time: 402 us; the launch traced here: 395 us
  waiting for transfers between devices  171 us (43%)
  local copies, waits for them, and re-layouts  99.5 us (25%)
  matrix products  61.4 us (15%)
  starting transfers between devices  28.8 us (7%)
  other arithmetic  19 us (5%)
  between operations  15.1 us (4%)
    psum x1, waiting for transfers between devices, body(): lax.psum((grad_encode, grad_conv, grad_head), ('sim', 'grp'))  166 us
    unnamed x86, local copies, waits for them, and re-layouts  36.3 us
    dot_general x2, matrix products, advance(): jnp.einsum('cxyzp,pq->cxyzq', field, stencil, precision=lax.Precision.HIG...  24.5 us
    dot_general x2, matrix products, advance(): jnp.einsum('cxyzq,pq->cxyzp', beside - faces, select, precision=lax.Preci...  14.5 us
    ppermute x4, starting transfers between devices, passed_along(): return lax.ppermute(value, axis, pairs)  10.8 us
    ppermute x4, starting transfers between devices, from_behind(): return lax.ppermute(block, axis, route)  9.3 us
  transfers between devices with their start and end apart: 11, of which 3 were waited for; matrix products, arithmetic and copies ran while one was open for 16% of the time, Pallas kernels for 0%

commit v1 on v0

v1 whole, which is shorter than its diff:
```python
import functools

import jax
import jax.numpy as jnp
import ml_dtypes
import numpy as np
from jax import lax
from jax.experimental import pallas as pl
from jax.experimental.pallas import tpu as pltpu
from jax.sharding import PartitionSpec as P

NP = 8
EX = 2
EY = 4
STEPS = 2

VISCOSITY = 0.2
TIME_STEP = 0.005
PENALTY = 100.0
LOSS_WEIGHT = 64.0
FACE_RATE = TIME_STEP * VISCOSITY * PENALTY

F32 = jnp.float32
BF16 = jnp.bfloat16
VMEM_LIMIT = 40 * 1024 * 1024


def derivative_matrix(count):
    places = np.arange(count)
    points = -np.cos(np.pi * places / (count - 1))
    weights = np.where(places % 2 == 0, 1.0, -1.0)
    weights[0] = weights[0] * 0.5
    weights[count - 1] = weights[count - 1] * 0.5
    identity = np.eye(count)
    spread = points[:, None] - points[None, :] + identity
    deriv = weights[None, :] / weights[:, None] / spread
    deriv = deriv * (1.0 - identity)
    return deriv - identity * deriv.sum(axis=1)[:, None]


def short(table):
    return np.asarray(table, np.float32).astype(ml_dtypes.bfloat16)


def in_three(table):
    table = np.asarray(table, np.float32)
    high = table.astype(ml_dtypes.bfloat16)
    low = (table - high.astype(np.float32)).astype(ml_dtypes.bfloat16)
    return np.concatenate([high, high, low], axis=0)


@functools.lru_cache(maxsize=None)
def element_tables():
    count = NP
    deriv = derivative_matrix(count)
    single = np.eye(count)
    square = np.eye(count * count)
    along_x = np.kron(deriv, square)
    along_y = np.kron(single, np.kron(deriv, single))
    along_z = np.kron(square, deriv)
    laplace = along_x @ along_x + along_y @ along_y + along_z @ along_z
    half = count**3 // 2
    grid = np.arange(count**3).reshape(count, count, count)
    final = count - 1
    faces = [
        grid[0].ravel(),
        grid[final].ravel(),
        grid[:, 0].ravel(),
        grid[:, final].ravel(),
        grid[:, :, 0].ravel(),
        grid[:, :, final].ravel(),
    ]

    def pick(which):
        table = np.zeros((count**3, count * count))
        table[which, np.arange(count * count)] = 1.0
        return table

    picks = [pick(which) for which in faces]
    none = np.zeros_like(picks[0])
    taken = np.concatenate([picks[i] for i in (1, 0, 3, 2, 5, 4)], axis=1)
    placed = np.concatenate(picks, axis=1).T
    shares = np.concatenate(picks, axis=1).sum(axis=1)[None, :]
    bottom = np.zeros((count**3, count * count))
    for first in range(count):
        for middle in range(count):
            for inner in range(count):
                bottom[grid[first, middle, inner], first * count + inner] = (
                    VISCOSITY * deriv[0, middle]
                )
    return {
        "lap": in_three(TIME_STEP * VISCOSITY * laplace.T),
        "kx": in_three(-TIME_STEP * along_x.T),
        "ky": in_three(-TIME_STEP * along_y.T[:half, :half]),
        "kz": in_three(-TIME_STEP * along_z.T[:half, :half]),
        "taken": short(taken),
        "placed": short(placed),
        "keep": np.asarray(1.0 - FACE_RATE * shares, np.float32),
        "low_first": short(np.concatenate([picks[2], none], axis=1)),
        "low_second": short(np.concatenate([none, picks[2]], axis=1)),
        "top_first": short(np.concatenate([picks[3], none], axis=1)),
        "top_second": short(np.concatenate([none, picks[3]], axis=1)),
        "wall_first": in_three(np.concatenate([bottom, none], axis=1)),
        "wall_second": in_three(np.concatenate([none, bottom], axis=1)),
    }


def dot(left, right):
    return jnp.dot(left, right, preferred_element_type=F32)


def dot_nt(left, right):
    return lax.dot_general(left, right, (((1,), (1,)), ((), ())), preferred_element_type=F32)


def split_two(value):
    high = value.astype(BF16)
    return high, (value - high.astype(F32)).astype(BF16)


def moved(order, value):
    high = value.astype(BF16)
    rest = value - high.astype(F32)
    middle, low = split_two(rest)
    return dot(order, high) + dot(order, middle) + dot(order, low)


def slot_matrix(slots):
    count = slots.shape[1]
    rows = lax.broadcasted_iota(jnp.int32, (count, count), 0)
    return jnp.where(rows == slots, 1.0, 0.0).astype(F32)


def layer_rows(value, layer, ez):
    step = EY * ez
    start = layer * ez
    return value[start : start + ez], value[step + start : step + start + ez]


def write_edges(fields, tabs, outs, ez):
    lf, ls, tf, ts = tabs
    to_left, to_right, to_below, to_above = outs
    side = NP * NP
    half = EY * ez // 2
    last = NP * side - side
    for c, field in enumerate(fields):
        near = field[0 : 2 * half, 0:side]
        far = field[2 * half : 4 * half, last : last + side]
        to_left[c] = jnp.concatenate([near[:half], near[half:]], axis=1).astype(BF16)
        to_right[c] = jnp.concatenate([far[:half], far[half:]], axis=1).astype(BF16)
        one, two = layer_rows(field, 0, ez)
        to_below[c] = (dot(one.astype(BF16), lf[...]) + dot(two.astype(BF16), ls[...])).astype(BF16)
        one, two = layer_rows(field, EY - 1, ez)
        to_above[c] = (dot(one.astype(BF16), tf[...]) + dot(two.astype(BF16), ts[...])).astype(BF16)


def add_edges(part, c, from_left, from_right, from_below, from_above, tabs, ez):
    lf, ls, tf, ts = tabs
    side = NP * NP
    half = EY * ez // 2
    width = NP * side
    value = part[c]
    left = FACE_RATE * from_left[c].astype(F32)
    right = FACE_RATE * from_right[c].astype(F32)
    below = from_below[c]
    above = from_above[c]
    rest = jnp.zeros((half, width - side), F32)
    x_add = jnp.concatenate(
        [
            jnp.concatenate([left[:, :side], rest], axis=1),
            jnp.concatenate([left[:, side:], rest], axis=1),
            jnp.concatenate([rest, right[:, :side]], axis=1),
            jnp.concatenate([rest, right[:, side:]], axis=1),
        ],
        axis=0,
    )
    none = jnp.zeros(((EY - 2) * ez, width), F32)
    y_add = jnp.concatenate(
        [
            dot_nt(below, lf[...]),
            none,
            dot_nt(above, tf[...]),
            dot_nt(below, ls[...]),
            none,
            dot_nt(above, ts[...]),
        ],
        axis=0,
    )
    return value + x_add + FACE_RATE * y_add


def prepare_kernel(vel, slots, lf, ls, tf, ts, field, to_left, to_right, to_below, to_above):
    ez = vel.shape[1] // (EX * EY)
    order = slot_matrix(slots[...]).T.astype(BF16)
    fields = [moved(order, vel[c]) for c in range(3)]
    for c in range(3):
        field[c] = fields[c]
    write_edges(fields, (lf, ls, tf, ts), (to_left, to_right, to_below, to_above), ez)


def inside_kernel(field, lap, kx, ky, kz, taken, placed, keep, part):
    rows = field.shape[1]
    width = field.shape[2]
    ez = rows // (EX * EY)
    half = width // 2
    whole = field[...].reshape(3 * rows, width)
    high, low = split_two(whole)
    lanes = lax.broadcasted_iota(jnp.int32, (1, 2 * NP * NP), 1)
    first = lanes < NP * NP

    faces = dot(high, taken[...])
    in_x = faces[:, 0 : 2 * NP * NP].reshape(3, EX, EY * ez, 2 * NP * NP)
    beside_x = jnp.concatenate(
        [
            jnp.where(first, 0.0, in_x[:, 1:2]),
            jnp.where(first, in_x[:, 0:1], 0.0),
        ],
        axis=1,
    ).reshape(3 * rows, 2 * NP * NP)
    in_y = faces[:, 2 * NP * NP : 4 * NP * NP].reshape(3 * EX, EY, ez, 2 * NP * NP)
    wall = jnp.zeros((3 * EX, 1, ez, 2 * NP * NP), F32)
    beside_y = jnp.where(
        first,
        jnp.concatenate([wall, in_y[:, :-1]], axis=1),
        jnp.concatenate([in_y[:, 1:], wall], axis=1),
    ).reshape(3 * rows, 2 * NP * NP)
    in_z = faces[:, 4 * NP * NP :].reshape(3 * EX * EY, ez, 2 * NP * NP)
    beside_z = jnp.where(
        first, pltpu.roll(in_z, 1, 1), pltpu.roll(in_z, ez - 1, 1)
    ).reshape(3 * rows, 2 * NP * NP)
    beside = jnp.concatenate([beside_x, beside_y, beside_z], axis=1).astype(BF16)

    three = jnp.concatenate([high, low, high], axis=1)
    for n in range(2):
        cols = slice(n * half, (n + 1) * half)
        own = jnp.concatenate([high[:, cols], low[:, cols], high[:, cols]], axis=1)
        value = whole[:, cols] * keep[:, cols] + dot(three, lap[:, cols])
        value = value + FACE_RATE * dot(beside, placed[:, cols])
        for d, slope in enumerate((dot(three, kx[:, cols]), dot(own, ky[...]), dot(own, kz[...]))):
            speed = field[d][:, cols]
            value = value + (slope.reshape(3, rows, half) * speed[None]).reshape(3 * rows, half)
        part[:, :, cols] = value.reshape(3, rows, half)


def join_kernel(
    part, from_left, from_right, from_below, from_above, lf, ls, tf, ts,
    field, to_left, to_right, to_below, to_above,
):
    ez = part.shape[1] // (EX * EY)
    tabs = (lf, ls, tf, ts)
    fields = [
        add_edges(part, c, from_left, from_right, from_below, from_above, tabs, ez)
        for c in range(3)
    ]
    for c in range(3):
        field[c] = fields[c]
    write_edges(fields, tabs, (to_left, to_right, to_below, to_above), ez)


def encode_kernel(
    part, from_left, from_right, from_below, from_above, lf, ls, tf, ts, wall_one, wall_two,
    w_encode, field, snapshot, target, z1, h1,
):
    ez = part.shape[1] // (EX * EY)
    tabs = (lf, ls, tf, ts)
    fields = [
        add_edges(part, c, from_left, from_right, from_below, from_above, tabs, ez)
        for c in range(3)
    ]
    for c in range(3):
        field[c] = fields[c]
    high0, low0 = split_two(fields[0])
    high2, low2 = split_two(fields[2])
    snap = jnp.concatenate([high0, high2], axis=1)
    snapshot[...] = snap
    target[...] = (
        dot(jnp.concatenate([high0, low0, high0], axis=1), wall_one[...])
        + dot(jnp.concatenate([high2, low2, high2], axis=1), wall_two[...])
    ).astype(BF16)
    hidden = dot(snap, w_encode[...])
    z1[...] = hidden
    h1[...] = (hidden * jax.nn.sigmoid(hidden)).astype(BF16)


def restore_kernel(field, slots, out):
    order = slot_matrix(slots[...]).astype(BF16)
    for c in range(3):
        out[c] = moved(order, field[c])


def silu_grad(value):
    sigma = jax.nn.sigmoid(value)
    return sigma * (1.0 + value * (1.0 - sigma))


def with_layers(own, behind, ahead, ez, groups):
    channels = own.shape[-1]
    place = lax.axis_index("grp")
    grid = own[...].astype(F32).reshape(EX, EY, ez, channels)
    before = behind[...].reshape(EX, EY, ez, channels)[:, EY - 1 :].astype(F32)
    after = ahead[...].reshape(EX, EY, ez, channels)[:, :1].astype(F32)
    before = jnp.where(place > 0, before, 0.0)
    after = jnp.where(place < groups - 1, after, 0.0)
    return jnp.concatenate([before, grid, after], axis=1)


def along_span(grid, ez, groups):
    shape = grid.shape
    rows = int(np.prod(shape[:-1]))
    crop = ez // groups
    flat = grid.reshape(rows, shape[-1])
    place = lax.rem(lax.broadcasted_iota(jnp.int32, (rows, 1), 0), crop)
    before = jnp.where(place == 0, 0.0, pltpu.roll(flat, 1, 0))
    after = jnp.where(place == crop - 1, 0.0, pltpu.roll(flat, rows - 1, 0))
    return before.reshape(shape), after.reshape(shape)


def forward_kernel(groups, total, h1, behind, ahead, w_conv, w_head, target, dz2, h2, resid, padded, z2):
    rows, channels = h1.shape
    ez = rows // (EX * EY)
    grid = with_layers(h1, behind, ahead, ez, groups)
    before, after = along_span(grid, ez, groups)
    padded[...] = jnp.concatenate([before, grid, after], axis=-1).astype(BF16)
    half = rows // 2
    for dy in range(3):
        taken = padded[:, dy : dy + EY].reshape(EX, half, 3 * channels)
        first = 3 * dy
        both = dot(taken.reshape(rows, 3 * channels), w_conv[9 + first : 12 + first].reshape(-1, channels))
        ahead_x = dot(taken[1], w_conv[18 + first : 21 + first].reshape(-1, channels))
        behind_x = dot(taken[0], w_conv[first : 3 + first].reshape(-1, channels))
        step = both + jnp.concatenate([ahead_x, behind_x], axis=0)
        if dy == 0:
            z2[...] = step
        else:
            z2[...] += step
    hidden = z2[...]
    act = (hidden * jax.nn.sigmoid(hidden)).astype(BF16)
    output = dot(act, w_head[...])
    miss = (LOSS_WEIGHT * (output - target[...].astype(F32)) / total).astype(BF16)
    h2[...] = act
    resid[...] = miss
    dz2[...] = (dot_nt(miss, w_head[...]) * silu_grad(hidden)).astype(BF16)


def back_kernel(groups, dz2, behind, ahead, w_conv, z1, snapshot, h2, resid, out, dh1):
    rows, channels = dz2.shape
    ez = rows // (EX * EY)
    half = rows // 2
    grid = with_layers(dz2, behind, ahead, ez, groups)
    before, after = along_span(grid, ez, groups)
    shifted = [part.astype(BF16) for part in (after, grid, before)]
    features = snapshot.shape[1]
    out[:, features:] = dot(h2[...].astype(F32).T.astype(BF16), resid[...]).astype(BF16)
    for dy in range(3):
        for dz in range(3):
            tap = 3 * dy + dz
            taken = shifted[dz][:, 2 - dy : 2 - dy + EY].reshape(EX, half, channels)
            both = dot_nt(taken.reshape(rows, channels), w_conv[9 + tap])
            ahead_x = dot_nt(taken[0], w_conv[18 + tap])
            behind_x = dot_nt(taken[1], w_conv[tap])
            step = both + jnp.concatenate([behind_x, ahead_x], axis=0)
            if tap == 0:
                dh1[...] = step
            else:
                dh1[...] += step
    dz1 = dh1[...] * silu_grad(z1[...])
    out[:, :features] = dot(dz1.T.astype(BF16), snapshot[...]).astype(BF16)


def taps_kernel(groups, h_own, h_one, h_two, h_three, d_own, d_one, d_two, d_three, out, h_all, r_all):
    rows, channels = h_own.shape
    ez = rows // (EX * EY)
    quarter = channels // groups
    crop = ez // groups
    place = lax.axis_index("grp")
    layer = EY * ez
    lane = lax.broadcasted_iota(jnp.int32, (channels, channels), 1)
    channel = lax.broadcasted_iota(jnp.int32, (channels, channels), 0)
    chosen = jnp.where(
        (channel == place * quarter + lax.rem(lane, quarter)) & (lane < 3 * quarter), 1.0, 0.0
    ).astype(BF16)
    pairs = ((h_own, d_own), (h_one, d_one), (h_two, d_two), (h_three, d_three))
    for k, (h, d) in enumerate(pairs):
        at = lax.rem(place - k + groups, groups)
        mine = dot(d[...], chosen)
        for x in range(EX):
            h_all[x, at] = h[x * layer : (x + 1) * layer]
            r_all[x, at] = mine[x * layer : (x + 1) * layer]
    deep = groups * layer
    flat = r_all[...].reshape(EX * deep, channels)
    spot = lax.rem(lax.broadcasted_iota(jnp.int32, (EX * deep, 1), 0), crop)
    lane = lax.broadcasted_iota(jnp.int32, (1, channels), 1)
    after = jnp.where(spot == crop - 1, 0.0, pltpu.roll(flat, EX * deep - 1, 0))
    before = jnp.where(spot == 0, 0.0, pltpu.roll(flat, 1, 0))
    mixed = jnp.where(lane < quarter, after, jnp.where(lane < 2 * quarter, flat, before))
    turned = mixed.T
    spot = lax.rem(lax.broadcasted_iota(jnp.int32, (1, EX * deep), 1), deep)
    up = jnp.where(spot >= deep - ez, 0.0, pltpu.roll(turned, EX * deep - ez, 1))
    down = jnp.where(spot < ez, 0.0, pltpu.roll(turned, ez, 1))
    whole = h_all[...].reshape(EX * deep, channels)
    for dy, side in enumerate((up, turned, down)):
        side = side.astype(BF16)
        for dx in range(3):
            if dx == 0:
                got = dot(side[:, deep:], whole[:deep])
            elif dx == 1:
                got = dot(side, whole)
            else:
                got = dot(side[:, :deep], whole[deep:])
            start = (9 * dx + 3 * dy) * quarter
            out[start : start + 3 * quarter] = got[: 3 * quarter].astype(BF16)


def call(kernel, outs, scratch=(), flops=0):
    return pl.pallas_call(
        kernel,
        out_shape=outs,
        scratch_shapes=list(scratch),
        compiler_params=pltpu.CompilerParams(vmem_limit_bytes=VMEM_LIMIT),
        cost_estimate=pl.CostEstimate(flops=flops, bytes_accessed=4_000_000, transcendentals=0),
    )


def shaped(shape, kind):
    return jax.ShapeDtypeStruct(shape, kind)


def ring(value, axis, steps):
    count = lax.axis_size(axis)
    return lax.ppermute(value, axis, [(i, (i + steps) % count) for i in range(count)])


def line(value, axis, steps):
    count = lax.axis_size(axis)
    return lax.ppermute(value, axis, [(i, i + steps) for i in range(count) if 0 <= i + steps < count])


def exchanged(edges):
    to_left, to_right, to_below, to_above = edges
    from_left = ring(to_right, "sim", 1)
    from_right = ring(to_left, "sim", -1)
    from_below = line(to_above, "grp", 1)
    from_above = line(to_below, "grp", -1)
    return from_left, from_right, from_below, from_above


def body(velocity, slot_of, w_encode, w_conv, w_head):
    tables = {name: jnp.asarray(table) for name, table in element_tables().items()}
    block = velocity[0, 0]
    slots = slot_of[0]
    rows, width = block.shape[1:]
    ez = rows // (EX * EY)
    channels = w_encode.shape[1]
    features = w_encode.shape[0]
    outputs = w_head.shape[1]
    sims = lax.axis_size("sim")
    groups = lax.axis_size("grp")
    total = rows * sims * groups
    quarter = channels // groups

    whole = shaped((3, rows, width), F32)
    x_edge = shaped((3, EY * ez // 2, 2 * NP * NP), BF16)
    y_edge = shaped((3, ez, 2 * NP * NP), BF16)
    edge_shapes = (x_edge, x_edge, y_edge, y_edge)
    picks = [tables[name] for name in ("low_first", "low_second", "top_first", "top_second")]
    inside = [tables[name] for name in ("lap", "kx", "ky", "kz", "taken", "placed", "keep")]

    field, *edges = call(prepare_kernel, (whole,) + edge_shapes, flops=10**9)(block, slots, *picks)
    halos = exchanged(edges)
    part = call(inside_kernel, whole, flops=8 * 10**9)(field, *inside)
    field, *edges = call(join_kernel, (whole,) + edge_shapes, flops=10**9)(part, *halos, *picks)
    halos = exchanged(edges)
    part = call(inside_kernel, whole, flops=8 * 10**9)(field, *inside)
    field, snapshot, target, z1, h1 = call(
        encode_kernel,
        (
            whole,
            shaped((rows, features), BF16),
            shaped((rows, outputs), BF16),
            shaped((rows, channels), F32),
            shaped((rows, channels), BF16),
        ),
        flops=10**9,
    )(part, *halos, *picks, tables["wall_first"], tables["wall_second"], w_encode)

    h_one = ring(h1, "grp", 1)
    h_three = ring(h1, "grp", -1)
    h_two = ring(h1, "grp", 2)
    rows_bf = shaped((rows, channels), BF16)
    dz2, h2, resid = call(
        functools.partial(forward_kernel, groups, total),
        (rows_bf, rows_bf, shaped((rows, outputs), BF16)),
        (
            pltpu.VMEM((EX, EY + 2, ez, 3 * channels), BF16),
            pltpu.VMEM((rows, channels), F32),
        ),
        flops=10**9,
    )(h1, h_one, h_three, w_conv, w_head, target)

    d_one = ring(dz2, "grp", 1)
    d_three = ring(dz2, "grp", -1)
    d_two = ring(dz2, "grp", 2)
    dense = call(
        functools.partial(back_kernel, groups),
        shaped((channels, features + outputs), BF16),
        (pltpu.VMEM((rows, channels), F32),),
        flops=2 * 10**9,
    )(dz2, d_one, d_three, w_conv, z1, snapshot, h2, resid)
    taps = call(
        functools.partial(taps_kernel, groups),
        shaped((27 * quarter, channels), BF16),
        (
            pltpu.VMEM((EX, groups, EY * ez, channels), BF16),
            pltpu.VMEM((EX, groups, EY * ez, channels), F32),
        ),
        flops=2 * 10**9,
    )(h1, h_one, h_two, h_three, dz2, d_one, d_two, d_three)

    velocity_next = call(restore_kernel, whole, flops=10**9)(field, slots)

    tap_rows = 27 * quarter // sims
    taps = lax.all_to_all(taps.reshape(sims, tap_rows, channels), "sim", 0, 0, tiled=True)
    taps = jnp.sum(taps.astype(F32), axis=0).astype(BF16)
    own_rows = quarter // sims
    dense = dense.reshape(groups, sims, own_rows, features + outputs).transpose(1, 0, 2, 3)
    dense = dense.reshape(sims * groups, own_rows, features + outputs)
    dense = lax.all_to_all(dense, ("sim", "grp"), 0, 0, tiled=True)
    dense = jnp.sum(dense.astype(F32), axis=0).astype(BF16)
    extra = -(features + outputs) % channels
    dense = jnp.pad(dense, ((0, 0), (0, extra)))
    mine = jnp.concatenate([taps, dense.reshape(-1, channels)], axis=0)
    everything = lax.all_gather(mine, "sim")
    taps = everything[:, :tap_rows].reshape(27, quarter, channels).astype(F32)
    dense = everything[:, tap_rows:].reshape(quarter, -1)[:, : features + outputs].astype(F32)
    return (
        velocity_next[None, None],
        dense[:, :features].T,
        taps.transpose(0, 2, 1),
        dense[:, features:],
    )


def solution(mesh):
    placed = (P("sim", "grp", None, None, None), P("sim", "grp", None), P(), P(), P())
    return jax.shard_map(
        body,
        mesh=mesh,
        in_specs=placed,
        out_specs=(
            P("sim", "grp", None, None, None),
            P(None, "grp"),
            P(None, None, "grp"),
            P("grp", None),
        ),
        check_vma=False,
    )
```

time: 402 us -> 166 us (0.41); the launches traced: 395 us -> 165 us
  waiting for transfers between devices: 171 us -> 81.5 us
  local copies, waits for them, and re-layouts: 99.5 us -> 13.3 us
  matrix products: 61.4 us -> 0 us
  Pallas kernels: 0 us -> 20.2 us
  other arithmetic: 19 us -> 2.33 us
  starting transfers between devices: 28.8 us -> 33.5 us
    psum x1 -> x0, waiting for transfers between devices: 166 us -> none  [body(): lax.psum((grad_encode, grad_conv, grad_head), ('sim', 'grp'))]
    dot_general x15 -> x0, matrix products: 61.4 us -> none  [the longest x2 24.5 us: advance(): jnp.einsum('cxyzp,pq->cxyzq', field, stencil, precision=lax.Precision.HIG...]
    all_gather x0 -> x1, waiting for transfers between devices: none -> 36.4 us  [body(): everything = lax.all_gather(mine, 'sim')]
    unnamed x86 -> x52, local copies, waits for them, and re-layouts: 36.3 us -> 8.76 us
    ppermute x8 -> x14, waiting for transfers between devices: 0.02 us -> 22.8 us  [the longest x10 22.7 us: ring(): lax.ppermute(value, axis, [(i, (i + steps) % count) for i in range(count)])]
    pallas_call x0 -> x9, Pallas kernels: none -> 20.2 us  [the longest x2 9.3 us: body(): part = call(inside_kernel, whole, flops=8 * 10 ** 9)(field, *inside)]
    convert_element_type x17 -> x0, local copies, waits for them, and re-layouts: 18.9 us -> none  [the longest x8 7.81 us: short(): return part.astype(jnp.bfloat16) if part.dtype == jnp.float32 else part]
    all_to_all x2, waiting for transfers between devices: 5.6 us -> 22.4 us  [the longest x1 22.2 us: body(): lax.all_to_all(taps.reshape(sims, tap_rows, channels), 'sim', 0, 0, tiled...]
  transfers between devices with their start and end apart: 11 -> 17, of which waited for: 3 -> 9; matrix products, arithmetic and copies ran while one was open for 16% -> 0% of each run, Pallas kernels for 0% -> 8%
where the time goes in v1:
time: 166 us; the launch traced here: 165 us
  waiting for transfers between devices  81.5 us (49%)
  starting transfers between devices  33.5 us (20%)
  Pallas kernels  20.2 us (12%)
  between operations  14.4 us (9%)
  local copies, waits for them, and re-layouts  13.3 us (8%)
  other arithmetic  2.33 us (1%)
    all_gather x1, waiting for transfers between devices, body(): everything = lax.all_gather(mine, 'sim')  36.4 us
    ppermute x10, waiting for transfers between devices, ring(): lax.ppermute(value, axis, [(i, (i + steps) % count) for i in range(count)])  22.7 us
    all_to_all x1, waiting for transfers between devices, body(): lax.all_to_all(taps.reshape(sims, tap_rows, channels), 'sim', 0, 0, tiled...  22.2 us
    ppermute x10, starting transfers between devices, ring(): lax.ppermute(value, axis, [(i, (i + steps) % count) for i in range(count)])  15.4 us
    pallas_call x2, Pallas kernels, body(): part = call(inside_kernel, whole, flops=8 * 10 ** 9)(field, *inside)  9.3 us
    ppermute x4, starting transfers between devices, line(): lax.ppermute(value, axis, [(i, i + steps) for i in range(count) if 0 <= i...  9 us
    unnamed x52, local copies, waits for them, and re-layouts  8.76 us
    all_to_all x1, starting transfers between devices, body(): lax.all_to_all(taps.reshape(sims, tap_rows, channels), 'sim', 0, 0, tiled...  6.42 us
  transfers between devices with their start and end apart: 17, of which 9 were waited for; matrix products, arithmetic and copies ran while one was open for 0% of the time, Pallas kernels for 8%

profile of v1, /device:TPU:0, one launch (start us, length us, event | category | flops | bytes accessed | tf_op | source)
XLA Modules:
  0.0 165.2 jit_solution(15049651531754539877)
XLA Ops:
  7.2 1.4 copy-done.2
  14.0 2.4 %collective-permute-start.2 = (bf16[3,32,128]{2,1,0:T(8,128)(2,1)S(1)}, bf16[3,32,128]{2,1,0:T(8,128)(2,1)S(1)}, u32[]{:S(2)}, u32[]{:S(2)}) collective-permute-start(bf16[3,32,128]{2,1,0:T(8,128)(2,1)S(1)} %get-tuple-element.25), channel_id=1, source_target_pairs={{0,1},{1,2},{2,3},{4,5},{5,6},{6,7},{8,9},{9,10},{10,11},{12,13},{... | collective-permute-start | bytes 73736 | tf_op jit(solution)/shard_map/ppermute | solution.py:435
  17.6 2.4 %collective-permute-start = (bf16[3,64,128]{2,1,0:T(8,128)(2,1)S(1)}, bf16[3,64,128]{2,1,0:T(8,128)(2,1)S(1)}, u32[]{:S(2)}, u32[]{:S(2)}) collective-permute-start(bf16[3,64,128]{2,1,0:T(8,128)(2,1)S(1)} %get-tuple-element.23), channel_id=1, source_target_pairs={{0,4},{4,8},{8,12},{12,16},{16,20},{20,24},{24,28},{28,0},{1,5},{5... | collective-permute-start | bytes 147464 | tf_op jit(solution)/shard_map/ppermute | solution.py:430
  20.0 3.1 %collective-permute-start.1 = (bf16[3,64,128]{2,1,0:T(8,128)(2,1)S(1)}, bf16[3,64,128]{2,1,0:T(8,128)(2,1)S(1)}, u32[]{:S(2)}, u32[]{:S(2)}) collective-permute-start(bf16[3,64,128]{2,1,0:T(8,128)(2,1)S(1)} %get-tuple-element.24), channel_id=1, source_target_pairs={{0,28},{4,0},{8,4},{12,8},{16,12},{20,16},{24,20},{28,24},{1,29},{... | collective-permute-start | bytes 147464 | tf_op jit(solution)/shard_map/ppermute | solution.py:430
  26.1 4.7 %shard_map.202.part = f32[3,256,512]{2,1,0:T(8,128)S(1)} custom-call(f32[3,256,512]{2,1,0:T(8,128)S(1)} %get-tuple-element.22.field, bf16[1536,512]{1,0:T(8,128)(2,1)S(1)} %copy-done.7, bf16[1536,512]{1,0:T(8,128)(2,1)S(1)} %copy-done.6, bf16[768,256]{1,0:T(8,128)(2,1)S(1)} %copy-done.15, bf16[768,256]{1,0:T(8,128)(2,1)S(1)} %copy-done.13, ...), custom_call_target="tpu_custom_call" | custom-call | flops 8000000000 | bytes 4000000 | tf_op jit(solution)/shard_map/pallas_call | solution.py:470
  31.8 4.1 %collective-permute-start.6 = (bf16[3,32,128]{2,1,0:T(8,128)(2,1)S(1)}, bf16[3,32,128]{2,1,0:T(8,128)(2,1)S(1)}, u32[]{:S(2)}, u32[]{:S(2)}) collective-permute-start(bf16[3,32,128]{2,1,0:T(8,128)(2,1)S(1)} %get-tuple-element.30), channel_id=1, source_target_pairs={{0,1},{1,2},{2,3},{4,5},{5,6},{6,7},{8,9},{9,10},{10,11},{12,13},{... | collective-permute-start | bytes 73736 | tf_op jit(solution)/shard_map/ppermute | solution.py:435
  37.2 4.7 %collective-permute-start.5 = (bf16[3,64,128]{2,1,0:T(8,128)(2,1)S(1)}, bf16[3,64,128]{2,1,0:T(8,128)(2,1)S(1)}, u32[]{:S(2)}, u32[]{:S(2)}) collective-permute-start(bf16[3,64,128]{2,1,0:T(8,128)(2,1)S(1)} %get-tuple-element.29), channel_id=1, source_target_pairs={{0,28},{4,0},{8,4},{12,8},{16,12},{20,16},{24,20},{28,24},{1,29},{... | collective-permute-start | bytes 147464 | tf_op jit(solution)/shard_map/ppermute | solution.py:430
  42.0 4.6 %shard_map.204.part = f32[3,256,512]{2,1,0:T(8,128)S(1)} custom-call(f32[3,256,512]{2,1,0:T(8,128)S(1)} %get-tuple-element.27.field, bf16[1536,512]{1,0:T(8,128)(2,1)S(1)} %copy-done.7, bf16[1536,512]{1,0:T(8,128)(2,1)S(1)} %copy-done.6, bf16[768,256]{1,0:T(8,128)(2,1)S(1)} %copy-done.16, bf16[768,256]{1,0:T(8,128)(2,1)S(1)} %copy-done.14, ...), custom_call_target="tpu_custom_call" | custom-call | flops 8000000000 | bytes 4000000 | tf_op jit(solution)/shard_map/pallas_call | solution.py:473
  48.0 2.3 %collective-permute-start.10 = (bf16[256,256]{1,0:T(8,128)(2,1)S(1)}, bf16[256,256]{1,0:T(8,128)(2,1)S(1)}, u32[]{:S(2)}, u32[]{:S(2)}) collective-permute-start(bf16[256,256]{1,0:T(8,128)(2,1)S(1)} %get-tuple-element.33.h1.h_own), channel_id=1, source_target_pairs={{0,3},{1,0},{2,1},{3,2},{4,7},{5,4},{6,5},{7,6},{8,11},{9,8},{10,9... | collective-permute-start | bytes 393224 | tf_op jit(solution)/shard_map/ppermute | solution.py:430
  50.5 2.3 %collective-permute-done.10.ahead.h_three = bf16[256,256]{1,0:T(8,128)(2,1)S(1)} collective-permute-done((bf16[256,256]{1,0:T(8,128)(2,1)S(1)}, bf16[256,256]{1,0:T(8,128)(2,1)S(1)}, u32[]{:S(2)}, u32[]{:S(2)}) %collective-permute-start.10) | collective-permute-done | bytes 131104 | tf_op jit(solution)/shard_map/ppermute | solution.py:430
  52.8 3.6 %collective-permute-done.8.behind.h_one = bf16[256,256]{1,0:T(8,128)(2,1)S(1)} collective-permute-done((bf16[256,256]{1,0:T(8,128)(2,1)S(1)}, bf16[256,256]{1,0:T(8,128)(2,1)S(1)}, u32[]{:S(2)}, u32[]{:S(2)}) %collective-permute-start.8) | collective-permute-done | bytes 131104 | tf_op jit(solution)/shard_map/ppermute | solution.py:430
  58.2 2.2 %collective-permute-done.13.d_three.ahead = bf16[256,256]{1,0:T(8,128)(2,1)S(1)} collective-permute-done((bf16[256,256]{1,0:T(8,128)(2,1)S(1)}, bf16[256,256]{1,0:T(8,128)(2,1)S(1)}, u32[]{:S(2)}, u32[]{:S(2)}) %collective-permute-start.13) | collective-permute-done | bytes 131104 | tf_op jit(solution)/shard_map/ppermute | solution.py:430
  60.3 2.9 %collective-permute-done.11.d_one.behind = bf16[256,256]{1,0:T(8,128)(2,1)S(1)} collective-permute-done((bf16[256,256]{1,0:T(8,128)(2,1)S(1)}, bf16[256,256]{1,0:T(8,128)(2,1)S(1)}, u32[]{:S(2)}, u32[]{:S(2)}) %collective-permute-start.11) | collective-permute-done | bytes 131104 | tf_op jit(solution)/shard_map/ppermute | solution.py:430
  63.3 1.8 %shard_map.209 = bf16[256,1152]{1,0:T(8,128)(2,1)S(1)} custom-call(bf16[256,256]{1,0:T(8,128)(2,1)S(1)} %get-tuple-element.35.d_own.dz2, bf16[256,256]{1,0:T(8,128)(2,1)S(1)} %collective-permute-done.11.d_one.behind, bf16[256,256]{1,0:T(8,128)(2,1)S(1)} %collective-permute-done.13.d_three.ahead, bf16[27,256,256]{2,1,0:T(8,128)(2,1)S(1)} %copy-done, ...), custom_call_target="tpu_custom_call" | custom-call | flops 2000000000 | bytes 4000000 | tf_op jit(solution)/shard_map/pallas_call | solution.py:503
  65.9 2.6 %all-to-all-start.1 = ((bf16[32,8,1152]{2,1,0:T(8,128)(2,1)}), bf16[32,8,1152]{2,1,0:T(8,128)(2,1)S(1)}, u32[]{:S(2)}, u32[]{:S(2)}) async-start(bf16[32,8,1152]{2,1,0:T(8,128)(2,1)} %bitcast.20), calls=%async_computation.1 | async-start | bytes 1179648 | tf_op jit(solution)/shard_map/all_to_all | solution.py:527
  68.5 1.8 %collective-permute-start.9 = (bf16[256,256]{1,0:T(8,128)(2,1)S(1)}, bf16[256,256]{1,0:T(8,128)(2,1)S(1)}, u32[]{:S(2)}, u32[]{:S(2)}) collective-permute-start(bf16[256,256]{1,0:T(8,128)(2,1)S(1)} %get-tuple-element.33.h1.h_own), channel_id=1, source_target_pairs={{0,2},{1,3},{2,0},{3,1},{4,6},{5,7},{6,4},{7,5},{8,10},{9,11},{10,... | collective-permute-start | bytes 393224 | tf_op jit(solution)/shard_map/ppermute | solution.py:430
  70.6 8.6 %collective-permute-done.9.h_two = bf16[256,256]{1,0:T(8,128)(2,1)S(1)} collective-permute-done((bf16[256,256]{1,0:T(8,128)(2,1)S(1)}, bf16[256,256]{1,0:T(8,128)(2,1)S(1)}, u32[]{:S(2)}, u32[]{:S(2)}) %collective-permute-start.9) | collective-permute-done | bytes 131104 | tf_op jit(solution)/shard_map/ppermute | solution.py:430
  79.2 3.2 %collective-permute-done.12.d_two = bf16[256,256]{1,0:T(8,128)(2,1)S(1)} collective-permute-done((bf16[256,256]{1,0:T(8,128)(2,1)S(1)}, bf16[256,256]{1,0:T(8,128)(2,1)S(1)}, u32[]{:S(2)}, u32[]{:S(2)}) %collective-permute-start.12) | collective-permute-done | bytes 131104 | tf_op jit(solution)/shard_map/ppermute | solution.py:430
  82.3 2.7 %shard_map.208 = bf16[1728,256]{1,0:T(8,128)(2,1)} custom-call(bf16[256,256]{1,0:T(8,128)(2,1)S(1)} %get-tuple-element.33.h1.h_own, bf16[256,256]{1,0:T(8,128)(2,1)S(1)} %collective-permute-done.8.behind.h_one, bf16[256,256]{1,0:T(8,128)(2,1)S(1)} %collective-permute-done.9.h_two, bf16[256,256]{1,0:T(8,128)(2,1)S(1)} %collective-permute-done.10.ahead.h_three, ...), custom_call_target="tpu_custom_call" | custom-call | flops 2000000000 | bytes 4000000 | tf_op jit(solution)/shard_map/pallas_call | solution.py:509
  85.2 6.4 %all-to-all-start = ((bf16[8,216,256]{2,1,0:T(8,128)(2,1)}), bf16[8,216,256]{2,1,0:T(8,128)(2,1)S(1)}, u32[]{:S(2)}, u32[]{:S(2)}) async-start(bf16[8,216,256]{2,1,0:T(8,128)(2,1)} %bitcast.3), calls=%async_computation | async-start | bytes 1769472 | tf_op jit(solution)/shard_map/all_to_all | solution.py:522
  91.9 22.2 %all-to-all-done = bf16[8,216,256]{2,1,0:T(8,128)(2,1)S(1)} async-done(((bf16[8,216,256]{2,1,0:T(8,128)(2,1)}), bf16[8,216,256]{2,1,0:T(8,128)(2,1)S(1)}, u32[]{:S(2)}, u32[]{:S(2)}) %all-to-all-start) | async-done | bytes 884768 | tf_op jit(solution)/shard_map/all_to_all | solution.py:522
  114.9 2.0 %shard_map.206 = f32[3,256,512]{2,1,0:T(8,128)} custom-call(f32[3,256,512]{2,1,0:T(8,128)S(1)} %get-tuple-element.32.field, s32[1,256]{1,0:T(1,128)S(1)} %bitcast.18), custom_call_target="tpu_custom_call" | custom-call | flops 1000000000 | bytes 4000000 | tf_op jit(solution)/shard_map/pallas_call | solution.py:519
  116.9 36.4 %all-gather.3.cloned.1.call-done = bf16[2048,256]{1,0:T(8,128)(2,1)} async-done(((bf16[256,256]{1,0:T(8,128)(2,1)}), bf16[2048,256]{1,0:T(8,128)(2,1)}) %all-gather.3.cloned.1.call-update) | async-done | bytes 1048592 | tf_op jit(solution)/shard_map/all_gather | solution.py:532
  156.9 1.4 convert_bitcast_fusion
  (85 shorter events, 21.2 us)
Async XLA Ops:
  12.9 10.2 %copy-start.7 = (bf16[1536,512]{1,0:T(8,128)(2,1)S(1)}, bf16[1536,512]{1,0:T(8,128)(2,1)}, u32[]{:S(2)}) copy-start(bf16[1536,512]{1,0:T(8,128)(2,1)} %constant.32.clone.lap) | copy-start | bytes 4718596
  12.9 10.2 %copy-start.10 = (bf16[384,512]{1,0:T(8,128)(2,1)S(1)}, bf16[384,512]{1,0:T(8,128)(2,1)}, u32[]{:S(2)}) copy-start(bf16[384,512]{1,0:T(8,128)(2,1)} %constant.37.clone.placed) | copy-start | bytes 1179652
  12.9 10.2 %copy-start.25 = (f32[1,512]{1,0:T(1,128)S(1)}, f32[1,512]{1,0:T(1,128)}, u32[]{:S(2)}) copy-start(f32[1,512]{1,0:T(1,128)} %constant.38.clone.keep) | copy-start | bytes 6148
  14.0 16.9 %collective-permute-start.2 = (bf16[3,32,128]{2,1,0:T(8,128)(2,1)S(1)}, bf16[3,32,128]{2,1,0:T(8,128)(2,1)S(1)}, u32[]{:S(2)}, u32[]{:S(2)}) collective-permute-start(bf16[3,32,128]{2,1,0:T(8,128)(2,1)S(1)} %get-tuple-element.25), channel_id=1, source_target_pairs={{0,1},{1,2},{2,3},{4,5},{5,6},{6,7},{8,9},{9,10},{10,11},{12,13},{... | collective-permute-start | bytes 73736 | tf_op jit(solution)/shard_map/ppermute | solution.py:435
  16.3 14.5 %collective-permute-start.3 = (bf16[3,32,128]{2,1,0:T(8,128)(2,1)S(1)}, bf16[3,32,128]{2,1,0:T(8,128)(2,1)S(1)}, u32[]{:S(2)}, u32[]{:S(2)}) collective-permute-start(bf16[3,32,128]{2,1,0:T(8,128)(2,1)S(1)} %get-tuple-element.26), channel_id=1, source_target_pairs={{1,0},{2,1},{3,2},{5,4},{6,5},{7,6},{9,8},{10,9},{11,10},{13,12},{... | collective-permute-start | bytes 73736 | tf_op jit(solution)/shard_map/ppermute | solution.py:435
  17.6 13.2 %collective-permute-start = (bf16[3,64,128]{2,1,0:T(8,128)(2,1)S(1)}, bf16[3,64,128]{2,1,0:T(8,128)(2,1)S(1)}, u32[]{:S(2)}, u32[]{:S(2)}) collective-permute-start(bf16[3,64,128]{2,1,0:T(8,128)(2,1)S(1)} %get-tuple-element.23), channel_id=1, source_target_pairs={{0,4},{4,8},{8,12},{12,16},{16,20},{20,24},{24,28},{28,0},{1,5},{5... | collective-permute-start | bytes 147464 | tf_op jit(solution)/shard_map/ppermute | solution.py:430
  20.0 10.9 %collective-permute-start.1 = (bf16[3,64,128]{2,1,0:T(8,128)(2,1)S(1)}, bf16[3,64,128]{2,1,0:T(8,128)(2,1)S(1)}, u32[]{:S(2)}, u32[]{:S(2)}) collective-permute-start(bf16[3,64,128]{2,1,0:T(8,128)(2,1)S(1)} %get-tuple-element.24), channel_id=1, source_target_pairs={{0,28},{4,0},{8,4},{12,8},{16,12},{20,16},{24,20},{28,24},{1,29},{... | collective-permute-start | bytes 147464 | tf_op jit(solution)/shard_map/ppermute | solution.py:430
  30.8 11.2 %copy-start.12 = (bf16[512,384]{1,0:T(8,128)(2,1)S(1)}, bf16[512,384]{1,0:T(8,128)(2,1)}, u32[]{:S(2)}) copy-start(bf16[512,384]{1,0:T(8,128)(2,1)} %constant.36.clone.taken) | copy-start | bytes 1179652
  30.8 11.1 %copy-start.14 = (bf16[768,256]{1,0:T(8,128)(2,1)S(1)}, bf16[768,256]{1,0:T(8,128)(2,1)}, u32[]{:S(2)}) copy-start(bf16[768,256]{1,0:T(8,128)(2,1)} %constant.35.clone.kz) | copy-start | bytes 1179652
  30.8 11.1 %copy-start.16 = (bf16[768,256]{1,0:T(8,128)(2,1)S(1)}, bf16[768,256]{1,0:T(8,128)(2,1)}, u32[]{:S(2)}) copy-start(bf16[768,256]{1,0:T(8,128)(2,1)} %constant.34.clone.ky) | copy-start | bytes 1179652
  31.8 14.9 %collective-permute-start.6 = (bf16[3,32,128]{2,1,0:T(8,128)(2,1)S(1)}, bf16[3,32,128]{2,1,0:T(8,128)(2,1)S(1)}, u32[]{:S(2)}, u32[]{:S(2)}) collective-permute-start(bf16[3,32,128]{2,1,0:T(8,128)(2,1)S(1)} %get-tuple-element.30), channel_id=1, source_target_pairs={{0,1},{1,2},{2,3},{4,5},{5,6},{6,7},{8,9},{9,10},{10,11},{12,13},{... | collective-permute-start | bytes 73736 | tf_op jit(solution)/shard_map/ppermute | solution.py:435
  35.9 10.8 %collective-permute-start.7 = (bf16[3,32,128]{2,1,0:T(8,128)(2,1)S(1)}, bf16[3,32,128]{2,1,0:T(8,128)(2,1)S(1)}, u32[]{:S(2)}, u32[]{:S(2)}) collective-permute-start(bf16[3,32,128]{2,1,0:T(8,128)(2,1)S(1)} %get-tuple-element.31), channel_id=1, source_target_pairs={{1,0},{2,1},{3,2},{5,4},{6,5},{7,6},{9,8},{10,9},{11,10},{13,12},{... | collective-permute-start | bytes 73736 | tf_op jit(solution)/shard_map/ppermute | solution.py:435
  37.2 9.5 %collective-permute-start.4 = (bf16[3,64,128]{2,1,0:T(8,128)(2,1)S(1)}, bf16[3,64,128]{2,1,0:T(8,128)(2,1)S(1)}, u32[]{:S(2)}, u32[]{:S(2)}) collective-permute-start(bf16[3,64,128]{2,1,0:T(8,128)(2,1)S(1)} %get-tuple-element.28), channel_id=1, source_target_pairs={{0,4},{4,8},{8,12},{12,16},{16,20},{20,24},{24,28},{28,0},{1,5},{5... | collective-permute-start | bytes 147464 | tf_op jit(solution)/shard_map/ppermute | solution.py:430
  37.2 9.5 %collective-permute-start.5 = (bf16[3,64,128]{2,1,0:T(8,128)(2,1)S(1)}, bf16[3,64,128]{2,1,0:T(8,128)(2,1)S(1)}, u32[]{:S(2)}, u32[]{:S(2)}) collective-permute-start(bf16[3,64,128]{2,1,0:T(8,128)(2,1)S(1)} %get-tuple-element.29), channel_id=1, source_target_pairs={{0,28},{4,0},{8,4},{12,8},{16,12},{20,16},{24,20},{28,24},{1,29},{... | collective-permute-start | bytes 147464 | tf_op jit(solution)/shard_map/ppermute | solution.py:430
  48.0 4.8 %collective-permute-start.10 = (bf16[256,256]{1,0:T(8,128)(2,1)S(1)}, bf16[256,256]{1,0:T(8,128)(2,1)S(1)}, u32[]{:S(2)}, u32[]{:S(2)}) collective-permute-start(bf16[256,256]{1,0:T(8,128)(2,1)S(1)} %get-tuple-element.33.h1.h_own), channel_id=1, source_target_pairs={{0,3},{1,0},{2,1},{3,2},{4,7},{5,4},{6,5},{7,6},{8,11},{9,8},{10,9... | collective-permute-start | bytes 393224 | tf_op jit(solution)/shard_map/ppermute | solution.py:430
  50.3 6.2 %collective-permute-start.8 = (bf16[256,256]{1,0:T(8,128)(2,1)S(1)}, bf16[256,256]{1,0:T(8,128)(2,1)S(1)}, u32[]{:S(2)}, u32[]{:S(2)}) collective-permute-start(bf16[256,256]{1,0:T(8,128)(2,1)S(1)} %get-tuple-element.33.h1.h_own), channel_id=1, source_target_pairs={{0,1},{1,2},{2,3},{3,0},{4,5},{5,6},{6,7},{7,4},{8,9},{9,10},{10,1... | collective-permute-start | bytes 393224 | tf_op jit(solution)/shard_map/ppermute | solution.py:430
  57.6 2.8 %collective-permute-start.13 = (bf16[256,256]{1,0:T(8,128)(2,1)S(1)}, bf16[256,256]{1,0:T(8,128)(2,1)S(1)}, u32[]{:S(2)}, u32[]{:S(2)}) collective-permute-start(bf16[256,256]{1,0:T(8,128)(2,1)S(1)} %get-tuple-element.35.d_own.dz2), channel_id=1, source_target_pairs={{0,3},{1,0},{2,1},{3,2},{4,7},{5,4},{6,5},{7,6},{8,11},{9,8},{10,9... | collective-permute-start | bytes 393224 | tf_op jit(solution)/shard_map/ppermute | solution.py:430
  57.7 5.6 %collective-permute-start.11 = (bf16[256,256]{1,0:T(8,128)(2,1)S(1)}, bf16[256,256]{1,0:T(8,128)(2,1)S(1)}, u32[]{:S(2)}, u32[]{:S(2)}) collective-permute-start(bf16[256,256]{1,0:T(8,128)(2,1)S(1)} %get-tuple-element.35.d_own.dz2), channel_id=1, source_target_pairs={{0,1},{1,2},{2,3},{3,0},{4,5},{5,6},{6,7},{7,4},{8,9},{9,10},{10,1... | collective-permute-start | bytes 393224 | tf_op jit(solution)/shard_map/ppermute | solution.py:430
  65.9 19.3 %all-to-all-start.1 = ((bf16[32,8,1152]{2,1,0:T(8,128)(2,1)}), bf16[32,8,1152]{2,1,0:T(8,128)(2,1)S(1)}, u32[]{:S(2)}, u32[]{:S(2)}) async-start(bf16[32,8,1152]{2,1,0:T(8,128)(2,1)} %bitcast.20), calls=%async_computation.1 | async-start | bytes 1179648 | tf_op jit(solution)/shard_map/all_to_all | solution.py:527
  68.5 10.6 %collective-permute-start.9 = (bf16[256,256]{1,0:T(8,128)(2,1)S(1)}, bf16[256,256]{1,0:T(8,128)(2,1)S(1)}, u32[]{:S(2)}, u32[]{:S(2)}) collective-permute-start(bf16[256,256]{1,0:T(8,128)(2,1)S(1)} %get-tuple-element.33.h1.h_own), channel_id=1, source_target_pairs={{0,2},{1,3},{2,0},{3,1},{4,6},{5,7},{6,4},{7,5},{8,10},{9,11},{10,... | collective-permute-start | bytes 393224 | tf_op jit(solution)/shard_map/ppermute | solution.py:430
  70.3 12.0 %collective-permute-start.12 = (bf16[256,256]{1,0:T(8,128)(2,1)S(1)}, bf16[256,256]{1,0:T(8,128)(2,1)S(1)}, u32[]{:S(2)}, u32[]{:S(2)}) collective-permute-start(bf16[256,256]{1,0:T(8,128)(2,1)S(1)} %get-tuple-element.35.d_own.dz2), channel_id=1, source_target_pairs={{0,2},{1,3},{2,0},{3,1},{4,6},{5,7},{6,4},{7,5},{8,10},{9,11},{10,... | collective-permute-start | bytes 393224 | tf_op jit(solution)/shard_map/ppermute | solution.py:430
  85.2 29.6 %copy-start.5 = (s32[1,1,256]{2,1,0:T(1,128)S(1)}, s32[1,1,256]{2,1,0:T(1,128)}, u32[]{:S(2)}) copy-start(s32[1,1,256]{2,1,0:T(1,128)} %param.19) | copy-start | bytes 3076
  85.2 28.8 %all-to-all-start = ((bf16[8,216,256]{2,1,0:T(8,128)(2,1)}), bf16[8,216,256]{2,1,0:T(8,128)(2,1)S(1)}, u32[]{:S(2)}, u32[]{:S(2)}) async-start(bf16[8,216,256]{2,1,0:T(8,128)(2,1)} %bitcast.3), calls=%async_computation | async-start | bytes 1769472 | tf_op jit(solution)/shard_map/all_to_all | solution.py:522
  91.7 61.6 %all-gather.3.cloned.1.call-start = ((), (), s32[]{:S(2)}) async-start(), calls=%async_computation.2 | async-start | bytes 1179648 | tf_op jit(solution)/shard_map/all_gather | solution.py:532
  (19 other events, 71.9 us)
Sparse Core Ops, SparseCore 0:
  115.0 38.1 all-gather.2

commit v2 on v1

--- a/solution.py
+++ b/solution.py
@@ -22,7 +22,7 @@
 
 F32 = jnp.float32
 BF16 = jnp.bfloat16
-VMEM_LIMIT = 40 * 1024 * 1024
+VMEM_LIMIT = 16 * 1024 * 1024
 
 
 def derivative_matrix(count):
@@ -80,7 +80,6 @@
     none = np.zeros_like(picks[0])
     taken = np.concatenate([picks[i] for i in (1, 0, 3, 2, 5, 4)], axis=1)
     placed = np.concatenate(picks, axis=1).T
-    shares = np.concatenate(picks, axis=1).sum(axis=1)[None, :]
     bottom = np.zeros((count**3, count * count))
     for first in range(count):
         for middle in range(count):
@@ -88,21 +87,21 @@
                 bottom[grid[first, middle, inner], first * count + inner] = (
                     VISCOSITY * deriv[0, middle]
                 )
-    return {
-        "lap": in_three(TIME_STEP * VISCOSITY * laplace.T),
-        "kx": in_three(-TIME_STEP * along_x.T),
-        "ky": in_three(-TIME_STEP * along_y.T[:half, :half]),
-        "kz": in_three(-TIME_STEP * along_z.T[:half, :half]),
-        "taken": short(taken),
-        "placed": short(placed),
-        "keep": np.asarray(1.0 - FACE_RATE * shares, np.float32),
-        "low_first": short(np.concatenate([picks[2], none], axis=1)),
-        "low_second": short(np.concatenate([none, picks[2]], axis=1)),
-        "top_first": short(np.concatenate([picks[3], none], axis=1)),
-        "top_second": short(np.concatenate([none, picks[3]], axis=1)),
-        "wall_first": in_three(np.concatenate([bottom, none], axis=1)),
-        "wall_second": in_three(np.concatenate([none, bottom], axis=1)),
-    }
+    first = in_three(TIME_STEP * VISCOSITY * laplace.T)
+    second = in_three(-TIME_STEP * along_x.T)
+    third = np.concatenate(
+        [
+            in_three(-TIME_STEP * along_y.T[:half, :half]),
+            in_three(-TIME_STEP * along_z.T[:half, :half]),
+        ],
+        axis=1,
+    )
+    filled = np.zeros((count**3, count**3 - taken.shape[1]))
+    fourth = short(placed)
+    fifth = short(np.concatenate([taken, filled], axis=1))
+    stencil = np.concatenate([first, second, third, fourth, fifth], axis=0)
+    wall = in_three(np.concatenate([bottom, none, none, bottom], axis=1))
+    return stencil, wall
 
 
 def dot(left, right):
@@ -137,33 +136,62 @@
     return value[start : start + ez], value[step + start : step + start + ez]
 
 
+def edge_tables():
+    side = NP * NP
+    point = lax.broadcasted_iota(jnp.int32, (NP * side, 2 * side), 0)
+    lane = lax.broadcasted_iota(jnp.int32, (NP * side, 2 * side), 1)
+    middle = lax.rem(lax.div(point, NP), NP)
+    place = lax.div(point, side) * NP + lax.rem(point, NP)
+
+    def table(level, shift):
+        return jnp.where((middle == level) & (lane == place + shift), 1.0, 0.0).astype(BF16)
+
+    return table(0, 0), table(0, side), table(NP - 1, 0), table(NP - 1, side)
+
+
+def is_even(axis):
+    return lax.rem(lax.axis_index(axis), 2) == 0
+
+
 def write_edges(fields, tabs, outs, ez):
     lf, ls, tf, ts = tabs
-    to_left, to_right, to_below, to_above = outs
+    pair_x, cross_x, pair_y, cross_y = outs
     side = NP * NP
     half = EY * ez // 2
     last = NP * side - side
+    even_x = is_even("sim")
+    even_y = is_even("grp")
     for c, field in enumerate(fields):
         near = field[0 : 2 * half, 0:side]
         far = field[2 * half : 4 * half, last : last + side]
-        to_left[c] = jnp.concatenate([near[:half], near[half:]], axis=1).astype(BF16)
-        to_right[c] = jnp.concatenate([far[:half], far[half:]], axis=1).astype(BF16)
+        to_left = jnp.concatenate([near[:half], near[half:]], axis=1)
+        to_right = jnp.concatenate([far[:half], far[half:]], axis=1)
+        pair_x[c] = jnp.where(even_x, to_right, to_left).astype(BF16)
+        cross_x[c] = jnp.where(even_x, to_left, to_right).astype(BF16)
         one, two = layer_rows(field, 0, ez)
-        to_below[c] = (dot(one.astype(BF16), lf[...]) + dot(two.astype(BF16), ls[...])).astype(BF16)
+        to_below = dot(one.astype(BF16), lf) + dot(two.astype(BF16), ls)
         one, two = layer_rows(field, EY - 1, ez)
-        to_above[c] = (dot(one.astype(BF16), tf[...]) + dot(two.astype(BF16), ts[...])).astype(BF16)
-
-
-def add_edges(part, c, from_left, from_right, from_below, from_above, tabs, ez):
+        to_above = dot(one.astype(BF16), tf) + dot(two.astype(BF16), ts)
+        pair_y[c] = jnp.where(even_y, to_above, to_below).astype(BF16)
+        cross_y[c] = jnp.where(even_y, to_below, to_above).astype(BF16)
+
+
+def add_edges(part, c, pair_x, cross_x, pair_y, cross_y, tabs, ez):
     lf, ls, tf, ts = tabs
     side = NP * NP
     half = EY * ez // 2
     width = NP * side
     value = part[c]
-    left = FACE_RATE * from_left[c].astype(F32)
-    right = FACE_RATE * from_right[c].astype(F32)
-    below = from_below[c]
-    above = from_above[c]
+    even_x = is_even("sim")
+    even_y = is_even("grp")
+    pair = FACE_RATE * pair_x[c].astype(F32)
+    cross = FACE_RATE * cross_x[c].astype(F32)
+    left = jnp.where(even_x, cross, pair)
+    right = jnp.where(even_x, pair, cross)
+    pair = pair_y[c].astype(F32)
+    cross = cross_y[c].astype(F32)
+    below = jnp.where(even_y, cross, pair).astype(BF16)
+    above = jnp.where(even_y, pair, cross).astype(BF16)
     rest = jnp.zeros((half, width - side), F32)
     x_add = jnp.concatenate(
         [
@@ -177,38 +205,55 @@
     none = jnp.zeros(((EY - 2) * ez, width), F32)
     y_add = jnp.concatenate(
         [
-            dot_nt(below, lf[...]),
+            dot_nt(below, lf),
             none,
-            dot_nt(above, tf[...]),
-            dot_nt(below, ls[...]),
+            dot_nt(above, tf),
+            dot_nt(below, ls),
             none,
-            dot_nt(above, ts[...]),
+            dot_nt(above, ts),
         ],
         axis=0,
     )
     return value + x_add + FACE_RATE * y_add
 
 
-def prepare_kernel(vel, slots, lf, ls, tf, ts, field, to_left, to_right, to_below, to_above):
+def prepare_kernel(vel, slots, field, *edges):
     ez = vel.shape[1] // (EX * EY)
     order = slot_matrix(slots[...]).T.astype(BF16)
     fields = [moved(order, vel[c]) for c in range(3)]
     for c in range(3):
         field[c] = fields[c]
-    write_edges(fields, (lf, ls, tf, ts), (to_left, to_right, to_below, to_above), ez)
-
-
-def inside_kernel(field, lap, kx, ky, kz, taken, placed, keep, part):
+    write_edges(fields, edge_tables(), edges, ez)
+
+
+def face_count(width):
+    point = lax.broadcasted_iota(jnp.int32, (1, width), 1)
+    count = jnp.zeros((1, width), F32)
+    for stride in (NP * NP, NP, 1):
+        index = lax.rem(lax.div(point, stride), NP)
+        count = count + jnp.where((index == 0) | (index == NP - 1), 1.0, 0.0)
+    return count
+
+
+def inside_kernel(field, stencil, part):
     rows = field.shape[1]
     width = field.shape[2]
     ez = rows // (EX * EY)
     half = width // 2
+    chosen = 6 * NP * NP
+    lap = stencil.at[0 : 3 * width]
+    kx = stencil.at[3 * width : 6 * width]
+    kyz = stencil.at[6 * width : 6 * width + 3 * half]
+    start = 6 * width + 3 * half
+    placed = stencil.at[start : start + chosen]
+    taken = stencil.at[start + chosen : start + chosen + width]
+    keep = 1.0 - FACE_RATE * face_count(width)
     whole = field[...].reshape(3 * rows, width)
     high, low = split_two(whole)
     lanes = lax.broadcasted_iota(jnp.int32, (1, 2 * NP * NP), 1)
     first = lanes < NP * NP
 
-    faces = dot(high, taken[...])
+    faces = dot(high, taken[:, :chosen])
     in_x = faces[:, 0 : 2 * NP * NP].reshape(3, EX, EY * ez, 2 * NP * NP)
     beside_x = jnp.concatenate(
         [
@@ -236,37 +281,30 @@
         own = jnp.concatenate([high[:, cols], low[:, cols], high[:, cols]], axis=1)
         value = whole[:, cols] * keep[:, cols] + dot(three, lap[:, cols])
         value = value + FACE_RATE * dot(beside, placed[:, cols])
-        for d, slope in enumerate((dot(three, kx[:, cols]), dot(own, ky[...]), dot(own, kz[...]))):
+        for d, slope in enumerate(
+            (dot(three, kx[:, cols]), dot(own, kyz[:, :half]), dot(own, kyz[:, half:]))
+        ):
             speed = field[d][:, cols]
             value = value + (slope.reshape(3, rows, half) * speed[None]).reshape(3 * rows, half)
         part[:, :, cols] = value.reshape(3, rows, half)
 
 
-def join_kernel(
-    part, from_left, from_right, from_below, from_above, lf, ls, tf, ts,
-    field, to_left, to_right, to_below, to_above,
+def join_kernel(part, pair_x, cross_x, pair_y, cross_y, field, *edges):
+    ez = part.shape[1] // (EX * EY)
+    tabs = edge_tables()
+    fields = [add_edges(part, c, pair_x, cross_x, pair_y, cross_y, tabs, ez) for c in range(3)]
+    for c in range(3):
+        field[c] = fields[c]
+    write_edges(fields, tabs, edges, ez)
+
+
+def encode_kernel(
+    part, pair_x, cross_x, pair_y, cross_y, wall, w_encode,
+    field, snapshot, target, z1, h1,
 ):
     ez = part.shape[1] // (EX * EY)
-    tabs = (lf, ls, tf, ts)
-    fields = [
-        add_edges(part, c, from_left, from_right, from_below, from_above, tabs, ez)
-        for c in range(3)
-    ]
-    for c in range(3):
-        field[c] = fields[c]
-    write_edges(fields, tabs, (to_left, to_right, to_below, to_above), ez)
-
-
-def encode_kernel(
-    part, from_left, from_right, from_below, from_above, lf, ls, tf, ts, wall_one, wall_two,
-    w_encode, field, snapshot, target, z1, h1,
-):
-    ez = part.shape[1] // (EX * EY)
-    tabs = (lf, ls, tf, ts)
-    fields = [
-        add_edges(part, c, from_left, from_right, from_below, from_above, tabs, ez)
-        for c in range(3)
-    ]
+    tabs = edge_tables()
+    fields = [add_edges(part, c, pair_x, cross_x, pair_y, cross_y, tabs, ez) for c in range(3)]
     for c in range(3):
         field[c] = fields[c]
     high0, low0 = split_two(fields[0])
@@ -274,8 +312,8 @@
     snap = jnp.concatenate([high0, high2], axis=1)
     snapshot[...] = snap
     target[...] = (
-        dot(jnp.concatenate([high0, low0, high0], axis=1), wall_one[...])
-        + dot(jnp.concatenate([high2, low2, high2], axis=1), wall_two[...])
+        dot(jnp.concatenate([high0, low0, high0], axis=1), wall[:, : 2 * NP * NP])
+        + dot(jnp.concatenate([high2, low2, high2], axis=1), wall[:, 2 * NP * NP :])
     ).astype(BF16)
     hidden = dot(snap, w_encode[...])
     z1[...] = hidden
@@ -293,12 +331,15 @@
     return sigma * (1.0 + value * (1.0 - sigma))
 
 
-def with_layers(own, behind, ahead, ez, groups):
+def with_layers(own, pair, cross, ez, groups):
     channels = own.shape[-1]
     place = lax.axis_index("grp")
     grid = own[...].astype(F32).reshape(EX, EY, ez, channels)
-    before = behind[...].reshape(EX, EY, ez, channels)[:, EY - 1 :].astype(F32)
-    after = ahead[...].reshape(EX, EY, ez, channels)[:, :1].astype(F32)
+    even = is_even("grp")
+    pair = pair[...].reshape(EX, EY, ez, channels).astype(F32)
+    cross = cross[...].reshape(EX, EY, ez, channels).astype(F32)
+    before = jnp.where(even, cross[:, EY - 1 :], pair[:, EY - 1 :])
+    after = jnp.where(even, pair[:, :1], cross[:, :1])
     before = jnp.where(place > 0, before, 0.0)
     after = jnp.where(place < groups - 1, after, 0.0)
     return jnp.concatenate([before, grid, after], axis=1)
@@ -315,10 +356,10 @@
     return before.reshape(shape), after.reshape(shape)
 
 
-def forward_kernel(groups, total, h1, behind, ahead, w_conv, w_head, target, dz2, h2, resid, padded, z2):
+def forward_kernel(groups, total, h1, pair, cross, w_conv, w_head, target, dz2, h2, resid, padded, z2):
     rows, channels = h1.shape
     ez = rows // (EX * EY)
-    grid = with_layers(h1, behind, ahead, ez, groups)
+    grid = with_layers(h1, pair, cross, ez, groups)
     before, after = along_span(grid, ez, groups)
     padded[...] = jnp.concatenate([before, grid, after], axis=-1).astype(BF16)
     half = rows // 2
@@ -342,15 +383,18 @@
     dz2[...] = (dot_nt(miss, w_head[...]) * silu_grad(hidden)).astype(BF16)
 
 
-def back_kernel(groups, dz2, behind, ahead, w_conv, z1, snapshot, h2, resid, out, dh1):
+def back_kernel(
+    groups, dz2, pair, cross, w_conv, z1, snapshot, h2, resid,
+    to_one, to_two, to_three, kept, dh1, out,
+):
     rows, channels = dz2.shape
     ez = rows // (EX * EY)
     half = rows // 2
-    grid = with_layers(dz2, behind, ahead, ez, groups)
+    grid = with_layers(dz2, pair, cross, ez, groups)
     before, after = along_span(grid, ez, groups)
     shifted = [part.astype(BF16) for part in (after, grid, before)]
     features = snapshot.shape[1]
-    out[:, features:] = dot(h2[...].astype(F32).T.astype(BF16), resid[...]).astype(BF16)
+    out[:, features:] = dot(h2[...].astype(F32).T.astype(BF16), resid[...])
     for dy in range(3):
         for dz in range(3):
             tap = 3 * dy + dz
@@ -364,10 +408,18 @@
             else:
                 dh1[...] += step
     dz1 = dh1[...] * silu_grad(z1[...])
-    out[:, :features] = dot(dz1.T.astype(BF16), snapshot[...]).astype(BF16)
-
-
-def taps_kernel(groups, h_own, h_one, h_two, h_three, d_own, d_one, d_two, d_three, out, h_all, r_all):
+    out[:, :features] = dot(dz1.T.astype(BF16), snapshot[...])
+    quarter = channels // groups
+    place = lax.axis_index("grp")
+    for k, piece in enumerate((kept, to_one, to_two, to_three)):
+        at = pl.multiple_of(jnp.bitwise_xor(place, k) * quarter, quarter)
+        piece[...] = out[pl.ds(at, quarter)].astype(piece.dtype)
+
+
+def taps_kernel(
+    groups, sims, h_own, h_one, h_two, h_three, d_own, d_one, d_two, d_three, after_this, *refs
+):
+    out, h_all, r_all = refs[-3:]
     rows, channels = h_own.shape
     ez = rows // (EX * EY)
     quarter = channels // groups
@@ -381,7 +433,7 @@
     ).astype(BF16)
     pairs = ((h_own, d_own), (h_one, d_one), (h_two, d_two), (h_three, d_three))
     for k, (h, d) in enumerate(pairs):
-        at = lax.rem(place - k + groups, groups)
+        at = jnp.bitwise_xor(place, k)
         mine = dot(d[...], chosen)
         for x in range(EX):
             h_all[x, at] = h[x * layer : (x + 1) * layer]
@@ -408,16 +460,92 @@
             else:
                 got = dot(side[:, :deep], whole[deep:])
             start = (9 * dx + 3 * dy) * quarter
-            out[start : start + 3 * quarter] = got[: 3 * quarter].astype(BF16)
-
-
-def call(kernel, outs, scratch=(), flops=0):
+            out[start : start + 3 * quarter] = got[: 3 * quarter]
+    me = lax.rem(lax.axis_index("sim"), sims)
+    piece_rows = 27 * quarter // sims
+    for k, piece in enumerate(refs[:-3]):
+        at = pl.multiple_of(jnp.bitwise_xor(me, k) * piece_rows, 8)
+        piece[...] = out[pl.ds(at, piece_rows)].astype(piece.dtype)
+
+
+def dense_kernel(sims, kept, one, two, three, out_kept, out_sent):
+    total = kept[...] + one[...].astype(F32) + two[...].astype(F32) + three[...].astype(F32)
+    own_rows = kept.shape[0] // sims
+    odd = lax.rem(lax.axis_index("sim"), 2)
+    grid = total.reshape(sims // 2, 2, own_rows, kept.shape[1])
+    even_part = grid[:, 0]
+    odd_part = grid[:, 1]
+    mine = jnp.where(odd == 1, odd_part, even_part)
+    out_kept[...] = mine
+    out_sent[...] = jnp.where(odd == 1, even_part, odd_part).reshape(out_sent.shape).astype(BF16)
+
+
+def packed(taps, dense):
+    channels = taps.shape[1]
+    parts = [taps]
+    for start in range(0, dense.shape[1], channels):
+        piece = dense[:, start : start + channels]
+        short_by = channels - piece.shape[1]
+        if short_by:
+            piece = jnp.concatenate([piece, jnp.zeros((piece.shape[0], short_by), F32)], axis=1)
+        parts.append(piece)
+    return jnp.concatenate(parts, axis=0)
+
+
+def pair_sum(mask, taps, taps_in, dense, dense_in):
+    at = lax.div(jnp.bitwise_xor(lax.axis_index("sim"), mask), 2)
+    own_rows = dense.shape[1]
+    got = dense_in[...].astype(F32).reshape(dense.shape)
+    also = dense[at]
+    for i in range(dense.shape[0]):
+        also = also + jnp.where(at == i, got[i], 0.0)
+    return packed(taps[...] + taps_in[...].astype(F32), also)
+
+
+def pair_kernel(mask, taps, taps_in, dense, dense_in, out):
+    out[...] = pair_sum(mask, taps, taps_in, dense, dense_in).astype(BF16)
+
+
+def share_kernel(taps, taps_in, dense, dense_in, *refs):
+    total = pair_sum(0, taps, taps_in, dense, dense_in)
+    for other in refs[:-1]:
+        total = total + other[...].astype(F32)
+    refs[-1][...] = total.astype(BF16)
+
+
+def spread_kernel(features, own, *refs):
+    count = len(refs) - 3 + 1
+    shares = (own,) + refs[:-3]
+    taps, encode, head = refs[-3:]
+    channels = own.shape[1]
+    tap_rows = taps.shape[0] // count
+    own_rows = encode.shape[0] // count
+    me = lax.axis_index("sim")
+    for k, share in enumerate(shares):
+        source = jnp.bitwise_xor(me, k)
+        value = share[...].astype(F32)
+        taps[pl.ds(pl.multiple_of(source * tap_rows, 8), tap_rows)] = value[:tap_rows]
+        rows = pl.ds(pl.multiple_of(source * own_rows, 8), own_rows)
+        start = tap_rows
+        for first in range(0, features, channels):
+            encode[rows, first : first + channels] = value[start : start + own_rows]
+            start += own_rows
+        head[rows] = value[start : start + own_rows, : head.shape[1]]
+
+
+def call(kernel, outs, scratch=(), ordered_after=0, inputs=0):
+    specs = {}
+    if ordered_after:
+        specs["in_specs"] = [pl.BlockSpec(memory_space=pltpu.VMEM)] * inputs + [
+            pl.BlockSpec(memory_space=pl.ANY)
+        ] * ordered_after
     return pl.pallas_call(
         kernel,
         out_shape=outs,
         scratch_shapes=list(scratch),
         compiler_params=pltpu.CompilerParams(vmem_limit_bytes=VMEM_LIMIT),
-        cost_estimate=pl.CostEstimate(flops=flops, bytes_accessed=4_000_000, transcendentals=0),
+        cost_estimate=pl.CostEstimate(flops=1000, bytes_accessed=1000, transcendentals=0),
+        **specs,
     )
 
 
@@ -425,27 +553,39 @@
     return jax.ShapeDtypeStruct(shape, kind)
 
 
-def ring(value, axis, steps):
+def swapped(value, axis, mask):
     count = lax.axis_size(axis)
-    return lax.ppermute(value, axis, [(i, (i + steps) % count) for i in range(count)])
-
-
-def line(value, axis, steps):
+    return lax.ppermute(value, axis, [(i, i ^ mask) for i in range(count)])
+
+
+def crossed(value, axis, periodic):
     count = lax.axis_size(axis)
-    return lax.ppermute(value, axis, [(i, i + steps) for i in range(count) if 0 <= i + steps < count])
+    route = [(i, i + 1 if i % 2 else i - 1) for i in range(count)]
+    if periodic:
+        route = [(i, j % count) for i, j in route]
+    return lax.ppermute(value, axis, [(i, j) for i, j in route if 0 <= j < count])
 
 
 def exchanged(edges):
-    to_left, to_right, to_below, to_above = edges
-    from_left = ring(to_right, "sim", 1)
-    from_right = ring(to_left, "sim", -1)
-    from_below = line(to_above, "grp", 1)
-    from_above = line(to_below, "grp", -1)
-    return from_left, from_right, from_below, from_above
+    pair_x, cross_x, pair_y, cross_y = edges
+    cross_x = crossed(cross_x, "sim", True)
+    pair_x = swapped(pair_x, "sim", 1)
+    cross_y = crossed(cross_y, "grp", False)
+    pair_y = swapped(pair_y, "grp", 1)
+    return pair_x, cross_x, pair_y, cross_y
+
+
+def gathered(share, sims):
+    got = {0: share}
+    for k in sorted(range(2, sims, 2), reverse=True):
+        got[k] = swapped(share, "sim", k)
+    for k in range(0, sims, 2):
+        got[k + 1] = swapped(got[k], "sim", 1)
+    return [got[k] for k in range(sims)]
 
 
 def body(velocity, slot_of, w_encode, w_conv, w_head):
-    tables = {name: jnp.asarray(table) for name, table in element_tables().items()}
+    stencil, wall = (jnp.asarray(table) for table in element_tables())
     block = velocity[0, 0]
     slots = slot_of[0]
     rows, width = block.shape[1:]
@@ -462,15 +602,13 @@
     x_edge = shaped((3, EY * ez // 2, 2 * NP * NP), BF16)
     y_edge = shaped((3, ez, 2 * NP * NP), BF16)
     edge_shapes = (x_edge, x_edge, y_edge, y_edge)
-    picks = [tables[name] for name in ("low_first", "low_second", "top_first", "top_second")]
-    inside = [tables[name] for name in ("lap", "kx", "ky", "kz", "taken", "placed", "keep")]
-
-    field, *edges = call(prepare_kernel, (whole,) + edge_shapes, flops=10**9)(block, slots, *picks)
+
+    field, *edges = call(prepare_kernel, (whole,) + edge_shapes)(block, slots)
     halos = exchanged(edges)
-    part = call(inside_kernel, whole, flops=8 * 10**9)(field, *inside)
-    field, *edges = call(join_kernel, (whole,) + edge_shapes, flops=10**9)(part, *halos, *picks)
+    part = call(inside_kernel, whole)(field, stencil)
+    field, *edges = call(join_kernel, (whole,) + edge_shapes)(part, *halos)
     halos = exchanged(edges)
-    part = call(inside_kernel, whole, flops=8 * 10**9)(field, *inside)
+    part = call(inside_kernel, whole)(field, stencil)
     field, snapshot, target, z1, h1 = call(
         encode_kernel,
         (
@@ -480,12 +618,11 @@
             shaped((rows, channels), F32),
             shaped((rows, channels), BF16),
         ),
-        flops=10**9,
-    )(part, *halos, *picks, tables["wall_first"], tables["wall_second"], w_encode)
-
-    h_one = ring(h1, "grp", 1)
-    h_three = ring(h1, "grp", -1)
-    h_two = ring(h1, "grp", 2)
+    )(part, *halos, wall, w_encode)
+
+    h_one = swapped(h1, "grp", 1)
+    h_three = swapped(h1, "grp", 3)
+    h_two = swapped(h1, "grp", 2)
     rows_bf = shaped((rows, channels), BF16)
     dz2, h2, resid = call(
         functools.partial(forward_kernel, groups, total),
@@ -494,50 +631,81 @@
             pltpu.VMEM((EX, EY + 2, ez, 3 * channels), BF16),
             pltpu.VMEM((rows, channels), F32),
         ),
-        flops=10**9,
     )(h1, h_one, h_three, w_conv, w_head, target)
 
-    d_one = ring(dz2, "grp", 1)
-    d_three = ring(dz2, "grp", -1)
-    d_two = ring(dz2, "grp", 2)
-    dense = call(
+    d_one = swapped(dz2, "grp", 1)
+    d_three = swapped(dz2, "grp", 3)
+    d_two = swapped(dz2, "grp", 2)
+    wide = features + outputs
+    piece = shaped((quarter, wide), BF16)
+    e_one, e_two, e_three, e_own = call(
         functools.partial(back_kernel, groups),
-        shaped((channels, features + outputs), BF16),
-        (pltpu.VMEM((rows, channels), F32),),
-        flops=2 * 10**9,
+        (piece, piece, piece, shaped((quarter, wide), F32)),
+        (pltpu.VMEM((rows, channels), F32), pltpu.VMEM((channels, wide), F32)),
     )(dz2, d_one, d_three, w_conv, z1, snapshot, h2, resid)
+    tap_rows = 27 * quarter // sims
+    own_rows = quarter // sims
+    direct = sims == 8
+    if direct:
+        pieces = [shaped((tap_rows, channels), BF16 if k % 2 else F32) for k in range(sims)]
+    else:
+        pieces = [shaped((27 * quarter, channels), BF16)]
     taps = call(
-        functools.partial(taps_kernel, groups),
-        shaped((27 * quarter, channels), BF16),
+        functools.partial(taps_kernel, groups, sims if direct else 1),
+        tuple(pieces),
         (
+            pltpu.VMEM((27 * quarter, channels), F32),
             pltpu.VMEM((EX, groups, EY * ez, channels), BF16),
             pltpu.VMEM((EX, groups, EY * ez, channels), F32),
         ),
-        flops=2 * 10**9,
-    )(h1, h_one, h_two, h_three, dz2, d_one, d_two, d_three)
-
-    velocity_next = call(restore_kernel, whole, flops=10**9)(field, slots)
-
-    tap_rows = 27 * quarter // sims
-    taps = lax.all_to_all(taps.reshape(sims, tap_rows, channels), "sim", 0, 0, tiled=True)
-    taps = jnp.sum(taps.astype(F32), axis=0).astype(BF16)
-    own_rows = quarter // sims
-    dense = dense.reshape(groups, sims, own_rows, features + outputs).transpose(1, 0, 2, 3)
-    dense = dense.reshape(sims * groups, own_rows, features + outputs)
-    dense = lax.all_to_all(dense, ("sim", "grp"), 0, 0, tiled=True)
-    dense = jnp.sum(dense.astype(F32), axis=0).astype(BF16)
-    extra = -(features + outputs) % channels
-    dense = jnp.pad(dense, ((0, 0), (0, extra)))
-    mine = jnp.concatenate([taps, dense.reshape(-1, channels)], axis=0)
-    everything = lax.all_gather(mine, "sim")
-    taps = everything[:, :tap_rows].reshape(27, quarter, channels).astype(F32)
-    dense = everything[:, tap_rows:].reshape(quarter, -1)[:, : features + outputs].astype(F32)
-    return (
-        velocity_next[None, None],
-        dense[:, :features].T,
-        taps.transpose(0, 2, 1),
-        dense[:, features:],
-    )
+        ordered_after=1,
+        inputs=8,
+    )(h1, h_one, h_two, h_three, dz2, d_one, d_two, d_three, e_own)
+    e_three = swapped(e_three, "grp", 3)
+    e_two = swapped(e_two, "grp", 2)
+    e_one = swapped(e_one, "grp", 1)
+
+    velocity_next = call(restore_kernel, whole)(field, slots)
+
+    if direct:
+        e_kept, e_sent = call(
+            functools.partial(dense_kernel, sims),
+            (
+                shaped((sims // 2, own_rows, wide), F32),
+                shaped((sims // 2 * own_rows, wide), BF16),
+            ),
+        )(e_own, e_one, e_two, e_three)
+        taps_in = {k: swapped(taps[k + 1], "sim", 1) for k in (6, 4, 2, 0)}
+        e_in = swapped(e_sent, "sim", 1)
+        blocks = -(-wide // channels)
+        share = shaped((tap_rows + blocks * own_rows, channels), BF16)
+        others = []
+        for k in (6, 4, 2):
+            both = call(functools.partial(pair_kernel, k), share)(taps[k], taps_in[k], e_kept, e_in)
+            others.append(swapped(both, "sim", k))
+        share = call(share_kernel, share)(taps[0], taps_in[0], e_kept, e_in, *others)
+        taps, encode, head = call(
+            functools.partial(spread_kernel, features),
+            (
+                shaped((27 * quarter, channels), F32),
+                shaped((quarter, features), F32),
+                shaped((quarter, outputs), F32),
+            ),
+        )(*gathered(share, sims))
+    else:
+        taps = taps[0].reshape(sims, tap_rows, channels)
+        taps = lax.all_to_all(taps, "sim", 0, 0, tiled=True)
+        taps = jnp.sum(taps.astype(F32), axis=0).astype(BF16)
+        taps = lax.all_gather(taps, "sim").astype(F32)
+        dense = e_own + e_one.astype(F32) + e_two.astype(F32) + e_three.astype(F32)
+        dense = dense.astype(BF16).reshape(sims, own_rows, wide)
+        dense = lax.all_to_all(dense, "sim", 0, 0, tiled=True)
+        dense = jnp.sum(dense.astype(F32), axis=0).astype(BF16)
+        dense = lax.all_gather(dense, "sim").reshape(quarter, wide).astype(F32)
+        encode = dense[:, :features]
+        head = dense[:, features:]
+    taps = taps.reshape(27, quarter, channels)
+    return velocity_next[None, None], encode.T, taps.transpose(0, 2, 1), head
 
 
 def solution(mesh):

time: 166 us -> 101 us (0.61)
  waiting for transfers between devices: 81.5 us -> 34.1 us
  between operations: 14.4 us -> 0.91 us
  local copies, waits for them, and re-layouts: 13.3 us -> 4.49 us
  starting transfers between devices: 33.5 us -> 40 us
  other arithmetic: 2.33 us -> 0 us
    all_gather x1 -> x0, waiting for transfers between devices: 36.4 us -> none  [body(): everything = lax.all_gather(mine, 'sim')]
    all_to_all x2 -> x0, waiting for transfers between devices: 22.4 us -> none  [the longest x1 22.2 us: body(): lax.all_to_all(taps.reshape(sims, tap_rows, channels), 'sim', 0, 0, tiled...]
    ppermute x14 -> x32, starting transfers between devices: 24.4 us -> 40 us  [the longest x28 33.1 us: swapped(): return lax.ppermute(value, axis, [(i, i ^ mask) for i in range(count)])]
    ppermute x14 -> x32, waiting for transfers between devices: 22.8 us -> 34.1 us  [the longest x28 34.1 us: swapped(): return lax.ppermute(value, axis, [(i, i ^ mask) for i in range(count)])]
    all_to_all x2 -> x0, starting transfers between devices: 9.03 us -> none  [the longest x1 6.42 us: body(): lax.all_to_all(taps.reshape(sims, tap_rows, channels), 'sim', 0, 0, tiled...]
    unnamed x52 -> x18, local copies, waits for them, and re-layouts: 8.76 us -> 4.49 us
    slice x3 -> x0, local copies, waits for them, and re-layouts: 2.78 us -> none  [the longest x1 1.23 us: body(): taps = everything[:, :tap_rows].reshape(27, quarter, channels).astype(F32)]
    pallas_call x7 -> x13, Pallas kernels: 17.7 us -> 18.9 us  [the longest x2 9.3 us: body(): part = call(inside_kernel, whole)(field, stencil)]
  transfers between devices with their start and end apart: 17 -> 32, of which waited for: 9 -> 13; matrix products, arithmetic and copies ran while one was open for 0% -> 0% of each run, Pallas kernels for 8% -> 13%
where the time goes in v2:
time: 101 us
  starting transfers between devices  40 us (40%)
  waiting for transfers between devices  34.1 us (34%)
  Pallas kernels  21.5 us (21%)
  local copies, waits for them, and re-layouts  4.49 us (4%)
    ppermute x28, waiting for transfers between devices, swapped(): return lax.ppermute(value, axis, [(i, i ^ mask) for i in range(count)])  34.1 us
    ppermute x28, starting transfers between devices, swapped(): return lax.ppermute(value, axis, [(i, i ^ mask) for i in range(count)])  33.1 us
    pallas_call x2, Pallas kernels, body(): part = call(inside_kernel, whole)(field, stencil)  9.3 us
    ppermute x4, starting transfers between devices, crossed(): lax.ppermute(value, axis, [(i, j) for i, j in route if 0 <= j < count])  6.95 us
    unnamed x18, local copies, waits for them, and re-layouts  4.49 us
  transfers between devices with their start and end apart: 32, of which 13 were waited for; matrix products, arithmetic and copies ran while one was open for 0% of the time, Pallas kernels for 13%

profile of v2, /device:TPU:0, one launch (start us, length us, event | category | flops | bytes accessed | tf_op | source)
XLA Modules:
  0.0 101.0 jit_solution(435707722894331827)
XLA Ops:
  3.9 3.0 %collective-permute-start = (bf16[3,64,128]{2,1,0:T(8,128)(2,1)S(1)}, bf16[3,64,128]{2,1,0:T(8,128)(2,1)S(1)}, u32[]{:S(2)}, u32[]{:S(2)}) collective-permute-start(bf16[3,64,128]{2,1,0:T(8,128)(2,1)S(1)} %get-tuple-element.40), channel_id=1, source_target_pairs={{0,4},{4,0},{8,12},{12,8},{16,20},{20,16},{24,28},{28,24},{1,5},{5... | collective-permute-start | bytes 147464 | tf_op jit(solution)/shard_map/ppermute | solution.py:558
  6.9 3.6 %collective-permute-start.1 = (bf16[3,64,128]{2,1,0:T(8,128)(2,1)S(1)}, bf16[3,64,128]{2,1,0:T(8,128)(2,1)S(1)}, u32[]{:S(2)}, u32[]{:S(2)}) collective-permute-start(bf16[3,64,128]{2,1,0:T(8,128)(2,1)S(1)} %get-tuple-element.41), channel_id=1, source_target_pairs={{0,28},{4,8},{8,4},{12,16},{16,12},{20,24},{24,20},{28,0},{1,29},{... | collective-permute-start | bytes 147464 | tf_op jit(solution)/shard_map/ppermute | solution.py:566
  11.1 2.4 %copy-done = bf16[4736,512]{1,0:T(8,128)(2,1)S(1)} copy-done((bf16[4736,512]{1,0:T(8,128)(2,1)S(1)}, bf16[4736,512]{1,0:T(8,128)(2,1)}, u32[]{:S(2)}) %copy-start) | copy-done | bytes 4849688
  13.5 4.7 %shard_map.103.part = f32[3,256,512]{2,1,0:T(8,128)S(1)} custom-call(f32[3,256,512]{2,1,0:T(8,128)S(1)} %get-tuple-element.39.field, bf16[4736,512]{1,0:T(8,128)(2,1)S(1)} %copy-done), custom_call_target="tpu_custom_call" | custom-call | flops 1000 | bytes 1000 | tf_op jit(solution)/shard_map/pallas_call | solution.py:608
  19.3 1.9 %collective-permute-start.5 = (bf16[3,64,128]{2,1,0:T(8,128)(2,1)S(1)}, bf16[3,64,128]{2,1,0:T(8,128)(2,1)S(1)}, u32[]{:S(2)}, u32[]{:S(2)}) collective-permute-start(bf16[3,64,128]{2,1,0:T(8,128)(2,1)S(1)} %get-tuple-element.46), channel_id=1, source_target_pairs={{0,28},{4,8},{8,4},{12,16},{16,12},{20,24},{24,20},{28,0},{1,29},{... | collective-permute-start | bytes 147464 | tf_op jit(solution)/shard_map/ppermute | solution.py:566
  21.2 2.3 %collective-permute-start.6 = (bf16[3,32,128]{2,1,0:T(8,128)(2,1)S(1)}, bf16[3,32,128]{2,1,0:T(8,128)(2,1)S(1)}, u32[]{:S(2)}, u32[]{:S(2)}) collective-permute-start(bf16[3,32,128]{2,1,0:T(8,128)(2,1)S(1)} %get-tuple-element.47), channel_id=1, source_target_pairs={{0,1},{1,0},{2,3},{3,2},{4,5},{5,4},{6,7},{7,6},{8,9},{9,8},{10,11... | collective-permute-start | bytes 73736 | tf_op jit(solution)/shard_map/ppermute | solution.py:558
  24.4 4.6 %shard_map.105.part = f32[3,256,512]{2,1,0:T(8,128)S(1)} custom-call(f32[3,256,512]{2,1,0:T(8,128)S(1)} %get-tuple-element.44.field, bf16[4736,512]{1,0:T(8,128)(2,1)S(1)} %copy-done.1), custom_call_target="tpu_custom_call" | custom-call | flops 1000 | bytes 1000 | tf_op jit(solution)/shard_map/pallas_call | solution.py:611
  31.8 1.8 %collective-permute-start.8 = (bf16[256,256]{1,0:T(8,128)(2,1)S(1)}, bf16[256,256]{1,0:T(8,128)(2,1)S(1)}, u32[]{:S(2)}, u32[]{:S(2)}) collective-permute-start(bf16[256,256]{1,0:T(8,128)(2,1)S(1)} %get-tuple-element.50.h1.h_own), channel_id=1, source_target_pairs={{0,1},{1,0},{2,3},{3,2},{4,5},{5,4},{6,7},{7,6},{8,9},{9,8},{10,11... | collective-permute-start | bytes 393224 | tf_op jit(solution)/shard_map/ppermute | solution.py:558
  36.2 1.8 %collective-permute-start.13 = (bf16[256,256]{1,0:T(8,128)(2,1)S(1)}, bf16[256,256]{1,0:T(8,128)(2,1)S(1)}, u32[]{:S(2)}, u32[]{:S(2)}) collective-permute-start(bf16[256,256]{1,0:T(8,128)(2,1)S(1)} %get-tuple-element.52.dz2.d_own), channel_id=1, source_target_pairs={{0,3},{1,2},{2,1},{3,0},{4,7},{5,6},{6,5},{7,4},{8,11},{9,10},{10,... | collective-permute-start | bytes 393224 | tf_op jit(solution)/shard_map/ppermute | solution.py:558
  41.0 1.8 %shard_map.109 = (bf16[64,1152]{1,0:T(8,128)(2,1)S(1)}, bf16[64,1152]{1,0:T(8,128)(2,1)S(1)}, bf16[64,1152]{1,0:T(8,128)(2,1)S(1)}, f32[64,1152]{1,0:T(8,128)S(1)}) custom-call(bf16[256,256]{1,0:T(8,128)(2,1)S(1)} %get-tuple-element.52.dz2.d_own, bf16[256,256]{1,0:T(8,128)(2,1)S(1)} %collective-permute-done.11.pair.d_one, ...), custom_call_target="tpu_custom_call" | custom-call | flops 1000 | bytes 1000 | tf_op jit(solution)/shard_map/pallas_call | solution.py:641
  42.9 2.1 %collective-permute-start.15 = (bf16[64,1152]{1,0:T(8,128)(2,1)S(1)}, bf16[64,1152]{1,0:T(8,128)(2,1)S(1)}, u32[]{:S(2)}, u32[]{:S(2)}) collective-permute-start(bf16[64,1152]{1,0:T(8,128)(2,1)S(1)} %get-tuple-element.60), channel_id=1, source_target_pairs={{0,1},{1,0},{2,3},{3,2},{4,5},{5,4},{6,7},{7,6},{8,9},{9,8},{10,11... | collective-permute-start | bytes 442376 | tf_op jit(solution)/shard_map/ppermute | solution.py:558
  48.4 2.9 %collective-permute-done.9.h_two = bf16[256,256]{1,0:T(8,128)(2,1)S(1)} collective-permute-done((bf16[256,256]{1,0:T(8,128)(2,1)S(1)}, bf16[256,256]{1,0:T(8,128)(2,1)S(1)}, u32[]{:S(2)}, u32[]{:S(2)}) %collective-permute-start.9) | collective-permute-done | bytes 131104 | tf_op jit(solution)/shard_map/ppermute | solution.py:558
  51.3 2.8 %collective-permute-done.12.d_two = bf16[256,256]{1,0:T(8,128)(2,1)S(1)} collective-permute-done((bf16[256,256]{1,0:T(8,128)(2,1)S(1)}, bf16[256,256]{1,0:T(8,128)(2,1)S(1)}, u32[]{:S(2)}, u32[]{:S(2)}) %collective-permute-start.12) | collective-permute-done | bytes 131104 | tf_op jit(solution)/shard_map/ppermute | solution.py:558
  54.1 1.9 %shard_map.110 = (f32[216,256]{1,0:T(8,128)S(1)}, bf16[216,256]{1,0:T(8,128)(2,1)S(1)}, f32[216,256]{1,0:T(8,128)S(1)}, bf16[216,256]{1,0:T(8,128)(2,1)S(1)}, f3...) custom-call(bf16[256,256]{1,0:T(8,128)(2,1)S(1)} %get-tuple-element., ...), custom_call_target="tpu_custom_call" | custom-call | flops 1000 | bytes 1000 | tf_op jit(solution)/shard_map/pallas_call | solution.py:653
  61.7 3.9 %collective-permute-done.18.dense_in = bf16[32,1152]{1,0:T(8,128)(2,1)S(1)} collective-permute-done((bf16[32,1152]{1,0:T(8,128)(2,1)S(1)}, bf16[32,1152]{1,0:T(8,128)(2,1)S(1)}, u32[]{:S(2)}, u32[]{:S(2)}) %collective-permute-start.18) | collective-permute-done | bytes 73760 | tf_op jit(solution)/shard_map/ppermute | solution.py:558
  68.6 1.9 %collective-permute-start.20 = (bf16[256,256]{1,0:T(8,128)(2,1)S(1)}, bf16[256,256]{1,0:T(8,128)(2,1)S(1)}, u32[]{:S(2)}, u32[]{:S(2)}) collective-permute-start(bf16[256,256]{1,0:T(8,128)(2,1)S(1)} %shard_map.112), channel_id=1, source_target_pairs={{0,24},{4,28},{8,16},{12,20},{16,8},{20,12},{24,0},{28,4},{1,25},{... | collective-permute-start | bytes 393224 | tf_op jit(solution)/shard_map/ppermute | solution.py:558
  71.0 4.1 %collective-permute-done.14.taps_in = bf16[216,256]{1,0:T(8,128)(2,1)S(1)} collective-permute-done((bf16[216,256]{1,0:T(8,128)(2,1)S(1)}, bf16[216,256]{1,0:T(8,128)(2,1)S(1)}, u32[]{:S(2)}, u32[]{:S(2)}) %collective-permute-start.14) | collective-permute-done | bytes 110624 | tf_op jit(solution)/shard_map/ppermute | solution.py:558
  75.2 4.9 %collective-permute-done.22.refs_1_ = bf16[256,256]{1,0:T(8,128)(2,1)S(1)} collective-permute-done((bf16[256,256]{1,0:T(8,128)(2,1)S(1)}, bf16[256,256]{1,0:T(8,128)(2,1)S(1)}, u32[]{:S(2)}, u32[]{:S(2)}) %collective-permute-start.22) | collective-permute-done | bytes 131104 | tf_op jit(solution)/shard_map/ppermute | solution.py:558
  80.2 3.4 %collective-permute-start.28 = (bf16[256,256]{1,0:T(8,128)(2,1)S(1)}, bf16[256,256]{1,0:T(8,128)(2,1)S(1)}, u32[]{:S(2)}, u32[]{:S(2)}) collective-permute-start(bf16[256,256]{1,0:T(8,128)(2,1)S(1)} %shard_map.115.own), channel_id=1, source_target_pairs={{0,16},{4,20},{8,24},{12,28},{16,0},{20,4},{24,8},{28,12},{1,17},{... | collective-permute-start | bytes 393224 | tf_op jit(solution)/shard_map/ppermute | solution.py:558
  84.7 3.3 %collective-permute-done.30.refs_5_ = bf16[256,256]{1,0:T(8,128)(2,1)S(1)} collective-permute-done((bf16[256,256]{1,0:T(8,128)(2,1)S(1)}, bf16[256,256]{1,0:T(8,128)(2,1)S(1)}, u32[]{:S(2)}, u32[]{:S(2)}) %collective-permute-start.30) | collective-permute-done | bytes 131104 | tf_op jit(solution)/shard_map/ppermute | solution.py:558
  88.0 4.4 %collective-permute-done.28.refs_3_ = bf16[256,256]{1,0:T(8,128)(2,1)S(1)} collective-permute-done((bf16[256,256]{1,0:T(8,128)(2,1)S(1)}, bf16[256,256]{1,0:T(8,128)(2,1)S(1)}, u32[]{:S(2)}, u32[]{:S(2)}) %collective-permute-start.28) | collective-permute-done | bytes 131104 | tf_op jit(solution)/shard_map/ppermute | solution.py:558
  92.5 2.0 %collective-permute-start.27 = (bf16[256,256]{1,0:T(8,128)(2,1)S(1)}, bf16[256,256]{1,0:T(8,128)(2,1)S(1)}, u32[]{:S(2)}, u32[]{:S(2)}) collective-permute-start(bf16[256,256]{1,0:T(8,128)(2,1)S(1)} %collective-permute-done.26.refs_1_), channel_id=1, source_target_pairs={{0,4},{4,0},{8,12},{12,8},{16,20},{20,16},{24,28},{28,24},{1,5},{5... | collective-permute-start | bytes 393224 | tf_op jit(solution)/shard_map/ppermute | solution.py:558
  94.5 2.0 %shard_map.107 = f32[3,256,512]{2,1,0:T(8,128)} custom-call(f32[3,256,512]{2,1,0:T(8,128)S(1)} %get-tuple-element.49.field, s32[1,256]{1,0:T(1,128)S(1)} %bitcast.9), custom_call_target="tpu_custom_call" | custom-call | flops 1000 | bytes 1000 | tf_op jit(solution)/shard_map/pallas_call | solution.py:668
  96.5 1.7 %collective-permute-done.29.refs_4_ = bf16[256,256]{1,0:T(8,128)(2,1)S(1)} collective-permute-done((bf16[256,256]{1,0:T(8,128)(2,1)S(1)}, bf16[256,256]{1,0:T(8,128)(2,1)S(1)}, u32[]{:S(2)}, u32[]{:S(2)}) %collective-permute-start.29) | collective-permute-done | bytes 131104 | tf_op jit(solution)/shard_map/ppermute | solution.py:558
  (73 shorter events, 30.8 us)
Async XLA Ops:
  3.9 14.3 %collective-permute-start = (bf16[3,64,128]{2,1,0:T(8,128)(2,1)S(1)}, bf16[3,64,128]{2,1,0:T(8,128)(2,1)S(1)}, u32[]{:S(2)}, u32[]{:S(2)}) collective-permute-start(bf16[3,64,128]{2,1,0:T(8,128)(2,1)S(1)} %get-tuple-element.40), channel_id=1, source_target_pairs={{0,4},{4,0},{8,12},{12,8},{16,20},{20,16},{24,28},{28,24},{1,5},{5... | collective-permute-start | bytes 147464 | tf_op jit(solution)/shard_map/ppermute | solution.py:558
  6.9 11.3 %collective-permute-start.1 = (bf16[3,64,128]{2,1,0:T(8,128)(2,1)S(1)}, bf16[3,64,128]{2,1,0:T(8,128)(2,1)S(1)}, u32[]{:S(2)}, u32[]{:S(2)}) collective-permute-start(bf16[3,64,128]{2,1,0:T(8,128)(2,1)S(1)} %get-tuple-element.41), channel_id=1, source_target_pairs={{0,28},{4,8},{8,4},{12,16},{16,12},{20,24},{24,20},{28,0},{1,29},{... | collective-permute-start | bytes 147464 | tf_op jit(solution)/shard_map/ppermute | solution.py:566
  10.4 7.7 %collective-permute-start.2 = (bf16[3,32,128]{2,1,0:T(8,128)(2,1)S(1)}, bf16[3,32,128]{2,1,0:T(8,128)(2,1)S(1)}, u32[]{:S(2)}, u32[]{:S(2)}) collective-permute-start(bf16[3,32,128]{2,1,0:T(8,128)(2,1)S(1)} %get-tuple-element.42), channel_id=1, source_target_pairs={{0,1},{1,0},{2,3},{3,2},{4,5},{5,4},{6,7},{7,6},{8,9},{9,8},{10,11... | collective-permute-start | bytes 73736 | tf_op jit(solution)/shard_map/ppermute | solution.py:558
  10.4 7.7 %collective-permute-start.3 = (bf16[3,32,128]{2,1,0:T(8,128)(2,1)S(1)}, bf16[3,32,128]{2,1,0:T(8,128)(2,1)S(1)}, u32[]{:S(2)}, u32[]{:S(2)}) collective-permute-start(bf16[3,32,128]{2,1,0:T(8,128)(2,1)S(1)} %get-tuple-element.43), channel_id=1, source_target_pairs={{1,2},{2,1},{5,6},{6,5},{9,10},{10,9},{13,14},{14,13},{17,18},{18,... | collective-permute-start | bytes 73736 | tf_op jit(solution)/shard_map/ppermute | solution.py:566
  19.2 9.9 %collective-permute-start.4 = (bf16[3,64,128]{2,1,0:T(8,128)(2,1)S(1)}, bf16[3,64,128]{2,1,0:T(8,128)(2,1)S(1)}, u32[]{:S(2)}, u32[]{:S(2)}) collective-permute-start(bf16[3,64,128]{2,1,0:T(8,128)(2,1)S(1)} %get-tuple-element.45), channel_id=1, source_target_pairs={{0,4},{4,0},{8,12},{12,8},{16,20},{20,16},{24,28},{28,24},{1,5},{5... | collective-permute-start | bytes 147464 | tf_op jit(solution)/shard_map/ppermute | solution.py:558
  19.3 9.8 %collective-permute-start.5 = (bf16[3,64,128]{2,1,0:T(8,128)(2,1)S(1)}, bf16[3,64,128]{2,1,0:T(8,128)(2,1)S(1)}, u32[]{:S(2)}, u32[]{:S(2)}) collective-permute-start(bf16[3,64,128]{2,1,0:T(8,128)(2,1)S(1)} %get-tuple-element.46), channel_id=1, source_target_pairs={{0,28},{4,8},{8,4},{12,16},{16,12},{20,24},{24,20},{28,0},{1,29},{... | collective-permute-start | bytes 147464 | tf_op jit(solution)/shard_map/ppermute | solution.py:566
  21.2 7.9 %collective-permute-start.6 = (bf16[3,32,128]{2,1,0:T(8,128)(2,1)S(1)}, bf16[3,32,128]{2,1,0:T(8,128)(2,1)S(1)}, u32[]{:S(2)}, u32[]{:S(2)}) collective-permute-start(bf16[3,32,128]{2,1,0:T(8,128)(2,1)S(1)} %get-tuple-element.47), channel_id=1, source_target_pairs={{0,1},{1,0},{2,3},{3,2},{4,5},{5,4},{6,7},{7,6},{8,9},{9,8},{10,11... | collective-permute-start | bytes 73736 | tf_op jit(solution)/shard_map/ppermute | solution.py:558
  42.9 15.2 %collective-permute-start.15 = (bf16[64,1152]{1,0:T(8,128)(2,1)S(1)}, bf16[64,1152]{1,0:T(8,128)(2,1)S(1)}, u32[]{:S(2)}, u32[]{:S(2)}) collective-permute-start(bf16[64,1152]{1,0:T(8,128)(2,1)S(1)} %get-tuple-element.60), channel_id=1, source_target_pairs={{0,1},{1,0},{2,3},{3,2},{4,5},{5,4},{6,7},{7,6},{8,9},{9,8},{10,11... | collective-permute-start | bytes 442376 | tf_op jit(solution)/shard_map/ppermute | solution.py:558
  44.9 6.4 %collective-permute-start.9 = (bf16[256,256]{1,0:T(8,128)(2,1)S(1)}, bf16[256,256]{1,0:T(8,128)(2,1)S(1)}, u32[]{:S(2)}, u32[]{:S(2)}) collective-permute-start(bf16[256,256]{1,0:T(8,128)(2,1)S(1)} %get-tuple-element.50.h1.h_own), channel_id=1, source_target_pairs={{0,2},{1,3},{2,0},{3,1},{4,6},{5,7},{6,4},{7,5},{8,10},{9,11},{10,... | collective-permute-start | bytes 393224 | tf_op jit(solution)/shard_map/ppermute | solution.py:558
  46.3 7.8 %collective-permute-start.12 = (bf16[256,256]{1,0:T(8,128)(2,1)S(1)}, bf16[256,256]{1,0:T(8,128)(2,1)S(1)}, u32[]{:S(2)}, u32[]{:S(2)}) collective-permute-start(bf16[256,256]{1,0:T(8,128)(2,1)S(1)} %get-tuple-element.52.dz2.d_own), channel_id=1, source_target_pairs={{0,2},{1,3},{2,0},{3,1},{4,6},{5,7},{6,4},{7,5},{8,10},{9,11},{10,... | collective-permute-start | bytes 393224 | tf_op jit(solution)/shard_map/ppermute | solution.py:558
  47.0 11.7 %collective-permute-start.16 = (bf16[64,1152]{1,0:T(8,128)(2,1)S(1)}, bf16[64,1152]{1,0:T(8,128)(2,1)S(1)}, u32[]{:S(2)}, u32[]{:S(2)}) collective-permute-start(bf16[64,1152]{1,0:T(8,128)(2,1)S(1)} %get-tuple-element.61), channel_id=1, source_target_pairs={{0,2},{1,3},{2,0},{3,1},{4,6},{5,7},{6,4},{7,5},{8,10},{9,11},{10,... | collective-permute-start | bytes 442376 | tf_op jit(solution)/shard_map/ppermute | solution.py:558
  48.4 10.5 %collective-permute-start.17 = (bf16[64,1152]{1,0:T(8,128)(2,1)S(1)}, bf16[64,1152]{1,0:T(8,128)(2,1)S(1)}, u32[]{:S(2)}, u32[]{:S(2)}) collective-permute-start(bf16[64,1152]{1,0:T(8,128)(2,1)S(1)} %get-tuple-element.62), channel_id=1, source_target_pairs={{0,3},{1,2},{2,1},{3,0},{4,7},{5,6},{6,5},{7,4},{8,11},{9,10},{10,... | collective-permute-start | bytes 442376 | tf_op jit(solution)/shard_map/ppermute | solution.py:558
  56.7 10.7 %collective-permute-start.21 = (bf16[216,256]{1,0:T(8,128)(2,1)S(1)}, bf16[216,256]{1,0:T(8,128)(2,1)S(1)}, u32[]{:S(2)}, u32[]{:S(2)}) collective-permute-start(bf16[216,256]{1,0:T(8,128)(2,1)S(1)} %get-tuple-element.68), channel_id=1, source_target_pairs={{0,4},{4,0},{8,12},{12,8},{16,20},{20,16},{24,28},{28,24},{1,5},{5... | collective-permute-start | bytes 331784 | tf_op jit(solution)/shard_map/ppermute | solution.py:558
  58.1 10.4 %collective-permute-start.19 = (bf16[216,256]{1,0:T(8,128)(2,1)S(1)}, bf16[216,256]{1,0:T(8,128)(2,1)S(1)}, u32[]{:S(2)}, u32[]{:S(2)}) collective-permute-start(bf16[216,256]{1,0:T(8,128)(2,1)S(1)} %get-tuple-element.66), channel_id=1, source_target_pairs={{0,4},{4,0},{8,12},{12,8},{16,20},{20,16},{24,28},{28,24},{1,5},{5... | collective-permute-start | bytes 331784 | tf_op jit(solution)/shard_map/ppermute | solution.py:558
  58.9 6.8 %collective-permute-start.18 = (bf16[32,1152]{1,0:T(8,128)(2,1)S(1)}, bf16[32,1152]{1,0:T(8,128)(2,1)S(1)}, u32[]{:S(2)}, u32[]{:S(2)}) collective-permute-start(bf16[32,1152]{1,0:T(8,128)(2,1)S(1)} %get-tuple-element.64), channel_id=1, source_target_pairs={{0,4},{4,0},{8,12},{12,8},{16,20},{20,16},{24,28},{28,24},{1,5},{5... | collective-permute-start | bytes 221192 | tf_op jit(solution)/shard_map/ppermute | solution.py:558
  65.7 9.4 %collective-permute-start.24 = (bf16[256,256]{1,0:T(8,128)(2,1)S(1)}, bf16[256,256]{1,0:T(8,128)(2,1)S(1)}, u32[]{:S(2)}, u32[]{:S(2)}) collective-permute-start(bf16[256,256]{1,0:T(8,128)(2,1)S(1)} %shard_map.114), channel_id=1, source_target_pairs={{0,8},{4,12},{8,0},{12,4},{16,24},{20,28},{24,16},{28,20},{1,9},{5... | collective-permute-start | bytes 393224 | tf_op jit(solution)/shard_map/ppermute | solution.py:558
  67.4 12.6 %collective-permute-start.22 = (bf16[256,256]{1,0:T(8,128)(2,1)S(1)}, bf16[256,256]{1,0:T(8,128)(2,1)S(1)}, u32[]{:S(2)}, u32[]{:S(2)}) collective-permute-start(bf16[256,256]{1,0:T(8,128)(2,1)S(1)} %shard_map.113), channel_id=1, source_target_pairs={{0,16},{4,20},{8,24},{12,28},{16,0},{20,4},{24,8},{28,12},{1,17},{... | collective-permute-start | bytes 393224 | tf_op jit(solution)/shard_map/ppermute | solution.py:558
  68.6 11.5 %collective-permute-start.20 = (bf16[256,256]{1,0:T(8,128)(2,1)S(1)}, bf16[256,256]{1,0:T(8,128)(2,1)S(1)}, u32[]{:S(2)}, u32[]{:S(2)}) collective-permute-start(bf16[256,256]{1,0:T(8,128)(2,1)S(1)} %shard_map.112), channel_id=1, source_target_pairs={{0,24},{4,28},{8,16},{12,20},{16,8},{20,12},{24,0},{28,4},{1,25},{... | collective-permute-start | bytes 393224 | tf_op jit(solution)/shard_map/ppermute | solution.py:558
  80.1 7.9 %collective-permute-start.30 = (bf16[256,256]{1,0:T(8,128)(2,1)S(1)}, bf16[256,256]{1,0:T(8,128)(2,1)S(1)}, u32[]{:S(2)}, u32[]{:S(2)}) collective-permute-start(bf16[256,256]{1,0:T(8,128)(2,1)S(1)} %shard_map.115.own), channel_id=1, source_target_pairs={{0,24},{4,28},{8,16},{12,20},{16,8},{20,12},{24,0},{28,4},{1,25},{... | collective-permute-start | bytes 393224 | tf_op jit(solution)/shard_map/ppermute | solution.py:558
  80.2 12.2 %collective-permute-start.28 = (bf16[256,256]{1,0:T(8,128)(2,1)S(1)}, bf16[256,256]{1,0:T(8,128)(2,1)S(1)}, u32[]{:S(2)}, u32[]{:S(2)}) collective-permute-start(bf16[256,256]{1,0:T(8,128)(2,1)S(1)} %shard_map.115.own), channel_id=1, source_target_pairs={{0,16},{4,20},{8,24},{12,28},{16,0},{20,4},{24,8},{28,12},{1,17},{... | collective-permute-start | bytes 393224 | tf_op jit(solution)/shard_map/ppermute | solution.py:558
  83.6 8.8 %collective-permute-start.26 = (bf16[256,256]{1,0:T(8,128)(2,1)S(1)}, bf16[256,256]{1,0:T(8,128)(2,1)S(1)}, u32[]{:S(2)}, u32[]{:S(2)}) collective-permute-start(bf16[256,256]{1,0:T(8,128)(2,1)S(1)} %shard_map.115.own), channel_id=1, source_target_pairs={{0,8},{4,12},{8,0},{12,4},{16,24},{20,28},{24,16},{28,20},{1,9},{5... | collective-permute-start | bytes 393224 | tf_op jit(solution)/shard_map/ppermute | solution.py:558
  84.6 11.9 %collective-permute-start.25 = (bf16[256,256]{1,0:T(8,128)(2,1)S(1)}, bf16[256,256]{1,0:T(8,128)(2,1)S(1)}, u32[]{:S(2)}, u32[]{:S(2)}) collective-permute-start(bf16[256,256]{1,0:T(8,128)(2,1)S(1)} %shard_map.115.own), channel_id=1, source_target_pairs={{0,4},{4,0},{8,12},{12,8},{16,20},{20,16},{24,28},{28,24},{1,5},{5... | collective-permute-start | bytes 393224 | tf_op jit(solution)/shard_map/ppermute | solution.py:558
  88.0 8.5 %collective-permute-start.31 = (bf16[256,256]{1,0:T(8,128)(2,1)S(1)}, bf16[256,256]{1,0:T(8,128)(2,1)S(1)}, u32[]{:S(2)}, u32[]{:S(2)}) collective-permute-start(bf16[256,256]{1,0:T(8,128)(2,1)S(1)} %collective-permute-done.30.refs_5_), channel_id=1, source_target_pairs={{0,4},{4,0},{8,12},{12,8},{16,20},{20,16},{24,28},{28,24},{1,5},{5... | collective-permute-start | bytes 393224 | tf_op jit(solution)/shard_map/ppermute | solution.py:558
  92.5 7.1 %collective-permute-start.27 = (bf16[256,256]{1,0:T(8,128)(2,1)S(1)}, bf16[256,256]{1,0:T(8,128)(2,1)S(1)}, u32[]{:S(2)}, u32[]{:S(2)}) collective-permute-start(bf16[256,256]{1,0:T(8,128)(2,1)S(1)} %collective-permute-done.26.refs_1_), channel_id=1, source_target_pairs={{0,4},{4,0},{8,12},{12,8},{16,20},{20,16},{24,28},{28,24},{1,5},{5... | collective-permute-start | bytes 393224 | tf_op jit(solution)/shard_map/ppermute | solution.py:558
  (17 other events, 114.4 us)

commit v3 on v2

--- a/solution.py
+++ b/solution.py
@@ -320,7 +320,7 @@
     h1[...] = (hidden * jax.nn.sigmoid(hidden)).astype(BF16)
 
 
-def restore_kernel(field, slots, out):
+def restore_kernel(field, slots, after_this, out):
     order = slot_matrix(slots[...]).astype(BF16)
     for c in range(3):
         out[c] = moved(order, field[c])
@@ -385,7 +385,7 @@
 
 def back_kernel(
     groups, dz2, pair, cross, w_conv, z1, snapshot, h2, resid,
-    to_one, to_two, to_three, kept, dh1, out,
+    kept, sent, dh1, out,
 ):
     rows, channels = dz2.shape
     ez = rows // (EX * EY)
@@ -411,9 +411,15 @@
     out[:, :features] = dot(dz1.T.astype(BF16), snapshot[...])
     quarter = channels // groups
     place = lax.axis_index("grp")
-    for k, piece in enumerate((kept, to_one, to_two, to_three)):
+    for k in range(groups):
+        piece = sent if k % 2 else kept
         at = pl.multiple_of(jnp.bitwise_xor(place, k) * quarter, quarter)
-        piece[...] = out[pl.ds(at, quarter)].astype(piece.dtype)
+        piece[k // 2] = out[pl.ds(at, quarter)].astype(piece.dtype)
+
+
+def core_kernel(kept, got, out_kept, out_sent):
+    out_kept[...] = kept[0] + got[0].astype(F32)
+    out_sent[...] = (kept[1] + got[1].astype(F32)).astype(BF16)
 
 
 def taps_kernel(
@@ -468,16 +474,19 @@
         piece[...] = out[pl.ds(at, piece_rows)].astype(piece.dtype)
 
 
-def dense_kernel(sims, kept, one, two, three, out_kept, out_sent):
-    total = kept[...] + one[...].astype(F32) + two[...].astype(F32) + three[...].astype(F32)
-    own_rows = kept.shape[0] // sims
-    odd = lax.rem(lax.axis_index("sim"), 2)
-    grid = total.reshape(sims // 2, 2, own_rows, kept.shape[1])
-    even_part = grid[:, 0]
-    odd_part = grid[:, 1]
-    mine = jnp.where(odd == 1, odd_part, even_part)
-    out_kept[...] = mine
-    out_sent[...] = jnp.where(odd == 1, even_part, odd_part).reshape(out_sent.shape).astype(BF16)
+def dense_kernel(kept, got, out_kept, out_sent):
+    total = kept[...] + got[...].astype(F32)
+    grid = total.reshape(2, 2, kept.shape[0] // 4, kept.shape[1])
+    odd = lax.rem(lax.div(lax.axis_index("sim"), 2), 2) == 1
+    out_kept[...] = jnp.where(odd, grid[:, 1], grid[:, 0])
+    out_sent[...] = jnp.where(odd, grid[:, 0], grid[:, 1]).astype(BF16)
+
+
+def half_kernel(scale, kept, got, out_kept, out_sent):
+    total = kept[...] + got[...].astype(F32)
+    upper = lax.rem(lax.div(lax.axis_index("sim"), scale), 2) == 1
+    out_kept[...] = jnp.where(upper, total[1], total[0])
+    out_sent[...] = jnp.where(upper, total[0], total[1]).astype(BF16)
 
 
 def packed(taps, dense):
@@ -492,25 +501,18 @@
     return jnp.concatenate(parts, axis=0)
 
 
-def pair_sum(mask, taps, taps_in, dense, dense_in):
-    at = lax.div(jnp.bitwise_xor(lax.axis_index("sim"), mask), 2)
-    own_rows = dense.shape[1]
-    got = dense_in[...].astype(F32).reshape(dense.shape)
-    also = dense[at]
-    for i in range(dense.shape[0]):
-        also = also + jnp.where(at == i, got[i], 0.0)
-    return packed(taps[...] + taps_in[...].astype(F32), also)
-
-
-def pair_kernel(mask, taps, taps_in, dense, dense_in, out):
-    out[...] = pair_sum(mask, taps, taps_in, dense, dense_in).astype(BF16)
-
-
-def share_kernel(taps, taps_in, dense, dense_in, *refs):
-    total = pair_sum(0, taps, taps_in, dense, dense_in)
-    for other in refs[:-1]:
+def sum_kernel(parts, kept, *refs):
+    total = kept[...]
+    for other in refs[: parts - 1]:
         total = total + other[...].astype(F32)
     refs[-1][...] = total.astype(BF16)
+
+
+def share_kernel(taps, one, two, three, dense, dense_in, out):
+    total = taps[...]
+    for other in (one, two, three):
+        total = total + other[...].astype(F32)
+    out[...] = packed(total, dense[...] + dense_in[...].astype(F32)).astype(BF16)
 
 
 def spread_kernel(features, own, *refs):
@@ -533,18 +535,18 @@
         head[rows] = value[start : start + own_rows, : head.shape[1]]
 
 
-def call(kernel, outs, scratch=(), ordered_after=0, inputs=0):
+def call(kernel, outs, scratch=(), in_hbm=(), inputs=0, flops=1000):
     specs = {}
-    if ordered_after:
-        specs["in_specs"] = [pl.BlockSpec(memory_space=pltpu.VMEM)] * inputs + [
-            pl.BlockSpec(memory_space=pl.ANY)
-        ] * ordered_after
+    if in_hbm:
+        specs["in_specs"] = [
+            pl.BlockSpec(memory_space=pl.ANY if i in in_hbm else pltpu.VMEM) for i in range(inputs)
+        ]
     return pl.pallas_call(
         kernel,
         out_shape=outs,
         scratch_shapes=list(scratch),
         compiler_params=pltpu.CompilerParams(vmem_limit_bytes=VMEM_LIMIT),
-        cost_estimate=pl.CostEstimate(flops=1000, bytes_accessed=1000, transcendentals=0),
+        cost_estimate=pl.CostEstimate(flops=flops, bytes_accessed=1000, transcendentals=0),
         **specs,
     )
 
@@ -603,7 +605,7 @@
     y_edge = shaped((3, ez, 2 * NP * NP), BF16)
     edge_shapes = (x_edge, x_edge, y_edge, y_edge)
 
-    field, *edges = call(prepare_kernel, (whole,) + edge_shapes)(block, slots)
+    field, *edges = call(prepare_kernel, (whole,) + edge_shapes, flops=4 * 10**9)(block, slots)
     halos = exchanged(edges)
     part = call(inside_kernel, whole)(field, stencil)
     field, *edges = call(join_kernel, (whole,) + edge_shapes)(part, *halos)
@@ -620,9 +622,9 @@
         ),
     )(part, *halos, wall, w_encode)
 
+    h_three = swapped(h1, "grp", 3)
     h_one = swapped(h1, "grp", 1)
-    h_three = swapped(h1, "grp", 3)
-    h_two = swapped(h1, "grp", 2)
+    h_two = swapped(h_three, "grp", 1)
     rows_bf = shaped((rows, channels), BF16)
     dz2, h2, resid = call(
         functools.partial(forward_kernel, groups, total),
@@ -633,16 +635,19 @@
         ),
     )(h1, h_one, h_three, w_conv, w_head, target)
 
+    d_three = swapped(dz2, "grp", 3)
     d_one = swapped(dz2, "grp", 1)
-    d_three = swapped(dz2, "grp", 3)
-    d_two = swapped(dz2, "grp", 2)
+    d_two = swapped(d_three, "grp", 1)
     wide = features + outputs
-    piece = shaped((quarter, wide), BF16)
-    e_one, e_two, e_three, e_own = call(
+    pair = (groups // 2, quarter, wide)
+    e_kept, e_sent = call(
         functools.partial(back_kernel, groups),
-        (piece, piece, piece, shaped((quarter, wide), F32)),
+        (shaped(pair, F32), shaped(pair, BF16)),
         (pltpu.VMEM((rows, channels), F32), pltpu.VMEM((channels, wide), F32)),
     )(dz2, d_one, d_three, w_conv, z1, snapshot, h2, resid)
+    e_got = swapped(e_sent, "grp", 1)
+    e_kept, e_sent = call(core_kernel, (shaped(pair[1:], F32), shaped(pair[1:], BF16)))(e_kept, e_got)
+    e_got = swapped(e_sent, "grp", 2)
     tap_rows = 27 * quarter // sims
     own_rows = quarter // sims
     direct = sims == 8
@@ -658,32 +663,33 @@
             pltpu.VMEM((EX, groups, EY * ez, channels), BF16),
             pltpu.VMEM((EX, groups, EY * ez, channels), F32),
         ),
-        ordered_after=1,
-        inputs=8,
-    )(h1, h_one, h_two, h_three, dz2, d_one, d_two, d_three, e_own)
-    e_three = swapped(e_three, "grp", 3)
-    e_two = swapped(e_two, "grp", 2)
-    e_one = swapped(e_one, "grp", 1)
-
-    velocity_next = call(restore_kernel, whole)(field, slots)
-
+        in_hbm=(8,),
+        inputs=9,
+    )(h1, h_one, h_two, h_three, dz2, d_one, d_two, d_three, e_kept)
     if direct:
-        e_kept, e_sent = call(
-            functools.partial(dense_kernel, sims),
-            (
-                shaped((sims // 2, own_rows, wide), F32),
-                shaped((sims // 2 * own_rows, wide), BF16),
-            ),
-        )(e_own, e_one, e_two, e_three)
         taps_in = {k: swapped(taps[k + 1], "sim", 1) for k in (6, 4, 2, 0)}
-        e_in = swapped(e_sent, "sim", 1)
+        tap_piece = shaped((tap_rows, channels), BF16)
+        part = (2, 2 * own_rows, wide)
+        e_kept, e_sent = call(dense_kernel, (shaped(part, F32), shaped(part, BF16)))(e_kept, e_got)
+        e_got = swapped(e_sent, "sim", 2)
+        add_two = call(functools.partial(sum_kernel, 2), tap_piece)
+        add_three = call(functools.partial(sum_kernel, 3), tap_piece)
+        six = swapped(add_two(taps[6], taps_in[6], e_sent), "sim", 2)
+        two = swapped(add_two(taps[2], taps_in[2]), "sim", 2)
+        part = shaped((2 * own_rows, wide), F32), shaped((2 * own_rows, wide), BF16)
+        e_kept, e_sent = call(functools.partial(half_kernel, 4), part)(e_kept, e_got)
+        e_got = swapped(e_sent, "sim", 4)
+        four = swapped(add_three(taps[4], taps_in[4], six, e_sent), "sim", 4)
+        part = shaped((own_rows, wide), F32), shaped((own_rows, wide), BF16)
+        e_kept, e_sent = call(functools.partial(half_kernel, 1), part)(
+            e_kept.reshape(2, own_rows, wide), e_got.reshape(2, own_rows, wide)
+        )
+        e_got = swapped(e_sent, "sim", 1)
         blocks = -(-wide // channels)
-        share = shaped((tap_rows + blocks * own_rows, channels), BF16)
-        others = []
-        for k in (6, 4, 2):
-            both = call(functools.partial(pair_kernel, k), share)(taps[k], taps_in[k], e_kept, e_in)
-            others.append(swapped(both, "sim", k))
-        share = call(share_kernel, share)(taps[0], taps_in[0], e_kept, e_in, *others)
+        share = call(share_kernel, shaped((tap_rows + blocks * own_rows, channels), BF16))(
+            taps[0], taps_in[0], two, four, e_kept, e_got
+        )
+        velocity_next = call(restore_kernel, whole, in_hbm=(2,), inputs=3)(field, slots, share)
         taps, encode, head = call(
             functools.partial(spread_kernel, features),
             (
@@ -697,7 +703,8 @@
         taps = lax.all_to_all(taps, "sim", 0, 0, tiled=True)
         taps = jnp.sum(taps.astype(F32), axis=0).astype(BF16)
         taps = lax.all_gather(taps, "sim").astype(F32)
-        dense = e_own + e_one.astype(F32) + e_two.astype(F32) + e_three.astype(F32)
+        velocity_next = call(restore_kernel, whole, in_hbm=(2,), inputs=3)(field, slots, e_kept)
+        dense = e_kept + e_got.astype(F32)
         dense = dense.astype(BF16).reshape(sims, own_rows, wide)
         dense = lax.all_to_all(dense, "sim", 0, 0, tiled=True)
         dense = jnp.sum(dense.astype(F32), axis=0).astype(BF16)

time: 101 us -> 90 us (0.89)
  waiting for transfers between devices: 34.1 us -> 23.6 us
  local copies, waits for them, and re-layouts: 4.49 us -> 2.46 us
  starting transfers between devices: 40 us -> 41.1 us
    ppermute x28 -> x29, waiting for transfers between devices: 34.1 us -> 23.6 us  [swapped(): return lax.ppermute(value, axis, [(i, i ^ mask) for i in range(count)])]
    unnamed x18, local copies, waits for them, and re-layouts: 4.49 us -> 2.46 us
    ppermute x28 -> x29, starting transfers between devices: 33.1 us -> 34.2 us  [swapped(): return lax.ppermute(value, axis, [(i, i ^ mask) for i in range(count)])]
    pallas_call x8 -> x11, Pallas kernels: 5.27 us -> 5.24 us  [the longest x1 1.98 us: body(): call(restore_kernel, whole, in_hbm=(2,), inputs=3)(field, slots, share)]
  transfers between devices with their start and end apart: 32 -> 33, of which waited for: 13 -> 11; matrix products, arithmetic and copies ran while one was open for 0% -> 0% of each run, Pallas kernels for 13% -> 15%
where the time goes in v3:
time: 90 us; the launch traced here: 89.8 us
  starting transfers between devices  41.1 us (46%)
  waiting for transfers between devices  23.6 us (26%)
  Pallas kernels  21.6 us (24%)
  local copies, waits for them, and re-layouts  2.46 us (3%)
  between operations  0.96 us (1%)
    ppermute x29, starting transfers between devices, swapped(): return lax.ppermute(value, axis, [(i, i ^ mask) for i in range(count)])  34.2 us
    ppermute x29, waiting for transfers between devices, swapped(): return lax.ppermute(value, axis, [(i, i ^ mask) for i in range(count)])  23.6 us
    pallas_call x2, Pallas kernels, body(): part = call(inside_kernel, whole)(field, stencil)  9.5 us
    ppermute x4, starting transfers between devices, crossed(): lax.ppermute(value, axis, [(i, j) for i, j in route if 0 <= j < count])  6.95 us
    unnamed x18, local copies, waits for them, and re-layouts  2.46 us
    pallas_call x1, Pallas kernels, body(): call(restore_kernel, whole, in_hbm=(2,), inputs=3)(field, slots, share)  1.98 us
    pallas_call x1, Pallas kernels, body(): call(functools.partial(taps_kernel, groups, sims if direct else 1), tuple...  1.86 us
    pallas_call x1, Pallas kernels, body(): call(functools.partial(back_kernel, groups), (shaped(pair, F32), shaped(p...  1.82 us
  transfers between devices with their start and end apart: 33, of which 11 were waited for; matrix products, arithmetic and copies ran while one was open for 0% of the time, Pallas kernels for 15%

profile of v3, /device:TPU:0, one launch (start us, length us, event | category | flops | bytes accessed | tf_op | source)
XLA Modules:
  0.0 89.8 jit_solution(18318826107901904070)
XLA Ops:
  4.2 3.0 %collective-permute-start = (bf16[3,64,128]{2,1,0:T(8,128)(2,1)S(1)}, bf16[3,64,128]{2,1,0:T(8,128)(2,1)S(1)}, u32[]{:S(2)}, u32[]{:S(2)}) collective-permute-start(bf16[3,64,128]{2,1,0:T(8,128)(2,1)S(1)} %get-tuple-element.44), channel_id=1, source_target_pairs={{0,4},{4,0},{8,12},{12,8},{16,20},{20,16},{24,28},{28,24},{1,5},{5... | collective-permute-start | bytes 147464 | tf_op jit(solution)/shard_map/ppermute | solution.py:560
  7.2 3.6 %collective-permute-start.1 = (bf16[3,64,128]{2,1,0:T(8,128)(2,1)S(1)}, bf16[3,64,128]{2,1,0:T(8,128)(2,1)S(1)}, u32[]{:S(2)}, u32[]{:S(2)}) collective-permute-start(bf16[3,64,128]{2,1,0:T(8,128)(2,1)S(1)} %get-tuple-element.45), channel_id=1, source_target_pairs={{0,28},{4,8},{8,4},{12,16},{16,12},{20,24},{24,20},{28,0},{1,29},{... | collective-permute-start | bytes 147464 | tf_op jit(solution)/shard_map/ppermute | solution.py:568
  11.5 4.8 %shard_map.103.part = f32[3,256,512]{2,1,0:T(8,128)S(1)} custom-call(f32[3,256,512]{2,1,0:T(8,128)S(1)} %get-tuple-element.43.field, bf16[4736,512]{1,0:T(8,128)(2,1)S(1)} %bitcast.10), custom_call_target="tpu_custom_call" | custom-call | flops 1000 | bytes 1000 | tf_op jit(solution)/shard_map/pallas_call | solution.py:610
  17.5 1.9 %collective-permute-start.5 = (bf16[3,64,128]{2,1,0:T(8,128)(2,1)S(1)}, bf16[3,64,128]{2,1,0:T(8,128)(2,1)S(1)}, u32[]{:S(2)}, u32[]{:S(2)}) collective-permute-start(bf16[3,64,128]{2,1,0:T(8,128)(2,1)S(1)} %get-tuple-element.50), channel_id=1, source_target_pairs={{0,28},{4,8},{8,4},{12,16},{16,12},{20,24},{24,20},{28,0},{1,29},{... | collective-permute-start | bytes 147464 | tf_op jit(solution)/shard_map/ppermute | solution.py:568
  19.4 2.3 %collective-permute-start.6 = (bf16[3,32,128]{2,1,0:T(8,128)(2,1)S(1)}, bf16[3,32,128]{2,1,0:T(8,128)(2,1)S(1)}, u32[]{:S(2)}, u32[]{:S(2)}) collective-permute-start(bf16[3,32,128]{2,1,0:T(8,128)(2,1)S(1)} %get-tuple-element.51), channel_id=1, source_target_pairs={{0,1},{1,0},{2,3},{3,2},{4,5},{5,4},{6,7},{7,6},{8,9},{9,8},{10,11... | collective-permute-start | bytes 73736 | tf_op jit(solution)/shard_map/ppermute | solution.py:560
  22.6 4.6 %shard_map.105.part = f32[3,256,512]{2,1,0:T(8,128)S(1)} custom-call(f32[3,256,512]{2,1,0:T(8,128)S(1)} %get-tuple-element.48.field, bf16[4736,512]{1,0:T(8,128)(2,1)S(1)} %bitcast.10), custom_call_target="tpu_custom_call" | custom-call | flops 1000 | bytes 1000 | tf_op jit(solution)/shard_map/pallas_call | solution.py:613
  30.0 1.8 %collective-permute-start.8 = (bf16[256,256]{1,0:T(8,128)(2,1)S(1)}, bf16[256,256]{1,0:T(8,128)(2,1)S(1)}, u32[]{:S(2)}, u32[]{:S(2)}) collective-permute-start(bf16[256,256]{1,0:T(8,128)(2,1)S(1)} %get-tuple-element.54.h1.h_own), channel_id=1, source_target_pairs={{0,1},{1,0},{2,3},{3,2},{4,5},{5,4},{6,7},{7,6},{8,9},{9,8},{10,11... | collective-permute-start | bytes 393224 | tf_op jit(solution)/shard_map/ppermute | solution.py:560
  34.4 1.8 %collective-permute-start.12 = (bf16[256,256]{1,0:T(8,128)(2,1)S(1)}, bf16[256,256]{1,0:T(8,128)(2,1)S(1)}, u32[]{:S(2)}, u32[]{:S(2)}) collective-permute-start(bf16[256,256]{1,0:T(8,128)(2,1)S(1)} %get-tuple-element.56.dz2.d_own), channel_id=1, source_target_pairs={{0,3},{1,2},{2,1},{3,0},{4,7},{5,6},{6,5},{7,4},{8,11},{9,10},{10,... | collective-permute-start | bytes 393224 | tf_op jit(solution)/shard_map/ppermute | solution.py:560
  39.2 1.8 %shard_map.108 = (f32[2,64,1152]{2,1,0:T(8,128)S(1)}, bf16[2,64,1152]{2,1,0:T(8,128)(2,1)S(1)}) custom-call(bf16[256,256]{1,0:T(8,128)(2,1)S(1)} %get-tuple-element.56.dz2.d_own, bf16[256,256]{1,0:T(8,128)(2,1)S(1)} %collective-permute-done.11.pair.d_one, bf16[256,256]{1,0:T(8,128)(2,1)S(1)} %collective-permute-done.12.cross.d_three, ...), custom_call_target="tpu_custom_call" | custom-call | flops 1000 | bytes 1000 | tf_op jit(solution)/shard_map/pallas_call | solution.py:643
  41.1 2.1 %collective-permute-start.14 = (bf16[2,64,1152]{2,1,0:T(8,128)(2,1)S(1)}, bf16[2,64,1152]{2,1,0:T(8,128)(2,1)S(1)}, u32[]{:S(2)}, u32[]{:S(2)}) collective-permute-start(bf16[2,64,1152]{2,1,0:T(8,128)(2,1)S(1)} %get-tuple-element.62), channel_id=1, source_target_pairs={{0,1},{1,0},{2,3},{3,2},{4,5},{5,4},{6,7},{7,6},{8,9},{9,8},{10,11... | collective-permute-start | bytes 884744 | tf_op jit(solution)/shard_map/ppermute | solution.py:560
  44.4 1.7 %collective-permute-start.20 = (bf16[64,1152]{1,0:T(8,128)(2,1)S(1)}, bf16[64,1152]{1,0:T(8,128)(2,1)S(1)}, u32[]{:S(2)}, u32[]{:S(2)}) collective-permute-start(bf16[64,1152]{1,0:T(8,128)(2,1)S(1)} %get-tuple-element.72), channel_id=1, source_target_pairs={{0,2},{1,3},{2,0},{3,1},{4,6},{5,7},{6,4},{7,5},{8,10},{9,11},{10,... | collective-permute-start | bytes 442376 | tf_op jit(solution)/shard_map/ppermute | solution.py:560
  46.1 1.9 %shard_map.110 = (f32[216,256]{1,0:T(8,128)S(1)}, bf16[216,256]{1,0:T(8,128)(2,1)S(1)}, f32[216,256]{1,0:T(8,128)S(1)}, bf16[216,256]{1,0:T(8,128)(2,1)S(1)}, f3...) custom-call(bf16[256,256]{1,0:T(8,128)(2,1)S(1)} %get-tuple-element., ...), custom_call_target="tpu_custom_call" | custom-call | flops 1000 | bytes 1000 | tf_op jit(solution)/shard_map/pallas_call | solution.py:658
  50.8 3.3 %collective-permute-done.19.refs_0_ = bf16[216,256]{1,0:T(8,128)(2,1)S(1)} collective-permute-done((bf16[216,256]{1,0:T(8,128)(2,1)S(1)}, bf16[216,256]{1,0:T(8,128)(2,1)S(1)}, u32[]{:S(2)}, u32[]{:S(2)}) %collective-permute-start.19) | collective-permute-done | bytes 110624 | tf_op jit(solution)/shard_map/ppermute | solution.py:560
  54.1 1.7 %collective-permute-start.21 = (bf16[216,256]{1,0:T(8,128)(2,1)S(1)}, bf16[216,256]{1,0:T(8,128)(2,1)S(1)}, u32[]{:S(2)}, u32[]{:S(2)}) collective-permute-start(bf16[216,256]{1,0:T(8,128)(2,1)S(1)} %shard_map.113), channel_id=1, source_target_pairs={{0,8},{4,12},{8,0},{12,4},{16,24},{20,28},{24,16},{28,20},{1,9},{5... | collective-permute-start | bytes 331784 | tf_op jit(solution)/shard_map/ppermute | solution.py:560
  56.8 1.7 %collective-permute-start.17 = (bf16[216,256]{1,0:T(8,128)(2,1)S(1)}, bf16[216,256]{1,0:T(8,128)(2,1)S(1)}, u32[]{:S(2)}, u32[]{:S(2)}) collective-permute-start(bf16[216,256]{1,0:T(8,128)(2,1)S(1)} %shard_map.111), channel_id=1, source_target_pairs={{0,8},{4,12},{8,0},{12,4},{16,24},{20,28},{24,16},{28,20},{1,9},{5... | collective-permute-start | bytes 331784 | tf_op jit(solution)/shard_map/ppermute | solution.py:560
  58.4 2.3 %collective-permute-done.22.got = bf16[2,16,1152]{2,1,0:T(8,128)(2,1)S(1)} collective-permute-done((bf16[2,16,1152]{2,1,0:T(8,128)(2,1)S(1)}, bf16[2,16,1152]{2,1,0:T(8,128)(2,1)S(1)}, u32[]{:S(2)}, u32[]{:S(2)}) %collective-permute-start.22) | collective-permute-done | bytes 73760 | tf_op jit(solution)/shard_map/ppermute | solution.py:560
  60.9 2.9 %collective-permute-start.24 = (bf16[16,1152]{1,0:T(8,128)(2,1)S(1)}, bf16[16,1152]{1,0:T(8,128)(2,1)S(1)}, u32[]{:S(2)}, u32[]{:S(2)}) collective-permute-start(bf16[16,1152]{1,0:T(8,128)(2,1)S(1)} %get-tuple-element.75.refs_2_), channel_id=1, source_target_pairs={{0,16},{4,20},{8,24},{12,28},{16,0},{20,4},{24,8},{28,12},{1,17},{... | collective-permute-start | bytes 110600 | tf_op jit(solution)/shard_map/ppermute | solution.py:560
  63.8 3.1 %collective-permute-done.24 = bf16[16,1152]{1,0:T(8,128)(2,1)S(1)} collective-permute-done((bf16[16,1152]{1,0:T(8,128)(2,1)S(1)}, bf16[16,1152]{1,0:T(8,128)(2,1)S(1)}, u32[]{:S(2)}, u32[]{:S(2)}) %collective-permute-start.24) | collective-permute-done | bytes 36896 | tf_op jit(solution)/shard_map/ppermute | solution.py:560
  67.6 3.2 %collective-permute-done.25.dense_in = bf16[8,1152]{1,0:T(8,128)(2,1)S(1)} collective-permute-done((bf16[8,1152]{1,0:T(8,128)(2,1)S(1)}, bf16[8,1152]{1,0:T(8,128)(2,1)S(1)}, u32[]{:S(2)}, u32[]{:S(2)}) %collective-permute-start.25) | collective-permute-done | bytes 18464 | tf_op jit(solution)/shard_map/ppermute | solution.py:560
  70.8 4.0 %collective-permute-start.31 = (bf16[256,256]{1,0:T(8,128)(2,1)S(1)}, bf16[256,256]{1,0:T(8,128)(2,1)S(1)}, u32[]{:S(2)}, u32[]{:S(2)}) collective-permute-start(bf16[256,256]{1,0:T(8,128)(2,1)S(1)} %shard_map.117.after_this.own), channel_id=1, source_target_pairs={{0,24},{4,28},{8,16},{12,20},{16,8},{20,12},{24,0},{28,4},{1,25},{... | collective-permute-start | bytes 393224 | tf_op jit(solution)/shard_map/ppermute | solution.py:560
  75.8 2.1 %collective-permute-done.31.refs_5_ = bf16[256,256]{1,0:T(8,128)(2,1)S(1)} collective-permute-done((bf16[256,256]{1,0:T(8,128)(2,1)S(1)}, bf16[256,256]{1,0:T(8,128)(2,1)S(1)}, u32[]{:S(2)}, u32[]{:S(2)}) %collective-permute-start.31) | collective-permute-done | bytes 131104 | tf_op jit(solution)/shard_map/ppermute | solution.py:560
  78.3 3.7 %collective-permute-done.29.refs_3_ = bf16[256,256]{1,0:T(8,128)(2,1)S(1)} collective-permute-done((bf16[256,256]{1,0:T(8,128)(2,1)S(1)}, bf16[256,256]{1,0:T(8,128)(2,1)S(1)}, u32[]{:S(2)}, u32[]{:S(2)}) %collective-permute-start.29) | collective-permute-done | bytes 131104 | tf_op jit(solution)/shard_map/ppermute | solution.py:560
  82.4 1.6 %collective-permute-start.28 = (bf16[256,256]{1,0:T(8,128)(2,1)S(1)}, bf16[256,256]{1,0:T(8,128)(2,1)S(1)}, u32[]{:S(2)}, u32[]{:S(2)}) collective-permute-start(bf16[256,256]{1,0:T(8,128)(2,1)S(1)} %collective-permute-done.27.refs_1_), channel_id=1, source_target_pairs={{0,4},{4,0},{8,12},{12,8},{16,20},{20,16},{24,28},{28,24},{1,5},{5... | collective-permute-start | bytes 393224 | tf_op jit(solution)/shard_map/ppermute | solution.py:560
  84.0 2.0 %shard_map.118 = f32[3,256,512]{2,1,0:T(8,128)} custom-call(f32[3,256,512]{2,1,0:T(8,128)S(1)} %get-tuple-element.53.field, s32[1,256]{1,0:T(1,128)S(1)} %bitcast.14, bf16[256,256]{1,0:T(8,128)(2,1)S(1)} %shard_map.117.after_this.own), custom_call_target="tpu_custom_call" | custom-call | flops 1000 | bytes 1000 | tf_op jit(solution)/shard_map/pallas_call | solution.py:692
  (79 shorter events, 26.0 us)
Async XLA Ops:
  4.2 12.1 %collective-permute-start = (bf16[3,64,128]{2,1,0:T(8,128)(2,1)S(1)}, bf16[3,64,128]{2,1,0:T(8,128)(2,1)S(1)}, u32[]{:S(2)}, u32[]{:S(2)}) collective-permute-start(bf16[3,64,128]{2,1,0:T(8,128)(2,1)S(1)} %get-tuple-element.44), channel_id=1, source_target_pairs={{0,4},{4,0},{8,12},{12,8},{16,20},{20,16},{24,28},{28,24},{1,5},{5... | collective-permute-start | bytes 147464 | tf_op jit(solution)/shard_map/ppermute | solution.py:560
  7.2 9.2 %collective-permute-start.1 = (bf16[3,64,128]{2,1,0:T(8,128)(2,1)S(1)}, bf16[3,64,128]{2,1,0:T(8,128)(2,1)S(1)}, u32[]{:S(2)}, u32[]{:S(2)}) collective-permute-start(bf16[3,64,128]{2,1,0:T(8,128)(2,1)S(1)} %get-tuple-element.45), channel_id=1, source_target_pairs={{0,28},{4,8},{8,4},{12,16},{16,12},{20,24},{24,20},{28,0},{1,29},{... | collective-permute-start | bytes 147464 | tf_op jit(solution)/shard_map/ppermute | solution.py:568
  10.8 5.5 %collective-permute-start.2 = (bf16[3,32,128]{2,1,0:T(8,128)(2,1)S(1)}, bf16[3,32,128]{2,1,0:T(8,128)(2,1)S(1)}, u32[]{:S(2)}, u32[]{:S(2)}) collective-permute-start(bf16[3,32,128]{2,1,0:T(8,128)(2,1)S(1)} %get-tuple-element.46), channel_id=1, source_target_pairs={{0,1},{1,0},{2,3},{3,2},{4,5},{5,4},{6,7},{7,6},{8,9},{9,8},{10,11... | collective-permute-start | bytes 73736 | tf_op jit(solution)/shard_map/ppermute | solution.py:560
  10.8 5.6 %collective-permute-start.3 = (bf16[3,32,128]{2,1,0:T(8,128)(2,1)S(1)}, bf16[3,32,128]{2,1,0:T(8,128)(2,1)S(1)}, u32[]{:S(2)}, u32[]{:S(2)}) collective-permute-start(bf16[3,32,128]{2,1,0:T(8,128)(2,1)S(1)} %get-tuple-element.47), channel_id=1, source_target_pairs={{1,2},{2,1},{5,6},{6,5},{9,10},{10,9},{13,14},{14,13},{17,18},{18,... | collective-permute-start | bytes 73736 | tf_op jit(solution)/shard_map/ppermute | solution.py:568
  17.4 9.9 %collective-permute-start.4 = (bf16[3,64,128]{2,1,0:T(8,128)(2,1)S(1)}, bf16[3,64,128]{2,1,0:T(8,128)(2,1)S(1)}, u32[]{:S(2)}, u32[]{:S(2)}) collective-permute-start(bf16[3,64,128]{2,1,0:T(8,128)(2,1)S(1)} %get-tuple-element.49), channel_id=1, source_target_pairs={{0,4},{4,0},{8,12},{12,8},{16,20},{20,16},{24,28},{28,24},{1,5},{5... | collective-permute-start | bytes 147464 | tf_op jit(solution)/shard_map/ppermute | solution.py:560
  17.5 9.8 %collective-permute-start.5 = (bf16[3,64,128]{2,1,0:T(8,128)(2,1)S(1)}, bf16[3,64,128]{2,1,0:T(8,128)(2,1)S(1)}, u32[]{:S(2)}, u32[]{:S(2)}) collective-permute-start(bf16[3,64,128]{2,1,0:T(8,128)(2,1)S(1)} %get-tuple-element.50), channel_id=1, source_target_pairs={{0,28},{4,8},{8,4},{12,16},{16,12},{20,24},{24,20},{28,0},{1,29},{... | collective-permute-start | bytes 147464 | tf_op jit(solution)/shard_map/ppermute | solution.py:568
  19.4 7.9 %collective-permute-start.6 = (bf16[3,32,128]{2,1,0:T(8,128)(2,1)S(1)}, bf16[3,32,128]{2,1,0:T(8,128)(2,1)S(1)}, u32[]{:S(2)}, u32[]{:S(2)}) collective-permute-start(bf16[3,32,128]{2,1,0:T(8,128)(2,1)S(1)} %get-tuple-element.51), channel_id=1, source_target_pairs={{0,1},{1,0},{2,3},{3,2},{4,5},{5,4},{6,7},{7,6},{8,9},{9,8},{10,11... | collective-permute-start | bytes 73736 | tf_op jit(solution)/shard_map/ppermute | solution.py:560
  21.7 5.6 %collective-permute-start.7 = (bf16[3,32,128]{2,1,0:T(8,128)(2,1)S(1)}, bf16[3,32,128]{2,1,0:T(8,128)(2,1)S(1)}, u32[]{:S(2)}, u32[]{:S(2)}) collective-permute-start(bf16[3,32,128]{2,1,0:T(8,128)(2,1)S(1)} %get-tuple-element.52), channel_id=1, source_target_pairs={{1,2},{2,1},{5,6},{6,5},{9,10},{10,9},{13,14},{14,13},{17,18},{18,... | collective-permute-start | bytes 73736 | tf_op jit(solution)/shard_map/ppermute | solution.py:568
  44.4 6.3 %collective-permute-start.20 = (bf16[64,1152]{1,0:T(8,128)(2,1)S(1)}, bf16[64,1152]{1,0:T(8,128)(2,1)S(1)}, u32[]{:S(2)}, u32[]{:S(2)}) collective-permute-start(bf16[64,1152]{1,0:T(8,128)(2,1)S(1)} %get-tuple-element.72), channel_id=1, source_target_pairs={{0,2},{1,3},{2,0},{3,1},{4,6},{5,7},{6,4},{7,5},{8,10},{9,11},{10,... | collective-permute-start | bytes 442376 | tf_op jit(solution)/shard_map/ppermute | solution.py:560
  48.0 6.0 %collective-permute-start.19 = (bf16[216,256]{1,0:T(8,128)(2,1)S(1)}, bf16[216,256]{1,0:T(8,128)(2,1)S(1)}, u32[]{:S(2)}, u32[]{:S(2)}) collective-permute-start(bf16[216,256]{1,0:T(8,128)(2,1)S(1)} %get-tuple-element.71), channel_id=1, source_target_pairs={{0,4},{4,0},{8,12},{12,8},{16,20},{20,16},{24,28},{28,24},{1,5},{5... | collective-permute-start | bytes 331784 | tf_op jit(solution)/shard_map/ppermute | solution.py:560
  48.7 8.1 %collective-permute-start.16 = (bf16[216,256]{1,0:T(8,128)(2,1)S(1)}, bf16[216,256]{1,0:T(8,128)(2,1)S(1)}, u32[]{:S(2)}, u32[]{:S(2)}) collective-permute-start(bf16[216,256]{1,0:T(8,128)(2,1)S(1)} %get-tuple-element.67), channel_id=1, source_target_pairs={{0,4},{4,0},{8,12},{12,8},{16,20},{20,16},{24,28},{28,24},{1,5},{5... | collective-permute-start | bytes 331784 | tf_op jit(solution)/shard_map/ppermute | solution.py:560
  50.1 10.6 %collective-permute-start.18 = (bf16[216,256]{1,0:T(8,128)(2,1)S(1)}, bf16[216,256]{1,0:T(8,128)(2,1)S(1)}, u32[]{:S(2)}, u32[]{:S(2)}) collective-permute-start(bf16[216,256]{1,0:T(8,128)(2,1)S(1)} %get-tuple-element.69), channel_id=1, source_target_pairs={{0,4},{4,0},{8,12},{12,8},{16,20},{20,16},{24,28},{28,24},{1,5},{5... | collective-permute-start | bytes 331784 | tf_op jit(solution)/shard_map/ppermute | solution.py:560
  54.1 6.7 %collective-permute-start.21 = (bf16[216,256]{1,0:T(8,128)(2,1)S(1)}, bf16[216,256]{1,0:T(8,128)(2,1)S(1)}, u32[]{:S(2)}, u32[]{:S(2)}) collective-permute-start(bf16[216,256]{1,0:T(8,128)(2,1)S(1)} %shard_map.113), channel_id=1, source_target_pairs={{0,8},{4,12},{8,0},{12,4},{16,24},{20,28},{24,16},{28,20},{1,9},{5... | collective-permute-start | bytes 331784 | tf_op jit(solution)/shard_map/ppermute | solution.py:560
  55.7 5.0 %collective-permute-start.22 = (bf16[2,16,1152]{2,1,0:T(8,128)(2,1)S(1)}, bf16[2,16,1152]{2,1,0:T(8,128)(2,1)S(1)}, u32[]{:S(2)}, u32[]{:S(2)}) collective-permute-start(bf16[2,16,1152]{2,1,0:T(8,128)(2,1)S(1)} %get-tuple-element.73.refs_1_), channel_id=1, source_target_pairs={{0,8},{4,12},{8,0},{12,4},{16,24},{20,28},{24,16},{28,20},{1,9},{5... | collective-permute-start | bytes 221192 | tf_op jit(solution)/shard_map/ppermute | solution.py:560
  56.2 11.4 %collective-permute-start.15 = (bf16[216,256]{1,0:T(8,128)(2,1)S(1)}, bf16[216,256]{1,0:T(8,128)(2,1)S(1)}, u32[]{:S(2)}, u32[]{:S(2)}) collective-permute-start(bf16[216,256]{1,0:T(8,128)(2,1)S(1)} %get-tuple-element.65), channel_id=1, source_target_pairs={{0,4},{4,0},{8,12},{12,8},{16,20},{20,16},{24,28},{28,24},{1,5},{5... | collective-permute-start | bytes 331784 | tf_op jit(solution)/shard_map/ppermute | solution.py:560
  56.8 10.8 %collective-permute-start.17 = (bf16[216,256]{1,0:T(8,128)(2,1)S(1)}, bf16[216,256]{1,0:T(8,128)(2,1)S(1)}, u32[]{:S(2)}, u32[]{:S(2)}) collective-permute-start(bf16[216,256]{1,0:T(8,128)(2,1)S(1)} %shard_map.111), channel_id=1, source_target_pairs={{0,8},{4,12},{8,0},{12,4},{16,24},{20,28},{24,16},{28,20},{1,9},{5... | collective-permute-start | bytes 331784 | tf_op jit(solution)/shard_map/ppermute | solution.py:560
  60.8 10.0 %collective-permute-start.23 = (bf16[216,256]{1,0:T(8,128)(2,1)S(1)}, bf16[216,256]{1,0:T(8,128)(2,1)S(1)}, u32[]{:S(2)}, u32[]{:S(2)}) collective-permute-start(bf16[216,256]{1,0:T(8,128)(2,1)S(1)} %shard_map.115), channel_id=1, source_target_pairs={{0,16},{4,20},{8,24},{12,28},{16,0},{20,4},{24,8},{28,12},{1,17},{... | collective-permute-start | bytes 331784 | tf_op jit(solution)/shard_map/ppermute | solution.py:560
  60.9 6.0 %collective-permute-start.24 = (bf16[16,1152]{1,0:T(8,128)(2,1)S(1)}, bf16[16,1152]{1,0:T(8,128)(2,1)S(1)}, u32[]{:S(2)}, u32[]{:S(2)}) collective-permute-start(bf16[16,1152]{1,0:T(8,128)(2,1)S(1)} %get-tuple-element.75.refs_2_), channel_id=1, source_target_pairs={{0,16},{4,20},{8,24},{12,28},{16,0},{20,4},{24,8},{28,12},{1,17},{... | collective-permute-start | bytes 110600 | tf_op jit(solution)/shard_map/ppermute | solution.py:560
  70.8 7.1 %collective-permute-start.31 = (bf16[256,256]{1,0:T(8,128)(2,1)S(1)}, bf16[256,256]{1,0:T(8,128)(2,1)S(1)}, u32[]{:S(2)}, u32[]{:S(2)}) collective-permute-start(bf16[256,256]{1,0:T(8,128)(2,1)S(1)} %shard_map.117.after_this.own), channel_id=1, source_target_pairs={{0,24},{4,28},{8,16},{12,20},{16,8},{20,12},{24,0},{28,4},{1,25},{... | collective-permute-start | bytes 393224 | tf_op jit(solution)/shard_map/ppermute | solution.py:560
  74.9 7.2 %collective-permute-start.29 = (bf16[256,256]{1,0:T(8,128)(2,1)S(1)}, bf16[256,256]{1,0:T(8,128)(2,1)S(1)}, u32[]{:S(2)}, u32[]{:S(2)}) collective-permute-start(bf16[256,256]{1,0:T(8,128)(2,1)S(1)} %shard_map.117.after_this.own), channel_id=1, source_target_pairs={{0,16},{4,20},{8,24},{12,28},{16,0},{20,4},{24,8},{28,12},{1,17},{... | collective-permute-start | bytes 393224 | tf_op jit(solution)/shard_map/ppermute | solution.py:560
  75.0 7.4 %collective-permute-start.27 = (bf16[256,256]{1,0:T(8,128)(2,1)S(1)}, bf16[256,256]{1,0:T(8,128)(2,1)S(1)}, u32[]{:S(2)}, u32[]{:S(2)}) collective-permute-start(bf16[256,256]{1,0:T(8,128)(2,1)S(1)} %shard_map.117.after_this.own), channel_id=1, source_target_pairs={{0,8},{4,12},{8,0},{12,4},{16,24},{20,28},{24,16},{28,20},{1,9},{5... | collective-permute-start | bytes 393224 | tf_op jit(solution)/shard_map/ppermute | solution.py:560
  75.5 10.5 %collective-permute-start.26 = (bf16[256,256]{1,0:T(8,128)(2,1)S(1)}, bf16[256,256]{1,0:T(8,128)(2,1)S(1)}, u32[]{:S(2)}, u32[]{:S(2)}) collective-permute-start(bf16[256,256]{1,0:T(8,128)(2,1)S(1)} %shard_map.117.after_this.own), channel_id=1, source_target_pairs={{0,4},{4,0},{8,12},{12,8},{16,20},{20,16},{24,28},{28,24},{1,5},{5... | collective-permute-start | bytes 393224 | tf_op jit(solution)/shard_map/ppermute | solution.py:560
  77.9 8.1 %collective-permute-start.32 = (bf16[256,256]{1,0:T(8,128)(2,1)S(1)}, bf16[256,256]{1,0:T(8,128)(2,1)S(1)}, u32[]{:S(2)}, u32[]{:S(2)}) collective-permute-start(bf16[256,256]{1,0:T(8,128)(2,1)S(1)} %collective-permute-done.31.refs_5_), channel_id=1, source_target_pairs={{0,4},{4,0},{8,12},{12,8},{16,20},{20,16},{24,28},{28,24},{1,5},{5... | collective-permute-start | bytes 393224 | tf_op jit(solution)/shard_map/ppermute | solution.py:560
  82.4 6.0 %collective-permute-start.28 = (bf16[256,256]{1,0:T(8,128)(2,1)S(1)}, bf16[256,256]{1,0:T(8,128)(2,1)S(1)}, u32[]{:S(2)}, u32[]{:S(2)}) collective-permute-start(bf16[256,256]{1,0:T(8,128)(2,1)S(1)} %collective-permute-done.27.refs_1_), channel_id=1, source_target_pairs={{0,4},{4,0},{8,12},{12,8},{16,20},{20,16},{24,28},{28,24},{1,5},{5... | collective-permute-start | bytes 393224 | tf_op jit(solution)/shard_map/ppermute | solution.py:560
  (18 other events, 117.3 us)

commit v4 on v3

--- a/solution.py
+++ b/solution.py
@@ -55,11 +55,6 @@
     deriv = derivative_matrix(count)
     single = np.eye(count)
     square = np.eye(count * count)
-    along_x = np.kron(deriv, square)
-    along_y = np.kron(single, np.kron(deriv, single))
-    along_z = np.kron(square, deriv)
-    laplace = along_x @ along_x + along_y @ along_y + along_z @ along_z
-    half = count**3 // 2
     grid = np.arange(count**3).reshape(count, count, count)
     final = count - 1
     faces = [
@@ -78,8 +73,8 @@
 
     picks = [pick(which) for which in faces]
     none = np.zeros_like(picks[0])
-    taken = np.concatenate([picks[i] for i in (1, 0, 3, 2, 5, 4)], axis=1)
-    placed = np.concatenate(picks, axis=1).T
+    taken = np.concatenate([picks[i] for i in (3, 2, 5, 4)], axis=1)
+    placed = np.concatenate(picks[2:], axis=1).T
     bottom = np.zeros((count**3, count * count))
     for first in range(count):
         for middle in range(count):
@@ -87,19 +82,44 @@
                 bottom[grid[first, middle, inner], first * count + inner] = (
                     VISCOSITY * deriv[0, middle]
                 )
-    first = in_three(TIME_STEP * VISCOSITY * laplace.T)
-    second = in_three(-TIME_STEP * along_x.T)
-    third = np.concatenate(
+    mirrored = np.concatenate([deriv, deriv @ deriv], axis=0)[:, ::-1].reshape(2, count, count)
+    straight = np.stack([deriv, deriv @ deriv])
+    half = count // 2
+    scale = np.array([-TIME_STEP, TIME_STEP * VISCOSITY])[:, None, None]
+
+    def along_first(sign):
+        mixed = (0.5 * scale * (straight + sign * mirrored))[:, :half, :half]
+        return in_three(np.concatenate([np.kron(part.T, square) for part in mixed], axis=1))
+
+    small_y = np.kron(deriv, single)
+    small_z = np.kron(single, deriv)
+    curved = TIME_STEP * VISCOSITY * (small_y @ small_y + small_z @ small_z).T
+    small_y = -TIME_STEP * small_y.T
+    small_z = -TIME_STEP * small_z.T
+    blank = np.zeros_like(curved)
+
+    def across(blocks):
+        table = in_three(np.concatenate(blocks, axis=1))
+        return np.concatenate([table, np.zeros((count * count, table.shape[1]), table.dtype)], axis=0)
+
+    both = np.concatenate(
         [
-            in_three(-TIME_STEP * along_y.T[:half, :half]),
-            in_three(-TIME_STEP * along_z.T[:half, :half]),
+            across([small_y, curved, small_z, blank]),
+            across([curved, small_y, blank, small_z]),
         ],
         axis=1,
     )
     filled = np.zeros((count**3, count**3 - taken.shape[1]))
-    fourth = short(placed)
-    fifth = short(np.concatenate([taken, filled], axis=1))
-    stencil = np.concatenate([first, second, third, fourth, fifth], axis=0)
+    stencil = np.concatenate(
+        [
+            along_first(1.0),
+            along_first(-1.0),
+            both,
+            short(placed),
+            short(np.concatenate([taken, filled], axis=1)),
+        ],
+        axis=0,
+    )
     wall = in_three(np.concatenate([bottom, none, none, bottom], axis=1))
     return stencil, wall
 
@@ -240,53 +260,84 @@
     width = field.shape[2]
     ez = rows // (EX * EY)
     half = width // 2
-    chosen = 6 * NP * NP
-    lap = stencil.at[0 : 3 * width]
-    kx = stencil.at[3 * width : 6 * width]
-    kyz = stencil.at[6 * width : 6 * width + 3 * half]
-    start = 6 * width + 3 * half
-    placed = stencil.at[start : start + chosen]
-    taken = stencil.at[start + chosen : start + chosen + width]
+    side = NP * NP
+    pair = 2 * side
+    tiles = width // pair
+    even = stencil.at[0 : 3 * half]
+    odd = stencil.at[3 * half : 6 * half]
+    start = 6 * half
+    across = stencil.at[start : start + 4 * side]
+    placed = stencil.at[start + 4 * side : start + 8 * side]
+    taken = stencil.at[start + 8 * side : start + 8 * side + width]
     keep = 1.0 - FACE_RATE * face_count(width)
-    whole = field[...].reshape(3 * rows, width)
-    high, low = split_two(whole)
-    lanes = lax.broadcasted_iota(jnp.int32, (1, 2 * NP * NP), 1)
-    first = lanes < NP * NP
-
-    faces = dot(high, taken[:, :chosen])
-    in_x = faces[:, 0 : 2 * NP * NP].reshape(3, EX, EY * ez, 2 * NP * NP)
-    beside_x = jnp.concatenate(
-        [
-            jnp.where(first, 0.0, in_x[:, 1:2]),
-            jnp.where(first, in_x[:, 0:1], 0.0),
-        ],
-        axis=1,
-    ).reshape(3 * rows, 2 * NP * NP)
-    in_y = faces[:, 2 * NP * NP : 4 * NP * NP].reshape(3 * EX, EY, ez, 2 * NP * NP)
-    wall = jnp.zeros((3 * EX, 1, ez, 2 * NP * NP), F32)
+    lanes = lax.broadcasted_iota(jnp.int32, (1, pair), 1)
+    first = lanes < side
+    tile = [field[:, :, j * pair : (j + 1) * pair].reshape(3 * rows, pair) for j in range(tiles)]
+    swap = [pltpu.roll(value, side, 1) for value in tile]
+
+    high = [value.astype(BF16).astype(F32) for value in tile]
+    high_swap = [value.astype(BF16).astype(F32) for value in swap]
+
+    faces = dot(jnp.concatenate(high, axis=1).astype(BF16), taken[:, : 4 * side])
+    in_y = faces[:, :pair].reshape(3 * EX, EY, ez, pair)
+    wall = jnp.zeros((3 * EX, 1, ez, pair), F32)
     beside_y = jnp.where(
         first,
         jnp.concatenate([wall, in_y[:, :-1]], axis=1),
         jnp.concatenate([in_y[:, 1:], wall], axis=1),
-    ).reshape(3 * rows, 2 * NP * NP)
-    in_z = faces[:, 4 * NP * NP :].reshape(3 * EX * EY, ez, 2 * NP * NP)
+    ).reshape(3 * rows, pair)
+    in_z = faces[:, pair:].reshape(3 * EX * EY, ez, pair)
     beside_z = jnp.where(
         first, pltpu.roll(in_z, 1, 1), pltpu.roll(in_z, ez - 1, 1)
-    ).reshape(3 * rows, 2 * NP * NP)
-    beside = jnp.concatenate([beside_x, beside_y, beside_z], axis=1).astype(BF16)
-
-    three = jnp.concatenate([high, low, high], axis=1)
-    for n in range(2):
-        cols = slice(n * half, (n + 1) * half)
-        own = jnp.concatenate([high[:, cols], low[:, cols], high[:, cols]], axis=1)
-        value = whole[:, cols] * keep[:, cols] + dot(three, lap[:, cols])
+    ).reshape(3 * rows, pair)
+    beside = jnp.concatenate([beside_y, beside_z], axis=1).astype(BF16)
+
+    def three(value):
+        top, rest = split_two(value)
+        return jnp.concatenate([top, rest, top], axis=1)
+
+    mirror = jnp.concatenate([swap[tiles - 1 - j] for j in range(tiles // 2)], axis=1)
+    near = jnp.concatenate(tile[: tiles // 2], axis=1)
+    from_even = dot(three(near + mirror), even[...])
+    from_odd = dot(three(near - mirror), odd[...])
+
+    for j in range(tiles):
+        cols = slice(j * pair, (j + 1) * pair)
+        low = tile[j] - high[j]
+        low_swap = swap[j] - high_swap[j]
+        one = jnp.concatenate([jnp.where(first, high[j], low_swap), high[j]], axis=1).astype(BF16)
+        two = jnp.concatenate([jnp.where(first, high_swap[j], low), high_swap[j]], axis=1).astype(BF16)
+        got_one = dot(one, across[:, : 4 * side])
+        got_two = dot(two, across[:, 4 * side :])
+        slope_y = jnp.where(first, got_one[:, :pair], got_two[:, :pair])
+        slope_z = got_one[:, pair:] + got_two[:, pair:]
+        curve = jnp.where(first, got_two[:, :pair], got_one[:, :pair])
+        if j < tiles // 2:
+            at = slice(j * pair, (j + 1) * pair)
+            up = slice(half + j * pair, half + (j + 1) * pair)
+            slope_x = from_odd[:, at] + from_even[:, at]
+            curve = pltpu.roll(curve, side, 1) + (from_even[:, up] + from_odd[:, up])
+        else:
+            k = tiles - 1 - j
+            at = slice(k * pair, (k + 1) * pair)
+            up = slice(half + k * pair, half + (k + 1) * pair)
+            slope_x = pltpu.roll(from_odd[:, at] - from_even[:, at], side, 1)
+            curve = pltpu.roll(curve + (from_even[:, up] - from_odd[:, up]), side, 1)
+        value = tile[j] * keep[:, cols] + curve
         value = value + FACE_RATE * dot(beside, placed[:, cols])
-        for d, slope in enumerate(
-            (dot(three, kx[:, cols]), dot(own, kyz[:, :half]), dot(own, kyz[:, half:]))
-        ):
-            speed = field[d][:, cols]
-            value = value + (slope.reshape(3, rows, half) * speed[None]).reshape(3 * rows, half)
-        part[:, :, cols] = value.reshape(3, rows, half)
+        value = value.reshape(3, rows, pair)
+        for d, slope in enumerate((slope_x, slope_y, slope_z)):
+            value = value + slope.reshape(3, rows, pair) * tile[j].reshape(3, rows, pair)[d][None]
+        layer = EY * ez
+        if j == 0:
+            beyond = swap[tiles - 1].reshape(3, rows, pair)[:, :layer]
+            beyond = jnp.where(first, FACE_RATE * beyond, 0.0)
+            value = jnp.concatenate([value[:, :layer], value[:, layer:] + beyond], axis=1)
+        if j == tiles - 1:
+            beyond = swap[0].reshape(3, rows, pair)[:, layer:]
+            beyond = jnp.where(first, 0.0, FACE_RATE * beyond)
+            value = jnp.concatenate([value[:, :layer] + beyond, value[:, layer:]], axis=1)
+        part[:, :, cols] = value
 
 
 def join_kernel(part, pair_x, cross_x, pair_y, cross_y, field, *edges):
@@ -474,7 +525,10 @@
         piece[...] = out[pl.ds(at, piece_rows)].astype(piece.dtype)
 
 
-def dense_kernel(kept, got, out_kept, out_sent):
+def dense_kernel(kept, got, *refs):
+    out_kept, out_sent = refs[-5:-3]
+    for source, target in zip(refs[:3], refs[-3:]):
+        target[...] = source[...]
     total = kept[...] + got[...].astype(F32)
     grid = total.reshape(2, 2, kept.shape[0] // 4, kept.shape[1])
     odd = lax.rem(lax.div(lax.axis_index("sim"), 2), 2) == 1
@@ -667,11 +721,14 @@
         inputs=9,
     )(h1, h_one, h_two, h_three, dz2, d_one, d_two, d_three, e_kept)
     if direct:
-        taps_in = {k: swapped(taps[k + 1], "sim", 1) for k in (6, 4, 2, 0)}
         tap_piece = shaped((tap_rows, channels), BF16)
         part = (2, 2 * own_rows, wide)
-        e_kept, e_sent = call(dense_kernel, (shaped(part, F32), shaped(part, BF16)))(e_kept, e_got)
+        e_kept, e_sent, *later = call(
+            dense_kernel, (shaped(part, F32), shaped(part, BF16)) + (tap_piece,) * 3
+        )(e_kept, e_got, taps[5], taps[3], taps[1])
         e_got = swapped(e_sent, "sim", 2)
+        taps_in = {6: swapped(taps[7], "sim", 1)}
+        taps_in.update((k, swapped(piece, "sim", 1)) for k, piece in zip((4, 2, 0), later))
         add_two = call(functools.partial(sum_kernel, 2), tap_piece)
         add_three = call(functools.partial(sum_kernel, 3), tap_piece)
         six = swapped(add_two(taps[6], taps_in[6], e_sent), "sim", 2)
@@ -681,7 +738,7 @@
         e_got = swapped(e_sent, "sim", 4)
         four = swapped(add_three(taps[4], taps_in[4], six, e_sent), "sim", 4)
         part = shaped((own_rows, wide), F32), shaped((own_rows, wide), BF16)
-        e_kept, e_sent = call(functools.partial(half_kernel, 1), part)(
+        e_kept, e_sent = call(functools.partial(half_kernel, 1), part, flops=4 * 10**9)(
             e_kept.reshape(2, own_rows, wide), e_got.reshape(2, own_rows, wide)
         )
         e_got = swapped(e_sent, "sim", 1)
@@ -689,7 +746,8 @@
         share = call(share_kernel, shaped((tap_rows + blocks * own_rows, channels), BF16))(
             taps[0], taps_in[0], two, four, e_kept, e_got
         )
-        velocity_next = call(restore_kernel, whole, in_hbm=(2,), inputs=3)(field, slots, share)
+        shares = gathered(share, sims)
+        velocity_next = call(restore_kernel, whole, in_hbm=(2,), inputs=3)(field, slots, shares[1])
         taps, encode, head = call(
             functools.partial(spread_kernel, features),
             (
@@ -697,7 +755,7 @@
                 shaped((quarter, features), F32),
                 shaped((quarter, outputs), F32),
             ),
-        )(*gathered(share, sims))
+        )(*shares)
     else:
         taps = taps[0].reshape(sims, tap_rows, channels)
         taps = lax.all_to_all(taps, "sim", 0, 0, tiled=True)

time: 90 us -> 84.1 us (0.934)
  Pallas kernels: 21.6 us -> 18.9 us
  waiting for transfers between devices: 23.6 us -> 21.2 us
    pallas_call x2, Pallas kernels: 9.5 us -> 6.73 us  [body(): part = call(inside_kernel, whole)(field, stencil)]
    ppermute x29, waiting for transfers between devices: 23.6 us -> 21.2 us  [swapped(): return lax.ppermute(value, axis, [(i, i ^ mask) for i in range(count)])]
    ppermute x29, starting transfers between devices: 34.2 us -> 33.2 us  [swapped(): return lax.ppermute(value, axis, [(i, i ^ mask) for i in range(count)])]
    unnamed x18 -> x16, local copies, waits for them, and re-layouts: 2.46 us -> 2.11 us
  transfers between devices with their start and end apart: 33 -> 33, of which waited for: 11 -> 14; matrix products, arithmetic and copies ran while one was open for 0% -> 0% of each run, Pallas kernels for 15% -> 13%
where the time goes in v4:
time: 84.1 us; the launch traced here: 83.9 us
  starting transfers between devices  40.8 us (49%)
  waiting for transfers between devices  21.2 us (25%)
  Pallas kernels  18.9 us (22%)
  local copies, waits for them, and re-layouts  2.11 us (3%)
  between operations  0.92 us (1%)
    ppermute x29, starting transfers between devices, swapped(): return lax.ppermute(value, axis, [(i, i ^ mask) for i in range(count)])  33.2 us
    ppermute x29, waiting for transfers between devices, swapped(): return lax.ppermute(value, axis, [(i, i ^ mask) for i in range(count)])  21.2 us
    ppermute x4, starting transfers between devices, crossed(): lax.ppermute(value, axis, [(i, j) for i, j in route if 0 <= j < count])  7.67 us
    pallas_call x2, Pallas kernels, body(): part = call(inside_kernel, whole)(field, stencil)  6.73 us
    unnamed x16, local copies, waits for them, and re-layouts  2.11 us
    pallas_call x1, Pallas kernels, body(): call(restore_kernel, whole, in_hbm=(2,), inputs=3)(field, slots, shares[1])  1.98 us
    pallas_call x1, Pallas kernels, body(): call(functools.partial(taps_kernel, groups, sims if direct else 1), tuple...  1.86 us
    pallas_call x1, Pallas kernels, body(): call(functools.partial(back_kernel, groups), (shaped(pair, F32), shaped(p...  1.82 us
  transfers between devices with their start and end apart: 33, of which 14 were waited for; matrix products, arithmetic and copies ran while one was open for 0% of the time, Pallas kernels for 13%

profile of v4, /device:TPU:0, one launch (start us, length us, event | category | flops | bytes accessed | tf_op | source)
XLA Modules:
  0.0 83.9 jit_solution(7171814481014711409)
XLA Ops:
  3.9 3.0 %collective-permute-start = (bf16[3,64,128]{2,1,0:T(8,128)(2,1)S(1)}, bf16[3,64,128]{2,1,0:T(8,128)(2,1)S(1)}, u32[]{:S(2)}, u32[]{:S(2)}) collective-permute-start(bf16[3,64,128]{2,1,0:T(8,128)(2,1)S(1)} %get-tuple-element.47), channel_id=1, source_target_pairs={{0,4},{4,0},{8,12},{12,8},{16,20},{20,16},{24,28},{28,24},{1,5},{5... | collective-permute-start | bytes 147464 | tf_op jit(solution)/shard_map/ppermute | solution.py:614
  6.9 3.6 %collective-permute-start.1 = (bf16[3,64,128]{2,1,0:T(8,128)(2,1)S(1)}, bf16[3,64,128]{2,1,0:T(8,128)(2,1)S(1)}, u32[]{:S(2)}, u32[]{:S(2)}) collective-permute-start(bf16[3,64,128]{2,1,0:T(8,128)(2,1)S(1)} %get-tuple-element.48), channel_id=1, source_target_pairs={{0,28},{4,8},{8,4},{12,16},{16,12},{20,24},{24,20},{28,0},{1,29},{... | collective-permute-start | bytes 147464 | tf_op jit(solution)/shard_map/ppermute | solution.py:622
  11.1 3.5 %shard_map.103.part = f32[3,256,512]{2,1,0:T(8,128)S(1)} custom-call(f32[3,256,512]{2,1,0:T(8,128)S(1)} %get-tuple-element.46.field, bf16[2560,512]{1,0:T(8,128)(2,1)S(1)} %copy-done.1), custom_call_target="tpu_custom_call" | custom-call | flops 1000 | bytes 1000 | tf_op jit(solution)/shard_map/pallas_call | solution.py:664
  15.8 2.6 %collective-permute-start.5 = (bf16[3,64,128]{2,1,0:T(8,128)(2,1)S(1)}, bf16[3,64,128]{2,1,0:T(8,128)(2,1)S(1)}, u32[]{:S(2)}, u32[]{:S(2)}) collective-permute-start(bf16[3,64,128]{2,1,0:T(8,128)(2,1)S(1)} %get-tuple-element.53), channel_id=1, source_target_pairs={{0,28},{4,8},{8,4},{12,16},{16,12},{20,24},{24,20},{28,0},{1,29},{... | collective-permute-start | bytes 147464 | tf_op jit(solution)/shard_map/ppermute | solution.py:622
  18.4 1.6 %collective-permute-start.6 = (bf16[3,32,128]{2,1,0:T(8,128)(2,1)S(1)}, bf16[3,32,128]{2,1,0:T(8,128)(2,1)S(1)}, u32[]{:S(2)}, u32[]{:S(2)}) collective-permute-start(bf16[3,32,128]{2,1,0:T(8,128)(2,1)S(1)} %get-tuple-element.54), channel_id=1, source_target_pairs={{0,1},{1,0},{2,3},{3,2},{4,5},{5,4},{6,7},{7,6},{8,9},{9,8},{10,11... | collective-permute-start | bytes 73736 | tf_op jit(solution)/shard_map/ppermute | solution.py:614
  20.9 3.2 %shard_map.105.part = f32[3,256,512]{2,1,0:T(8,128)S(1)} custom-call(f32[3,256,512]{2,1,0:T(8,128)S(1)} %get-tuple-element.51.field, bf16[2560,512]{1,0:T(8,128)(2,1)S(1)} %copy-done.1), custom_call_target="tpu_custom_call" | custom-call | flops 1000 | bytes 1000 | tf_op jit(solution)/shard_map/pallas_call | solution.py:667
  26.9 1.8 %collective-permute-start.8 = (bf16[256,256]{1,0:T(8,128)(2,1)S(1)}, bf16[256,256]{1,0:T(8,128)(2,1)S(1)}, u32[]{:S(2)}, u32[]{:S(2)}) collective-permute-start(bf16[256,256]{1,0:T(8,128)(2,1)S(1)} %get-tuple-element.57.h1.h_own), channel_id=1, source_target_pairs={{0,1},{1,0},{2,3},{3,2},{4,5},{5,4},{6,7},{7,6},{8,9},{9,8},{10,11... | collective-permute-start | bytes 393224 | tf_op jit(solution)/shard_map/ppermute | solution.py:614
  31.2 1.8 %collective-permute-start.12 = (bf16[256,256]{1,0:T(8,128)(2,1)S(1)}, bf16[256,256]{1,0:T(8,128)(2,1)S(1)}, u32[]{:S(2)}, u32[]{:S(2)}) collective-permute-start(bf16[256,256]{1,0:T(8,128)(2,1)S(1)} %get-tuple-element.59.dz2.d_own), channel_id=1, source_target_pairs={{0,3},{1,2},{2,1},{3,0},{4,7},{5,6},{6,5},{7,4},{8,11},{9,10},{10,... | collective-permute-start | bytes 393224 | tf_op jit(solution)/shard_map/ppermute | solution.py:614
  33.0 1.5 %collective-permute-start.11 = (bf16[256,256]{1,0:T(8,128)(2,1)S(1)}, bf16[256,256]{1,0:T(8,128)(2,1)S(1)}, u32[]{:S(2)}, u32[]{:S(2)}) collective-permute-start(bf16[256,256]{1,0:T(8,128)(2,1)S(1)} %get-tuple-element.59.dz2.d_own), channel_id=1, source_target_pairs={{0,1},{1,0},{2,3},{3,2},{4,5},{5,4},{6,7},{7,6},{8,9},{9,8},{10,11... | collective-permute-start | bytes 393224 | tf_op jit(solution)/shard_map/ppermute | solution.py:614
  36.1 1.8 %shard_map.108 = (f32[2,64,1152]{2,1,0:T(8,128)S(1)}, bf16[2,64,1152]{2,1,0:T(8,128)(2,1)S(1)}) custom-call(bf16[256,256]{1,0:T(8,128)(2,1)S(1)} %get-tuple-element.59.dz2.d_own, bf16[256,256]{1,0:T(8,128)(2,1)S(1)} %collective-permute-done.11.pair.d_one, bf16[256,256]{1,0:T(8,128)(2,1)S(1)} %collective-permute-done.12.cross.d_three, ...), custom_call_target="tpu_custom_call" | custom-call | flops 1000 | bytes 1000 | tf_op jit(solution)/shard_map/pallas_call | solution.py:697
  37.9 2.1 %collective-permute-start.14 = (bf16[2,64,1152]{2,1,0:T(8,128)(2,1)S(1)}, bf16[2,64,1152]{2,1,0:T(8,128)(2,1)S(1)}, u32[]{:S(2)}, u32[]{:S(2)}) collective-permute-start(bf16[2,64,1152]{2,1,0:T(8,128)(2,1)S(1)} %get-tuple-element.65), channel_id=1, source_target_pairs={{0,1},{1,0},{2,3},{3,2},{4,5},{5,4},{6,7},{7,6},{8,9},{9,8},{10,11... | collective-permute-start | bytes 884744 | tf_op jit(solution)/shard_map/ppermute | solution.py:614
  41.3 1.7 %collective-permute-start.15 = (bf16[64,1152]{1,0:T(8,128)(2,1)S(1)}, bf16[64,1152]{1,0:T(8,128)(2,1)S(1)}, u32[]{:S(2)}, u32[]{:S(2)}) collective-permute-start(bf16[64,1152]{1,0:T(8,128)(2,1)S(1)} %get-tuple-element.68), channel_id=1, source_target_pairs={{0,2},{1,3},{2,0},{3,1},{4,6},{5,7},{6,4},{7,5},{8,10},{9,11},{10,... | collective-permute-start | bytes 442376 | tf_op jit(solution)/shard_map/ppermute | solution.py:614
  43.0 1.9 %shard_map.110 = (f32[216,256]{1,0:T(8,128)S(1)}, bf16[216,256]{1,0:T(8,128)(2,1)S(1)}, f32[216,256]{1,0:T(8,128)S(1)}, bf16[216,256]{1,0:T(8,128)(2,1)S(1)}, f3...) custom-call(bf16[256,256]{1,0:T(8,128)(2,1)S(1)} %get-tuple-element., ...), custom_call_target="tpu_custom_call" | custom-call | flops 1000 | bytes 1000 | tf_op jit(solution)/shard_map/pallas_call | solution.py:712
  45.5 1.9 %collective-permute-done.15.got = bf16[64,1152]{1,0:T(8,128)(2,1)S(1)} collective-permute-done((bf16[64,1152]{1,0:T(8,128)(2,1)S(1)}, bf16[64,1152]{1,0:T(8,128)(2,1)S(1)}, u32[]{:S(2)}, u32[]{:S(2)}) %collective-permute-start.15) | collective-permute-done | bytes 147488 | tf_op jit(solution)/shard_map/ppermute | solution.py:614
  47.5 1.7 %collective-permute-start.22 = (bf16[2,16,1152]{2,1,0:T(8,128)(2,1)S(1)}, bf16[2,16,1152]{2,1,0:T(8,128)(2,1)S(1)}, u32[]{:S(2)}, u32[]{:S(2)}) collective-permute-start(bf16[2,16,1152]{2,1,0:T(8,128)(2,1)S(1)} %get-tuple-element.79.refs_1_), channel_id=1, source_target_pairs={{0,8},{4,12},{8,0},{12,4},{16,24},{20,28},{24,16},{28,20},{1,9},{5... | collective-permute-start | bytes 221192 | tf_op jit(solution)/shard_map/ppermute | solution.py:614
  52.2 1.9 %collective-permute-start.16 = (bf16[216,256]{1,0:T(8,128)(2,1)S(1)}, bf16[216,256]{1,0:T(8,128)(2,1)S(1)}, u32[]{:S(2)}, u32[]{:S(2)}) collective-permute-start(bf16[216,256]{1,0:T(8,128)(2,1)S(1)} %get-tuple-element.72), channel_id=1, source_target_pairs={{0,4},{4,0},{8,12},{12,8},{16,20},{20,16},{24,28},{28,24},{1,5},{5... | collective-permute-start | bytes 331784 | tf_op jit(solution)/shard_map/ppermute | solution.py:614
  57.9 1.8 %collective-permute-start.25 = (bf16[8,1152]{1,0:T(8,128)(2,1)S(1)}, bf16[8,1152]{1,0:T(8,128)(2,1)S(1)}, u32[]{:S(2)}, u32[]{:S(2)}) collective-permute-start(bf16[8,1152]{1,0:T(8,128)(2,1)S(1)} %get-tuple-element.84), channel_id=1, source_target_pairs={{0,4},{4,0},{8,12},{12,8},{16,20},{20,16},{24,28},{28,24},{1,5},{5... | collective-permute-start | bytes 55304 | tf_op jit(solution)/shard_map/ppermute | solution.py:614
  59.6 2.1 %collective-permute-done.25.dense_in = bf16[8,1152]{1,0:T(8,128)(2,1)S(1)} collective-permute-done((bf16[8,1152]{1,0:T(8,128)(2,1)S(1)}, bf16[8,1152]{1,0:T(8,128)(2,1)S(1)}, u32[]{:S(2)}, u32[]{:S(2)}) %collective-permute-start.25) | collective-permute-done | bytes 18464 | tf_op jit(solution)/shard_map/ppermute | solution.py:614
  61.7 3.1 %collective-permute-done.23.three = bf16[216,256]{1,0:T(8,128)(2,1)S(1)} collective-permute-done((bf16[216,256]{1,0:T(8,128)(2,1)S(1)}, bf16[216,256]{1,0:T(8,128)(2,1)S(1)}, u32[]{:S(2)}, u32[]{:S(2)}) %collective-permute-start.23) | collective-permute-done | bytes 110624 | tf_op jit(solution)/shard_map/ppermute | solution.py:614
  65.0 4.3 %collective-permute-start.27 = (bf16[256,256]{1,0:T(8,128)(2,1)S(1)}, bf16[256,256]{1,0:T(8,128)(2,1)S(1)}, u32[]{:S(2)}, u32[]{:S(2)}) collective-permute-start(bf16[256,256]{1,0:T(8,128)(2,1)S(1)} %shard_map.117.own), channel_id=1, source_target_pairs={{0,8},{4,12},{8,0},{12,4},{16,24},{20,28},{24,16},{28,20},{1,9},{5... | collective-permute-start | bytes 393224 | tf_op jit(solution)/shard_map/ppermute | solution.py:614
  69.8 2.1 %collective-permute-done.31.refs_5_ = bf16[256,256]{1,0:T(8,128)(2,1)S(1)} collective-permute-done((bf16[256,256]{1,0:T(8,128)(2,1)S(1)}, bf16[256,256]{1,0:T(8,128)(2,1)S(1)}, u32[]{:S(2)}, u32[]{:S(2)}) %collective-permute-start.31) | collective-permute-done | bytes 131104 | tf_op jit(solution)/shard_map/ppermute | solution.py:614
  72.3 2.6 %collective-permute-done.29.refs_3_ = bf16[256,256]{1,0:T(8,128)(2,1)S(1)} collective-permute-done((bf16[256,256]{1,0:T(8,128)(2,1)S(1)}, bf16[256,256]{1,0:T(8,128)(2,1)S(1)}, u32[]{:S(2)}, u32[]{:S(2)}) %collective-permute-start.29) | collective-permute-done | bytes 131104 | tf_op jit(solution)/shard_map/ppermute | solution.py:614
  77.0 2.0 %shard_map.118 = f32[3,256,512]{2,1,0:T(8,128)} custom-call(f32[3,256,512]{2,1,0:T(8,128)S(1)} %get-tuple-element.56.field, s32[1,256]{1,0:T(1,128)S(1)} %bitcast.10, bf16[256,256]{1,0:T(8,128)(2,1)S(1)} %collective-permute-done.26.after_this.refs_0_), custom_call_target="tpu_custom_call" | custom-call | flops 1000 | bytes 1000 | tf_op jit(solution)/shard_map/pallas_call | solution.py:750
  79.0 2.1 %collective-permute-done.30.refs_4_ = bf16[256,256]{1,0:T(8,128)(2,1)S(1)} collective-permute-done((bf16[256,256]{1,0:T(8,128)(2,1)S(1)}, bf16[256,256]{1,0:T(8,128)(2,1)S(1)}, u32[]{:S(2)}, u32[]{:S(2)}) %collective-permute-start.30) | collective-permute-done | bytes 131104 | tf_op jit(solution)/shard_map/ppermute | solution.py:614
  (76 shorter events, 27.2 us)
Async XLA Ops:
  3.9 10.8 %collective-permute-start = (bf16[3,64,128]{2,1,0:T(8,128)(2,1)S(1)}, bf16[3,64,128]{2,1,0:T(8,128)(2,1)S(1)}, u32[]{:S(2)}, u32[]{:S(2)}) collective-permute-start(bf16[3,64,128]{2,1,0:T(8,128)(2,1)S(1)} %get-tuple-element.47), channel_id=1, source_target_pairs={{0,4},{4,0},{8,12},{12,8},{16,20},{20,16},{24,28},{28,24},{1,5},{5... | collective-permute-start | bytes 147464 | tf_op jit(solution)/shard_map/ppermute | solution.py:614
  6.9 7.8 %collective-permute-start.1 = (bf16[3,64,128]{2,1,0:T(8,128)(2,1)S(1)}, bf16[3,64,128]{2,1,0:T(8,128)(2,1)S(1)}, u32[]{:S(2)}, u32[]{:S(2)}) collective-permute-start(bf16[3,64,128]{2,1,0:T(8,128)(2,1)S(1)} %get-tuple-element.48), channel_id=1, source_target_pairs={{0,28},{4,8},{8,4},{12,16},{16,12},{20,24},{24,20},{28,0},{1,29},{... | collective-permute-start | bytes 147464 | tf_op jit(solution)/shard_map/ppermute | solution.py:622
  15.7 8.4 %collective-permute-start.4 = (bf16[3,64,128]{2,1,0:T(8,128)(2,1)S(1)}, bf16[3,64,128]{2,1,0:T(8,128)(2,1)S(1)}, u32[]{:S(2)}, u32[]{:S(2)}) collective-permute-start(bf16[3,64,128]{2,1,0:T(8,128)(2,1)S(1)} %get-tuple-element.52), channel_id=1, source_target_pairs={{0,4},{4,0},{8,12},{12,8},{16,20},{20,16},{24,28},{28,24},{1,5},{5... | collective-permute-start | bytes 147464 | tf_op jit(solution)/shard_map/ppermute | solution.py:614
  15.8 8.3 %collective-permute-start.5 = (bf16[3,64,128]{2,1,0:T(8,128)(2,1)S(1)}, bf16[3,64,128]{2,1,0:T(8,128)(2,1)S(1)}, u32[]{:S(2)}, u32[]{:S(2)}) collective-permute-start(bf16[3,64,128]{2,1,0:T(8,128)(2,1)S(1)} %get-tuple-element.53), channel_id=1, source_target_pairs={{0,28},{4,8},{8,4},{12,16},{16,12},{20,24},{24,20},{28,0},{1,29},{... | collective-permute-start | bytes 147464 | tf_op jit(solution)/shard_map/ppermute | solution.py:622
  18.4 5.7 %collective-permute-start.6 = (bf16[3,32,128]{2,1,0:T(8,128)(2,1)S(1)}, bf16[3,32,128]{2,1,0:T(8,128)(2,1)S(1)}, u32[]{:S(2)}, u32[]{:S(2)}) collective-permute-start(bf16[3,32,128]{2,1,0:T(8,128)(2,1)S(1)} %get-tuple-element.54), channel_id=1, source_target_pairs={{0,1},{1,0},{2,3},{3,2},{4,5},{5,4},{6,7},{7,6},{8,9},{9,8},{10,11... | collective-permute-start | bytes 73736 | tf_op jit(solution)/shard_map/ppermute | solution.py:614
  25.6 4.5 %collective-permute-start.9 = (bf16[256,256]{1,0:T(8,128)(2,1)S(1)}, bf16[256,256]{1,0:T(8,128)(2,1)S(1)}, u32[]{:S(2)}, u32[]{:S(2)}) collective-permute-start(bf16[256,256]{1,0:T(8,128)(2,1)S(1)} %get-tuple-element.57.h1.h_own), channel_id=1, source_target_pairs={{0,3},{1,2},{2,1},{3,0},{4,7},{5,6},{6,5},{7,4},{8,11},{9,10},{10,... | collective-permute-start | bytes 393224 | tf_op jit(solution)/shard_map/ppermute | solution.py:614
  31.2 4.9 %collective-permute-start.12 = (bf16[256,256]{1,0:T(8,128)(2,1)S(1)}, bf16[256,256]{1,0:T(8,128)(2,1)S(1)}, u32[]{:S(2)}, u32[]{:S(2)}) collective-permute-start(bf16[256,256]{1,0:T(8,128)(2,1)S(1)} %get-tuple-element.59.dz2.d_own), channel_id=1, source_target_pairs={{0,3},{1,2},{2,1},{3,0},{4,7},{5,6},{6,5},{7,4},{8,11},{9,10},{10,... | collective-permute-start | bytes 393224 | tf_op jit(solution)/shard_map/ppermute | solution.py:614
  41.3 6.2 %collective-permute-start.15 = (bf16[64,1152]{1,0:T(8,128)(2,1)S(1)}, bf16[64,1152]{1,0:T(8,128)(2,1)S(1)}, u32[]{:S(2)}, u32[]{:S(2)}) collective-permute-start(bf16[64,1152]{1,0:T(8,128)(2,1)S(1)} %get-tuple-element.68), channel_id=1, source_target_pairs={{0,2},{1,3},{2,0},{3,1},{4,6},{5,7},{6,4},{7,5},{8,10},{9,11},{10,... | collective-permute-start | bytes 442376 | tf_op jit(solution)/shard_map/ppermute | solution.py:614
  44.9 6.3 %collective-permute-start.20 = (bf16[216,256]{1,0:T(8,128)(2,1)S(1)}, bf16[216,256]{1,0:T(8,128)(2,1)S(1)}, u32[]{:S(2)}, u32[]{:S(2)}) collective-permute-start(bf16[216,256]{1,0:T(8,128)(2,1)S(1)} %get-tuple-element.78), channel_id=1, source_target_pairs={{0,4},{4,0},{8,12},{12,8},{16,20},{20,16},{24,28},{28,24},{1,5},{5... | collective-permute-start | bytes 331784 | tf_op jit(solution)/shard_map/ppermute | solution.py:614
  47.5 4.4 %collective-permute-start.22 = (bf16[2,16,1152]{2,1,0:T(8,128)(2,1)S(1)}, bf16[2,16,1152]{2,1,0:T(8,128)(2,1)S(1)}, u32[]{:S(2)}, u32[]{:S(2)}) collective-permute-start(bf16[2,16,1152]{2,1,0:T(8,128)(2,1)S(1)} %get-tuple-element.79.refs_1_), channel_id=1, source_target_pairs={{0,8},{4,12},{8,0},{12,4},{16,24},{20,28},{24,16},{28,20},{1,9},{5... | collective-permute-start | bytes 221192 | tf_op jit(solution)/shard_map/ppermute | solution.py:614
  49.2 6.0 %collective-permute-start.17 = (bf16[216,256]{1,0:T(8,128)(2,1)S(1)}, bf16[216,256]{1,0:T(8,128)(2,1)S(1)}, u32[]{:S(2)}, u32[]{:S(2)}) collective-permute-start(bf16[216,256]{1,0:T(8,128)(2,1)S(1)} %get-tuple-element.74), channel_id=1, source_target_pairs={{0,4},{4,0},{8,12},{12,8},{16,20},{20,16},{24,28},{28,24},{1,5},{5... | collective-permute-start | bytes 331784 | tf_op jit(solution)/shard_map/ppermute | solution.py:614
  49.8 7.2 %collective-permute-start.19 = (bf16[216,256]{1,0:T(8,128)(2,1)S(1)}, bf16[216,256]{1,0:T(8,128)(2,1)S(1)}, u32[]{:S(2)}, u32[]{:S(2)}) collective-permute-start(bf16[216,256]{1,0:T(8,128)(2,1)S(1)} %get-tuple-element.76), channel_id=1, source_target_pairs={{0,4},{4,0},{8,12},{12,8},{16,20},{20,16},{24,28},{28,24},{1,5},{5... | collective-permute-start | bytes 331784 | tf_op jit(solution)/shard_map/ppermute | solution.py:614
  51.2 6.4 %collective-permute-start.21 = (bf16[216,256]{1,0:T(8,128)(2,1)S(1)}, bf16[216,256]{1,0:T(8,128)(2,1)S(1)}, u32[]{:S(2)}, u32[]{:S(2)}) collective-permute-start(bf16[216,256]{1,0:T(8,128)(2,1)S(1)} %shard_map.113), channel_id=1, source_target_pairs={{0,8},{4,12},{8,0},{12,4},{16,24},{20,28},{24,16},{28,20},{1,9},{5... | collective-permute-start | bytes 331784 | tf_op jit(solution)/shard_map/ppermute | solution.py:614
  52.0 5.9 %collective-permute-start.24 = (bf16[16,1152]{1,0:T(8,128)(2,1)S(1)}, bf16[16,1152]{1,0:T(8,128)(2,1)S(1)}, u32[]{:S(2)}, u32[]{:S(2)}) collective-permute-start(bf16[16,1152]{1,0:T(8,128)(2,1)S(1)} %get-tuple-element.81.refs_2_), channel_id=1, source_target_pairs={{0,16},{4,20},{8,24},{12,28},{16,0},{20,4},{24,8},{28,12},{1,17},{... | collective-permute-start | bytes 110600 | tf_op jit(solution)/shard_map/ppermute | solution.py:614
  52.2 7.4 %collective-permute-start.16 = (bf16[216,256]{1,0:T(8,128)(2,1)S(1)}, bf16[216,256]{1,0:T(8,128)(2,1)S(1)}, u32[]{:S(2)}, u32[]{:S(2)}) collective-permute-start(bf16[216,256]{1,0:T(8,128)(2,1)S(1)} %get-tuple-element.72), channel_id=1, source_target_pairs={{0,4},{4,0},{8,12},{12,8},{16,20},{20,16},{24,28},{28,24},{1,5},{5... | collective-permute-start | bytes 331784 | tf_op jit(solution)/shard_map/ppermute | solution.py:614
  55.2 6.5 %collective-permute-start.18 = (bf16[216,256]{1,0:T(8,128)(2,1)S(1)}, bf16[216,256]{1,0:T(8,128)(2,1)S(1)}, u32[]{:S(2)}, u32[]{:S(2)}) collective-permute-start(bf16[216,256]{1,0:T(8,128)(2,1)S(1)} %shard_map.112), channel_id=1, source_target_pairs={{0,8},{4,12},{8,0},{12,4},{16,24},{20,28},{24,16},{28,20},{1,9},{5... | collective-permute-start | bytes 331784 | tf_op jit(solution)/shard_map/ppermute | solution.py:614
  57.7 7.1 %collective-permute-start.23 = (bf16[216,256]{1,0:T(8,128)(2,1)S(1)}, bf16[216,256]{1,0:T(8,128)(2,1)S(1)}, u32[]{:S(2)}, u32[]{:S(2)}) collective-permute-start(bf16[216,256]{1,0:T(8,128)(2,1)S(1)} %shard_map.115), channel_id=1, source_target_pairs={{0,16},{4,20},{8,24},{12,28},{16,0},{20,4},{24,8},{28,12},{1,17},{... | collective-permute-start | bytes 331784 | tf_op jit(solution)/shard_map/ppermute | solution.py:614
  64.9 7.0 %collective-permute-start.31 = (bf16[256,256]{1,0:T(8,128)(2,1)S(1)}, bf16[256,256]{1,0:T(8,128)(2,1)S(1)}, u32[]{:S(2)}, u32[]{:S(2)}) collective-permute-start(bf16[256,256]{1,0:T(8,128)(2,1)S(1)} %shard_map.117.own), channel_id=1, source_target_pairs={{0,24},{4,28},{8,16},{12,20},{16,8},{20,12},{24,0},{28,4},{1,25},{... | collective-permute-start | bytes 393224 | tf_op jit(solution)/shard_map/ppermute | solution.py:614
  65.0 10.0 %collective-permute-start.29 = (bf16[256,256]{1,0:T(8,128)(2,1)S(1)}, bf16[256,256]{1,0:T(8,128)(2,1)S(1)}, u32[]{:S(2)}, u32[]{:S(2)}) collective-permute-start(bf16[256,256]{1,0:T(8,128)(2,1)S(1)} %shard_map.117.own), channel_id=1, source_target_pairs={{0,16},{4,20},{8,24},{12,28},{16,0},{20,4},{24,8},{28,12},{1,17},{... | collective-permute-start | bytes 393224 | tf_op jit(solution)/shard_map/ppermute | solution.py:614
  65.0 10.5 %collective-permute-start.27 = (bf16[256,256]{1,0:T(8,128)(2,1)S(1)}, bf16[256,256]{1,0:T(8,128)(2,1)S(1)}, u32[]{:S(2)}, u32[]{:S(2)}) collective-permute-start(bf16[256,256]{1,0:T(8,128)(2,1)S(1)} %shard_map.117.own), channel_id=1, source_target_pairs={{0,8},{4,12},{8,0},{12,4},{16,24},{20,28},{24,16},{28,20},{1,9},{5... | collective-permute-start | bytes 393224 | tf_op jit(solution)/shard_map/ppermute | solution.py:614
  69.3 7.7 %collective-permute-start.26 = (bf16[256,256]{1,0:T(8,128)(2,1)S(1)}, bf16[256,256]{1,0:T(8,128)(2,1)S(1)}, u32[]{:S(2)}, u32[]{:S(2)}) collective-permute-start(bf16[256,256]{1,0:T(8,128)(2,1)S(1)} %shard_map.117.own), channel_id=1, source_target_pairs={{0,4},{4,0},{8,12},{12,8},{16,20},{20,16},{24,28},{28,24},{1,5},{5... | collective-permute-start | bytes 393224 | tf_op jit(solution)/shard_map/ppermute | solution.py:614
  71.9 7.1 %collective-permute-start.32 = (bf16[256,256]{1,0:T(8,128)(2,1)S(1)}, bf16[256,256]{1,0:T(8,128)(2,1)S(1)}, u32[]{:S(2)}, u32[]{:S(2)}) collective-permute-start(bf16[256,256]{1,0:T(8,128)(2,1)S(1)} %collective-permute-done.31.refs_5_), channel_id=1, source_target_pairs={{0,4},{4,0},{8,12},{12,8},{16,20},{20,16},{24,28},{28,24},{1,5},{5... | collective-permute-start | bytes 393224 | tf_op jit(solution)/shard_map/ppermute | solution.py:614
  75.0 6.1 %collective-permute-start.30 = (bf16[256,256]{1,0:T(8,128)(2,1)S(1)}, bf16[256,256]{1,0:T(8,128)(2,1)S(1)}, u32[]{:S(2)}, u32[]{:S(2)}) collective-permute-start(bf16[256,256]{1,0:T(8,128)(2,1)S(1)} %collective-permute-done.29.refs_3_), channel_id=1, source_target_pairs={{0,4},{4,0},{8,12},{12,8},{16,20},{20,16},{24,28},{28,24},{1,5},{5... | collective-permute-start | bytes 393224 | tf_op jit(solution)/shard_map/ppermute | solution.py:614
  75.5 7.0 %collective-permute-start.28 = (bf16[256,256]{1,0:T(8,128)(2,1)S(1)}, bf16[256,256]{1,0:T(8,128)(2,1)S(1)}, u32[]{:S(2)}, u32[]{:S(2)}) collective-permute-start(bf16[256,256]{1,0:T(8,128)(2,1)S(1)} %collective-permute-done.27.refs_1_), channel_id=1, source_target_pairs={{0,4},{4,0},{8,12},{12,8},{16,20},{20,16},{24,28},{28,24},{1,5},{5... | collective-permute-start | bytes 393224 | tf_op jit(solution)/shard_map/ppermute | solution.py:614
  (17 other events, 83.3 us)

commit v5 on v4

--- a/solution.py
+++ b/solution.py
@@ -150,10 +150,9 @@
     return jnp.where(rows == slots, 1.0, 0.0).astype(F32)
 
 
-def layer_rows(value, layer, ez):
-    step = EY * ez
-    start = layer * ez
-    return value[start : start + ez], value[step + start : step + start + ez]
+def layer_rows(field, x, layer, ez):
+    start = (x * EY + layer) * ez
+    return field[:, start : start + ez].reshape(3 * ez, field.shape[2])
 
 
 def edge_tables():
@@ -169,81 +168,75 @@
     return table(0, 0), table(0, side), table(NP - 1, 0), table(NP - 1, side)
 
 
+def order_kernel(slots, order, back, tabs):
+    matrix = slot_matrix(slots[...])
+    back[...] = matrix.astype(BF16)
+    order[...] = matrix.T.astype(BF16)
+    for i, table in enumerate(edge_tables()):
+        tabs[i] = table
+
+
 def is_even(axis):
     return lax.rem(lax.axis_index(axis), 2) == 0
 
 
-def write_edges(fields, tabs, outs, ez):
-    lf, ls, tf, ts = tabs
+def write_edges(field, tabs, outs, ez):
     pair_x, cross_x, pair_y, cross_y = outs
     side = NP * NP
     half = EY * ez // 2
     last = NP * side - side
     even_x = is_even("sim")
     even_y = is_even("grp")
-    for c, field in enumerate(fields):
-        near = field[0 : 2 * half, 0:side]
-        far = field[2 * half : 4 * half, last : last + side]
-        to_left = jnp.concatenate([near[:half], near[half:]], axis=1)
-        to_right = jnp.concatenate([far[:half], far[half:]], axis=1)
-        pair_x[c] = jnp.where(even_x, to_right, to_left).astype(BF16)
-        cross_x[c] = jnp.where(even_x, to_left, to_right).astype(BF16)
-        one, two = layer_rows(field, 0, ez)
-        to_below = dot(one.astype(BF16), lf) + dot(two.astype(BF16), ls)
-        one, two = layer_rows(field, EY - 1, ez)
-        to_above = dot(one.astype(BF16), tf) + dot(two.astype(BF16), ts)
-        pair_y[c] = jnp.where(even_y, to_above, to_below).astype(BF16)
-        cross_y[c] = jnp.where(even_y, to_below, to_above).astype(BF16)
-
-
-def add_edges(part, c, pair_x, cross_x, pair_y, cross_y, tabs, ez):
-    lf, ls, tf, ts = tabs
+    near = field[:, 0 : 2 * half, 0 : 2 * side][:, :, :side]
+    far = field[:, 2 * half : 4 * half, last - side :][:, :, side:]
+    to_left = jnp.concatenate([near[:, :half], near[:, half:]], axis=2)
+    to_right = jnp.concatenate([far[:, :half], far[:, half:]], axis=2)
+    pair_x[...] = jnp.where(even_x, to_right, to_left).astype(BF16)
+    cross_x[...] = jnp.where(even_x, to_left, to_right).astype(BF16)
+    to_below, to_above = [
+        dot(layer_rows(field, 0, layer, ez).astype(BF16), tabs[at])
+        + dot(layer_rows(field, 1, layer, ez).astype(BF16), tabs[at + 1])
+        for layer, at in ((0, 0), (EY - 1, 2))
+    ]
+    pair_y[...] = jnp.where(even_y, to_above, to_below).astype(BF16).reshape(pair_y.shape)
+    cross_y[...] = jnp.where(even_y, to_below, to_above).astype(BF16).reshape(cross_y.shape)
+
+
+def add_edges(part, pair_x, cross_x, pair_y, cross_y, tabs, field, ez):
     side = NP * NP
     half = EY * ez // 2
     width = NP * side
-    value = part[c]
     even_x = is_even("sim")
     even_y = is_even("grp")
-    pair = FACE_RATE * pair_x[c].astype(F32)
-    cross = FACE_RATE * cross_x[c].astype(F32)
+    pair = FACE_RATE * pair_x[...].astype(F32)
+    cross = FACE_RATE * cross_x[...].astype(F32)
     left = jnp.where(even_x, cross, pair)
     right = jnp.where(even_x, pair, cross)
-    pair = pair_y[c].astype(F32)
-    cross = cross_y[c].astype(F32)
-    below = jnp.where(even_y, cross, pair).astype(BF16)
-    above = jnp.where(even_y, pair, cross).astype(BF16)
-    rest = jnp.zeros((half, width - side), F32)
-    x_add = jnp.concatenate(
-        [
-            jnp.concatenate([left[:, :side], rest], axis=1),
-            jnp.concatenate([left[:, side:], rest], axis=1),
-            jnp.concatenate([rest, right[:, :side]], axis=1),
-            jnp.concatenate([rest, right[:, side:]], axis=1),
-        ],
-        axis=0,
-    )
-    none = jnp.zeros(((EY - 2) * ez, width), F32)
-    y_add = jnp.concatenate(
-        [
-            dot_nt(below, lf),
-            none,
-            dot_nt(above, tf),
-            dot_nt(below, ls),
-            none,
-            dot_nt(above, ts),
-        ],
-        axis=0,
-    )
-    return value + x_add + FACE_RATE * y_add
-
-
-def prepare_kernel(vel, slots, field, *edges):
+    pair = pair_y[...].astype(F32)
+    cross = cross_y[...].astype(F32)
+    below = jnp.where(even_y, cross, pair).astype(BF16).reshape(3 * ez, 2 * side)
+    above = jnp.where(even_y, pair, cross).astype(BF16).reshape(3 * ez, 2 * side)
+    first = lax.broadcasted_iota(jnp.int32, (1, 1, 2 * side), 2) < side
+
+    field[...] = part[...]
+    turned = pltpu.roll(left, side, 2)
+    field[:, 0:half, : 2 * side] += jnp.where(first, left, 0.0)
+    field[:, half : 2 * half, : 2 * side] += jnp.where(first, turned, 0.0)
+    turned = pltpu.roll(right, side, 2)
+    field[:, 2 * half : 3 * half, width - 2 * side :] += jnp.where(first, 0.0, turned)
+    field[:, 3 * half : 4 * half, width - 2 * side :] += jnp.where(first, 0.0, right)
+    for x in range(EX):
+        for layer, value, at in ((0, below, 0), (EY - 1, above, 2)):
+            start = (x * EY + layer) * ez
+            more = FACE_RATE * dot_nt(value, tabs[at + x])
+            field[:, start : start + ez] += more.reshape(3, ez, width)
+
+
+def prepare_kernel(vel, order, tabs, field, *edges):
     ez = vel.shape[1] // (EX * EY)
-    order = slot_matrix(slots[...]).T.astype(BF16)
-    fields = [moved(order, vel[c]) for c in range(3)]
     for c in range(3):
-        field[c] = fields[c]
-    write_edges(fields, edge_tables(), edges, ez)
+        field[c] = moved(order[...], vel[c])
+    write_edges(field, tabs, edges, ez)
 
 
 def face_count(width):
@@ -340,26 +333,20 @@
         part[:, :, cols] = value
 
 
-def join_kernel(part, pair_x, cross_x, pair_y, cross_y, field, *edges):
+def join_kernel(part, pair_x, cross_x, pair_y, cross_y, tabs, field, *edges):
     ez = part.shape[1] // (EX * EY)
-    tabs = edge_tables()
-    fields = [add_edges(part, c, pair_x, cross_x, pair_y, cross_y, tabs, ez) for c in range(3)]
-    for c in range(3):
-        field[c] = fields[c]
-    write_edges(fields, tabs, edges, ez)
+    add_edges(part, pair_x, cross_x, pair_y, cross_y, tabs, field, ez)
+    write_edges(field, tabs, edges, ez)
 
 
 def encode_kernel(
-    part, pair_x, cross_x, pair_y, cross_y, wall, w_encode,
+    part, pair_x, cross_x, pair_y, cross_y, tabs, wall, w_encode,
     field, snapshot, target, z1, h1,
 ):
     ez = part.shape[1] // (EX * EY)
-    tabs = edge_tables()
-    fields = [add_edges(part, c, pair_x, cross_x, pair_y, cross_y, tabs, ez) for c in range(3)]
-    for c in range(3):
-        field[c] = fields[c]
-    high0, low0 = split_two(fields[0])
-    high2, low2 = split_two(fields[2])
+    add_edges(part, pair_x, cross_x, pair_y, cross_y, tabs, field, ez)
+    high0, low0 = split_two(field[0])
+    high2, low2 = split_two(field[2])
     snap = jnp.concatenate([high0, high2], axis=1)
     snapshot[...] = snap
     target[...] = (
@@ -371,10 +358,9 @@
     h1[...] = (hidden * jax.nn.sigmoid(hidden)).astype(BF16)
 
 
-def restore_kernel(field, slots, after_this, out):
-    order = slot_matrix(slots[...]).astype(BF16)
+def restore_kernel(field, back, after_this, out):
     for c in range(3):
-        out[c] = moved(order, field[c])
+        out[c] = moved(back[...], field[c])
 
 
 def silu_grad(value):
@@ -407,25 +393,37 @@
     return before.reshape(shape), after.reshape(shape)
 
 
-def forward_kernel(groups, total, h1, pair, cross, w_conv, w_head, target, dz2, h2, resid, padded, z2):
+def tap_sum(taken, w_conv, dy):
+    channels = w_conv.shape[1]
+    first = 3 * dy
+    rows = taken.shape[1]
+
+    def times(value, start):
+        return dot(value, w_conv[start + first : start + first + 3].reshape(-1, channels))
+
+    both = times(taken.reshape(EX * rows, taken.shape[2]), 9)
+    return both + jnp.concatenate([times(taken[1], 18), times(taken[0], 0)], axis=0)
+
+
+def centre_kernel(groups, h1, w_conv, z2):
+    rows, channels = h1.shape
+    ez = rows // (EX * EY)
+    grid = h1[...].astype(F32).reshape(EX, EY, ez, channels)
+    before, after = along_span(grid, ez, groups)
+    taken = jnp.concatenate([before, grid, after], axis=-1).astype(BF16)
+    z2[...] = tap_sum(taken.reshape(EX, rows // EX, 3 * channels), w_conv, 1)
+
+
+def forward_kernel(groups, total, z2, h1, pair, cross, w_conv, w_head, target, dz2, h2, resid, padded):
     rows, channels = h1.shape
     ez = rows // (EX * EY)
     grid = with_layers(h1, pair, cross, ez, groups)
     before, after = along_span(grid, ez, groups)
     padded[...] = jnp.concatenate([before, grid, after], axis=-1).astype(BF16)
-    half = rows // 2
-    for dy in range(3):
-        taken = padded[:, dy : dy + EY].reshape(EX, half, 3 * channels)
-        first = 3 * dy
-        both = dot(taken.reshape(rows, 3 * channels), w_conv[9 + first : 12 + first].reshape(-1, channels))
-        ahead_x = dot(taken[1], w_conv[18 + first : 21 + first].reshape(-1, channels))
-        behind_x = dot(taken[0], w_conv[first : 3 + first].reshape(-1, channels))
-        step = both + jnp.concatenate([ahead_x, behind_x], axis=0)
-        if dy == 0:
-            z2[...] = step
-        else:
-            z2[...] += step
     hidden = z2[...]
+    for dy in (0, 2):
+        taken = padded[:, dy : dy + EY].reshape(EX, rows // EX, 3 * channels)
+        hidden = hidden + tap_sum(taken, w_conv, dy)
     act = (hidden * jax.nn.sigmoid(hidden)).astype(BF16)
     output = dot(act, w_head[...])
     miss = (LOSS_WEIGHT * (output - target[...].astype(F32)) / total).astype(BF16)
@@ -434,31 +432,44 @@
     dz2[...] = (dot_nt(miss, w_head[...]) * silu_grad(hidden)).astype(BF16)
 
 
-def back_kernel(
-    groups, dz2, pair, cross, w_conv, z1, snapshot, h2, resid,
-    kept, sent, dh1, out,
-):
+def tap_sum_back(shifted, w_conv, dy):
+    total = 0.0
+    for dz, taken in enumerate(shifted):
+        tap = 3 * dy + dz
+        both = dot_nt(taken.reshape(-1, taken.shape[2]), w_conv[9 + tap])
+        ahead_x = dot_nt(taken[0], w_conv[18 + tap])
+        behind_x = dot_nt(taken[1], w_conv[tap])
+        total = total + both + jnp.concatenate([behind_x, ahead_x], axis=0)
+    return total
+
+
+def centre_back_kernel(groups, dz2, w_conv, h2, resid, dh1, head):
     rows, channels = dz2.shape
     ez = rows // (EX * EY)
-    half = rows // 2
+    grid = dz2[...].astype(F32).reshape(EX, EY, ez, channels)
+    before, after = along_span(grid, ez, groups)
+    shifted = [
+        part.astype(BF16).reshape(EX, rows // EX, channels) for part in (after, grid, before)
+    ]
+    dh1[...] = tap_sum_back(shifted, w_conv, 1)
+    head[...] = dot(h2[...].astype(F32).T.astype(BF16), resid[...])
+
+
+def back_kernel(groups, dh1, head, dz2, pair, cross, w_conv, z1, snapshot, kept, sent, out):
+    rows, channels = dz2.shape
+    ez = rows // (EX * EY)
     grid = with_layers(dz2, pair, cross, ez, groups)
     before, after = along_span(grid, ez, groups)
     shifted = [part.astype(BF16) for part in (after, grid, before)]
     features = snapshot.shape[1]
-    out[:, features:] = dot(h2[...].astype(F32).T.astype(BF16), resid[...])
-    for dy in range(3):
-        for dz in range(3):
-            tap = 3 * dy + dz
-            taken = shifted[dz][:, 2 - dy : 2 - dy + EY].reshape(EX, half, channels)
-            both = dot_nt(taken.reshape(rows, channels), w_conv[9 + tap])
-            ahead_x = dot_nt(taken[0], w_conv[18 + tap])
-            behind_x = dot_nt(taken[1], w_conv[tap])
-            step = both + jnp.concatenate([behind_x, ahead_x], axis=0)
-            if tap == 0:
-                dh1[...] = step
-            else:
-                dh1[...] += step
-    dz1 = dh1[...] * silu_grad(z1[...])
+    out[:, features:] = head[...]
+    total = dh1[...]
+    for dy in (0, 2):
+        taken = [
+            part[:, 2 - dy : 2 - dy + EY].reshape(EX, rows // EX, channels) for part in shifted
+        ]
+        total = total + tap_sum_back(taken, w_conv, dy)
+    dz1 = total * silu_grad(z1[...])
     out[:, :features] = dot(dz1.T.astype(BF16), snapshot[...])
     quarter = channels // groups
     place = lax.axis_index("grp")
@@ -526,8 +537,8 @@
 
 
 def dense_kernel(kept, got, *refs):
-    out_kept, out_sent = refs[-5:-3]
-    for source, target in zip(refs[:3], refs[-3:]):
+    out_kept, out_sent = refs[-4:-2]
+    for source, target in zip(refs[:2], refs[-2:]):
         target[...] = source[...]
     total = kept[...] + got[...].astype(F32)
     grid = total.reshape(2, 2, kept.shape[0] // 4, kept.shape[1])
@@ -659,10 +670,19 @@
     y_edge = shaped((3, ez, 2 * NP * NP), BF16)
     edge_shapes = (x_edge, x_edge, y_edge, y_edge)
 
-    field, *edges = call(prepare_kernel, (whole,) + edge_shapes, flops=4 * 10**9)(block, slots)
+    order, back, tabs = call(
+        order_kernel,
+        (
+            shaped((rows, rows), BF16),
+            shaped((rows, rows), BF16),
+            shaped((4, width, 2 * NP * NP), BF16),
+        ),
+        flops=4 * 10**9,
+    )(slots)
+    field, *edges = call(prepare_kernel, (whole,) + edge_shapes, flops=4 * 10**9)(block, order, tabs)
     halos = exchanged(edges)
     part = call(inside_kernel, whole)(field, stencil)
-    field, *edges = call(join_kernel, (whole,) + edge_shapes)(part, *halos)
+    field, *edges = call(join_kernel, (whole,) + edge_shapes)(part, *halos, tabs)
     halos = exchanged(edges)
     part = call(inside_kernel, whole)(field, stencil)
     field, snapshot, target, z1, h1 = call(
@@ -674,31 +694,35 @@
             shaped((rows, channels), F32),
             shaped((rows, channels), BF16),
         ),
-    )(part, *halos, wall, w_encode)
+    )(part, *halos, tabs, wall, w_encode)
 
     h_three = swapped(h1, "grp", 3)
     h_one = swapped(h1, "grp", 1)
     h_two = swapped(h_three, "grp", 1)
     rows_bf = shaped((rows, channels), BF16)
+    square = shaped((rows, channels), F32)
+    z2 = call(functools.partial(centre_kernel, groups), square, flops=2 * 10**9)(h1, w_conv)
     dz2, h2, resid = call(
         functools.partial(forward_kernel, groups, total),
         (rows_bf, rows_bf, shaped((rows, outputs), BF16)),
-        (
-            pltpu.VMEM((EX, EY + 2, ez, 3 * channels), BF16),
-            pltpu.VMEM((rows, channels), F32),
-        ),
-    )(h1, h_one, h_three, w_conv, w_head, target)
+        (pltpu.VMEM((EX, EY + 2, ez, 3 * channels), BF16),),
+    )(z2, h1, h_one, h_three, w_conv, w_head, target)
 
     d_three = swapped(dz2, "grp", 3)
     d_one = swapped(dz2, "grp", 1)
     d_two = swapped(d_three, "grp", 1)
     wide = features + outputs
     pair = (groups // 2, quarter, wide)
+    dh1, head = call(
+        functools.partial(centre_back_kernel, groups),
+        (square, shaped((channels, outputs), F32)),
+        flops=2 * 10**9,
+    )(dz2, w_conv, h2, resid)
     e_kept, e_sent = call(
         functools.partial(back_kernel, groups),
         (shaped(pair, F32), shaped(pair, BF16)),
-        (pltpu.VMEM((rows, channels), F32), pltpu.VMEM((channels, wide), F32)),
-    )(dz2, d_one, d_three, w_conv, z1, snapshot, h2, resid)
+        (pltpu.VMEM((channels, wide), F32),),
+    )(dh1, head, dz2, d_one, d_three, w_conv, z1, snapshot)
     e_got = swapped(e_sent, "grp", 1)
     e_kept, e_sent = call(core_kernel, (shaped(pair[1:], F32), shaped(pair[1:], BF16)))(e_kept, e_got)
     e_got = swapped(e_sent, "grp", 2)
@@ -724,11 +748,11 @@
         tap_piece = shaped((tap_rows, channels), BF16)
         part = (2, 2 * own_rows, wide)
         e_kept, e_sent, *later = call(
-            dense_kernel, (shaped(part, F32), shaped(part, BF16)) + (tap_piece,) * 3
-        )(e_kept, e_got, taps[5], taps[3], taps[1])
+            dense_kernel, (shaped(part, F32), shaped(part, BF16)) + (tap_piece,) * 2
+        )(e_kept, e_got, taps[3], taps[1])
         e_got = swapped(e_sent, "sim", 2)
-        taps_in = {6: swapped(taps[7], "sim", 1)}
-        taps_in.update((k, swapped(piece, "sim", 1)) for k, piece in zip((4, 2, 0), later))
+        taps_in = {k: swapped(taps[k + 1], "sim", 1) for k in (6, 4)}
+        taps_in.update((k, swapped(piece, "sim", 1)) for k, piece in zip((2, 0), later))
         add_two = call(functools.partial(sum_kernel, 2), tap_piece)
         add_three = call(functools.partial(sum_kernel, 3), tap_piece)
         six = swapped(add_two(taps[6], taps_in[6], e_sent), "sim", 2)
@@ -747,7 +771,7 @@
             taps[0], taps_in[0], two, four, e_kept, e_got
         )
         shares = gathered(share, sims)
-        velocity_next = call(restore_kernel, whole, in_hbm=(2,), inputs=3)(field, slots, shares[1])
+        velocity_next = call(restore_kernel, whole, in_hbm=(2,), inputs=3)(field, back, shares[1])
         taps, encode, head = call(
             functools.partial(spread_kernel, features),
             (
@@ -761,7 +785,7 @@
         taps = lax.all_to_all(taps, "sim", 0, 0, tiled=True)
         taps = jnp.sum(taps.astype(F32), axis=0).astype(BF16)
         taps = lax.all_gather(taps, "sim").astype(F32)
-        velocity_next = call(restore_kernel, whole, in_hbm=(2,), inputs=3)(field, slots, e_kept)
+        velocity_next = call(restore_kernel, whole, in_hbm=(2,), inputs=3)(field, back, e_kept)
         dense = e_kept + e_got.astype(F32)
         dense = dense.astype(BF16).reshape(sims, own_rows, wide)
         dense = lax.all_to_all(dense, "sim", 0, 0, tiled=True)

time: 84.1 us -> 81.8 us (0.973)
  waiting for transfers between devices: 21.2 us -> 13.1 us
  starting transfers between devices: 40.8 us -> 47.6 us
  Pallas kernels: 18.9 us -> 17.9 us
    ppermute x29, waiting for transfers between devices: 21.2 us -> 13.1 us  [swapped(): return lax.ppermute(value, axis, [(i, i ^ mask) for i in range(count)])]
    ppermute x29, starting transfers between devices: 33.2 us -> 39.6 us  [swapped(): return lax.ppermute(value, axis, [(i, i ^ mask) for i in range(count)])]
    pallas_call x2 -> x5, Pallas kernels: 3.03 us -> 3.52 us  [the longest x1 1.97 us: body(): call(restore_kernel, whole, in_hbm=(2,), inputs=3)(field, back, shares[1])]
    unnamed x16 -> x14, local copies, waits for them, and re-layouts: 2.11 us -> 1.98 us
  transfers between devices with their start and end apart: 33 -> 33, of which waited for: 14 -> 12; matrix products, arithmetic and copies ran while one was open for 0% -> 0% of each run, Pallas kernels for 13% -> 14%
where the time goes in v5:
time: 81.8 us; the launch traced here: 81.6 us
  starting transfers between devices  47.6 us (58%)
  Pallas kernels  17.9 us (22%)
  waiting for transfers between devices  13.1 us (16%)
  local copies, waits for them, and re-layouts  1.98 us (2%)
  between operations  0.92 us (1%)
    ppermute x29, starting transfers between devices, swapped(): return lax.ppermute(value, axis, [(i, i ^ mask) for i in range(count)])  39.6 us
    ppermute x29, waiting for transfers between devices, swapped(): return lax.ppermute(value, axis, [(i, i ^ mask) for i in range(count)])  13.1 us
    ppermute x4, starting transfers between devices, crossed(): lax.ppermute(value, axis, [(i, j) for i, j in route if 0 <= j < count])  7.97 us
    pallas_call x2, Pallas kernels, body(): part = call(inside_kernel, whole)(field, stencil)  6.41 us
    unnamed x14, local copies, waits for them, and re-layouts  1.98 us
    pallas_call x1, Pallas kernels, body(): call(restore_kernel, whole, in_hbm=(2,), inputs=3)(field, back, shares[1])  1.97 us
    pallas_call x1, Pallas kernels, body(): call(functools.partial(taps_kernel, groups, sims if direct else 1), tuple...  1.86 us
  transfers between devices with their start and end apart: 33, of which 12 were waited for; matrix products, arithmetic and copies ran while one was open for 0% of the time, Pallas kernels for 14%

profile of v5, /device:TPU:0, one launch (start us, length us, event | category | flops | bytes accessed | tf_op | source)
XLA Modules:
  0.0 81.6 jit_solution(3121996546775865125)
XLA Ops:
  3.8 3.0 %collective-permute-start = (bf16[3,64,128]{2,1,0:T(8,128)(2,1)S(1)}, bf16[3,64,128]{2,1,0:T(8,128)(2,1)S(1)}, u32[]{:S(2)}, u32[]{:S(2)}) collective-permute-start(bf16[3,64,128]{2,1,0:T(8,128)(2,1)S(1)} %get-tuple-element.53), channel_id=1, source_target_pairs={{0,4},{4,0},{8,12},{12,8},{16,20},{20,16},{24,28},{28,24},{1,5},{5... | collective-permute-start | bytes 147464 | tf_op jit(solution)/shard_map/ppermute | solution.py:625
  6.8 3.6 %collective-permute-start.1 = (bf16[3,64,128]{2,1,0:T(8,128)(2,1)S(1)}, bf16[3,64,128]{2,1,0:T(8,128)(2,1)S(1)}, u32[]{:S(2)}, u32[]{:S(2)}) collective-permute-start(bf16[3,64,128]{2,1,0:T(8,128)(2,1)S(1)} %get-tuple-element.54), channel_id=1, source_target_pairs={{0,28},{4,8},{8,4},{12,16},{16,12},{20,24},{24,20},{28,0},{1,29},{... | collective-permute-start | bytes 147464 | tf_op jit(solution)/shard_map/ppermute | solution.py:633
  11.0 3.2 %shard_map.104.part = f32[3,256,512]{2,1,0:T(8,128)S(1)} custom-call(f32[3,256,512]{2,1,0:T(8,128)S(1)} %get-tuple-element.52.field, bf16[2560,512]{1,0:T(8,128)(2,1)S(1)} %copy-done.1), custom_call_target="tpu_custom_call" | custom-call | flops 1000 | bytes 1000 | tf_op jit(solution)/shard_map/pallas_call | solution.py:684
  14.8 2.9 %collective-permute-start.5 = (bf16[3,64,128]{2,1,0:T(8,128)(2,1)S(1)}, bf16[3,64,128]{2,1,0:T(8,128)(2,1)S(1)}, u32[]{:S(2)}, u32[]{:S(2)}) collective-permute-start(bf16[3,64,128]{2,1,0:T(8,128)(2,1)S(1)} %get-tuple-element.59), channel_id=1, source_target_pairs={{0,28},{4,8},{8,4},{12,16},{16,12},{20,24},{24,20},{28,0},{1,29},{... | collective-permute-start | bytes 147464 | tf_op jit(solution)/shard_map/ppermute | solution.py:633
  19.9 3.2 %shard_map.106.part = f32[3,256,512]{2,1,0:T(8,128)S(1)} custom-call(f32[3,256,512]{2,1,0:T(8,128)S(1)} %get-tuple-element.57.field, bf16[2560,512]{1,0:T(8,128)(2,1)S(1)} %copy-done.1), custom_call_target="tpu_custom_call" | custom-call | flops 1000 | bytes 1000 | tf_op jit(solution)/shard_map/pallas_call | solution.py:687
  25.5 1.8 %collective-permute-start.8 = (bf16[256,256]{1,0:T(8,128)(2,1)S(1)}, bf16[256,256]{1,0:T(8,128)(2,1)S(1)}, u32[]{:S(2)}, u32[]{:S(2)}) collective-permute-start(bf16[256,256]{1,0:T(8,128)(2,1)S(1)} %get-tuple-element.64.h1.h_own), channel_id=1, source_target_pairs={{0,1},{1,0},{2,3},{3,2},{4,5},{5,4},{6,7},{7,6},{8,9},{9,8},{10,11... | collective-permute-start | bytes 393224 | tf_op jit(solution)/shard_map/ppermute | solution.py:625
  29.6 1.8 %collective-permute-start.12 = (bf16[256,256]{1,0:T(8,128)(2,1)S(1)}, bf16[256,256]{1,0:T(8,128)(2,1)S(1)}, u32[]{:S(2)}, u32[]{:S(2)}) collective-permute-start(bf16[256,256]{1,0:T(8,128)(2,1)S(1)} %get-tuple-element.66.dz2.d_own), channel_id=1, source_target_pairs={{0,3},{1,2},{2,1},{3,0},{4,7},{5,6},{6,5},{7,4},{8,11},{9,10},{10,... | collective-permute-start | bytes 393224 | tf_op jit(solution)/shard_map/ppermute | solution.py:625
  31.4 1.5 %collective-permute-start.11 = (bf16[256,256]{1,0:T(8,128)(2,1)S(1)}, bf16[256,256]{1,0:T(8,128)(2,1)S(1)}, u32[]{:S(2)}, u32[]{:S(2)}) collective-permute-start(bf16[256,256]{1,0:T(8,128)(2,1)S(1)} %get-tuple-element.66.dz2.d_own), channel_id=1, source_target_pairs={{0,1},{1,0},{2,3},{3,2},{4,5},{5,4},{6,7},{7,6},{8,9},{9,8},{10,11... | collective-permute-start | bytes 393224 | tf_op jit(solution)/shard_map/ppermute | solution.py:625
  34.5 1.4 %shard_map.111 = (f32[2,64,1152]{2,1,0:T(8,128)S(1)}, bf16[2,64,1152]{2,1,0:T(8,128)(2,1)S(1)}) custom-call(f32[256,256]{1,0:T(8,128)S(1)} %get-tuple-element.69.dh1, f32[256,128]{1,0:T(8,128)S(1)} %get-tuple-element.70.head, bf16[256,256]{1,0:T(8,128)(2,1)S(1)} %get-tuple-element.66.dz2.d_own, bf16[256,256]{1,0:T(8,128)(2,1)S(1)} %collective-permute-done.11.pair.d_one, ...), custom_call_target="tpu_custom_call" | custom-call | flops 1000 | bytes 1000 | tf_op jit(solution)/shard_map/pallas_call | solution.py:721
  35.9 2.1 %collective-permute-start.14 = (bf16[2,64,1152]{2,1,0:T(8,128)(2,1)S(1)}, bf16[2,64,1152]{2,1,0:T(8,128)(2,1)S(1)}, u32[]{:S(2)}, u32[]{:S(2)}) collective-permute-start(bf16[2,64,1152]{2,1,0:T(8,128)(2,1)S(1)} %get-tuple-element.74), channel_id=1, source_target_pairs={{0,1},{1,0},{2,3},{3,2},{4,5},{5,4},{6,7},{7,6},{8,9},{9,8},{10,11... | collective-permute-start | bytes 884744 | tf_op jit(solution)/shard_map/ppermute | solution.py:625
  39.3 1.7 %collective-permute-start.15 = (bf16[64,1152]{1,0:T(8,128)(2,1)S(1)}, bf16[64,1152]{1,0:T(8,128)(2,1)S(1)}, u32[]{:S(2)}, u32[]{:S(2)}) collective-permute-start(bf16[64,1152]{1,0:T(8,128)(2,1)S(1)} %get-tuple-element.77), channel_id=1, source_target_pairs={{0,2},{1,3},{2,0},{3,1},{4,6},{5,7},{6,4},{7,5},{8,10},{9,11},{10,... | collective-permute-start | bytes 442376 | tf_op jit(solution)/shard_map/ppermute | solution.py:625
  41.0 1.9 %shard_map.113 = (f32[216,256]{1,0:T(8,128)S(1)}, bf16[216,256]{1,0:T(8,128)(2,1)S(1)}, f32[216,256]{1,0:T(8,128)S(1)}, bf16[216,256]{1,0:T(8,128)(2,1)S(1)}, f3...) custom-call(bf16[256,256]{1,0:T(8,128)(2,1)S(1)} %get-tuple-element., ...), custom_call_target="tpu_custom_call" | custom-call | flops 1000 | bytes 1000 | tf_op jit(solution)/shard_map/pallas_call | solution.py:736
  46.2 1.6 %collective-permute-start.22 = (bf16[2,16,1152]{2,1,0:T(8,128)(2,1)S(1)}, bf16[2,16,1152]{2,1,0:T(8,128)(2,1)S(1)}, u32[]{:S(2)}, u32[]{:S(2)}) collective-permute-start(bf16[2,16,1152]{2,1,0:T(8,128)(2,1)S(1)} %get-tuple-element.87.refs_1_), channel_id=1, source_target_pairs={{0,8},{4,12},{8,0},{12,4},{16,24},{20,28},{24,16},{28,20},{1,9},{5... | collective-permute-start | bytes 221192 | tf_op jit(solution)/shard_map/ppermute | solution.py:625
  48.9 1.7 %collective-permute-start.21 = (bf16[216,256]{1,0:T(8,128)(2,1)S(1)}, bf16[216,256]{1,0:T(8,128)(2,1)S(1)}, u32[]{:S(2)}, u32[]{:S(2)}) collective-permute-start(bf16[216,256]{1,0:T(8,128)(2,1)S(1)} %shard_map.116), channel_id=1, source_target_pairs={{0,8},{4,12},{8,0},{12,4},{16,24},{20,28},{24,16},{28,20},{1,9},{5... | collective-permute-start | bytes 331784 | tf_op jit(solution)/shard_map/ppermute | solution.py:625
  53.0 2.0 %collective-permute-start.18 = (bf16[216,256]{1,0:T(8,128)(2,1)S(1)}, bf16[216,256]{1,0:T(8,128)(2,1)S(1)}, u32[]{:S(2)}, u32[]{:S(2)}) collective-permute-start(bf16[216,256]{1,0:T(8,128)(2,1)S(1)} %shard_map.115), channel_id=1, source_target_pairs={{0,8},{4,12},{8,0},{12,4},{16,24},{20,28},{24,16},{28,20},{1,9},{5... | collective-permute-start | bytes 331784 | tf_op jit(solution)/shard_map/ppermute | solution.py:625
  55.0 2.2 %collective-permute-start.23 = (bf16[216,256]{1,0:T(8,128)(2,1)S(1)}, bf16[216,256]{1,0:T(8,128)(2,1)S(1)}, u32[]{:S(2)}, u32[]{:S(2)}) collective-permute-start(bf16[216,256]{1,0:T(8,128)(2,1)S(1)} %shard_map.118), channel_id=1, source_target_pairs={{0,16},{4,20},{8,24},{12,28},{16,0},{20,4},{24,8},{28,12},{1,17},{... | collective-permute-start | bytes 331784 | tf_op jit(solution)/shard_map/ppermute | solution.py:625
  57.3 2.4 %collective-permute-start.25 = (bf16[8,1152]{1,0:T(8,128)(2,1)S(1)}, bf16[8,1152]{1,0:T(8,128)(2,1)S(1)}, u32[]{:S(2)}, u32[]{:S(2)}) collective-permute-start(bf16[8,1152]{1,0:T(8,128)(2,1)S(1)} %get-tuple-element.92), channel_id=1, source_target_pairs={{0,4},{4,0},{8,12},{12,8},{16,20},{20,16},{24,28},{28,24},{1,5},{5... | collective-permute-start | bytes 55304 | tf_op jit(solution)/shard_map/ppermute | solution.py:625
  59.7 1.7 %collective-permute-done.25.dense_in = bf16[8,1152]{1,0:T(8,128)(2,1)S(1)} collective-permute-done((bf16[8,1152]{1,0:T(8,128)(2,1)S(1)}, bf16[8,1152]{1,0:T(8,128)(2,1)S(1)}, u32[]{:S(2)}, u32[]{:S(2)}) %collective-permute-start.25) | collective-permute-done | bytes 18464 | tf_op jit(solution)/shard_map/ppermute | solution.py:625
  62.5 2.4 %collective-permute-start.31 = (bf16[256,256]{1,0:T(8,128)(2,1)S(1)}, bf16[256,256]{1,0:T(8,128)(2,1)S(1)}, u32[]{:S(2)}, u32[]{:S(2)}) collective-permute-start(bf16[256,256]{1,0:T(8,128)(2,1)S(1)} %shard_map.120.own), channel_id=1, source_target_pairs={{0,24},{4,28},{8,16},{12,20},{16,8},{20,12},{24,0},{28,4},{1,25},{... | collective-permute-start | bytes 393224 | tf_op jit(solution)/shard_map/ppermute | solution.py:625
  64.9 2.1 %collective-permute-start.27 = (bf16[256,256]{1,0:T(8,128)(2,1)S(1)}, bf16[256,256]{1,0:T(8,128)(2,1)S(1)}, u32[]{:S(2)}, u32[]{:S(2)}) collective-permute-start(bf16[256,256]{1,0:T(8,128)(2,1)S(1)} %shard_map.120.own), channel_id=1, source_target_pairs={{0,8},{4,12},{8,0},{12,4},{16,24},{20,28},{24,16},{28,20},{1,9},{5... | collective-permute-start | bytes 393224 | tf_op jit(solution)/shard_map/ppermute | solution.py:625
  67.0 1.9 %collective-permute-start.26 = (bf16[256,256]{1,0:T(8,128)(2,1)S(1)}, bf16[256,256]{1,0:T(8,128)(2,1)S(1)}, u32[]{:S(2)}, u32[]{:S(2)}) collective-permute-start(bf16[256,256]{1,0:T(8,128)(2,1)S(1)} %shard_map.120.own), channel_id=1, source_target_pairs={{0,4},{4,0},{8,12},{12,8},{16,20},{20,16},{24,28},{28,24},{1,5},{5... | collective-permute-start | bytes 393224 | tf_op jit(solution)/shard_map/ppermute | solution.py:625
  69.5 1.9 %collective-permute-start.32 = (bf16[256,256]{1,0:T(8,128)(2,1)S(1)}, bf16[256,256]{1,0:T(8,128)(2,1)S(1)}, u32[]{:S(2)}, u32[]{:S(2)}) collective-permute-start(bf16[256,256]{1,0:T(8,128)(2,1)S(1)} %collective-permute-done.31.refs_5_), channel_id=1, source_target_pairs={{0,4},{4,0},{8,12},{12,8},{16,20},{20,16},{24,28},{28,24},{1,5},{5... | collective-permute-start | bytes 393224 | tf_op jit(solution)/shard_map/ppermute | solution.py:625
  71.5 1.8 %collective-permute-done.29.refs_3_ = bf16[256,256]{1,0:T(8,128)(2,1)S(1)} collective-permute-done((bf16[256,256]{1,0:T(8,128)(2,1)S(1)}, bf16[256,256]{1,0:T(8,128)(2,1)S(1)}, u32[]{:S(2)}, u32[]{:S(2)}) %collective-permute-start.29) | collective-permute-done | bytes 131104 | tf_op jit(solution)/shard_map/ppermute | solution.py:625
  75.4 2.0 %shard_map.121 = f32[3,256,512]{2,1,0:T(8,128)} custom-call(f32[3,256,512]{2,1,0:T(8,128)S(1)} %get-tuple-element.62.field, bf16[256,256]{1,0:T(8,128)(2,1)S(1)} %get-tuple-element.63.back, bf16[256,256]{1,0:T(8,128)(2,1)S(1)} %collective-permute-done.26.after_this.refs_0_), custom_call_target="tpu_custom_call" | custom-call | flops 1000 | bytes 1000 | tf_op jit(solution)/shard_map/pallas_call | solution.py:774
  (77 shorter events, 28.7 us)
Async XLA Ops:
  3.8 10.5 %collective-permute-start = (bf16[3,64,128]{2,1,0:T(8,128)(2,1)S(1)}, bf16[3,64,128]{2,1,0:T(8,128)(2,1)S(1)}, u32[]{:S(2)}, u32[]{:S(2)}) collective-permute-start(bf16[3,64,128]{2,1,0:T(8,128)(2,1)S(1)} %get-tuple-element.53), channel_id=1, source_target_pairs={{0,4},{4,0},{8,12},{12,8},{16,20},{20,16},{24,28},{28,24},{1,5},{5... | collective-permute-start | bytes 147464 | tf_op jit(solution)/shard_map/ppermute | solution.py:625
  6.8 7.5 %collective-permute-start.1 = (bf16[3,64,128]{2,1,0:T(8,128)(2,1)S(1)}, bf16[3,64,128]{2,1,0:T(8,128)(2,1)S(1)}, u32[]{:S(2)}, u32[]{:S(2)}) collective-permute-start(bf16[3,64,128]{2,1,0:T(8,128)(2,1)S(1)} %get-tuple-element.54), channel_id=1, source_target_pairs={{0,28},{4,8},{8,4},{12,16},{16,12},{20,24},{24,20},{28,0},{1,29},{... | collective-permute-start | bytes 147464 | tf_op jit(solution)/shard_map/ppermute | solution.py:633
  14.8 8.4 %collective-permute-start.4 = (bf16[3,64,128]{2,1,0:T(8,128)(2,1)S(1)}, bf16[3,64,128]{2,1,0:T(8,128)(2,1)S(1)}, u32[]{:S(2)}, u32[]{:S(2)}) collective-permute-start(bf16[3,64,128]{2,1,0:T(8,128)(2,1)S(1)} %get-tuple-element.58), channel_id=1, source_target_pairs={{0,4},{4,0},{8,12},{12,8},{16,20},{20,16},{24,28},{28,24},{1,5},{5... | collective-permute-start | bytes 147464 | tf_op jit(solution)/shard_map/ppermute | solution.py:625
  14.8 8.3 %collective-permute-start.5 = (bf16[3,64,128]{2,1,0:T(8,128)(2,1)S(1)}, bf16[3,64,128]{2,1,0:T(8,128)(2,1)S(1)}, u32[]{:S(2)}, u32[]{:S(2)}) collective-permute-start(bf16[3,64,128]{2,1,0:T(8,128)(2,1)S(1)} %get-tuple-element.59), channel_id=1, source_target_pairs={{0,28},{4,8},{8,4},{12,16},{16,12},{20,24},{24,20},{28,0},{1,29},{... | collective-permute-start | bytes 147464 | tf_op jit(solution)/shard_map/ppermute | solution.py:633
  17.8 5.4 %collective-permute-start.6 = (bf16[3,32,128]{2,1,0:T(8,128)(2,1)S(1)}, bf16[3,32,128]{2,1,0:T(8,128)(2,1)S(1)}, u32[]{:S(2)}, u32[]{:S(2)}) collective-permute-start(bf16[3,32,128]{2,1,0:T(8,128)(2,1)S(1)} %get-tuple-element.60), channel_id=1, source_target_pairs={{0,1},{1,0},{2,3},{3,2},{4,5},{5,4},{6,7},{7,6},{8,9},{9,8},{10,11... | collective-permute-start | bytes 73736 | tf_op jit(solution)/shard_map/ppermute | solution.py:625
  24.2 4.5 %collective-permute-start.9 = (bf16[256,256]{1,0:T(8,128)(2,1)S(1)}, bf16[256,256]{1,0:T(8,128)(2,1)S(1)}, u32[]{:S(2)}, u32[]{:S(2)}) collective-permute-start(bf16[256,256]{1,0:T(8,128)(2,1)S(1)} %get-tuple-element.64.h1.h_own), channel_id=1, source_target_pairs={{0,3},{1,2},{2,1},{3,0},{4,7},{5,6},{6,5},{7,4},{8,11},{9,10},{10,... | collective-permute-start | bytes 393224 | tf_op jit(solution)/shard_map/ppermute | solution.py:625
  29.6 4.8 %collective-permute-start.12 = (bf16[256,256]{1,0:T(8,128)(2,1)S(1)}, bf16[256,256]{1,0:T(8,128)(2,1)S(1)}, u32[]{:S(2)}, u32[]{:S(2)}) collective-permute-start(bf16[256,256]{1,0:T(8,128)(2,1)S(1)} %get-tuple-element.66.dz2.d_own), channel_id=1, source_target_pairs={{0,3},{1,2},{2,1},{3,0},{4,7},{5,6},{6,5},{7,4},{8,11},{9,10},{10,... | collective-permute-start | bytes 393224 | tf_op jit(solution)/shard_map/ppermute | solution.py:625
  39.3 6.2 %collective-permute-start.15 = (bf16[64,1152]{1,0:T(8,128)(2,1)S(1)}, bf16[64,1152]{1,0:T(8,128)(2,1)S(1)}, u32[]{:S(2)}, u32[]{:S(2)}) collective-permute-start(bf16[64,1152]{1,0:T(8,128)(2,1)S(1)} %get-tuple-element.77), channel_id=1, source_target_pairs={{0,2},{1,3},{2,0},{3,1},{4,6},{5,7},{6,4},{7,5},{8,10},{9,11},{10,... | collective-permute-start | bytes 442376 | tf_op jit(solution)/shard_map/ppermute | solution.py:625
  42.9 6.0 %collective-permute-start.20 = (bf16[216,256]{1,0:T(8,128)(2,1)S(1)}, bf16[216,256]{1,0:T(8,128)(2,1)S(1)}, u32[]{:S(2)}, u32[]{:S(2)}) collective-permute-start(bf16[216,256]{1,0:T(8,128)(2,1)S(1)} %get-tuple-element.86), channel_id=1, source_target_pairs={{0,4},{4,0},{8,12},{12,8},{16,20},{20,16},{24,28},{28,24},{1,5},{5... | collective-permute-start | bytes 331784 | tf_op jit(solution)/shard_map/ppermute | solution.py:625
  43.6 11.4 %collective-permute-start.19 = (bf16[216,256]{1,0:T(8,128)(2,1)S(1)}, bf16[216,256]{1,0:T(8,128)(2,1)S(1)}, u32[]{:S(2)}, u32[]{:S(2)}) collective-permute-start(bf16[216,256]{1,0:T(8,128)(2,1)S(1)} %get-tuple-element.84), channel_id=1, source_target_pairs={{0,4},{4,0},{8,12},{12,8},{16,20},{20,16},{24,28},{28,24},{1,5},{5... | collective-permute-start | bytes 331784 | tf_op jit(solution)/shard_map/ppermute | solution.py:625
  45.5 7.4 %collective-permute-start.17 = (bf16[216,256]{1,0:T(8,128)(2,1)S(1)}, bf16[216,256]{1,0:T(8,128)(2,1)S(1)}, u32[]{:S(2)}, u32[]{:S(2)}) collective-permute-start(bf16[216,256]{1,0:T(8,128)(2,1)S(1)} %get-tuple-element.82), channel_id=1, source_target_pairs={{0,4},{4,0},{8,12},{12,8},{16,20},{20,16},{24,28},{28,24},{1,5},{5... | collective-permute-start | bytes 331784 | tf_op jit(solution)/shard_map/ppermute | solution.py:625
  46.2 5.1 %collective-permute-start.22 = (bf16[2,16,1152]{2,1,0:T(8,128)(2,1)S(1)}, bf16[2,16,1152]{2,1,0:T(8,128)(2,1)S(1)}, u32[]{:S(2)}, u32[]{:S(2)}) collective-permute-start(bf16[2,16,1152]{2,1,0:T(8,128)(2,1)S(1)} %get-tuple-element.87.refs_1_), channel_id=1, source_target_pairs={{0,8},{4,12},{8,0},{12,4},{16,24},{20,28},{24,16},{28,20},{1,9},{5... | collective-permute-start | bytes 221192 | tf_op jit(solution)/shard_map/ppermute | solution.py:625
  48.9 6.0 %collective-permute-start.21 = (bf16[216,256]{1,0:T(8,128)(2,1)S(1)}, bf16[216,256]{1,0:T(8,128)(2,1)S(1)}, u32[]{:S(2)}, u32[]{:S(2)}) collective-permute-start(bf16[216,256]{1,0:T(8,128)(2,1)S(1)} %shard_map.116), channel_id=1, source_target_pairs={{0,8},{4,12},{8,0},{12,4},{16,24},{20,28},{24,16},{28,20},{1,9},{5... | collective-permute-start | bytes 331784 | tf_op jit(solution)/shard_map/ppermute | solution.py:625
  51.4 5.8 %collective-permute-start.24 = (bf16[16,1152]{1,0:T(8,128)(2,1)S(1)}, bf16[16,1152]{1,0:T(8,128)(2,1)S(1)}, u32[]{:S(2)}, u32[]{:S(2)}) collective-permute-start(bf16[16,1152]{1,0:T(8,128)(2,1)S(1)} %get-tuple-element.89.refs_2_), channel_id=1, source_target_pairs={{0,16},{4,20},{8,24},{12,28},{16,0},{20,4},{24,8},{28,12},{1,17},{... | collective-permute-start | bytes 110600 | tf_op jit(solution)/shard_map/ppermute | solution.py:625
  52.7 7.0 %collective-permute-start.16 = (bf16[216,256]{1,0:T(8,128)(2,1)S(1)}, bf16[216,256]{1,0:T(8,128)(2,1)S(1)}, u32[]{:S(2)}, u32[]{:S(2)}) collective-permute-start(bf16[216,256]{1,0:T(8,128)(2,1)S(1)} %get-tuple-element.80), channel_id=1, source_target_pairs={{0,4},{4,0},{8,12},{12,8},{16,20},{20,16},{24,28},{28,24},{1,5},{5... | collective-permute-start | bytes 331784 | tf_op jit(solution)/shard_map/ppermute | solution.py:625
  53.0 8.5 %collective-permute-start.18 = (bf16[216,256]{1,0:T(8,128)(2,1)S(1)}, bf16[216,256]{1,0:T(8,128)(2,1)S(1)}, u32[]{:S(2)}, u32[]{:S(2)}) collective-permute-start(bf16[216,256]{1,0:T(8,128)(2,1)S(1)} %shard_map.115), channel_id=1, source_target_pairs={{0,8},{4,12},{8,0},{12,4},{16,24},{20,28},{24,16},{28,20},{1,9},{5... | collective-permute-start | bytes 331784 | tf_op jit(solution)/shard_map/ppermute | solution.py:625
  55.0 7.4 %collective-permute-start.23 = (bf16[216,256]{1,0:T(8,128)(2,1)S(1)}, bf16[216,256]{1,0:T(8,128)(2,1)S(1)}, u32[]{:S(2)}, u32[]{:S(2)}) collective-permute-start(bf16[216,256]{1,0:T(8,128)(2,1)S(1)} %shard_map.118), channel_id=1, source_target_pairs={{0,16},{4,20},{8,24},{12,28},{16,0},{20,4},{24,8},{28,12},{1,17},{... | collective-permute-start | bytes 331784 | tf_op jit(solution)/shard_map/ppermute | solution.py:625
  62.5 7.0 %collective-permute-start.31 = (bf16[256,256]{1,0:T(8,128)(2,1)S(1)}, bf16[256,256]{1,0:T(8,128)(2,1)S(1)}, u32[]{:S(2)}, u32[]{:S(2)}) collective-permute-start(bf16[256,256]{1,0:T(8,128)(2,1)S(1)} %shard_map.120.own), channel_id=1, source_target_pairs={{0,24},{4,28},{8,16},{12,20},{16,8},{20,12},{24,0},{28,4},{1,25},{... | collective-permute-start | bytes 393224 | tf_op jit(solution)/shard_map/ppermute | solution.py:625
  64.9 8.4 %collective-permute-start.29 = (bf16[256,256]{1,0:T(8,128)(2,1)S(1)}, bf16[256,256]{1,0:T(8,128)(2,1)S(1)}, u32[]{:S(2)}, u32[]{:S(2)}) collective-permute-start(bf16[256,256]{1,0:T(8,128)(2,1)S(1)} %shard_map.120.own), channel_id=1, source_target_pairs={{0,16},{4,20},{8,24},{12,28},{16,0},{20,4},{24,8},{28,12},{1,17},{... | collective-permute-start | bytes 393224 | tf_op jit(solution)/shard_map/ppermute | solution.py:625
  64.9 9.6 %collective-permute-start.27 = (bf16[256,256]{1,0:T(8,128)(2,1)S(1)}, bf16[256,256]{1,0:T(8,128)(2,1)S(1)}, u32[]{:S(2)}, u32[]{:S(2)}) collective-permute-start(bf16[256,256]{1,0:T(8,128)(2,1)S(1)} %shard_map.120.own), channel_id=1, source_target_pairs={{0,8},{4,12},{8,0},{12,4},{16,24},{20,28},{24,16},{28,20},{1,9},{5... | collective-permute-start | bytes 393224 | tf_op jit(solution)/shard_map/ppermute | solution.py:625
  67.0 8.4 %collective-permute-start.26 = (bf16[256,256]{1,0:T(8,128)(2,1)S(1)}, bf16[256,256]{1,0:T(8,128)(2,1)S(1)}, u32[]{:S(2)}, u32[]{:S(2)}) collective-permute-start(bf16[256,256]{1,0:T(8,128)(2,1)S(1)} %shard_map.120.own), channel_id=1, source_target_pairs={{0,4},{4,0},{8,12},{12,8},{16,20},{20,16},{24,28},{28,24},{1,5},{5... | collective-permute-start | bytes 393224 | tf_op jit(solution)/shard_map/ppermute | solution.py:625
  69.5 7.8 %collective-permute-start.32 = (bf16[256,256]{1,0:T(8,128)(2,1)S(1)}, bf16[256,256]{1,0:T(8,128)(2,1)S(1)}, u32[]{:S(2)}, u32[]{:S(2)}) collective-permute-start(bf16[256,256]{1,0:T(8,128)(2,1)S(1)} %collective-permute-done.31.refs_5_), channel_id=1, source_target_pairs={{0,4},{4,0},{8,12},{12,8},{16,20},{20,16},{24,28},{28,24},{1,5},{5... | collective-permute-start | bytes 393224 | tf_op jit(solution)/shard_map/ppermute | solution.py:625
  73.3 5.4 %collective-permute-start.30 = (bf16[256,256]{1,0:T(8,128)(2,1)S(1)}, bf16[256,256]{1,0:T(8,128)(2,1)S(1)}, u32[]{:S(2)}, u32[]{:S(2)}) collective-permute-start(bf16[256,256]{1,0:T(8,128)(2,1)S(1)} %collective-permute-done.29.refs_3_), channel_id=1, source_target_pairs={{0,4},{4,0},{8,12},{12,8},{16,20},{20,16},{24,28},{28,24},{1,5},{5... | collective-permute-start | bytes 393224 | tf_op jit(solution)/shard_map/ppermute | solution.py:625
  74.5 5.6 %collective-permute-start.28 = (bf16[256,256]{1,0:T(8,128)(2,1)S(1)}, bf16[256,256]{1,0:T(8,128)(2,1)S(1)}, u32[]{:S(2)}, u32[]{:S(2)}) collective-permute-start(bf16[256,256]{1,0:T(8,128)(2,1)S(1)} %collective-permute-done.27.refs_1_), channel_id=1, source_target_pairs={{0,4},{4,0},{8,12},{12,8},{16,20},{20,16},{24,28},{28,24},{1,5},{5... | collective-permute-start | bytes 393224 | tf_op jit(solution)/shard_map/ppermute | solution.py:625
  (16 other events, 57.1 us)

commit v6 on v5

--- a/solution.py
+++ b/solution.py
@@ -358,9 +358,14 @@
     h1[...] = (hidden * jax.nn.sigmoid(hidden)).astype(BF16)
 
 
-def restore_kernel(field, back, after_this, out):
+def same_kernel(value, out):
+    out[...] = value[...]
+
+
+def restore_kernel(field, back, after_this, out, done):
     for c in range(3):
         out[c] = moved(back[...], field[c])
+    done[...] = jnp.zeros_like(done)
 
 
 def silu_grad(value):
@@ -573,31 +578,63 @@
     refs[-1][...] = total.astype(BF16)
 
 
-def share_kernel(taps, one, two, three, dense, dense_in, out):
+def share_kernel(taps, one, two, three, dense, dense_in, after_this, out):
     total = taps[...]
     for other in (one, two, three):
         total = total + other[...].astype(F32)
     out[...] = packed(total, dense[...] + dense_in[...].astype(F32)).astype(BF16)
 
 
-def spread_kernel(features, own, *refs):
-    count = len(refs) - 3 + 1
-    shares = (own,) + refs[:-3]
-    taps, encode, head = refs[-3:]
-    channels = own.shape[1]
-    tap_rows = taps.shape[0] // count
-    own_rows = encode.shape[0] // count
+def place_kernel(masks, count, *refs):
+    shares = refs[: len(masks)]
+    outs = refs[-7:-4]
+    held = refs[-4:-1]
+    sems = refs[-1]
+    channels = shares[0].shape[1]
+    tap_rows, own_rows = [out.shape[0] // count for out in outs[:2]]
+    features = outs[1].shape[1]
     me = lax.axis_index("sim")
-    for k, share in enumerate(shares):
-        source = jnp.bitwise_xor(me, k)
+    copies = []
+    for i, (mask, share) in enumerate(zip(masks, shares)):
+        source = jnp.bitwise_xor(me, mask)
         value = share[...].astype(F32)
-        taps[pl.ds(pl.multiple_of(source * tap_rows, 8), tap_rows)] = value[:tap_rows]
-        rows = pl.ds(pl.multiple_of(source * own_rows, 8), own_rows)
+        held[0][i] = value[:tap_rows]
         start = tap_rows
         for first in range(0, features, channels):
-            encode[rows, first : first + channels] = value[start : start + own_rows]
+            held[1][i, :, first : first + channels] = value[start : start + own_rows]
             start += own_rows
-        head[rows] = value[start : start + own_rows, : head.shape[1]]
+        held[2][i] = value[start : start + own_rows, : outs[2].shape[1]]
+        for j, out in enumerate(outs):
+            size = tap_rows if j == 0 else own_rows
+            rows = pl.ds(pl.multiple_of(source * size, 8), size)
+            copy = pltpu.make_async_copy(held[j].at[i], out.at[rows], sems.at[i, j])
+            copy.start()
+            copies.append(copy)
+    for copy in copies:
+        copy.wait()
+
+
+def placed_shares(shares, shapes, count):
+    outs = ()
+    for first in range(0, count, 2):
+        masks = (first, first + 1)
+        tap_rows, own_rows = [shape.shape[0] // count for shape in shapes[:2]]
+        sizes = (tap_rows, own_rows, own_rows)
+        held = [
+            pltpu.VMEM((2, size, shape.shape[1]), F32) for size, shape in zip(sizes, shapes)
+        ]
+        anywhere = pl.BlockSpec(memory_space=pl.ANY)
+        outs = pl.pallas_call(
+            functools.partial(place_kernel, masks, count),
+            out_shape=shapes,
+            in_specs=[pl.BlockSpec(memory_space=pltpu.VMEM)] * 2 + [anywhere] * len(outs),
+            out_specs=(anywhere,) * 3,
+            scratch_shapes=held + [pltpu.SemaphoreType.DMA((2, 3))],
+            input_output_aliases={2 + i: i for i in range(len(outs))},
+            compiler_params=pltpu.CompilerParams(vmem_limit_bytes=VMEM_LIMIT),
+            cost_estimate=pl.CostEstimate(flops=1000, bytes_accessed=1000, transcendentals=0),
+        )(shares[first], shares[first + 1], *outs)
+    return outs
 
 
 def call(kernel, outs, scratch=(), in_hbm=(), inputs=0, flops=1000):
@@ -644,7 +681,7 @@
 
 def gathered(share, sims):
     got = {0: share}
-    for k in sorted(range(2, sims, 2), reverse=True):
+    for k in range(2, sims, 2):
         got[k] = swapped(share, "sim", k)
     for k in range(0, sims, 2):
         got[k + 1] = swapped(got[k], "sim", 1)
@@ -706,7 +743,7 @@
         functools.partial(forward_kernel, groups, total),
         (rows_bf, rows_bf, shaped((rows, outputs), BF16)),
         (pltpu.VMEM((EX, EY + 2, ez, 3 * channels), BF16),),
-    )(z2, h1, h_one, h_three, w_conv, w_head, target)
+    )(z2, h1, h_one, call(same_kernel, rows_bf, flops=2 * 10**9)(h_three), w_conv, w_head, target)
 
     d_three = swapped(dz2, "grp", 3)
     d_one = swapped(dz2, "grp", 1)
@@ -722,7 +759,7 @@
         functools.partial(back_kernel, groups),
         (shaped(pair, F32), shaped(pair, BF16)),
         (pltpu.VMEM((channels, wide), F32),),
-    )(dh1, head, dz2, d_one, d_three, w_conv, z1, snapshot)
+    )(dh1, head, dz2, d_one, call(same_kernel, rows_bf, flops=2 * 10**9)(d_three), w_conv, z1, snapshot)
     e_got = swapped(e_sent, "grp", 1)
     e_kept, e_sent = call(core_kernel, (shaped(pair[1:], F32), shaped(pair[1:], BF16)))(e_kept, e_got)
     e_got = swapped(e_sent, "grp", 2)
@@ -744,6 +781,7 @@
         in_hbm=(8,),
         inputs=9,
     )(h1, h_one, h_two, h_three, dz2, d_one, d_two, d_three, e_kept)
+    restore = call(restore_kernel, (whole, shaped((8, 128), F32)), in_hbm=(2,), inputs=3)
     if direct:
         tap_piece = shaped((tap_rows, channels), BF16)
         part = (2, 2 * own_rows, wide)
@@ -756,36 +794,35 @@
         add_two = call(functools.partial(sum_kernel, 2), tap_piece)
         add_three = call(functools.partial(sum_kernel, 3), tap_piece)
         six = swapped(add_two(taps[6], taps_in[6], e_sent), "sim", 2)
-        two = swapped(add_two(taps[2], taps_in[2]), "sim", 2)
         part = shaped((2 * own_rows, wide), F32), shaped((2 * own_rows, wide), BF16)
         e_kept, e_sent = call(functools.partial(half_kernel, 4), part)(e_kept, e_got)
         e_got = swapped(e_sent, "sim", 4)
-        four = swapped(add_three(taps[4], taps_in[4], six, e_sent), "sim", 4)
+        two = add_two(taps[2], taps_in[2], e_sent)
+        four = swapped(add_three(taps[4], taps_in[4], six, two), "sim", 4)
+        two = swapped(two, "sim", 2)
         part = shaped((own_rows, wide), F32), shaped((own_rows, wide), BF16)
         e_kept, e_sent = call(functools.partial(half_kernel, 1), part, flops=4 * 10**9)(
             e_kept.reshape(2, own_rows, wide), e_got.reshape(2, own_rows, wide)
         )
+        velocity_next, done = restore(field, back, e_sent)
         e_got = swapped(e_sent, "sim", 1)
         blocks = -(-wide // channels)
         share = call(share_kernel, shaped((tap_rows + blocks * own_rows, channels), BF16))(
-            taps[0], taps_in[0], two, four, e_kept, e_got
+            taps[0], taps_in[0], two, four, e_kept, e_got, done
         )
         shares = gathered(share, sims)
-        velocity_next = call(restore_kernel, whole, in_hbm=(2,), inputs=3)(field, back, shares[1])
-        taps, encode, head = call(
-            functools.partial(spread_kernel, features),
-            (
-                shaped((27 * quarter, channels), F32),
-                shaped((quarter, features), F32),
-                shaped((quarter, outputs), F32),
-            ),
-        )(*shares)
+        shapes = (
+            shaped((27 * quarter, channels), F32),
+            shaped((quarter, features), F32),
+            shaped((quarter, outputs), F32),
+        )
+        taps, encode, head = placed_shares(shares, shapes, sims)
     else:
         taps = taps[0].reshape(sims, tap_rows, channels)
         taps = lax.all_to_all(taps, "sim", 0, 0, tiled=True)
         taps = jnp.sum(taps.astype(F32), axis=0).astype(BF16)
         taps = lax.all_gather(taps, "sim").astype(F32)
-        velocity_next = call(restore_kernel, whole, in_hbm=(2,), inputs=3)(field, back, e_kept)
+        velocity_next, done = restore(field, back, e_kept)
         dense = e_kept + e_got.astype(F32)
         dense = dense.astype(BF16).reshape(sims, own_rows, wide)
         dense = lax.all_to_all(dense, "sim", 0, 0, tiled=True)

time: 81.8 us -> 80.2 us (0.980)
  waiting for transfers between devices: 13.1 us -> 10.4 us
  Pallas kernels: 17.9 us -> 19.9 us
  starting transfers between devices: 47.6 us -> 46.6 us
    ppermute x29, waiting for transfers between devices: 13.1 us -> 10.4 us  [swapped(): return lax.ppermute(value, axis, [(i, i ^ mask) for i in range(count)])]
    pallas_call x4 -> x9, Pallas kernels: 3.48 us -> 5.44 us  [the longest x4 3.38 us: placed_shares(): pl.pallas_call(functools.partial(place_kernel, masks, count), out_shape=s...]
    ppermute x29, starting transfers between devices: 39.6 us -> 38.6 us  [swapped(): return lax.ppermute(value, axis, [(i, i ^ mask) for i in range(count)])]
  transfers between devices with their start and end apart: 33 -> 33, of which waited for: 12 -> 11; matrix products, arithmetic and copies ran while one was open for 0% -> 0% of each run, Pallas kernels for 14% -> 17%
where the time goes in v6:
time: 80.2 us; the launch traced here: 80 us
  starting transfers between devices  46.6 us (58%)
  Pallas kernels  19.9 us (25%)
  waiting for transfers between devices  10.4 us (13%)
  local copies, waits for them, and re-layouts  1.98 us (2%)
  between operations  1.14 us (1%)
    ppermute x29, starting transfers between devices, swapped(): return lax.ppermute(value, axis, [(i, i ^ mask) for i in range(count)])  38.6 us
    ppermute x29, waiting for transfers between devices, swapped(): return lax.ppermute(value, axis, [(i, i ^ mask) for i in range(count)])  10.4 us
    ppermute x4, starting transfers between devices, crossed(): lax.ppermute(value, axis, [(i, j) for i, j in route if 0 <= j < count])  7.97 us
    pallas_call x2, Pallas kernels, body(): part = call(inside_kernel, whole)(field, stencil)  6.41 us
    pallas_call x4, Pallas kernels, placed_shares(): pl.pallas_call(functools.partial(place_kernel, masks, count), out_shape=s...  3.38 us
    unnamed x14, local copies, waits for them, and re-layouts  1.98 us
    pallas_call x1, Pallas kernels, body(): velocity_next, done = restore(field, back, e_sent)  1.97 us
    pallas_call x1, Pallas kernels, body(): call(functools.partial(taps_kernel, groups, sims if direct else 1), tuple...  1.86 us
  transfers between devices with their start and end apart: 33, of which 11 were waited for; matrix products, arithmetic and copies ran while one was open for 0% of the time, Pallas kernels for 17%

profile of v6, /device:TPU:0, one launch (start us, length us, event | category | flops | bytes accessed | tf_op | source)
XLA Modules:
  0.0 80.0 jit_solution(15017727573655691051)
XLA Ops:
  3.8 3.0 %collective-permute-start = (bf16[3,64,128]{2,1,0:T(8,128)(2,1)S(1)}, bf16[3,64,128]{2,1,0:T(8,128)(2,1)S(1)}, u32[]{:S(2)}, u32[]{:S(2)}) collective-permute-start(bf16[3,64,128]{2,1,0:T(8,128)(2,1)S(1)} %get-tuple-element.64), channel_id=1, source_target_pairs={{0,4},{4,0},{8,12},{12,8},{16,20},{20,16},{24,28},{28,24},{1,5},{5... | collective-permute-start | bytes 147464 | tf_op jit(solution)/shard_map/ppermute | solution.py:662
  6.8 3.6 %collective-permute-start.1 = (bf16[3,64,128]{2,1,0:T(8,128)(2,1)S(1)}, bf16[3,64,128]{2,1,0:T(8,128)(2,1)S(1)}, u32[]{:S(2)}, u32[]{:S(2)}) collective-permute-start(bf16[3,64,128]{2,1,0:T(8,128)(2,1)S(1)} %get-tuple-element.65), channel_id=1, source_target_pairs={{0,28},{4,8},{8,4},{12,16},{16,12},{20,24},{24,20},{28,0},{1,29},{... | collective-permute-start | bytes 147464 | tf_op jit(solution)/shard_map/ppermute | solution.py:670
  11.0 3.2 %shard_map.104.part = f32[3,256,512]{2,1,0:T(8,128)S(1)} custom-call(f32[3,256,512]{2,1,0:T(8,128)S(1)} %get-tuple-element.63.field, bf16[2560,512]{1,0:T(8,128)(2,1)S(1)} %copy-done.1), custom_call_target="tpu_custom_call" | custom-call | flops 1000 | bytes 1000 | tf_op jit(solution)/shard_map/pallas_call | solution.py:721
  14.8 2.9 %collective-permute-start.5 = (bf16[3,64,128]{2,1,0:T(8,128)(2,1)S(1)}, bf16[3,64,128]{2,1,0:T(8,128)(2,1)S(1)}, u32[]{:S(2)}, u32[]{:S(2)}) collective-permute-start(bf16[3,64,128]{2,1,0:T(8,128)(2,1)S(1)} %get-tuple-element.70), channel_id=1, source_target_pairs={{0,28},{4,8},{8,4},{12,16},{16,12},{20,24},{24,20},{28,0},{1,29},{... | collective-permute-start | bytes 147464 | tf_op jit(solution)/shard_map/ppermute | solution.py:670
  19.9 3.2 %shard_map.106.part = f32[3,256,512]{2,1,0:T(8,128)S(1)} custom-call(f32[3,256,512]{2,1,0:T(8,128)S(1)} %get-tuple-element.68.field, bf16[2560,512]{1,0:T(8,128)(2,1)S(1)} %copy-done.1), custom_call_target="tpu_custom_call" | custom-call | flops 1000 | bytes 1000 | tf_op jit(solution)/shard_map/pallas_call | solution.py:724
  25.5 1.8 %collective-permute-start.8 = (bf16[256,256]{1,0:T(8,128)(2,1)S(1)}, bf16[256,256]{1,0:T(8,128)(2,1)S(1)}, u32[]{:S(2)}, u32[]{:S(2)}) collective-permute-start(bf16[256,256]{1,0:T(8,128)(2,1)S(1)} %get-tuple-element.75.h1.h_own), channel_id=1, source_target_pairs={{0,1},{1,0},{2,3},{3,2},{4,5},{5,4},{6,7},{7,6},{8,9},{9,8},{10,11... | collective-permute-start | bytes 393224 | tf_op jit(solution)/shard_map/ppermute | solution.py:662
  29.6 1.8 %collective-permute-start.11 = (bf16[256,256]{1,0:T(8,128)(2,1)S(1)}, bf16[256,256]{1,0:T(8,128)(2,1)S(1)}, u32[]{:S(2)}, u32[]{:S(2)}) collective-permute-start(bf16[256,256]{1,0:T(8,128)(2,1)S(1)} %get-tuple-element.77.dz2.d_own), channel_id=1, source_target_pairs={{0,3},{1,2},{2,1},{3,0},{4,7},{5,6},{6,5},{7,4},{8,11},{9,10},{10,... | collective-permute-start | bytes 393224 | tf_op jit(solution)/shard_map/ppermute | solution.py:662
  31.4 1.5 %collective-permute-start.10 = (bf16[256,256]{1,0:T(8,128)(2,1)S(1)}, bf16[256,256]{1,0:T(8,128)(2,1)S(1)}, u32[]{:S(2)}, u32[]{:S(2)}) collective-permute-start(bf16[256,256]{1,0:T(8,128)(2,1)S(1)} %get-tuple-element.77.dz2.d_own), channel_id=1, source_target_pairs={{0,1},{1,0},{2,3},{3,2},{4,5},{5,4},{6,7},{7,6},{8,9},{9,8},{10,11... | collective-permute-start | bytes 393224 | tf_op jit(solution)/shard_map/ppermute | solution.py:662
  34.5 1.5 %shard_map.113 = (f32[2,64,1152]{2,1,0:T(8,128)S(1)}, bf16[2,64,1152]{2,1,0:T(8,128)(2,1)S(1)}) custom-call(f32[256,256]{1,0:T(8,128)S(1)} %get-tuple-element.80.dh1, f32[256,128]{1,0:T(8,128)S(1)} %get-tuple-element.81.head, bf16[256,256]{1,0:T(8,128)(2,1)S(1)} %get-tuple-element.77.dz2.d_own, bf16[256,256]{1,0:T(8,128)(2,1)S(1)} %collective-permute-done.10.pair.d_one, ...), custom_call_target="tpu_custom_call" | custom-call | flops 1000 | bytes 1000 | tf_op jit(solution)/shard_map/pallas_call | solution.py:758
  36.0 2.1 %collective-permute-start.12 = (bf16[2,64,1152]{2,1,0:T(8,128)(2,1)S(1)}, bf16[2,64,1152]{2,1,0:T(8,128)(2,1)S(1)}, u32[]{:S(2)}, u32[]{:S(2)}) collective-permute-start(bf16[2,64,1152]{2,1,0:T(8,128)(2,1)S(1)} %get-tuple-element.85), channel_id=1, source_target_pairs={{0,1},{1,0},{2,3},{3,2},{4,5},{5,4},{6,7},{7,6},{8,9},{9,8},{10,11... | collective-permute-start | bytes 884744 | tf_op jit(solution)/shard_map/ppermute | solution.py:662
  39.3 1.7 %collective-permute-start.13 = (bf16[64,1152]{1,0:T(8,128)(2,1)S(1)}, bf16[64,1152]{1,0:T(8,128)(2,1)S(1)}, u32[]{:S(2)}, u32[]{:S(2)}) collective-permute-start(bf16[64,1152]{1,0:T(8,128)(2,1)S(1)} %get-tuple-element.87), channel_id=1, source_target_pairs={{0,2},{1,3},{2,0},{3,1},{4,6},{5,7},{6,4},{7,5},{8,10},{9,11},{10,... | collective-permute-start | bytes 442376 | tf_op jit(solution)/shard_map/ppermute | solution.py:662
  41.1 1.9 %shard_map.115 = (f32[216,256]{1,0:T(8,128)S(1)}, bf16[216,256]{1,0:T(8,128)(2,1)S(1)}, f32[216,256]{1,0:T(8,128)S(1)}, bf16[216,256]{1,0:T(8,128)(2,1)S(1)}, f3...) custom-call(bf16[256,256]{1,0:T(8,128)(2,1)S(1)} %get-tuple-element., ...), custom_call_target="tpu_custom_call" | custom-call | flops 1000 | bytes 1000 | tf_op jit(solution)/shard_map/pallas_call | solution.py:773
  43.6 1.4 %collective-permute-start.21 = (bf16[216,256]{1,0:T(8,128)(2,1)S(1)}, bf16[216,256]{1,0:T(8,128)(2,1)S(1)}, u32[]{:S(2)}, u32[]{:S(2)}) collective-permute-start(bf16[216,256]{1,0:T(8,128)(2,1)S(1)} %get-tuple-element.101), channel_id=1, source_target_pairs={{0,4},{4,0},{8,12},{12,8},{16,20},{20,16},{24,28},{28,24},{1,5},{5... | collective-permute-start | bytes 331784 | tf_op jit(solution)/shard_map/ppermute | solution.py:662
  46.3 1.6 %collective-permute-start.16 = (bf16[2,16,1152]{2,1,0:T(8,128)(2,1)S(1)}, bf16[2,16,1152]{2,1,0:T(8,128)(2,1)S(1)}, u32[]{:S(2)}, u32[]{:S(2)}) collective-permute-start(bf16[2,16,1152]{2,1,0:T(8,128)(2,1)S(1)} %get-tuple-element.91.refs_1_), channel_id=1, source_target_pairs={{0,8},{4,12},{8,0},{12,4},{16,24},{20,28},{24,16},{28,20},{1,9},{5... | collective-permute-start | bytes 221192 | tf_op jit(solution)/shard_map/ppermute | solution.py:662
  49.0 1.7 %collective-permute-start.23 = (bf16[216,256]{1,0:T(8,128)(2,1)S(1)}, bf16[216,256]{1,0:T(8,128)(2,1)S(1)}, u32[]{:S(2)}, u32[]{:S(2)}) collective-permute-start(bf16[216,256]{1,0:T(8,128)(2,1)S(1)} %shard_map.121), channel_id=1, source_target_pairs={{0,8},{4,12},{8,0},{12,4},{16,24},{20,28},{24,16},{28,20},{1,9},{5... | collective-permute-start | bytes 331784 | tf_op jit(solution)/shard_map/ppermute | solution.py:662
  51.4 1.3 %collective-permute-start.17 = (bf16[16,1152]{1,0:T(8,128)(2,1)S(1)}, bf16[16,1152]{1,0:T(8,128)(2,1)S(1)}, u32[]{:S(2)}, u32[]{:S(2)}) collective-permute-start(bf16[16,1152]{1,0:T(8,128)(2,1)S(1)} %get-tuple-element.93.refs_1_), channel_id=1, source_target_pairs={{0,16},{4,20},{8,24},{12,28},{16,0},{20,4},{24,8},{28,12},{1,17},{... | collective-permute-start | bytes 110600 | tf_op jit(solution)/shard_map/ppermute | solution.py:662
  53.0 2.0 %collective-permute-start.20 = (bf16[216,256]{1,0:T(8,128)(2,1)S(1)}, bf16[216,256]{1,0:T(8,128)(2,1)S(1)}, u32[]{:S(2)}, u32[]{:S(2)}) collective-permute-start(bf16[216,256]{1,0:T(8,128)(2,1)S(1)} %shard_map.120.refs_2_), channel_id=1, source_target_pairs={{0,8},{4,12},{8,0},{12,4},{16,24},{20,28},{24,16},{28,20},{1,9},{5... | collective-permute-start | bytes 331784 | tf_op jit(solution)/shard_map/ppermute | solution.py:662
  55.1 2.2 %collective-permute-start.24 = (bf16[216,256]{1,0:T(8,128)(2,1)S(1)}, bf16[216,256]{1,0:T(8,128)(2,1)S(1)}, u32[]{:S(2)}, u32[]{:S(2)}) collective-permute-start(bf16[216,256]{1,0:T(8,128)(2,1)S(1)} %shard_map.122), channel_id=1, source_target_pairs={{0,16},{4,20},{8,24},{12,28},{16,0},{20,4},{24,8},{28,12},{1,17},{... | collective-permute-start | bytes 331784 | tf_op jit(solution)/shard_map/ppermute | solution.py:662
  57.3 2.4 %collective-permute-start.25 = (bf16[8,1152]{1,0:T(8,128)(2,1)S(1)}, bf16[8,1152]{1,0:T(8,128)(2,1)S(1)}, u32[]{:S(2)}, u32[]{:S(2)}) collective-permute-start(bf16[8,1152]{1,0:T(8,128)(2,1)S(1)} %get-tuple-element.94.after_this), channel_id=1, source_target_pairs={{0,4},{4,0},{8,12},{12,8},{16,20},{20,16},{24,28},{28,24},{1,5},{5... | collective-permute-start | bytes 55304 | tf_op jit(solution)/shard_map/ppermute | solution.py:662
  59.7 2.0 %shard_map.119 = (f32[3,256,512]{2,1,0:T(8,128)}, f32[8,128]{1,0:T(8,128)S(1)}) custom-call(f32[3,256,512]{2,1,0:T(8,128)S(1)} %get-tuple-element.73.field, bf16[256,256]{1,0:T(8,128)(2,1)S(1)} %get-tuple-element.74.back, bf16[8,1152]{1,0:T(8,128)(2,1)S(1)} %get-tuple-element.94.after_this), custom_call_target="tpu_custom_call" | custom-call | flops 1000 | bytes 1000 | tf_op jit(solution)/shard_map/pallas_call | solution.py:807
  62.3 2.8 %collective-permute-start.28 = (bf16[256,256]{1,0:T(8,128)(2,1)S(1)}, bf16[256,256]{1,0:T(8,128)(2,1)S(1)}, u32[]{:S(2)}, u32[]{:S(2)}) collective-permute-start(bf16[256,256]{1,0:T(8,128)(2,1)S(1)} %shard_map.123.refs_0_), channel_id=1, source_target_pairs={{0,16},{4,20},{8,24},{12,28},{16,0},{20,4},{24,8},{28,12},{1,17},{... | collective-permute-start | bytes 393224 | tf_op jit(solution)/shard_map/ppermute | solution.py:662
  65.2 1.3 %collective-permute-start.26 = (bf16[256,256]{1,0:T(8,128)(2,1)S(1)}, bf16[256,256]{1,0:T(8,128)(2,1)S(1)}, u32[]{:S(2)}, u32[]{:S(2)}) collective-permute-start(bf16[256,256]{1,0:T(8,128)(2,1)S(1)} %shard_map.123.refs_0_), channel_id=1, source_target_pairs={{0,24},{4,28},{8,16},{12,20},{16,8},{20,12},{24,0},{28,4},{1,25},{... | collective-permute-start | bytes 393224 | tf_op jit(solution)/shard_map/ppermute | solution.py:662
  66.5 1.5 %collective-permute-start.32 = (bf16[256,256]{1,0:T(8,128)(2,1)S(1)}, bf16[256,256]{1,0:T(8,128)(2,1)S(1)}, u32[]{:S(2)}, u32[]{:S(2)}) collective-permute-start(bf16[256,256]{1,0:T(8,128)(2,1)S(1)} %shard_map.123.refs_0_), channel_id=1, source_target_pairs={{0,4},{4,0},{8,12},{12,8},{16,20},{20,16},{24,28},{28,24},{1,5},{5... | collective-permute-start | bytes 393224 | tf_op jit(solution)/shard_map/ppermute | solution.py:662
  70.2 2.4 %collective-permute-done.28.refs_0_ = bf16[256,256]{1,0:T(8,128)(2,1)S(1)} collective-permute-done((bf16[256,256]{1,0:T(8,128)(2,1)S(1)}, bf16[256,256]{1,0:T(8,128)(2,1)S(1)}, u32[]{:S(2)}, u32[]{:S(2)}) %collective-permute-start.28) | collective-permute-done | bytes 131104 | tf_op jit(solution)/shard_map/ppermute | solution.py:662
  (82 shorter events, 28.0 us)
Async XLA Ops:
  3.8 10.5 %collective-permute-start = (bf16[3,64,128]{2,1,0:T(8,128)(2,1)S(1)}, bf16[3,64,128]{2,1,0:T(8,128)(2,1)S(1)}, u32[]{:S(2)}, u32[]{:S(2)}) collective-permute-start(bf16[3,64,128]{2,1,0:T(8,128)(2,1)S(1)} %get-tuple-element.64), channel_id=1, source_target_pairs={{0,4},{4,0},{8,12},{12,8},{16,20},{20,16},{24,28},{28,24},{1,5},{5... | collective-permute-start | bytes 147464 | tf_op jit(solution)/shard_map/ppermute | solution.py:662
  6.8 7.5 %collective-permute-start.1 = (bf16[3,64,128]{2,1,0:T(8,128)(2,1)S(1)}, bf16[3,64,128]{2,1,0:T(8,128)(2,1)S(1)}, u32[]{:S(2)}, u32[]{:S(2)}) collective-permute-start(bf16[3,64,128]{2,1,0:T(8,128)(2,1)S(1)} %get-tuple-element.65), channel_id=1, source_target_pairs={{0,28},{4,8},{8,4},{12,16},{16,12},{20,24},{24,20},{28,0},{1,29},{... | collective-permute-start | bytes 147464 | tf_op jit(solution)/shard_map/ppermute | solution.py:670
  14.8 8.4 %collective-permute-start.4 = (bf16[3,64,128]{2,1,0:T(8,128)(2,1)S(1)}, bf16[3,64,128]{2,1,0:T(8,128)(2,1)S(1)}, u32[]{:S(2)}, u32[]{:S(2)}) collective-permute-start(bf16[3,64,128]{2,1,0:T(8,128)(2,1)S(1)} %get-tuple-element.69), channel_id=1, source_target_pairs={{0,4},{4,0},{8,12},{12,8},{16,20},{20,16},{24,28},{28,24},{1,5},{5... | collective-permute-start | bytes 147464 | tf_op jit(solution)/shard_map/ppermute | solution.py:662
  14.8 8.3 %collective-permute-start.5 = (bf16[3,64,128]{2,1,0:T(8,128)(2,1)S(1)}, bf16[3,64,128]{2,1,0:T(8,128)(2,1)S(1)}, u32[]{:S(2)}, u32[]{:S(2)}) collective-permute-start(bf16[3,64,128]{2,1,0:T(8,128)(2,1)S(1)} %get-tuple-element.70), channel_id=1, source_target_pairs={{0,28},{4,8},{8,4},{12,16},{16,12},{20,24},{24,20},{28,0},{1,29},{... | collective-permute-start | bytes 147464 | tf_op jit(solution)/shard_map/ppermute | solution.py:670
  17.8 5.4 %collective-permute-start.6 = (bf16[3,32,128]{2,1,0:T(8,128)(2,1)S(1)}, bf16[3,32,128]{2,1,0:T(8,128)(2,1)S(1)}, u32[]{:S(2)}, u32[]{:S(2)}) collective-permute-start(bf16[3,32,128]{2,1,0:T(8,128)(2,1)S(1)} %get-tuple-element.71), channel_id=1, source_target_pairs={{0,1},{1,0},{2,3},{3,2},{4,5},{5,4},{6,7},{7,6},{8,9},{9,8},{10,11... | collective-permute-start | bytes 73736 | tf_op jit(solution)/shard_map/ppermute | solution.py:662
  24.2 4.5 %collective-permute-start.9 = (bf16[256,256]{1,0:T(8,128)(2,1)S(1)}, bf16[256,256]{1,0:T(8,128)(2,1)S(1)}, u32[]{:S(2)}, u32[]{:S(2)}) collective-permute-start(bf16[256,256]{1,0:T(8,128)(2,1)S(1)} %get-tuple-element.75.h1.h_own), channel_id=1, source_target_pairs={{0,3},{1,2},{2,1},{3,0},{4,7},{5,6},{6,5},{7,4},{8,11},{9,10},{10,... | collective-permute-start | bytes 393224 | tf_op jit(solution)/shard_map/ppermute | solution.py:662
  29.6 4.8 %collective-permute-start.11 = (bf16[256,256]{1,0:T(8,128)(2,1)S(1)}, bf16[256,256]{1,0:T(8,128)(2,1)S(1)}, u32[]{:S(2)}, u32[]{:S(2)}) collective-permute-start(bf16[256,256]{1,0:T(8,128)(2,1)S(1)} %get-tuple-element.77.dz2.d_own), channel_id=1, source_target_pairs={{0,3},{1,2},{2,1},{3,0},{4,7},{5,6},{6,5},{7,4},{8,11},{9,10},{10,... | collective-permute-start | bytes 393224 | tf_op jit(solution)/shard_map/ppermute | solution.py:662
  39.3 6.2 %collective-permute-start.13 = (bf16[64,1152]{1,0:T(8,128)(2,1)S(1)}, bf16[64,1152]{1,0:T(8,128)(2,1)S(1)}, u32[]{:S(2)}, u32[]{:S(2)}) collective-permute-start(bf16[64,1152]{1,0:T(8,128)(2,1)S(1)} %get-tuple-element.87), channel_id=1, source_target_pairs={{0,2},{1,3},{2,0},{3,1},{4,6},{5,7},{6,4},{7,5},{8,10},{9,11},{10,... | collective-permute-start | bytes 442376 | tf_op jit(solution)/shard_map/ppermute | solution.py:662
  42.9 6.0 %collective-permute-start.22 = (bf16[216,256]{1,0:T(8,128)(2,1)S(1)}, bf16[216,256]{1,0:T(8,128)(2,1)S(1)}, u32[]{:S(2)}, u32[]{:S(2)}) collective-permute-start(bf16[216,256]{1,0:T(8,128)(2,1)S(1)} %get-tuple-element.103), channel_id=1, source_target_pairs={{0,4},{4,0},{8,12},{12,8},{16,20},{20,16},{24,28},{28,24},{1,5},{5... | collective-permute-start | bytes 331784 | tf_op jit(solution)/shard_map/ppermute | solution.py:662
  43.6 11.4 %collective-permute-start.21 = (bf16[216,256]{1,0:T(8,128)(2,1)S(1)}, bf16[216,256]{1,0:T(8,128)(2,1)S(1)}, u32[]{:S(2)}, u32[]{:S(2)}) collective-permute-start(bf16[216,256]{1,0:T(8,128)(2,1)S(1)} %get-tuple-element.101), channel_id=1, source_target_pairs={{0,4},{4,0},{8,12},{12,8},{16,20},{20,16},{24,28},{28,24},{1,5},{5... | collective-permute-start | bytes 331784 | tf_op jit(solution)/shard_map/ppermute | solution.py:662
  45.6 7.4 %collective-permute-start.19 = (bf16[216,256]{1,0:T(8,128)(2,1)S(1)}, bf16[216,256]{1,0:T(8,128)(2,1)S(1)}, u32[]{:S(2)}, u32[]{:S(2)}) collective-permute-start(bf16[216,256]{1,0:T(8,128)(2,1)S(1)} %get-tuple-element.99), channel_id=1, source_target_pairs={{0,4},{4,0},{8,12},{12,8},{16,20},{20,16},{24,28},{28,24},{1,5},{5... | collective-permute-start | bytes 331784 | tf_op jit(solution)/shard_map/ppermute | solution.py:662
  46.3 5.1 %collective-permute-start.16 = (bf16[2,16,1152]{2,1,0:T(8,128)(2,1)S(1)}, bf16[2,16,1152]{2,1,0:T(8,128)(2,1)S(1)}, u32[]{:S(2)}, u32[]{:S(2)}) collective-permute-start(bf16[2,16,1152]{2,1,0:T(8,128)(2,1)S(1)} %get-tuple-element.91.refs_1_), channel_id=1, source_target_pairs={{0,8},{4,12},{8,0},{12,4},{16,24},{20,28},{24,16},{28,20},{1,9},{5... | collective-permute-start | bytes 221192 | tf_op jit(solution)/shard_map/ppermute | solution.py:662
  49.0 6.0 %collective-permute-start.23 = (bf16[216,256]{1,0:T(8,128)(2,1)S(1)}, bf16[216,256]{1,0:T(8,128)(2,1)S(1)}, u32[]{:S(2)}, u32[]{:S(2)}) collective-permute-start(bf16[216,256]{1,0:T(8,128)(2,1)S(1)} %shard_map.121), channel_id=1, source_target_pairs={{0,8},{4,12},{8,0},{12,4},{16,24},{20,28},{24,16},{28,20},{1,9},{5... | collective-permute-start | bytes 331784 | tf_op jit(solution)/shard_map/ppermute | solution.py:662
  51.4 5.8 %collective-permute-start.17 = (bf16[16,1152]{1,0:T(8,128)(2,1)S(1)}, bf16[16,1152]{1,0:T(8,128)(2,1)S(1)}, u32[]{:S(2)}, u32[]{:S(2)}) collective-permute-start(bf16[16,1152]{1,0:T(8,128)(2,1)S(1)} %get-tuple-element.93.refs_1_), channel_id=1, source_target_pairs={{0,16},{4,20},{8,24},{12,28},{16,0},{20,4},{24,8},{28,12},{1,17},{... | collective-permute-start | bytes 110600 | tf_op jit(solution)/shard_map/ppermute | solution.py:662
  52.7 9.0 %collective-permute-start.18 = (bf16[216,256]{1,0:T(8,128)(2,1)S(1)}, bf16[216,256]{1,0:T(8,128)(2,1)S(1)}, u32[]{:S(2)}, u32[]{:S(2)}) collective-permute-start(bf16[216,256]{1,0:T(8,128)(2,1)S(1)} %get-tuple-element.97), channel_id=1, source_target_pairs={{0,4},{4,0},{8,12},{12,8},{16,20},{20,16},{24,28},{28,24},{1,5},{5... | collective-permute-start | bytes 331784 | tf_op jit(solution)/shard_map/ppermute | solution.py:662
  53.0 9.0 %collective-permute-start.20 = (bf16[216,256]{1,0:T(8,128)(2,1)S(1)}, bf16[216,256]{1,0:T(8,128)(2,1)S(1)}, u32[]{:S(2)}, u32[]{:S(2)}) collective-permute-start(bf16[216,256]{1,0:T(8,128)(2,1)S(1)} %shard_map.120.refs_2_), channel_id=1, source_target_pairs={{0,8},{4,12},{8,0},{12,4},{16,24},{20,28},{24,16},{28,20},{1,9},{5... | collective-permute-start | bytes 331784 | tf_op jit(solution)/shard_map/ppermute | solution.py:662
  55.1 6.9 %collective-permute-start.24 = (bf16[216,256]{1,0:T(8,128)(2,1)S(1)}, bf16[216,256]{1,0:T(8,128)(2,1)S(1)}, u32[]{:S(2)}, u32[]{:S(2)}) collective-permute-start(bf16[216,256]{1,0:T(8,128)(2,1)S(1)} %shard_map.122), channel_id=1, source_target_pairs={{0,16},{4,20},{8,24},{12,28},{16,0},{20,4},{24,8},{28,12},{1,17},{... | collective-permute-start | bytes 331784 | tf_op jit(solution)/shard_map/ppermute | solution.py:662
  62.0 6.9 %collective-permute-start.30 = (bf16[256,256]{1,0:T(8,128)(2,1)S(1)}, bf16[256,256]{1,0:T(8,128)(2,1)S(1)}, u32[]{:S(2)}, u32[]{:S(2)}) collective-permute-start(bf16[256,256]{1,0:T(8,128)(2,1)S(1)} %shard_map.123.refs_0_), channel_id=1, source_target_pairs={{0,8},{4,12},{8,0},{12,4},{16,24},{20,28},{24,16},{28,20},{1,9},{5... | collective-permute-start | bytes 393224 | tf_op jit(solution)/shard_map/ppermute | solution.py:662
  62.3 10.3 %collective-permute-start.28 = (bf16[256,256]{1,0:T(8,128)(2,1)S(1)}, bf16[256,256]{1,0:T(8,128)(2,1)S(1)}, u32[]{:S(2)}, u32[]{:S(2)}) collective-permute-start(bf16[256,256]{1,0:T(8,128)(2,1)S(1)} %shard_map.123.refs_0_), channel_id=1, source_target_pairs={{0,16},{4,20},{8,24},{12,28},{16,0},{20,4},{24,8},{28,12},{1,17},{... | collective-permute-start | bytes 393224 | tf_op jit(solution)/shard_map/ppermute | solution.py:662
  65.2 8.7 %collective-permute-start.26 = (bf16[256,256]{1,0:T(8,128)(2,1)S(1)}, bf16[256,256]{1,0:T(8,128)(2,1)S(1)}, u32[]{:S(2)}, u32[]{:S(2)}) collective-permute-start(bf16[256,256]{1,0:T(8,128)(2,1)S(1)} %shard_map.123.refs_0_), channel_id=1, source_target_pairs={{0,24},{4,28},{8,16},{12,20},{16,8},{20,12},{24,0},{28,4},{1,25},{... | collective-permute-start | bytes 393224 | tf_op jit(solution)/shard_map/ppermute | solution.py:662
  66.5 8.1 %collective-permute-start.32 = (bf16[256,256]{1,0:T(8,128)(2,1)S(1)}, bf16[256,256]{1,0:T(8,128)(2,1)S(1)}, u32[]{:S(2)}, u32[]{:S(2)}) collective-permute-start(bf16[256,256]{1,0:T(8,128)(2,1)S(1)} %shard_map.123.refs_0_), channel_id=1, source_target_pairs={{0,4},{4,0},{8,12},{12,8},{16,20},{20,16},{24,28},{28,24},{1,5},{5... | collective-permute-start | bytes 393224 | tf_op jit(solution)/shard_map/ppermute | solution.py:662
  68.9 6.6 %collective-permute-start.31 = (bf16[256,256]{1,0:T(8,128)(2,1)S(1)}, bf16[256,256]{1,0:T(8,128)(2,1)S(1)}, u32[]{:S(2)}, u32[]{:S(2)}) collective-permute-start(bf16[256,256]{1,0:T(8,128)(2,1)S(1)} %collective-permute-done.30.refs_0_), channel_id=1, source_target_pairs={{0,4},{4,0},{8,12},{12,8},{16,20},{20,16},{24,28},{28,24},{1,5},{5... | collective-permute-start | bytes 393224 | tf_op jit(solution)/shard_map/ppermute | solution.py:662
  72.6 5.0 %collective-permute-start.29 = (bf16[256,256]{1,0:T(8,128)(2,1)S(1)}, bf16[256,256]{1,0:T(8,128)(2,1)S(1)}, u32[]{:S(2)}, u32[]{:S(2)}) collective-permute-start(bf16[256,256]{1,0:T(8,128)(2,1)S(1)} %collective-permute-done.28.refs_0_), channel_id=1, source_target_pairs={{0,4},{4,0},{8,12},{12,8},{16,20},{20,16},{24,28},{28,24},{1,5},{5... | collective-permute-start | bytes 393224 | tf_op jit(solution)/shard_map/ppermute | solution.py:662
  73.9 5.1 %collective-permute-start.27 = (bf16[256,256]{1,0:T(8,128)(2,1)S(1)}, bf16[256,256]{1,0:T(8,128)(2,1)S(1)}, u32[]{:S(2)}, u32[]{:S(2)}) collective-permute-start(bf16[256,256]{1,0:T(8,128)(2,1)S(1)} %collective-permute-done.26.refs_0_), channel_id=1, source_target_pairs={{0,4},{4,0},{8,12},{12,8},{16,20},{20,16},{24,28},{28,24},{1,5},{5... | collective-permute-start | bytes 393224 | tf_op jit(solution)/shard_map/ppermute | solution.py:662
  (16 other events, 53.9 us)

commit v7 on v6

--- a/solution.py
+++ b/solution.py
@@ -499,27 +499,26 @@
     crop = ez // groups
     place = lax.axis_index("grp")
     layer = EY * ez
-    lane = lax.broadcasted_iota(jnp.int32, (channels, channels), 1)
-    channel = lax.broadcasted_iota(jnp.int32, (channels, channels), 0)
-    chosen = jnp.where(
-        (channel == place * quarter + lax.rem(lane, quarter)) & (lane < 3 * quarter), 1.0, 0.0
-    ).astype(BF16)
+    taken = 3 * quarter
+    slot = lax.broadcasted_iota(jnp.int32, (taken, channels), 0)
+    channel = lax.broadcasted_iota(jnp.int32, (taken, channels), 1)
+    chosen = jnp.where(channel == place * quarter + lax.rem(slot, quarter), 1.0, 0.0).astype(BF16)
     pairs = ((h_own, d_own), (h_one, d_one), (h_two, d_two), (h_three, d_three))
     for k, (h, d) in enumerate(pairs):
         at = jnp.bitwise_xor(place, k)
-        mine = dot(d[...], chosen)
+        mine = dot_nt(chosen, d[...])
         for x in range(EX):
             h_all[x, at] = h[x * layer : (x + 1) * layer]
-            r_all[x, at] = mine[x * layer : (x + 1) * layer]
+            r_all[x, at] = mine[:, x * layer : (x + 1) * layer]
     deep = groups * layer
-    flat = r_all[...].reshape(EX * deep, channels)
-    spot = lax.rem(lax.broadcasted_iota(jnp.int32, (EX * deep, 1), 0), crop)
-    lane = lax.broadcasted_iota(jnp.int32, (1, channels), 1)
-    after = jnp.where(spot == crop - 1, 0.0, pltpu.roll(flat, EX * deep - 1, 0))
-    before = jnp.where(spot == 0, 0.0, pltpu.roll(flat, 1, 0))
-    mixed = jnp.where(lane < quarter, after, jnp.where(lane < 2 * quarter, flat, before))
-    turned = mixed.T
-    spot = lax.rem(lax.broadcasted_iota(jnp.int32, (1, EX * deep), 1), deep)
+    turned = jnp.concatenate([r_all[x, g] for x in range(EX) for g in range(groups)], axis=1)
+    spot = lax.broadcasted_iota(jnp.int32, (1, EX * deep), 1)
+    after = pltpu.roll(turned[:quarter], EX * deep - 1, 1)
+    after = jnp.where(lax.rem(spot, crop) == crop - 1, 0.0, after)
+    before = pltpu.roll(turned[2 * quarter :], 1, 1)
+    before = jnp.where(lax.rem(spot, crop) == 0, 0.0, before)
+    turned = jnp.concatenate([after, turned[quarter : 2 * quarter], before], axis=0)
+    spot = lax.rem(spot, deep)
     up = jnp.where(spot >= deep - ez, 0.0, pltpu.roll(turned, EX * deep - ez, 1))
     down = jnp.where(spot < ez, 0.0, pltpu.roll(turned, ez, 1))
     whole = h_all[...].reshape(EX * deep, channels)
@@ -533,7 +532,7 @@
             else:
                 got = dot(side[:, :deep], whole[deep:])
             start = (9 * dx + 3 * dy) * quarter
-            out[start : start + 3 * quarter] = got[: 3 * quarter]
+            out[start : start + taken] = got
     me = lax.rem(lax.axis_index("sim"), sims)
     piece_rows = 27 * quarter // sims
     for k, piece in enumerate(refs[:-3]):
@@ -542,8 +541,8 @@
 
 
 def dense_kernel(kept, got, *refs):
-    out_kept, out_sent = refs[-4:-2]
-    for source, target in zip(refs[:2], refs[-2:]):
+    out_kept, out_sent = refs[-3:-1]
+    for source, target in zip(refs[:1], refs[-1:]):
         target[...] = source[...]
     total = kept[...] + got[...].astype(F32)
     grid = total.reshape(2, 2, kept.shape[0] // 4, kept.shape[1])
@@ -616,24 +615,25 @@
 
 def placed_shares(shares, shapes, count):
     outs = ()
-    for first in range(0, count, 2):
-        masks = (first, first + 1)
+    groups = [(first, first + 1) for first in range(0, count - 4, 2)]
+    for masks in groups + [(count - 4, count - 3, count - 2), (count - 1,)]:
         tap_rows, own_rows = [shape.shape[0] // count for shape in shapes[:2]]
         sizes = (tap_rows, own_rows, own_rows)
         held = [
-            pltpu.VMEM((2, size, shape.shape[1]), F32) for size, shape in zip(sizes, shapes)
+            pltpu.VMEM((len(masks), size, shape.shape[1]), F32)
+            for size, shape in zip(sizes, shapes)
         ]
         anywhere = pl.BlockSpec(memory_space=pl.ANY)
         outs = pl.pallas_call(
             functools.partial(place_kernel, masks, count),
             out_shape=shapes,
-            in_specs=[pl.BlockSpec(memory_space=pltpu.VMEM)] * 2 + [anywhere] * len(outs),
+            in_specs=[pl.BlockSpec(memory_space=pltpu.VMEM)] * len(masks) + [anywhere] * len(outs),
             out_specs=(anywhere,) * 3,
-            scratch_shapes=held + [pltpu.SemaphoreType.DMA((2, 3))],
-            input_output_aliases={2 + i: i for i in range(len(outs))},
+            scratch_shapes=held + [pltpu.SemaphoreType.DMA((len(masks), 3))],
+            input_output_aliases={len(masks) + i: i for i in range(len(outs))},
             compiler_params=pltpu.CompilerParams(vmem_limit_bytes=VMEM_LIMIT),
             cost_estimate=pl.CostEstimate(flops=1000, bytes_accessed=1000, transcendentals=0),
-        )(shares[first], shares[first + 1], *outs)
+        )(*[shares[mask] for mask in masks], *outs)
     return outs
 
 
@@ -776,7 +776,7 @@
         (
             pltpu.VMEM((27 * quarter, channels), F32),
             pltpu.VMEM((EX, groups, EY * ez, channels), BF16),
-            pltpu.VMEM((EX, groups, EY * ez, channels), F32),
+            pltpu.VMEM((EX, groups, 3 * quarter, EY * ez), F32),
         ),
         in_hbm=(8,),
         inputs=9,
@@ -786,11 +786,11 @@
         tap_piece = shaped((tap_rows, channels), BF16)
         part = (2, 2 * own_rows, wide)
         e_kept, e_sent, *later = call(
-            dense_kernel, (shaped(part, F32), shaped(part, BF16)) + (tap_piece,) * 2
-        )(e_kept, e_got, taps[3], taps[1])
+            dense_kernel, (shaped(part, F32), shaped(part, BF16)) + (tap_piece,)
+        )(e_kept, e_got, taps[1])
         e_got = swapped(e_sent, "sim", 2)
-        taps_in = {k: swapped(taps[k + 1], "sim", 1) for k in (6, 4)}
-        taps_in.update((k, swapped(piece, "sim", 1)) for k, piece in zip((2, 0), later))
+        taps_in = {k: swapped(taps[k + 1], "sim", 1) for k in (6, 4, 2)}
+        taps_in.update((k, swapped(piece, "sim", 1)) for k, piece in zip((0,), later))
         add_two = call(functools.partial(sum_kernel, 2), tap_piece)
         add_three = call(functools.partial(sum_kernel, 3), tap_piece)
         six = swapped(add_two(taps[6], taps_in[6], e_sent), "sim", 2)

time: 80.2 us -> 79.4 us (0.990)
  starting transfers between devices: 46.6 us -> 44.4 us
  waiting for transfers between devices: 10.4 us -> 12.3 us
    ppermute x29, starting transfers between devices: 38.6 us -> 36.4 us  [swapped(): return lax.ppermute(value, axis, [(i, i ^ mask) for i in range(count)])]
    ppermute x29, waiting for transfers between devices: 10.4 us -> 12.3 us  [swapped(): return lax.ppermute(value, axis, [(i, i ^ mask) for i in range(count)])]
  transfers between devices with their start and end apart: 33 -> 33, of which waited for: 11 -> 13; matrix products, arithmetic and copies ran while one was open for 0% -> 0% of each run, Pallas kernels for 17% -> 17%
where the time goes in v7:
time: 79.4 us; the launch traced here: 79.2 us
  starting transfers between devices  44.4 us (56%)
  Pallas kernels  19.4 us (24%)
  waiting for transfers between devices  12.3 us (15%)
  local copies, waits for them, and re-layouts  1.98 us (2%)
  between operations  1.13 us (1%)
    ppermute x29, starting transfers between devices, swapped(): return lax.ppermute(value, axis, [(i, i ^ mask) for i in range(count)])  36.4 us
    ppermute x29, waiting for transfers between devices, swapped(): return lax.ppermute(value, axis, [(i, i ^ mask) for i in range(count)])  12.3 us
    ppermute x4, starting transfers between devices, crossed(): lax.ppermute(value, axis, [(i, j) for i, j in route if 0 <= j < count])  7.97 us
    pallas_call x2, Pallas kernels, body(): part = call(inside_kernel, whole)(field, stencil)  6.41 us
    pallas_call x4, Pallas kernels, placed_shares(): pl.pallas_call(functools.partial(place_kernel, masks, count), out_shape=s...  3.38 us
    unnamed x14, local copies, waits for them, and re-layouts  1.98 us
    pallas_call x1, Pallas kernels, body(): velocity_next, done = restore(field, back, e_sent)  1.97 us
  transfers between devices with their start and end apart: 33, of which 13 were waited for; matrix products, arithmetic and copies ran while one was open for 0% of the time, Pallas kernels for 17%

profile of v7, /device:TPU:0, one launch (start us, length us, event | category | flops | bytes accessed | tf_op | source)
XLA Modules:
  0.0 79.2 jit_solution(17058933277263383248)
XLA Ops:
  3.8 3.0 %collective-permute-start = (bf16[3,64,128]{2,1,0:T(8,128)(2,1)S(1)}, bf16[3,64,128]{2,1,0:T(8,128)(2,1)S(1)}, u32[]{:S(2)}, u32[]{:S(2)}) collective-permute-start(bf16[3,64,128]{2,1,0:T(8,128)(2,1)S(1)} %get-tuple-element.63), channel_id=1, source_target_pairs={{0,4},{4,0},{8,12},{12,8},{16,20},{20,16},{24,28},{28,24},{1,5},{5... | collective-permute-start | bytes 147464 | tf_op jit(solution)/shard_map/ppermute | solution.py:662
  6.8 3.6 %collective-permute-start.1 = (bf16[3,64,128]{2,1,0:T(8,128)(2,1)S(1)}, bf16[3,64,128]{2,1,0:T(8,128)(2,1)S(1)}, u32[]{:S(2)}, u32[]{:S(2)}) collective-permute-start(bf16[3,64,128]{2,1,0:T(8,128)(2,1)S(1)} %get-tuple-element.64), channel_id=1, source_target_pairs={{0,28},{4,8},{8,4},{12,16},{16,12},{20,24},{24,20},{28,0},{1,29},{... | collective-permute-start | bytes 147464 | tf_op jit(solution)/shard_map/ppermute | solution.py:670
  11.0 3.2 %shard_map.104.part = f32[3,256,512]{2,1,0:T(8,128)S(1)} custom-call(f32[3,256,512]{2,1,0:T(8,128)S(1)} %get-tuple-element.62.field, bf16[2560,512]{1,0:T(8,128)(2,1)S(1)} %copy-done.1), custom_call_target="tpu_custom_call" | custom-call | flops 1000 | bytes 1000 | tf_op jit(solution)/shard_map/pallas_call | solution.py:721
  14.8 2.9 %collective-permute-start.5 = (bf16[3,64,128]{2,1,0:T(8,128)(2,1)S(1)}, bf16[3,64,128]{2,1,0:T(8,128)(2,1)S(1)}, u32[]{:S(2)}, u32[]{:S(2)}) collective-permute-start(bf16[3,64,128]{2,1,0:T(8,128)(2,1)S(1)} %get-tuple-element.69), channel_id=1, source_target_pairs={{0,28},{4,8},{8,4},{12,16},{16,12},{20,24},{24,20},{28,0},{1,29},{... | collective-permute-start | bytes 147464 | tf_op jit(solution)/shard_map/ppermute | solution.py:670
  17.8 1.3 %collective-permute-start.6 = (bf16[3,32,128]{2,1,0:T(8,128)(2,1)S(1)}, bf16[3,32,128]{2,1,0:T(8,128)(2,1)S(1)}, u32[]{:S(2)}, u32[]{:S(2)}) collective-permute-start(bf16[3,32,128]{2,1,0:T(8,128)(2,1)S(1)} %get-tuple-element.70), channel_id=1, source_target_pairs={{0,1},{1,0},{2,3},{3,2},{4,5},{5,4},{6,7},{7,6},{8,9},{9,8},{10,11... | collective-permute-start | bytes 73736 | tf_op jit(solution)/shard_map/ppermute | solution.py:662
  19.9 3.2 %shard_map.106.part = f32[3,256,512]{2,1,0:T(8,128)S(1)} custom-call(f32[3,256,512]{2,1,0:T(8,128)S(1)} %get-tuple-element.67.field, bf16[2560,512]{1,0:T(8,128)(2,1)S(1)} %copy-done.1), custom_call_target="tpu_custom_call" | custom-call | flops 1000 | bytes 1000 | tf_op jit(solution)/shard_map/pallas_call | solution.py:724
  25.5 1.8 %collective-permute-start.8 = (bf16[256,256]{1,0:T(8,128)(2,1)S(1)}, bf16[256,256]{1,0:T(8,128)(2,1)S(1)}, u32[]{:S(2)}, u32[]{:S(2)}) collective-permute-start(bf16[256,256]{1,0:T(8,128)(2,1)S(1)} %get-tuple-element.74.h1.h_own), channel_id=1, source_target_pairs={{0,1},{1,0},{2,3},{3,2},{4,5},{5,4},{6,7},{7,6},{8,9},{9,8},{10,11... | collective-permute-start | bytes 393224 | tf_op jit(solution)/shard_map/ppermute | solution.py:662
  29.6 1.8 %collective-permute-start.11 = (bf16[256,256]{1,0:T(8,128)(2,1)S(1)}, bf16[256,256]{1,0:T(8,128)(2,1)S(1)}, u32[]{:S(2)}, u32[]{:S(2)}) collective-permute-start(bf16[256,256]{1,0:T(8,128)(2,1)S(1)} %get-tuple-element.76.dz2.d_own), channel_id=1, source_target_pairs={{0,3},{1,2},{2,1},{3,0},{4,7},{5,6},{6,5},{7,4},{8,11},{9,10},{10,... | collective-permute-start | bytes 393224 | tf_op jit(solution)/shard_map/ppermute | solution.py:662
  31.4 1.5 %collective-permute-start.10 = (bf16[256,256]{1,0:T(8,128)(2,1)S(1)}, bf16[256,256]{1,0:T(8,128)(2,1)S(1)}, u32[]{:S(2)}, u32[]{:S(2)}) collective-permute-start(bf16[256,256]{1,0:T(8,128)(2,1)S(1)} %get-tuple-element.76.dz2.d_own), channel_id=1, source_target_pairs={{0,1},{1,0},{2,3},{3,2},{4,5},{5,4},{6,7},{7,6},{8,9},{9,8},{10,11... | collective-permute-start | bytes 393224 | tf_op jit(solution)/shard_map/ppermute | solution.py:662
  34.5 1.5 %shard_map.113 = (f32[2,64,1152]{2,1,0:T(8,128)S(1)}, bf16[2,64,1152]{2,1,0:T(8,128)(2,1)S(1)}) custom-call(f32[256,256]{1,0:T(8,128)S(1)} %get-tuple-element.79.dh1, f32[256,128]{1,0:T(8,128)S(1)} %get-tuple-element.80.head, bf16[256,256]{1,0:T(8,128)(2,1)S(1)} %get-tuple-element.76.dz2.d_own, bf16[256,256]{1,0:T(8,128)(2,1)S(1)} %collective-permute-done.10.pair.d_one, ...), custom_call_target="tpu_custom_call" | custom-call | flops 1000 | bytes 1000 | tf_op jit(solution)/shard_map/pallas_call | solution.py:758
  36.0 2.1 %collective-permute-start.12 = (bf16[2,64,1152]{2,1,0:T(8,128)(2,1)S(1)}, bf16[2,64,1152]{2,1,0:T(8,128)(2,1)S(1)}, u32[]{:S(2)}, u32[]{:S(2)}) collective-permute-start(bf16[2,64,1152]{2,1,0:T(8,128)(2,1)S(1)} %get-tuple-element.84), channel_id=1, source_target_pairs={{0,1},{1,0},{2,3},{3,2},{4,5},{5,4},{6,7},{7,6},{8,9},{9,8},{10,11... | collective-permute-start | bytes 884744 | tf_op jit(solution)/shard_map/ppermute | solution.py:662
  39.3 1.7 %collective-permute-start.13 = (bf16[64,1152]{1,0:T(8,128)(2,1)S(1)}, bf16[64,1152]{1,0:T(8,128)(2,1)S(1)}, u32[]{:S(2)}, u32[]{:S(2)}) collective-permute-start(bf16[64,1152]{1,0:T(8,128)(2,1)S(1)} %get-tuple-element.86), channel_id=1, source_target_pairs={{0,2},{1,3},{2,0},{3,1},{4,6},{5,7},{6,4},{7,5},{8,10},{9,11},{10,... | collective-permute-start | bytes 442376 | tf_op jit(solution)/shard_map/ppermute | solution.py:662
  41.1 1.4 %shard_map.115 = (f32[216,256]{1,0:T(8,128)S(1)}, bf16[216,256]{1,0:T(8,128)(2,1)S(1)}, f32[216,256]{1,0:T(8,128)S(1)}, bf16[216,256]{1,0:T(8,128)(2,1)S(1)}, f3...) custom-call(bf16[256,256]{1,0:T(8,128)(2,1)S(1)} %get-tuple-element., ...), custom_call_target="tpu_custom_call" | custom-call | flops 1000 | bytes 1000 | tf_op jit(solution)/shard_map/pallas_call | solution.py:773
  43.1 1.4 %collective-permute-start.19 = (bf16[216,256]{1,0:T(8,128)(2,1)S(1)}, bf16[216,256]{1,0:T(8,128)(2,1)S(1)}, u32[]{:S(2)}, u32[]{:S(2)}) collective-permute-start(bf16[216,256]{1,0:T(8,128)(2,1)S(1)} %get-tuple-element.97), channel_id=1, source_target_pairs={{0,4},{4,0},{8,12},{12,8},{16,20},{20,16},{24,28},{28,24},{1,5},{5... | collective-permute-start | bytes 331784 | tf_op jit(solution)/shard_map/ppermute | solution.py:662
  45.6 1.6 %collective-permute-start.16 = (bf16[2,16,1152]{2,1,0:T(8,128)(2,1)S(1)}, bf16[2,16,1152]{2,1,0:T(8,128)(2,1)S(1)}, u32[]{:S(2)}, u32[]{:S(2)}) collective-permute-start(bf16[2,16,1152]{2,1,0:T(8,128)(2,1)S(1)} %get-tuple-element.89.refs_1_), channel_id=1, source_target_pairs={{0,8},{4,12},{8,0},{12,4},{16,24},{20,28},{24,16},{28,20},{1,9},{5... | collective-permute-start | bytes 221192 | tf_op jit(solution)/shard_map/ppermute | solution.py:662
  48.5 1.7 %collective-permute-start.23 = (bf16[216,256]{1,0:T(8,128)(2,1)S(1)}, bf16[216,256]{1,0:T(8,128)(2,1)S(1)}, u32[]{:S(2)}, u32[]{:S(2)}) collective-permute-start(bf16[216,256]{1,0:T(8,128)(2,1)S(1)} %shard_map.121), channel_id=1, source_target_pairs={{0,8},{4,12},{8,0},{12,4},{16,24},{20,28},{24,16},{28,20},{1,9},{5... | collective-permute-start | bytes 331784 | tf_op jit(solution)/shard_map/ppermute | solution.py:662
  52.6 2.2 %collective-permute-start.20 = (bf16[216,256]{1,0:T(8,128)(2,1)S(1)}, bf16[216,256]{1,0:T(8,128)(2,1)S(1)}, u32[]{:S(2)}, u32[]{:S(2)}) collective-permute-start(bf16[216,256]{1,0:T(8,128)(2,1)S(1)} %shard_map.120.refs_2_), channel_id=1, source_target_pairs={{0,8},{4,12},{8,0},{12,4},{16,24},{20,28},{24,16},{28,20},{1,9},{5... | collective-permute-start | bytes 331784 | tf_op jit(solution)/shard_map/ppermute | solution.py:662
  54.8 1.6 %collective-permute-start.24 = (bf16[216,256]{1,0:T(8,128)(2,1)S(1)}, bf16[216,256]{1,0:T(8,128)(2,1)S(1)}, u32[]{:S(2)}, u32[]{:S(2)}) collective-permute-start(bf16[216,256]{1,0:T(8,128)(2,1)S(1)} %shard_map.122), channel_id=1, source_target_pairs={{0,16},{4,20},{8,24},{12,28},{16,0},{20,4},{24,8},{28,12},{1,17},{... | collective-permute-start | bytes 331784 | tf_op jit(solution)/shard_map/ppermute | solution.py:662
  57.5 1.3 %collective-permute-start.25 = (bf16[8,1152]{1,0:T(8,128)(2,1)S(1)}, bf16[8,1152]{1,0:T(8,128)(2,1)S(1)}, u32[]{:S(2)}, u32[]{:S(2)}) collective-permute-start(bf16[8,1152]{1,0:T(8,128)(2,1)S(1)} %get-tuple-element.92.after_this), channel_id=1, source_target_pairs={{0,4},{4,0},{8,12},{12,8},{16,20},{20,16},{24,28},{28,24},{1,5},{5... | collective-permute-start | bytes 55304 | tf_op jit(solution)/shard_map/ppermute | solution.py:662
  58.9 2.0 %shard_map.119 = (f32[3,256,512]{2,1,0:T(8,128)}, f32[8,128]{1,0:T(8,128)S(1)}) custom-call(f32[3,256,512]{2,1,0:T(8,128)S(1)} %get-tuple-element.72.field, bf16[256,256]{1,0:T(8,128)(2,1)S(1)} %get-tuple-element.73.back, bf16[8,1152]{1,0:T(8,128)(2,1)S(1)} %get-tuple-element.92.after_this), custom_call_target="tpu_custom_call" | custom-call | flops 1000 | bytes 1000 | tf_op jit(solution)/shard_map/pallas_call | solution.py:807
  61.7 2.3 %collective-permute-start.28 = (bf16[256,256]{1,0:T(8,128)(2,1)S(1)}, bf16[256,256]{1,0:T(8,128)(2,1)S(1)}, u32[]{:S(2)}, u32[]{:S(2)}) collective-permute-start(bf16[256,256]{1,0:T(8,128)(2,1)S(1)} %shard_map.123.refs_0_), channel_id=1, source_target_pairs={{0,16},{4,20},{8,24},{12,28},{16,0},{20,4},{24,8},{28,12},{1,17},{... | collective-permute-start | bytes 393224 | tf_op jit(solution)/shard_map/ppermute | solution.py:662
  64.1 1.9 %collective-permute-start.26 = (bf16[256,256]{1,0:T(8,128)(2,1)S(1)}, bf16[256,256]{1,0:T(8,128)(2,1)S(1)}, u32[]{:S(2)}, u32[]{:S(2)}) collective-permute-start(bf16[256,256]{1,0:T(8,128)(2,1)S(1)} %shard_map.123.refs_0_), channel_id=1, source_target_pairs={{0,24},{4,28},{8,16},{12,20},{16,8},{20,12},{24,0},{28,4},{1,25},{... | collective-permute-start | bytes 393224 | tf_op jit(solution)/shard_map/ppermute | solution.py:662
  69.1 2.8 %collective-permute-done.28.refs_0_ = bf16[256,256]{1,0:T(8,128)(2,1)S(1)} collective-permute-done((bf16[256,256]{1,0:T(8,128)(2,1)S(1)}, bf16[256,256]{1,0:T(8,128)(2,1)S(1)}, u32[]{:S(2)}, u32[]{:S(2)}) %collective-permute-start.28) | collective-permute-done | bytes 131104 | tf_op jit(solution)/shard_map/ppermute | solution.py:662
  72.6 1.4 %collective-permute-start.27 = (bf16[256,256]{1,0:T(8,128)(2,1)S(1)}, bf16[256,256]{1,0:T(8,128)(2,1)S(1)}, u32[]{:S(2)}, u32[]{:S(2)}) collective-permute-start(bf16[256,256]{1,0:T(8,128)(2,1)S(1)} %collective-permute-done.26.refs_2_), channel_id=1, source_target_pairs={{0,4},{4,0},{8,12},{12,8},{16,20},{20,16},{24,28},{28,24},{1,5},{5... | collective-permute-start | bytes 393224 | tf_op jit(solution)/shard_map/ppermute | solution.py:662
  (82 shorter events, 28.9 us)
Async XLA Ops:
  3.8 10.5 %collective-permute-start = (bf16[3,64,128]{2,1,0:T(8,128)(2,1)S(1)}, bf16[3,64,128]{2,1,0:T(8,128)(2,1)S(1)}, u32[]{:S(2)}, u32[]{:S(2)}) collective-permute-start(bf16[3,64,128]{2,1,0:T(8,128)(2,1)S(1)} %get-tuple-element.63), channel_id=1, source_target_pairs={{0,4},{4,0},{8,12},{12,8},{16,20},{20,16},{24,28},{28,24},{1,5},{5... | collective-permute-start | bytes 147464 | tf_op jit(solution)/shard_map/ppermute | solution.py:662
  6.8 7.5 %collective-permute-start.1 = (bf16[3,64,128]{2,1,0:T(8,128)(2,1)S(1)}, bf16[3,64,128]{2,1,0:T(8,128)(2,1)S(1)}, u32[]{:S(2)}, u32[]{:S(2)}) collective-permute-start(bf16[3,64,128]{2,1,0:T(8,128)(2,1)S(1)} %get-tuple-element.64), channel_id=1, source_target_pairs={{0,28},{4,8},{8,4},{12,16},{16,12},{20,24},{24,20},{28,0},{1,29},{... | collective-permute-start | bytes 147464 | tf_op jit(solution)/shard_map/ppermute | solution.py:670
  14.8 8.4 %collective-permute-start.4 = (bf16[3,64,128]{2,1,0:T(8,128)(2,1)S(1)}, bf16[3,64,128]{2,1,0:T(8,128)(2,1)S(1)}, u32[]{:S(2)}, u32[]{:S(2)}) collective-permute-start(bf16[3,64,128]{2,1,0:T(8,128)(2,1)S(1)} %get-tuple-element.68), channel_id=1, source_target_pairs={{0,4},{4,0},{8,12},{12,8},{16,20},{20,16},{24,28},{28,24},{1,5},{5... | collective-permute-start | bytes 147464 | tf_op jit(solution)/shard_map/ppermute | solution.py:662
  14.8 8.3 %collective-permute-start.5 = (bf16[3,64,128]{2,1,0:T(8,128)(2,1)S(1)}, bf16[3,64,128]{2,1,0:T(8,128)(2,1)S(1)}, u32[]{:S(2)}, u32[]{:S(2)}) collective-permute-start(bf16[3,64,128]{2,1,0:T(8,128)(2,1)S(1)} %get-tuple-element.69), channel_id=1, source_target_pairs={{0,28},{4,8},{8,4},{12,16},{16,12},{20,24},{24,20},{28,0},{1,29},{... | collective-permute-start | bytes 147464 | tf_op jit(solution)/shard_map/ppermute | solution.py:670
  17.8 5.4 %collective-permute-start.6 = (bf16[3,32,128]{2,1,0:T(8,128)(2,1)S(1)}, bf16[3,32,128]{2,1,0:T(8,128)(2,1)S(1)}, u32[]{:S(2)}, u32[]{:S(2)}) collective-permute-start(bf16[3,32,128]{2,1,0:T(8,128)(2,1)S(1)} %get-tuple-element.70), channel_id=1, source_target_pairs={{0,1},{1,0},{2,3},{3,2},{4,5},{5,4},{6,7},{7,6},{8,9},{9,8},{10,11... | collective-permute-start | bytes 73736 | tf_op jit(solution)/shard_map/ppermute | solution.py:662
  24.2 4.5 %collective-permute-start.9 = (bf16[256,256]{1,0:T(8,128)(2,1)S(1)}, bf16[256,256]{1,0:T(8,128)(2,1)S(1)}, u32[]{:S(2)}, u32[]{:S(2)}) collective-permute-start(bf16[256,256]{1,0:T(8,128)(2,1)S(1)} %get-tuple-element.74.h1.h_own), channel_id=1, source_target_pairs={{0,3},{1,2},{2,1},{3,0},{4,7},{5,6},{6,5},{7,4},{8,11},{9,10},{10,... | collective-permute-start | bytes 393224 | tf_op jit(solution)/shard_map/ppermute | solution.py:662
  29.6 4.8 %collective-permute-start.11 = (bf16[256,256]{1,0:T(8,128)(2,1)S(1)}, bf16[256,256]{1,0:T(8,128)(2,1)S(1)}, u32[]{:S(2)}, u32[]{:S(2)}) collective-permute-start(bf16[256,256]{1,0:T(8,128)(2,1)S(1)} %get-tuple-element.76.dz2.d_own), channel_id=1, source_target_pairs={{0,3},{1,2},{2,1},{3,0},{4,7},{5,6},{6,5},{7,4},{8,11},{9,10},{10,... | collective-permute-start | bytes 393224 | tf_op jit(solution)/shard_map/ppermute | solution.py:662
  39.3 6.2 %collective-permute-start.13 = (bf16[64,1152]{1,0:T(8,128)(2,1)S(1)}, bf16[64,1152]{1,0:T(8,128)(2,1)S(1)}, u32[]{:S(2)}, u32[]{:S(2)}) collective-permute-start(bf16[64,1152]{1,0:T(8,128)(2,1)S(1)} %get-tuple-element.86), channel_id=1, source_target_pairs={{0,2},{1,3},{2,0},{3,1},{4,6},{5,7},{6,4},{7,5},{8,10},{9,11},{10,... | collective-permute-start | bytes 442376 | tf_op jit(solution)/shard_map/ppermute | solution.py:662
  42.4 6.0 %collective-permute-start.22 = (bf16[216,256]{1,0:T(8,128)(2,1)S(1)}, bf16[216,256]{1,0:T(8,128)(2,1)S(1)}, u32[]{:S(2)}, u32[]{:S(2)}) collective-permute-start(bf16[216,256]{1,0:T(8,128)(2,1)S(1)} %get-tuple-element.101), channel_id=1, source_target_pairs={{0,4},{4,0},{8,12},{12,8},{16,20},{20,16},{24,28},{28,24},{1,5},{5... | collective-permute-start | bytes 331784 | tf_op jit(solution)/shard_map/ppermute | solution.py:662
  43.1 9.4 %collective-permute-start.19 = (bf16[216,256]{1,0:T(8,128)(2,1)S(1)}, bf16[216,256]{1,0:T(8,128)(2,1)S(1)}, u32[]{:S(2)}, u32[]{:S(2)}) collective-permute-start(bf16[216,256]{1,0:T(8,128)(2,1)S(1)} %get-tuple-element.97), channel_id=1, source_target_pairs={{0,4},{4,0},{8,12},{12,8},{16,20},{20,16},{24,28},{28,24},{1,5},{5... | collective-permute-start | bytes 331784 | tf_op jit(solution)/shard_map/ppermute | solution.py:662
  44.5 10.2 %collective-permute-start.21 = (bf16[216,256]{1,0:T(8,128)(2,1)S(1)}, bf16[216,256]{1,0:T(8,128)(2,1)S(1)}, u32[]{:S(2)}, u32[]{:S(2)}) collective-permute-start(bf16[216,256]{1,0:T(8,128)(2,1)S(1)} %get-tuple-element.99), channel_id=1, source_target_pairs={{0,4},{4,0},{8,12},{12,8},{16,20},{20,16},{24,28},{28,24},{1,5},{5... | collective-permute-start | bytes 331784 | tf_op jit(solution)/shard_map/ppermute | solution.py:662
  45.6 5.2 %collective-permute-start.16 = (bf16[2,16,1152]{2,1,0:T(8,128)(2,1)S(1)}, bf16[2,16,1152]{2,1,0:T(8,128)(2,1)S(1)}, u32[]{:S(2)}, u32[]{:S(2)}) collective-permute-start(bf16[2,16,1152]{2,1,0:T(8,128)(2,1)S(1)} %get-tuple-element.89.refs_1_), channel_id=1, source_target_pairs={{0,8},{4,12},{8,0},{12,4},{16,24},{20,28},{24,16},{28,20},{1,9},{5... | collective-permute-start | bytes 221192 | tf_op jit(solution)/shard_map/ppermute | solution.py:662
  48.5 6.3 %collective-permute-start.23 = (bf16[216,256]{1,0:T(8,128)(2,1)S(1)}, bf16[216,256]{1,0:T(8,128)(2,1)S(1)}, u32[]{:S(2)}, u32[]{:S(2)}) collective-permute-start(bf16[216,256]{1,0:T(8,128)(2,1)S(1)} %shard_map.121), channel_id=1, source_target_pairs={{0,8},{4,12},{8,0},{12,4},{16,24},{20,28},{24,16},{28,20},{1,9},{5... | collective-permute-start | bytes 331784 | tf_op jit(solution)/shard_map/ppermute | solution.py:662
  50.8 6.7 %collective-permute-start.17 = (bf16[16,1152]{1,0:T(8,128)(2,1)S(1)}, bf16[16,1152]{1,0:T(8,128)(2,1)S(1)}, u32[]{:S(2)}, u32[]{:S(2)}) collective-permute-start(bf16[16,1152]{1,0:T(8,128)(2,1)S(1)} %get-tuple-element.91.refs_1_), channel_id=1, source_target_pairs={{0,16},{4,20},{8,24},{12,28},{16,0},{20,4},{24,8},{28,12},{1,17},{... | collective-permute-start | bytes 110600 | tf_op jit(solution)/shard_map/ppermute | solution.py:662
  51.6 9.2 %collective-permute-start.18 = (bf16[216,256]{1,0:T(8,128)(2,1)S(1)}, bf16[216,256]{1,0:T(8,128)(2,1)S(1)}, u32[]{:S(2)}, u32[]{:S(2)}) collective-permute-start(bf16[216,256]{1,0:T(8,128)(2,1)S(1)} %get-tuple-element.95), channel_id=1, source_target_pairs={{0,4},{4,0},{8,12},{12,8},{16,20},{20,16},{24,28},{28,24},{1,5},{5... | collective-permute-start | bytes 331784 | tf_op jit(solution)/shard_map/ppermute | solution.py:662
  52.6 8.8 %collective-permute-start.20 = (bf16[216,256]{1,0:T(8,128)(2,1)S(1)}, bf16[216,256]{1,0:T(8,128)(2,1)S(1)}, u32[]{:S(2)}, u32[]{:S(2)}) collective-permute-start(bf16[216,256]{1,0:T(8,128)(2,1)S(1)} %shard_map.120.refs_2_), channel_id=1, source_target_pairs={{0,8},{4,12},{8,0},{12,4},{16,24},{20,28},{24,16},{28,20},{1,9},{5... | collective-permute-start | bytes 331784 | tf_op jit(solution)/shard_map/ppermute | solution.py:662
  54.8 6.6 %collective-permute-start.24 = (bf16[216,256]{1,0:T(8,128)(2,1)S(1)}, bf16[216,256]{1,0:T(8,128)(2,1)S(1)}, u32[]{:S(2)}, u32[]{:S(2)}) collective-permute-start(bf16[216,256]{1,0:T(8,128)(2,1)S(1)} %shard_map.122), channel_id=1, source_target_pairs={{0,16},{4,20},{8,24},{12,28},{16,0},{20,4},{24,8},{28,12},{1,17},{... | collective-permute-start | bytes 331784 | tf_op jit(solution)/shard_map/ppermute | solution.py:662
  61.5 6.8 %collective-permute-start.30 = (bf16[256,256]{1,0:T(8,128)(2,1)S(1)}, bf16[256,256]{1,0:T(8,128)(2,1)S(1)}, u32[]{:S(2)}, u32[]{:S(2)}) collective-permute-start(bf16[256,256]{1,0:T(8,128)(2,1)S(1)} %shard_map.123.refs_0_), channel_id=1, source_target_pairs={{0,8},{4,12},{8,0},{12,4},{16,24},{20,28},{24,16},{28,20},{1,9},{5... | collective-permute-start | bytes 393224 | tf_op jit(solution)/shard_map/ppermute | solution.py:662
  61.7 10.2 %collective-permute-start.28 = (bf16[256,256]{1,0:T(8,128)(2,1)S(1)}, bf16[256,256]{1,0:T(8,128)(2,1)S(1)}, u32[]{:S(2)}, u32[]{:S(2)}) collective-permute-start(bf16[256,256]{1,0:T(8,128)(2,1)S(1)} %shard_map.123.refs_0_), channel_id=1, source_target_pairs={{0,16},{4,20},{8,24},{12,28},{16,0},{20,4},{24,8},{28,12},{1,17},{... | collective-permute-start | bytes 393224 | tf_op jit(solution)/shard_map/ppermute | solution.py:662
  64.1 8.6 %collective-permute-start.26 = (bf16[256,256]{1,0:T(8,128)(2,1)S(1)}, bf16[256,256]{1,0:T(8,128)(2,1)S(1)}, u32[]{:S(2)}, u32[]{:S(2)}) collective-permute-start(bf16[256,256]{1,0:T(8,128)(2,1)S(1)} %shard_map.123.refs_0_), channel_id=1, source_target_pairs={{0,24},{4,28},{8,16},{12,20},{16,8},{20,12},{24,0},{28,4},{1,25},{... | collective-permute-start | bytes 393224 | tf_op jit(solution)/shard_map/ppermute | solution.py:662
  66.0 8.1 %collective-permute-start.32 = (bf16[256,256]{1,0:T(8,128)(2,1)S(1)}, bf16[256,256]{1,0:T(8,128)(2,1)S(1)}, u32[]{:S(2)}, u32[]{:S(2)}) collective-permute-start(bf16[256,256]{1,0:T(8,128)(2,1)S(1)} %shard_map.123.refs_0_), channel_id=1, source_target_pairs={{0,4},{4,0},{8,12},{12,8},{16,20},{20,16},{24,28},{28,24},{1,5},{5... | collective-permute-start | bytes 393224 | tf_op jit(solution)/shard_map/ppermute | solution.py:662
  68.3 6.6 %collective-permute-start.31 = (bf16[256,256]{1,0:T(8,128)(2,1)S(1)}, bf16[256,256]{1,0:T(8,128)(2,1)S(1)}, u32[]{:S(2)}, u32[]{:S(2)}) collective-permute-start(bf16[256,256]{1,0:T(8,128)(2,1)S(1)} %collective-permute-done.30.refs_0_), channel_id=1, source_target_pairs={{0,4},{4,0},{8,12},{12,8},{16,20},{20,16},{24,28},{28,24},{1,5},{5... | collective-permute-start | bytes 393224 | tf_op jit(solution)/shard_map/ppermute | solution.py:662
  72.0 5.0 %collective-permute-start.29 = (bf16[256,256]{1,0:T(8,128)(2,1)S(1)}, bf16[256,256]{1,0:T(8,128)(2,1)S(1)}, u32[]{:S(2)}, u32[]{:S(2)}) collective-permute-start(bf16[256,256]{1,0:T(8,128)(2,1)S(1)} %collective-permute-done.28.refs_0_), channel_id=1, source_target_pairs={{0,4},{4,0},{8,12},{12,8},{16,20},{20,16},{24,28},{28,24},{1,5},{5... | collective-permute-start | bytes 393224 | tf_op jit(solution)/shard_map/ppermute | solution.py:662
  72.6 5.7 %collective-permute-start.27 = (bf16[256,256]{1,0:T(8,128)(2,1)S(1)}, bf16[256,256]{1,0:T(8,128)(2,1)S(1)}, u32[]{:S(2)}, u32[]{:S(2)}) collective-permute-start(bf16[256,256]{1,0:T(8,128)(2,1)S(1)} %collective-permute-done.26.refs_2_), channel_id=1, source_target_pairs={{0,4},{4,0},{8,12},{12,8},{16,20},{20,16},{24,28},{28,24},{1,5},{5... | collective-permute-start | bytes 393224 | tf_op jit(solution)/shard_map/ppermute | solution.py:662
  (16 other events, 53.3 us)

commit v8 on v7

--- a/solution.py
+++ b/solution.py
@@ -317,7 +317,9 @@
             slope_x = pltpu.roll(from_odd[:, at] - from_even[:, at], side, 1)
             curve = pltpu.roll(curve + (from_even[:, up] - from_odd[:, up]), side, 1)
         value = tile[j] * keep[:, cols] + curve
-        value = value + FACE_RATE * dot(beside, placed[:, cols])
+        if j % 2 == 0:
+            outer = dot(beside, placed[:, j * pair : (j + 2) * pair])
+        value = value + FACE_RATE * outer[:, j % 2 * pair : (j % 2 + 1) * pair]
         value = value.reshape(3, rows, pair)
         for d, slope in enumerate((slope_x, slope_y, slope_z)):
             value = value + slope.reshape(3, rows, pair) * tile[j].reshape(3, rows, pair)[d][None]
@@ -340,19 +342,13 @@
 
 
 def encode_kernel(
-    part, pair_x, cross_x, pair_y, cross_y, tabs, wall, w_encode,
-    field, snapshot, target, z1, h1,
+    part, pair_x, cross_x, pair_y, cross_y, tabs, w_encode,
+    field, snapshot, z1, h1,
 ):
     ez = part.shape[1] // (EX * EY)
     add_edges(part, pair_x, cross_x, pair_y, cross_y, tabs, field, ez)
-    high0, low0 = split_two(field[0])
-    high2, low2 = split_two(field[2])
-    snap = jnp.concatenate([high0, high2], axis=1)
+    snap = jnp.concatenate([field[0].astype(BF16), field[2].astype(BF16)], axis=1)
     snapshot[...] = snap
-    target[...] = (
-        dot(jnp.concatenate([high0, low0, high0], axis=1), wall[:, : 2 * NP * NP])
-        + dot(jnp.concatenate([high2, low2, high2], axis=1), wall[:, 2 * NP * NP :])
-    ).astype(BF16)
     hidden = dot(snap, w_encode[...])
     z1[...] = hidden
     h1[...] = (hidden * jax.nn.sigmoid(hidden)).astype(BF16)
@@ -410,7 +406,13 @@
     return both + jnp.concatenate([times(taken[1], 18), times(taken[0], 0)], axis=0)
 
 
-def centre_kernel(groups, h1, w_conv, z2):
+def centre_kernel(groups, h1, w_conv, field, wall, z2, target):
+    found = 0.0
+    for c, start in ((0, 0), (2, 2 * NP * NP)):
+        high, low = split_two(field[c])
+        three = jnp.concatenate([high, low, high], axis=1)
+        found = found + dot(three, wall[:, start : start + 2 * NP * NP])
+    target[...] = found.astype(BF16)
     rows, channels = h1.shape
     ez = rows // (EX * EY)
     grid = h1[...].astype(F32).reshape(EX, EY, ez, channels)
@@ -722,23 +724,26 @@
     field, *edges = call(join_kernel, (whole,) + edge_shapes)(part, *halos, tabs)
     halos = exchanged(edges)
     part = call(inside_kernel, whole)(field, stencil)
-    field, snapshot, target, z1, h1 = call(
+    field, snapshot, z1, h1 = call(
         encode_kernel,
         (
             whole,
             shaped((rows, features), BF16),
-            shaped((rows, outputs), BF16),
             shaped((rows, channels), F32),
             shaped((rows, channels), BF16),
         ),
-    )(part, *halos, tabs, wall, w_encode)
+    )(part, *halos, tabs, w_encode)
 
     h_three = swapped(h1, "grp", 3)
     h_one = swapped(h1, "grp", 1)
     h_two = swapped(h_three, "grp", 1)
     rows_bf = shaped((rows, channels), BF16)
     square = shaped((rows, channels), F32)
-    z2 = call(functools.partial(centre_kernel, groups), square, flops=2 * 10**9)(h1, w_conv)
+    z2, target = call(
+        functools.partial(centre_kernel, groups),
+        (square, shaped((rows, outputs), BF16)),
+        flops=2 * 10**9,
+    )(h1, w_conv, field, wall)
     dz2, h2, resid = call(
         functools.partial(forward_kernel, groups, total),
         (rows_bf, rows_bf, shaped((rows, outputs), BF16)),

time: 79.4 us -> 78.9 us (level)
  waiting for transfers between devices: 12.3 us -> 11 us
  starting transfers between devices: 44.4 us -> 45.2 us
    ppermute x29, waiting for transfers between devices: 12.3 us -> 10.9 us  [swapped(): return lax.ppermute(value, axis, [(i, i ^ mask) for i in range(count)])]
  transfers between devices with their start and end apart: 33 -> 33, of which waited for: 13 -> 11; matrix products, arithmetic and copies ran while one was open for 0% -> 0% of each run, Pallas kernels for 17% -> 18%
where the time goes in v8:
time: 78.9 us; the launch traced here: 78.6 us
  starting transfers between devices  45.2 us (57%)
  Pallas kernels  19.1 us (24%)
  waiting for transfers between devices  11 us (14%)
  local copies, waits for them, and re-layouts  2.17 us (3%)
  between operations  1.12 us (1%)
    ppermute x29, starting transfers between devices, swapped(): return lax.ppermute(value, axis, [(i, i ^ mask) for i in range(count)])  37.1 us
    ppermute x29, waiting for transfers between devices, swapped(): return lax.ppermute(value, axis, [(i, i ^ mask) for i in range(count)])  10.9 us
    ppermute x4, starting transfers between devices, crossed(): lax.ppermute(value, axis, [(i, j) for i, j in route if 0 <= j < count])  8.09 us
    pallas_call x2, Pallas kernels, body(): part = call(inside_kernel, whole)(field, stencil)  6.21 us
    pallas_call x4, Pallas kernels, placed_shares(): pl.pallas_call(functools.partial(place_kernel, masks, count), out_shape=s...  3.38 us
    unnamed x14, local copies, waits for them, and re-layouts  2.17 us
    pallas_call x1, Pallas kernels, body(): velocity_next, done = restore(field, back, e_sent)  1.97 us
  transfers between devices with their start and end apart: 33, of which 11 were waited for; matrix products, arithmetic and copies ran while one was open for 0% of the time, Pallas kernels for 18%

profile of v8, /device:TPU:0, one launch (start us, length us, event | category | flops | bytes accessed | tf_op | source)
XLA Modules:
  0.0 78.6 jit_solution(5808576494460634007)
XLA Ops:
  1.4 1.3 %copy-done.4 = f32[1,1,3,256,512]{4,3,2,1,0:T(8,128)S(1)} copy-done((f32[1,1,3,256,512]{4,3,2,1,0:T(8,128)S(1)}, f32[1,1,3,256,512]{4,3,2,1,0:T(8,128)}, u32[]{:S(2)}) %copy-start.4) | copy-done | bytes 1572888
  3.8 3.0 %collective-permute-start = (bf16[3,64,128]{2,1,0:T(8,128)(2,1)S(1)}, bf16[3,64,128]{2,1,0:T(8,128)(2,1)S(1)}, u32[]{:S(2)}, u32[]{:S(2)}) collective-permute-start(bf16[3,64,128]{2,1,0:T(8,128)(2,1)S(1)} %get-tuple-element.64), channel_id=1, source_target_pairs={{0,4},{4,0},{8,12},{12,8},{16,20},{20,16},{24,28},{28,24},{1,5},{5... | collective-permute-start | bytes 147464 | tf_op jit(solution)/shard_map/ppermute | solution.py:664
  6.8 3.6 %collective-permute-start.1 = (bf16[3,64,128]{2,1,0:T(8,128)(2,1)S(1)}, bf16[3,64,128]{2,1,0:T(8,128)(2,1)S(1)}, u32[]{:S(2)}, u32[]{:S(2)}) collective-permute-start(bf16[3,64,128]{2,1,0:T(8,128)(2,1)S(1)} %get-tuple-element.65), channel_id=1, source_target_pairs={{0,28},{4,8},{8,4},{12,16},{16,12},{20,24},{24,20},{28,0},{1,29},{... | collective-permute-start | bytes 147464 | tf_op jit(solution)/shard_map/ppermute | solution.py:672
  11.0 3.1 %shard_map.104.part = f32[3,256,512]{2,1,0:T(8,128)S(1)} custom-call(f32[3,256,512]{2,1,0:T(8,128)S(1)} %get-tuple-element.63.field, bf16[2560,512]{1,0:T(8,128)(2,1)S(1)} %copy-done.1), custom_call_target="tpu_custom_call" | custom-call | flops 1000 | bytes 1000 | tf_op jit(solution)/shard_map/pallas_call | solution.py:723
  14.8 3.0 %collective-permute-start.5 = (bf16[3,64,128]{2,1,0:T(8,128)(2,1)S(1)}, bf16[3,64,128]{2,1,0:T(8,128)(2,1)S(1)}, u32[]{:S(2)}, u32[]{:S(2)}) collective-permute-start(bf16[3,64,128]{2,1,0:T(8,128)(2,1)S(1)} %get-tuple-element.70), channel_id=1, source_target_pairs={{0,28},{4,8},{8,4},{12,16},{16,12},{20,24},{24,20},{28,0},{1,29},{... | collective-permute-start | bytes 147464 | tf_op jit(solution)/shard_map/ppermute | solution.py:672
  19.8 3.1 %shard_map.106.part = f32[3,256,512]{2,1,0:T(8,128)S(1)} custom-call(f32[3,256,512]{2,1,0:T(8,128)S(1)} %get-tuple-element.68.field, bf16[2560,512]{1,0:T(8,128)(2,1)S(1)} %copy-done.1), custom_call_target="tpu_custom_call" | custom-call | flops 1000 | bytes 1000 | tf_op jit(solution)/shard_map/pallas_call | solution.py:726
  24.8 1.8 %collective-permute-start.8 = (bf16[256,256]{1,0:T(8,128)(2,1)S(1)}, bf16[256,256]{1,0:T(8,128)(2,1)S(1)}, u32[]{:S(2)}, u32[]{:S(2)}) collective-permute-start(bf16[256,256]{1,0:T(8,128)(2,1)S(1)} %get-tuple-element.75.h1.h_own), channel_id=1, source_target_pairs={{0,1},{1,0},{2,3},{3,2},{4,5},{5,4},{6,7},{7,6},{8,9},{9,8},{10,11... | collective-permute-start | bytes 393224 | tf_op jit(solution)/shard_map/ppermute | solution.py:664
  29.2 1.6 %collective-permute-start.11 = (bf16[256,256]{1,0:T(8,128)(2,1)S(1)}, bf16[256,256]{1,0:T(8,128)(2,1)S(1)}, u32[]{:S(2)}, u32[]{:S(2)}) collective-permute-start(bf16[256,256]{1,0:T(8,128)(2,1)S(1)} %get-tuple-element.78.dz2.d_own), channel_id=1, source_target_pairs={{0,3},{1,2},{2,1},{3,0},{4,7},{5,6},{6,5},{7,4},{8,11},{9,10},{10,... | collective-permute-start | bytes 393224 | tf_op jit(solution)/shard_map/ppermute | solution.py:664
  30.8 1.5 %collective-permute-start.10 = (bf16[256,256]{1,0:T(8,128)(2,1)S(1)}, bf16[256,256]{1,0:T(8,128)(2,1)S(1)}, u32[]{:S(2)}, u32[]{:S(2)}) collective-permute-start(bf16[256,256]{1,0:T(8,128)(2,1)S(1)} %get-tuple-element.78.dz2.d_own), channel_id=1, source_target_pairs={{0,1},{1,0},{2,3},{3,2},{4,5},{5,4},{6,7},{7,6},{8,9},{9,8},{10,11... | collective-permute-start | bytes 393224 | tf_op jit(solution)/shard_map/ppermute | solution.py:664
  33.9 1.4 %shard_map.113 = (f32[2,64,1152]{2,1,0:T(8,128)S(1)}, bf16[2,64,1152]{2,1,0:T(8,128)(2,1)S(1)}) custom-call(f32[256,256]{1,0:T(8,128)S(1)} %get-tuple-element.81.dh1, f32[256,128]{1,0:T(8,128)S(1)} %get-tuple-element.82.head, bf16[256,256]{1,0:T(8,128)(2,1)S(1)} %get-tuple-element.78.dz2.d_own, bf16[256,256]{1,0:T(8,128)(2,1)S(1)} %collective-permute-done.10.pair.d_one, ...), custom_call_target="tpu_custom_call" | custom-call | flops 1000 | bytes 1000 | tf_op jit(solution)/shard_map/pallas_call | solution.py:763
  35.3 2.1 %collective-permute-start.12 = (bf16[2,64,1152]{2,1,0:T(8,128)(2,1)S(1)}, bf16[2,64,1152]{2,1,0:T(8,128)(2,1)S(1)}, u32[]{:S(2)}, u32[]{:S(2)}) collective-permute-start(bf16[2,64,1152]{2,1,0:T(8,128)(2,1)S(1)} %get-tuple-element.86), channel_id=1, source_target_pairs={{0,1},{1,0},{2,3},{3,2},{4,5},{5,4},{6,7},{7,6},{8,9},{9,8},{10,11... | collective-permute-start | bytes 884744 | tf_op jit(solution)/shard_map/ppermute | solution.py:664
  38.7 1.7 %collective-permute-start.13 = (bf16[64,1152]{1,0:T(8,128)(2,1)S(1)}, bf16[64,1152]{1,0:T(8,128)(2,1)S(1)}, u32[]{:S(2)}, u32[]{:S(2)}) collective-permute-start(bf16[64,1152]{1,0:T(8,128)(2,1)S(1)} %get-tuple-element.88), channel_id=1, source_target_pairs={{0,2},{1,3},{2,0},{3,1},{4,6},{5,7},{6,4},{7,5},{8,10},{9,11},{10,... | collective-permute-start | bytes 442376 | tf_op jit(solution)/shard_map/ppermute | solution.py:664
  40.4 1.4 %shard_map.115 = (f32[216,256]{1,0:T(8,128)S(1)}, bf16[216,256]{1,0:T(8,128)(2,1)S(1)}, f32[216,256]{1,0:T(8,128)S(1)}, bf16[216,256]{1,0:T(8,128)(2,1)S(1)}, f3...) custom-call(bf16[256,256]{1,0:T(8,128)(2,1)S(1)} %get-tuple-element., ...), custom_call_target="tpu_custom_call" | custom-call | flops 1000 | bytes 1000 | tf_op jit(solution)/shard_map/pallas_call | solution.py:778
  42.5 1.4 %collective-permute-start.19 = (bf16[216,256]{1,0:T(8,128)(2,1)S(1)}, bf16[216,256]{1,0:T(8,128)(2,1)S(1)}, u32[]{:S(2)}, u32[]{:S(2)}) collective-permute-start(bf16[216,256]{1,0:T(8,128)(2,1)S(1)} %get-tuple-element.99), channel_id=1, source_target_pairs={{0,4},{4,0},{8,12},{12,8},{16,20},{20,16},{24,28},{28,24},{1,5},{5... | collective-permute-start | bytes 331784 | tf_op jit(solution)/shard_map/ppermute | solution.py:664
  44.9 1.6 %collective-permute-start.16 = (bf16[2,16,1152]{2,1,0:T(8,128)(2,1)S(1)}, bf16[2,16,1152]{2,1,0:T(8,128)(2,1)S(1)}, u32[]{:S(2)}, u32[]{:S(2)}) collective-permute-start(bf16[2,16,1152]{2,1,0:T(8,128)(2,1)S(1)} %get-tuple-element.91.refs_1_), channel_id=1, source_target_pairs={{0,8},{4,12},{8,0},{12,4},{16,24},{20,28},{24,16},{28,20},{1,9},{5... | collective-permute-start | bytes 221192 | tf_op jit(solution)/shard_map/ppermute | solution.py:664
  47.8 1.7 %collective-permute-start.23 = (bf16[216,256]{1,0:T(8,128)(2,1)S(1)}, bf16[216,256]{1,0:T(8,128)(2,1)S(1)}, u32[]{:S(2)}, u32[]{:S(2)}) collective-permute-start(bf16[216,256]{1,0:T(8,128)(2,1)S(1)} %shard_map.121), channel_id=1, source_target_pairs={{0,8},{4,12},{8,0},{12,4},{16,24},{20,28},{24,16},{28,20},{1,9},{5... | collective-permute-start | bytes 331784 | tf_op jit(solution)/shard_map/ppermute | solution.py:664
  51.9 2.3 %collective-permute-start.20 = (bf16[216,256]{1,0:T(8,128)(2,1)S(1)}, bf16[216,256]{1,0:T(8,128)(2,1)S(1)}, u32[]{:S(2)}, u32[]{:S(2)}) collective-permute-start(bf16[216,256]{1,0:T(8,128)(2,1)S(1)} %shard_map.120.refs_2_), channel_id=1, source_target_pairs={{0,8},{4,12},{8,0},{12,4},{16,24},{20,28},{24,16},{28,20},{1,9},{5... | collective-permute-start | bytes 331784 | tf_op jit(solution)/shard_map/ppermute | solution.py:664
  54.3 1.5 %collective-permute-start.24 = (bf16[216,256]{1,0:T(8,128)(2,1)S(1)}, bf16[216,256]{1,0:T(8,128)(2,1)S(1)}, u32[]{:S(2)}, u32[]{:S(2)}) collective-permute-start(bf16[216,256]{1,0:T(8,128)(2,1)S(1)} %shard_map.122), channel_id=1, source_target_pairs={{0,16},{4,20},{8,24},{12,28},{16,0},{20,4},{24,8},{28,12},{1,17},{... | collective-permute-start | bytes 331784 | tf_op jit(solution)/shard_map/ppermute | solution.py:664
  55.8 2.4 %collective-permute-start.25 = (bf16[8,1152]{1,0:T(8,128)(2,1)S(1)}, bf16[8,1152]{1,0:T(8,128)(2,1)S(1)}, u32[]{:S(2)}, u32[]{:S(2)}) collective-permute-start(bf16[8,1152]{1,0:T(8,128)(2,1)S(1)} %get-tuple-element.94.after_this), channel_id=1, source_target_pairs={{0,4},{4,0},{8,12},{12,8},{16,20},{20,16},{24,28},{28,24},{1,5},{5... | collective-permute-start | bytes 55304 | tf_op jit(solution)/shard_map/ppermute | solution.py:664
  58.2 2.0 %shard_map.119 = (f32[3,256,512]{2,1,0:T(8,128)}, f32[8,128]{1,0:T(8,128)S(1)}) custom-call(f32[3,256,512]{2,1,0:T(8,128)S(1)} %get-tuple-element.73.field, bf16[256,256]{1,0:T(8,128)(2,1)S(1)} %get-tuple-element.74.back, bf16[8,1152]{1,0:T(8,128)(2,1)S(1)} %get-tuple-element.94.after_this), custom_call_target="tpu_custom_call" | custom-call | flops 1000 | bytes 1000 | tf_op jit(solution)/shard_map/pallas_call | solution.py:812
  61.1 2.3 %collective-permute-start.28 = (bf16[256,256]{1,0:T(8,128)(2,1)S(1)}, bf16[256,256]{1,0:T(8,128)(2,1)S(1)}, u32[]{:S(2)}, u32[]{:S(2)}) collective-permute-start(bf16[256,256]{1,0:T(8,128)(2,1)S(1)} %shard_map.123.refs_0_), channel_id=1, source_target_pairs={{0,16},{4,20},{8,24},{12,28},{16,0},{20,4},{24,8},{28,12},{1,17},{... | collective-permute-start | bytes 393224 | tf_op jit(solution)/shard_map/ppermute | solution.py:664
  63.4 1.9 %collective-permute-start.26 = (bf16[256,256]{1,0:T(8,128)(2,1)S(1)}, bf16[256,256]{1,0:T(8,128)(2,1)S(1)}, u32[]{:S(2)}, u32[]{:S(2)}) collective-permute-start(bf16[256,256]{1,0:T(8,128)(2,1)S(1)} %shard_map.123.refs_0_), channel_id=1, source_target_pairs={{0,24},{4,28},{8,16},{12,20},{16,8},{20,12},{24,0},{28,4},{1,25},{... | collective-permute-start | bytes 393224 | tf_op jit(solution)/shard_map/ppermute | solution.py:664
  68.5 2.9 %collective-permute-done.28.refs_0_ = bf16[256,256]{1,0:T(8,128)(2,1)S(1)} collective-permute-done((bf16[256,256]{1,0:T(8,128)(2,1)S(1)}, bf16[256,256]{1,0:T(8,128)(2,1)S(1)}, u32[]{:S(2)}, u32[]{:S(2)}) %collective-permute-start.28) | collective-permute-done | bytes 131104 | tf_op jit(solution)/shard_map/ppermute | solution.py:664
  72.0 1.4 %collective-permute-start.27 = (bf16[256,256]{1,0:T(8,128)(2,1)S(1)}, bf16[256,256]{1,0:T(8,128)(2,1)S(1)}, u32[]{:S(2)}, u32[]{:S(2)}) collective-permute-start(bf16[256,256]{1,0:T(8,128)(2,1)S(1)} %collective-permute-done.26.refs_2_), channel_id=1, source_target_pairs={{0,4},{4,0},{8,12},{12,8},{16,20},{20,16},{24,28},{28,24},{1,5},{5... | collective-permute-start | bytes 393224 | tf_op jit(solution)/shard_map/ppermute | solution.py:664
  (82 shorter events, 27.3 us)
Async XLA Ops:
  3.8 10.4 %collective-permute-start = (bf16[3,64,128]{2,1,0:T(8,128)(2,1)S(1)}, bf16[3,64,128]{2,1,0:T(8,128)(2,1)S(1)}, u32[]{:S(2)}, u32[]{:S(2)}) collective-permute-start(bf16[3,64,128]{2,1,0:T(8,128)(2,1)S(1)} %get-tuple-element.64), channel_id=1, source_target_pairs={{0,4},{4,0},{8,12},{12,8},{16,20},{20,16},{24,28},{28,24},{1,5},{5... | collective-permute-start | bytes 147464 | tf_op jit(solution)/shard_map/ppermute | solution.py:664
  6.8 7.4 %collective-permute-start.1 = (bf16[3,64,128]{2,1,0:T(8,128)(2,1)S(1)}, bf16[3,64,128]{2,1,0:T(8,128)(2,1)S(1)}, u32[]{:S(2)}, u32[]{:S(2)}) collective-permute-start(bf16[3,64,128]{2,1,0:T(8,128)(2,1)S(1)} %get-tuple-element.65), channel_id=1, source_target_pairs={{0,28},{4,8},{8,4},{12,16},{16,12},{20,24},{24,20},{28,0},{1,29},{... | collective-permute-start | bytes 147464 | tf_op jit(solution)/shard_map/ppermute | solution.py:672
  14.7 8.3 %collective-permute-start.4 = (bf16[3,64,128]{2,1,0:T(8,128)(2,1)S(1)}, bf16[3,64,128]{2,1,0:T(8,128)(2,1)S(1)}, u32[]{:S(2)}, u32[]{:S(2)}) collective-permute-start(bf16[3,64,128]{2,1,0:T(8,128)(2,1)S(1)} %get-tuple-element.69), channel_id=1, source_target_pairs={{0,4},{4,0},{8,12},{12,8},{16,20},{20,16},{24,28},{28,24},{1,5},{5... | collective-permute-start | bytes 147464 | tf_op jit(solution)/shard_map/ppermute | solution.py:664
  14.8 8.2 %collective-permute-start.5 = (bf16[3,64,128]{2,1,0:T(8,128)(2,1)S(1)}, bf16[3,64,128]{2,1,0:T(8,128)(2,1)S(1)}, u32[]{:S(2)}, u32[]{:S(2)}) collective-permute-start(bf16[3,64,128]{2,1,0:T(8,128)(2,1)S(1)} %get-tuple-element.70), channel_id=1, source_target_pairs={{0,28},{4,8},{8,4},{12,16},{16,12},{20,24},{24,20},{28,0},{1,29},{... | collective-permute-start | bytes 147464 | tf_op jit(solution)/shard_map/ppermute | solution.py:672
  17.8 5.2 %collective-permute-start.6 = (bf16[3,32,128]{2,1,0:T(8,128)(2,1)S(1)}, bf16[3,32,128]{2,1,0:T(8,128)(2,1)S(1)}, u32[]{:S(2)}, u32[]{:S(2)}) collective-permute-start(bf16[3,32,128]{2,1,0:T(8,128)(2,1)S(1)} %get-tuple-element.71), channel_id=1, source_target_pairs={{0,1},{1,0},{2,3},{3,2},{4,5},{5,4},{6,7},{7,6},{8,9},{9,8},{10,11... | collective-permute-start | bytes 73736 | tf_op jit(solution)/shard_map/ppermute | solution.py:664
  23.6 4.5 %collective-permute-start.9 = (bf16[256,256]{1,0:T(8,128)(2,1)S(1)}, bf16[256,256]{1,0:T(8,128)(2,1)S(1)}, u32[]{:S(2)}, u32[]{:S(2)}) collective-permute-start(bf16[256,256]{1,0:T(8,128)(2,1)S(1)} %get-tuple-element.75.h1.h_own), channel_id=1, source_target_pairs={{0,3},{1,2},{2,1},{3,0},{4,7},{5,6},{6,5},{7,4},{8,11},{9,10},{10,... | collective-permute-start | bytes 393224 | tf_op jit(solution)/shard_map/ppermute | solution.py:664
  29.2 4.7 %collective-permute-start.11 = (bf16[256,256]{1,0:T(8,128)(2,1)S(1)}, bf16[256,256]{1,0:T(8,128)(2,1)S(1)}, u32[]{:S(2)}, u32[]{:S(2)}) collective-permute-start(bf16[256,256]{1,0:T(8,128)(2,1)S(1)} %get-tuple-element.78.dz2.d_own), channel_id=1, source_target_pairs={{0,3},{1,2},{2,1},{3,0},{4,7},{5,6},{6,5},{7,4},{8,11},{9,10},{10,... | collective-permute-start | bytes 393224 | tf_op jit(solution)/shard_map/ppermute | solution.py:664
  38.7 6.2 %collective-permute-start.13 = (bf16[64,1152]{1,0:T(8,128)(2,1)S(1)}, bf16[64,1152]{1,0:T(8,128)(2,1)S(1)}, u32[]{:S(2)}, u32[]{:S(2)}) collective-permute-start(bf16[64,1152]{1,0:T(8,128)(2,1)S(1)} %get-tuple-element.88), channel_id=1, source_target_pairs={{0,2},{1,3},{2,0},{3,1},{4,6},{5,7},{6,4},{7,5},{8,10},{9,11},{10,... | collective-permute-start | bytes 442376 | tf_op jit(solution)/shard_map/ppermute | solution.py:664
  41.8 6.0 %collective-permute-start.22 = (bf16[216,256]{1,0:T(8,128)(2,1)S(1)}, bf16[216,256]{1,0:T(8,128)(2,1)S(1)}, u32[]{:S(2)}, u32[]{:S(2)}) collective-permute-start(bf16[216,256]{1,0:T(8,128)(2,1)S(1)} %get-tuple-element.103), channel_id=1, source_target_pairs={{0,4},{4,0},{8,12},{12,8},{16,20},{20,16},{24,28},{28,24},{1,5},{5... | collective-permute-start | bytes 331784 | tf_op jit(solution)/shard_map/ppermute | solution.py:664
  42.5 9.4 %collective-permute-start.19 = (bf16[216,256]{1,0:T(8,128)(2,1)S(1)}, bf16[216,256]{1,0:T(8,128)(2,1)S(1)}, u32[]{:S(2)}, u32[]{:S(2)}) collective-permute-start(bf16[216,256]{1,0:T(8,128)(2,1)S(1)} %get-tuple-element.99), channel_id=1, source_target_pairs={{0,4},{4,0},{8,12},{12,8},{16,20},{20,16},{24,28},{28,24},{1,5},{5... | collective-permute-start | bytes 331784 | tf_op jit(solution)/shard_map/ppermute | solution.py:664
  43.9 10.4 %collective-permute-start.21 = (bf16[216,256]{1,0:T(8,128)(2,1)S(1)}, bf16[216,256]{1,0:T(8,128)(2,1)S(1)}, u32[]{:S(2)}, u32[]{:S(2)}) collective-permute-start(bf16[216,256]{1,0:T(8,128)(2,1)S(1)} %get-tuple-element.101), channel_id=1, source_target_pairs={{0,4},{4,0},{8,12},{12,8},{16,20},{20,16},{24,28},{28,24},{1,5},{5... | collective-permute-start | bytes 331784 | tf_op jit(solution)/shard_map/ppermute | solution.py:664
  44.9 5.2 %collective-permute-start.16 = (bf16[2,16,1152]{2,1,0:T(8,128)(2,1)S(1)}, bf16[2,16,1152]{2,1,0:T(8,128)(2,1)S(1)}, u32[]{:S(2)}, u32[]{:S(2)}) collective-permute-start(bf16[2,16,1152]{2,1,0:T(8,128)(2,1)S(1)} %get-tuple-element.91.refs_1_), channel_id=1, source_target_pairs={{0,8},{4,12},{8,0},{12,4},{16,24},{20,28},{24,16},{28,20},{1,9},{5... | collective-permute-start | bytes 221192 | tf_op jit(solution)/shard_map/ppermute | solution.py:664
  47.8 6.4 %collective-permute-start.23 = (bf16[216,256]{1,0:T(8,128)(2,1)S(1)}, bf16[216,256]{1,0:T(8,128)(2,1)S(1)}, u32[]{:S(2)}, u32[]{:S(2)}) collective-permute-start(bf16[216,256]{1,0:T(8,128)(2,1)S(1)} %shard_map.121), channel_id=1, source_target_pairs={{0,8},{4,12},{8,0},{12,4},{16,24},{20,28},{24,16},{28,20},{1,9},{5... | collective-permute-start | bytes 331784 | tf_op jit(solution)/shard_map/ppermute | solution.py:664
  50.2 5.6 %collective-permute-start.17 = (bf16[16,1152]{1,0:T(8,128)(2,1)S(1)}, bf16[16,1152]{1,0:T(8,128)(2,1)S(1)}, u32[]{:S(2)}, u32[]{:S(2)}) collective-permute-start(bf16[16,1152]{1,0:T(8,128)(2,1)S(1)} %get-tuple-element.93.refs_1_), channel_id=1, source_target_pairs={{0,16},{4,20},{8,24},{12,28},{16,0},{20,4},{24,8},{28,12},{1,17},{... | collective-permute-start | bytes 110600 | tf_op jit(solution)/shard_map/ppermute | solution.py:664
  51.1 9.1 %collective-permute-start.18 = (bf16[216,256]{1,0:T(8,128)(2,1)S(1)}, bf16[216,256]{1,0:T(8,128)(2,1)S(1)}, u32[]{:S(2)}, u32[]{:S(2)}) collective-permute-start(bf16[216,256]{1,0:T(8,128)(2,1)S(1)} %get-tuple-element.97), channel_id=1, source_target_pairs={{0,4},{4,0},{8,12},{12,8},{16,20},{20,16},{24,28},{28,24},{1,5},{5... | collective-permute-start | bytes 331784 | tf_op jit(solution)/shard_map/ppermute | solution.py:664
  51.9 8.3 %collective-permute-start.20 = (bf16[216,256]{1,0:T(8,128)(2,1)S(1)}, bf16[216,256]{1,0:T(8,128)(2,1)S(1)}, u32[]{:S(2)}, u32[]{:S(2)}) collective-permute-start(bf16[216,256]{1,0:T(8,128)(2,1)S(1)} %shard_map.120.refs_2_), channel_id=1, source_target_pairs={{0,8},{4,12},{8,0},{12,4},{16,24},{20,28},{24,16},{28,20},{1,9},{5... | collective-permute-start | bytes 331784 | tf_op jit(solution)/shard_map/ppermute | solution.py:664
  54.3 6.5 %collective-permute-start.24 = (bf16[216,256]{1,0:T(8,128)(2,1)S(1)}, bf16[216,256]{1,0:T(8,128)(2,1)S(1)}, u32[]{:S(2)}, u32[]{:S(2)}) collective-permute-start(bf16[216,256]{1,0:T(8,128)(2,1)S(1)} %shard_map.122), channel_id=1, source_target_pairs={{0,16},{4,20},{8,24},{12,28},{16,0},{20,4},{24,8},{28,12},{1,17},{... | collective-permute-start | bytes 331784 | tf_op jit(solution)/shard_map/ppermute | solution.py:664
  60.9 6.8 %collective-permute-start.30 = (bf16[256,256]{1,0:T(8,128)(2,1)S(1)}, bf16[256,256]{1,0:T(8,128)(2,1)S(1)}, u32[]{:S(2)}, u32[]{:S(2)}) collective-permute-start(bf16[256,256]{1,0:T(8,128)(2,1)S(1)} %shard_map.123.refs_0_), channel_id=1, source_target_pairs={{0,8},{4,12},{8,0},{12,4},{16,24},{20,28},{24,16},{28,20},{1,9},{5... | collective-permute-start | bytes 393224 | tf_op jit(solution)/shard_map/ppermute | solution.py:664
  61.1 10.2 %collective-permute-start.28 = (bf16[256,256]{1,0:T(8,128)(2,1)S(1)}, bf16[256,256]{1,0:T(8,128)(2,1)S(1)}, u32[]{:S(2)}, u32[]{:S(2)}) collective-permute-start(bf16[256,256]{1,0:T(8,128)(2,1)S(1)} %shard_map.123.refs_0_), channel_id=1, source_target_pairs={{0,16},{4,20},{8,24},{12,28},{16,0},{20,4},{24,8},{28,12},{1,17},{... | collective-permute-start | bytes 393224 | tf_op jit(solution)/shard_map/ppermute | solution.py:664
  63.4 8.5 %collective-permute-start.26 = (bf16[256,256]{1,0:T(8,128)(2,1)S(1)}, bf16[256,256]{1,0:T(8,128)(2,1)S(1)}, u32[]{:S(2)}, u32[]{:S(2)}) collective-permute-start(bf16[256,256]{1,0:T(8,128)(2,1)S(1)} %shard_map.123.refs_0_), channel_id=1, source_target_pairs={{0,24},{4,28},{8,16},{12,20},{16,8},{20,12},{24,0},{28,4},{1,25},{... | collective-permute-start | bytes 393224 | tf_op jit(solution)/shard_map/ppermute | solution.py:664
  65.3 8.1 %collective-permute-start.32 = (bf16[256,256]{1,0:T(8,128)(2,1)S(1)}, bf16[256,256]{1,0:T(8,128)(2,1)S(1)}, u32[]{:S(2)}, u32[]{:S(2)}) collective-permute-start(bf16[256,256]{1,0:T(8,128)(2,1)S(1)} %shard_map.123.refs_0_), channel_id=1, source_target_pairs={{0,4},{4,0},{8,12},{12,8},{16,20},{20,16},{24,28},{28,24},{1,5},{5... | collective-permute-start | bytes 393224 | tf_op jit(solution)/shard_map/ppermute | solution.py:664
  67.7 6.6 %collective-permute-start.31 = (bf16[256,256]{1,0:T(8,128)(2,1)S(1)}, bf16[256,256]{1,0:T(8,128)(2,1)S(1)}, u32[]{:S(2)}, u32[]{:S(2)}) collective-permute-start(bf16[256,256]{1,0:T(8,128)(2,1)S(1)} %collective-permute-done.30.refs_0_), channel_id=1, source_target_pairs={{0,4},{4,0},{8,12},{12,8},{16,20},{20,16},{24,28},{28,24},{1,5},{5... | collective-permute-start | bytes 393224 | tf_op jit(solution)/shard_map/ppermute | solution.py:664
  71.4 5.0 %collective-permute-start.29 = (bf16[256,256]{1,0:T(8,128)(2,1)S(1)}, bf16[256,256]{1,0:T(8,128)(2,1)S(1)}, u32[]{:S(2)}, u32[]{:S(2)}) collective-permute-start(bf16[256,256]{1,0:T(8,128)(2,1)S(1)} %collective-permute-done.28.refs_0_), channel_id=1, source_target_pairs={{0,4},{4,0},{8,12},{12,8},{16,20},{20,16},{24,28},{28,24},{1,5},{5... | collective-permute-start | bytes 393224 | tf_op jit(solution)/shard_map/ppermute | solution.py:664
  72.0 5.8 %collective-permute-start.27 = (bf16[256,256]{1,0:T(8,128)(2,1)S(1)}, bf16[256,256]{1,0:T(8,128)(2,1)S(1)}, u32[]{:S(2)}, u32[]{:S(2)}) collective-permute-start(bf16[256,256]{1,0:T(8,128)(2,1)S(1)} %collective-permute-done.26.refs_2_), channel_id=1, source_target_pairs={{0,4},{4,0},{8,12},{12,8},{16,20},{20,16},{24,28},{28,24},{1,5},{5... | collective-permute-start | bytes 393224 | tf_op jit(solution)/shard_map/ppermute | solution.py:664
  (16 other events, 56.4 us)

commit v9 on v8

--- a/solution.py
+++ b/solution.py
@@ -235,7 +235,8 @@
 def prepare_kernel(vel, order, tabs, field, *edges):
     ez = vel.shape[1] // (EX * EY)
     for c in range(3):
-        field[c] = moved(order[...], vel[c])
+        high, low = split_two(vel[c])
+        field[c] = dot(order[...], high) + dot(order[...], low)
     write_edges(field, tabs, edges, ez)
 
 

time: 78.9 us -> 78.6 us (level)
  no operation moved by 1% of the time
where the time goes in v9:
time: 78.6 us; the launch traced here: 78.4 us
  starting transfers between devices  45.2 us (58%)
  Pallas kernels  18.9 us (24%)
  waiting for transfers between devices  11 us (14%)
  local copies, waits for them, and re-layouts  2.17 us (3%)
  between operations  1.12 us (1%)
    ppermute x29, starting transfers between devices, swapped(): return lax.ppermute(value, axis, [(i, i ^ mask) for i in range(count)])  37.1 us
    ppermute x29, waiting for transfers between devices, swapped(): return lax.ppermute(value, axis, [(i, i ^ mask) for i in range(count)])  11 us
    ppermute x4, starting transfers between devices, crossed(): lax.ppermute(value, axis, [(i, j) for i, j in route if 0 <= j < count])  8.08 us
    pallas_call x2, Pallas kernels, body(): part = call(inside_kernel, whole)(field, stencil)  6.21 us
    pallas_call x4, Pallas kernels, placed_shares(): pl.pallas_call(functools.partial(place_kernel, masks, count), out_shape=s...  3.38 us
    unnamed x14, local copies, waits for them, and re-layouts  2.17 us
    pallas_call x1, Pallas kernels, body(): velocity_next, done = restore(field, back, e_sent)  1.97 us
  transfers between devices with their start and end apart: 33, of which 11 were waited for; matrix products, arithmetic and copies ran while one was open for 0% of the time, Pallas kernels for 18%

profile of v9, /device:TPU:0, one launch (start us, length us, event | category | flops | bytes accessed | tf_op | source)
XLA Modules:
  0.0 78.4 jit_solution(2841784294916076805)
XLA Ops:
  1.4 1.3 %copy-done.4 = f32[1,1,3,256,512]{4,3,2,1,0:T(8,128)S(1)} copy-done((f32[1,1,3,256,512]{4,3,2,1,0:T(8,128)S(1)}, f32[1,1,3,256,512]{4,3,2,1,0:T(8,128)}, u32[]{:S(2)}) %copy-start.4) | copy-done | bytes 1572888
  3.5 3.0 %collective-permute-start = (bf16[3,64,128]{2,1,0:T(8,128)(2,1)S(1)}, bf16[3,64,128]{2,1,0:T(8,128)(2,1)S(1)}, u32[]{:S(2)}, u32[]{:S(2)}) collective-permute-start(bf16[3,64,128]{2,1,0:T(8,128)(2,1)S(1)} %get-tuple-element.64), channel_id=1, source_target_pairs={{0,4},{4,0},{8,12},{12,8},{16,20},{20,16},{24,28},{28,24},{1,5},{5... | collective-permute-start | bytes 147464 | tf_op jit(solution)/shard_map/ppermute | solution.py:665
  6.5 3.6 %collective-permute-start.1 = (bf16[3,64,128]{2,1,0:T(8,128)(2,1)S(1)}, bf16[3,64,128]{2,1,0:T(8,128)(2,1)S(1)}, u32[]{:S(2)}, u32[]{:S(2)}) collective-permute-start(bf16[3,64,128]{2,1,0:T(8,128)(2,1)S(1)} %get-tuple-element.65), channel_id=1, source_target_pairs={{0,28},{4,8},{8,4},{12,16},{16,12},{20,24},{24,20},{28,0},{1,29},{... | collective-permute-start | bytes 147464 | tf_op jit(solution)/shard_map/ppermute | solution.py:673
  10.8 3.1 %shard_map.104.part = f32[3,256,512]{2,1,0:T(8,128)S(1)} custom-call(f32[3,256,512]{2,1,0:T(8,128)S(1)} %get-tuple-element.63.field, bf16[2560,512]{1,0:T(8,128)(2,1)S(1)} %copy-done.1), custom_call_target="tpu_custom_call" | custom-call | flops 1000 | bytes 1000 | tf_op jit(solution)/shard_map/pallas_call | solution.py:724
  14.5 3.0 %collective-permute-start.5 = (bf16[3,64,128]{2,1,0:T(8,128)(2,1)S(1)}, bf16[3,64,128]{2,1,0:T(8,128)(2,1)S(1)}, u32[]{:S(2)}, u32[]{:S(2)}) collective-permute-start(bf16[3,64,128]{2,1,0:T(8,128)(2,1)S(1)} %get-tuple-element.70), channel_id=1, source_target_pairs={{0,28},{4,8},{8,4},{12,16},{16,12},{20,24},{24,20},{28,0},{1,29},{... | collective-permute-start | bytes 147464 | tf_op jit(solution)/shard_map/ppermute | solution.py:673
  19.6 3.1 %shard_map.106.part = f32[3,256,512]{2,1,0:T(8,128)S(1)} custom-call(f32[3,256,512]{2,1,0:T(8,128)S(1)} %get-tuple-element.68.field, bf16[2560,512]{1,0:T(8,128)(2,1)S(1)} %copy-done.1), custom_call_target="tpu_custom_call" | custom-call | flops 1000 | bytes 1000 | tf_op jit(solution)/shard_map/pallas_call | solution.py:727
  24.6 1.8 %collective-permute-start.8 = (bf16[256,256]{1,0:T(8,128)(2,1)S(1)}, bf16[256,256]{1,0:T(8,128)(2,1)S(1)}, u32[]{:S(2)}, u32[]{:S(2)}) collective-permute-start(bf16[256,256]{1,0:T(8,128)(2,1)S(1)} %get-tuple-element.75.h1.h_own), channel_id=1, source_target_pairs={{0,1},{1,0},{2,3},{3,2},{4,5},{5,4},{6,7},{7,6},{8,9},{9,8},{10,11... | collective-permute-start | bytes 393224 | tf_op jit(solution)/shard_map/ppermute | solution.py:665
  29.0 1.6 %collective-permute-start.11 = (bf16[256,256]{1,0:T(8,128)(2,1)S(1)}, bf16[256,256]{1,0:T(8,128)(2,1)S(1)}, u32[]{:S(2)}, u32[]{:S(2)}) collective-permute-start(bf16[256,256]{1,0:T(8,128)(2,1)S(1)} %get-tuple-element.78.dz2.d_own), channel_id=1, source_target_pairs={{0,3},{1,2},{2,1},{3,0},{4,7},{5,6},{6,5},{7,4},{8,11},{9,10},{10,... | collective-permute-start | bytes 393224 | tf_op jit(solution)/shard_map/ppermute | solution.py:665
  30.6 1.5 %collective-permute-start.10 = (bf16[256,256]{1,0:T(8,128)(2,1)S(1)}, bf16[256,256]{1,0:T(8,128)(2,1)S(1)}, u32[]{:S(2)}, u32[]{:S(2)}) collective-permute-start(bf16[256,256]{1,0:T(8,128)(2,1)S(1)} %get-tuple-element.78.dz2.d_own), channel_id=1, source_target_pairs={{0,1},{1,0},{2,3},{3,2},{4,5},{5,4},{6,7},{7,6},{8,9},{9,8},{10,11... | collective-permute-start | bytes 393224 | tf_op jit(solution)/shard_map/ppermute | solution.py:665
  33.6 1.4 %shard_map.113 = (f32[2,64,1152]{2,1,0:T(8,128)S(1)}, bf16[2,64,1152]{2,1,0:T(8,128)(2,1)S(1)}) custom-call(f32[256,256]{1,0:T(8,128)S(1)} %get-tuple-element.81.dh1, f32[256,128]{1,0:T(8,128)S(1)} %get-tuple-element.82.head, bf16[256,256]{1,0:T(8,128)(2,1)S(1)} %get-tuple-element.78.dz2.d_own, bf16[256,256]{1,0:T(8,128)(2,1)S(1)} %collective-permute-done.10.pair.d_one, ...), custom_call_target="tpu_custom_call" | custom-call | flops 1000 | bytes 1000 | tf_op jit(solution)/shard_map/pallas_call | solution.py:764
  35.1 2.1 %collective-permute-start.12 = (bf16[2,64,1152]{2,1,0:T(8,128)(2,1)S(1)}, bf16[2,64,1152]{2,1,0:T(8,128)(2,1)S(1)}, u32[]{:S(2)}, u32[]{:S(2)}) collective-permute-start(bf16[2,64,1152]{2,1,0:T(8,128)(2,1)S(1)} %get-tuple-element.86), channel_id=1, source_target_pairs={{0,1},{1,0},{2,3},{3,2},{4,5},{5,4},{6,7},{7,6},{8,9},{9,8},{10,11... | collective-permute-start | bytes 884744 | tf_op jit(solution)/shard_map/ppermute | solution.py:665
  38.5 1.7 %collective-permute-start.13 = (bf16[64,1152]{1,0:T(8,128)(2,1)S(1)}, bf16[64,1152]{1,0:T(8,128)(2,1)S(1)}, u32[]{:S(2)}, u32[]{:S(2)}) collective-permute-start(bf16[64,1152]{1,0:T(8,128)(2,1)S(1)} %get-tuple-element.88), channel_id=1, source_target_pairs={{0,2},{1,3},{2,0},{3,1},{4,6},{5,7},{6,4},{7,5},{8,10},{9,11},{10,... | collective-permute-start | bytes 442376 | tf_op jit(solution)/shard_map/ppermute | solution.py:665
  40.2 1.4 %shard_map.115 = (f32[216,256]{1,0:T(8,128)S(1)}, bf16[216,256]{1,0:T(8,128)(2,1)S(1)}, f32[216,256]{1,0:T(8,128)S(1)}, bf16[216,256]{1,0:T(8,128)(2,1)S(1)}, f3...) custom-call(bf16[256,256]{1,0:T(8,128)(2,1)S(1)} %get-tuple-element., ...), custom_call_target="tpu_custom_call" | custom-call | flops 1000 | bytes 1000 | tf_op jit(solution)/shard_map/pallas_call | solution.py:779
  42.2 1.4 %collective-permute-start.19 = (bf16[216,256]{1,0:T(8,128)(2,1)S(1)}, bf16[216,256]{1,0:T(8,128)(2,1)S(1)}, u32[]{:S(2)}, u32[]{:S(2)}) collective-permute-start(bf16[216,256]{1,0:T(8,128)(2,1)S(1)} %get-tuple-element.99), channel_id=1, source_target_pairs={{0,4},{4,0},{8,12},{12,8},{16,20},{20,16},{24,28},{28,24},{1,5},{5... | collective-permute-start | bytes 331784 | tf_op jit(solution)/shard_map/ppermute | solution.py:665
  44.7 1.6 %collective-permute-start.16 = (bf16[2,16,1152]{2,1,0:T(8,128)(2,1)S(1)}, bf16[2,16,1152]{2,1,0:T(8,128)(2,1)S(1)}, u32[]{:S(2)}, u32[]{:S(2)}) collective-permute-start(bf16[2,16,1152]{2,1,0:T(8,128)(2,1)S(1)} %get-tuple-element.91.refs_1_), channel_id=1, source_target_pairs={{0,8},{4,12},{8,0},{12,4},{16,24},{20,28},{24,16},{28,20},{1,9},{5... | collective-permute-start | bytes 221192 | tf_op jit(solution)/shard_map/ppermute | solution.py:665
  47.6 1.6 %collective-permute-start.23 = (bf16[216,256]{1,0:T(8,128)(2,1)S(1)}, bf16[216,256]{1,0:T(8,128)(2,1)S(1)}, u32[]{:S(2)}, u32[]{:S(2)}) collective-permute-start(bf16[216,256]{1,0:T(8,128)(2,1)S(1)} %shard_map.121), channel_id=1, source_target_pairs={{0,8},{4,12},{8,0},{12,4},{16,24},{20,28},{24,16},{28,20},{1,9},{5... | collective-permute-start | bytes 331784 | tf_op jit(solution)/shard_map/ppermute | solution.py:665
  51.7 2.3 %collective-permute-start.20 = (bf16[216,256]{1,0:T(8,128)(2,1)S(1)}, bf16[216,256]{1,0:T(8,128)(2,1)S(1)}, u32[]{:S(2)}, u32[]{:S(2)}) collective-permute-start(bf16[216,256]{1,0:T(8,128)(2,1)S(1)} %shard_map.120.refs_2_), channel_id=1, source_target_pairs={{0,8},{4,12},{8,0},{12,4},{16,24},{20,28},{24,16},{28,20},{1,9},{5... | collective-permute-start | bytes 331784 | tf_op jit(solution)/shard_map/ppermute | solution.py:665
  54.1 1.5 %collective-permute-start.24 = (bf16[216,256]{1,0:T(8,128)(2,1)S(1)}, bf16[216,256]{1,0:T(8,128)(2,1)S(1)}, u32[]{:S(2)}, u32[]{:S(2)}) collective-permute-start(bf16[216,256]{1,0:T(8,128)(2,1)S(1)} %shard_map.122), channel_id=1, source_target_pairs={{0,16},{4,20},{8,24},{12,28},{16,0},{20,4},{24,8},{28,12},{1,17},{... | collective-permute-start | bytes 331784 | tf_op jit(solution)/shard_map/ppermute | solution.py:665
  55.6 2.4 %collective-permute-start.25 = (bf16[8,1152]{1,0:T(8,128)(2,1)S(1)}, bf16[8,1152]{1,0:T(8,128)(2,1)S(1)}, u32[]{:S(2)}, u32[]{:S(2)}) collective-permute-start(bf16[8,1152]{1,0:T(8,128)(2,1)S(1)} %get-tuple-element.94.after_this), channel_id=1, source_target_pairs={{0,4},{4,0},{8,12},{12,8},{16,20},{20,16},{24,28},{28,24},{1,5},{5... | collective-permute-start | bytes 55304 | tf_op jit(solution)/shard_map/ppermute | solution.py:665
  58.0 2.0 %shard_map.119 = (f32[3,256,512]{2,1,0:T(8,128)}, f32[8,128]{1,0:T(8,128)S(1)}) custom-call(f32[3,256,512]{2,1,0:T(8,128)S(1)} %get-tuple-element.73.field, bf16[256,256]{1,0:T(8,128)(2,1)S(1)} %get-tuple-element.74.back, bf16[8,1152]{1,0:T(8,128)(2,1)S(1)} %get-tuple-element.94.after_this), custom_call_target="tpu_custom_call" | custom-call | flops 1000 | bytes 1000 | tf_op jit(solution)/shard_map/pallas_call | solution.py:813
  60.9 2.3 %collective-permute-start.28 = (bf16[256,256]{1,0:T(8,128)(2,1)S(1)}, bf16[256,256]{1,0:T(8,128)(2,1)S(1)}, u32[]{:S(2)}, u32[]{:S(2)}) collective-permute-start(bf16[256,256]{1,0:T(8,128)(2,1)S(1)} %shard_map.123.refs_0_), channel_id=1, source_target_pairs={{0,16},{4,20},{8,24},{12,28},{16,0},{20,4},{24,8},{28,12},{1,17},{... | collective-permute-start | bytes 393224 | tf_op jit(solution)/shard_map/ppermute | solution.py:665
  63.2 1.9 %collective-permute-start.26 = (bf16[256,256]{1,0:T(8,128)(2,1)S(1)}, bf16[256,256]{1,0:T(8,128)(2,1)S(1)}, u32[]{:S(2)}, u32[]{:S(2)}) collective-permute-start(bf16[256,256]{1,0:T(8,128)(2,1)S(1)} %shard_map.123.refs_0_), channel_id=1, source_target_pairs={{0,24},{4,28},{8,16},{12,20},{16,8},{20,12},{24,0},{28,4},{1,25},{... | collective-permute-start | bytes 393224 | tf_op jit(solution)/shard_map/ppermute | solution.py:665
  68.2 2.9 %collective-permute-done.28.refs_0_ = bf16[256,256]{1,0:T(8,128)(2,1)S(1)} collective-permute-done((bf16[256,256]{1,0:T(8,128)(2,1)S(1)}, bf16[256,256]{1,0:T(8,128)(2,1)S(1)}, u32[]{:S(2)}, u32[]{:S(2)}) %collective-permute-start.28) | collective-permute-done | bytes 131104 | tf_op jit(solution)/shard_map/ppermute | solution.py:665
  71.7 1.5 %collective-permute-start.27 = (bf16[256,256]{1,0:T(8,128)(2,1)S(1)}, bf16[256,256]{1,0:T(8,128)(2,1)S(1)}, u32[]{:S(2)}, u32[]{:S(2)}) collective-permute-start(bf16[256,256]{1,0:T(8,128)(2,1)S(1)} %collective-permute-done.26.refs_2_), channel_id=1, source_target_pairs={{0,4},{4,0},{8,12},{12,8},{16,20},{20,16},{24,28},{28,24},{1,5},{5... | collective-permute-start | bytes 393224 | tf_op jit(solution)/shard_map/ppermute | solution.py:665
  (82 shorter events, 27.1 us)
Async XLA Ops:
  3.5 10.4 %collective-permute-start = (bf16[3,64,128]{2,1,0:T(8,128)(2,1)S(1)}, bf16[3,64,128]{2,1,0:T(8,128)(2,1)S(1)}, u32[]{:S(2)}, u32[]{:S(2)}) collective-permute-start(bf16[3,64,128]{2,1,0:T(8,128)(2,1)S(1)} %get-tuple-element.64), channel_id=1, source_target_pairs={{0,4},{4,0},{8,12},{12,8},{16,20},{20,16},{24,28},{28,24},{1,5},{5... | collective-permute-start | bytes 147464 | tf_op jit(solution)/shard_map/ppermute | solution.py:665
  6.5 7.4 %collective-permute-start.1 = (bf16[3,64,128]{2,1,0:T(8,128)(2,1)S(1)}, bf16[3,64,128]{2,1,0:T(8,128)(2,1)S(1)}, u32[]{:S(2)}, u32[]{:S(2)}) collective-permute-start(bf16[3,64,128]{2,1,0:T(8,128)(2,1)S(1)} %get-tuple-element.65), channel_id=1, source_target_pairs={{0,28},{4,8},{8,4},{12,16},{16,12},{20,24},{24,20},{28,0},{1,29},{... | collective-permute-start | bytes 147464 | tf_op jit(solution)/shard_map/ppermute | solution.py:673
  14.5 8.3 %collective-permute-start.4 = (bf16[3,64,128]{2,1,0:T(8,128)(2,1)S(1)}, bf16[3,64,128]{2,1,0:T(8,128)(2,1)S(1)}, u32[]{:S(2)}, u32[]{:S(2)}) collective-permute-start(bf16[3,64,128]{2,1,0:T(8,128)(2,1)S(1)} %get-tuple-element.69), channel_id=1, source_target_pairs={{0,4},{4,0},{8,12},{12,8},{16,20},{20,16},{24,28},{28,24},{1,5},{5... | collective-permute-start | bytes 147464 | tf_op jit(solution)/shard_map/ppermute | solution.py:665
  14.5 8.2 %collective-permute-start.5 = (bf16[3,64,128]{2,1,0:T(8,128)(2,1)S(1)}, bf16[3,64,128]{2,1,0:T(8,128)(2,1)S(1)}, u32[]{:S(2)}, u32[]{:S(2)}) collective-permute-start(bf16[3,64,128]{2,1,0:T(8,128)(2,1)S(1)} %get-tuple-element.70), channel_id=1, source_target_pairs={{0,28},{4,8},{8,4},{12,16},{16,12},{20,24},{24,20},{28,0},{1,29},{... | collective-permute-start | bytes 147464 | tf_op jit(solution)/shard_map/ppermute | solution.py:673
  17.6 5.2 %collective-permute-start.6 = (bf16[3,32,128]{2,1,0:T(8,128)(2,1)S(1)}, bf16[3,32,128]{2,1,0:T(8,128)(2,1)S(1)}, u32[]{:S(2)}, u32[]{:S(2)}) collective-permute-start(bf16[3,32,128]{2,1,0:T(8,128)(2,1)S(1)} %get-tuple-element.71), channel_id=1, source_target_pairs={{0,1},{1,0},{2,3},{3,2},{4,5},{5,4},{6,7},{7,6},{8,9},{9,8},{10,11... | collective-permute-start | bytes 73736 | tf_op jit(solution)/shard_map/ppermute | solution.py:665
  23.4 4.5 %collective-permute-start.9 = (bf16[256,256]{1,0:T(8,128)(2,1)S(1)}, bf16[256,256]{1,0:T(8,128)(2,1)S(1)}, u32[]{:S(2)}, u32[]{:S(2)}) collective-permute-start(bf16[256,256]{1,0:T(8,128)(2,1)S(1)} %get-tuple-element.75.h1.h_own), channel_id=1, source_target_pairs={{0,3},{1,2},{2,1},{3,0},{4,7},{5,6},{6,5},{7,4},{8,11},{9,10},{10,... | collective-permute-start | bytes 393224 | tf_op jit(solution)/shard_map/ppermute | solution.py:665
  29.0 4.7 %collective-permute-start.11 = (bf16[256,256]{1,0:T(8,128)(2,1)S(1)}, bf16[256,256]{1,0:T(8,128)(2,1)S(1)}, u32[]{:S(2)}, u32[]{:S(2)}) collective-permute-start(bf16[256,256]{1,0:T(8,128)(2,1)S(1)} %get-tuple-element.78.dz2.d_own), channel_id=1, source_target_pairs={{0,3},{1,2},{2,1},{3,0},{4,7},{5,6},{6,5},{7,4},{8,11},{9,10},{10,... | collective-permute-start | bytes 393224 | tf_op jit(solution)/shard_map/ppermute | solution.py:665
  38.5 6.2 %collective-permute-start.13 = (bf16[64,1152]{1,0:T(8,128)(2,1)S(1)}, bf16[64,1152]{1,0:T(8,128)(2,1)S(1)}, u32[]{:S(2)}, u32[]{:S(2)}) collective-permute-start(bf16[64,1152]{1,0:T(8,128)(2,1)S(1)} %get-tuple-element.88), channel_id=1, source_target_pairs={{0,2},{1,3},{2,0},{3,1},{4,6},{5,7},{6,4},{7,5},{8,10},{9,11},{10,... | collective-permute-start | bytes 442376 | tf_op jit(solution)/shard_map/ppermute | solution.py:665
  41.6 6.0 %collective-permute-start.22 = (bf16[216,256]{1,0:T(8,128)(2,1)S(1)}, bf16[216,256]{1,0:T(8,128)(2,1)S(1)}, u32[]{:S(2)}, u32[]{:S(2)}) collective-permute-start(bf16[216,256]{1,0:T(8,128)(2,1)S(1)} %get-tuple-element.103), channel_id=1, source_target_pairs={{0,4},{4,0},{8,12},{12,8},{16,20},{20,16},{24,28},{28,24},{1,5},{5... | collective-permute-start | bytes 331784 | tf_op jit(solution)/shard_map/ppermute | solution.py:665
  42.2 9.4 %collective-permute-start.19 = (bf16[216,256]{1,0:T(8,128)(2,1)S(1)}, bf16[216,256]{1,0:T(8,128)(2,1)S(1)}, u32[]{:S(2)}, u32[]{:S(2)}) collective-permute-start(bf16[216,256]{1,0:T(8,128)(2,1)S(1)} %get-tuple-element.99), channel_id=1, source_target_pairs={{0,4},{4,0},{8,12},{12,8},{16,20},{20,16},{24,28},{28,24},{1,5},{5... | collective-permute-start | bytes 331784 | tf_op jit(solution)/shard_map/ppermute | solution.py:665
  43.7 10.4 %collective-permute-start.21 = (bf16[216,256]{1,0:T(8,128)(2,1)S(1)}, bf16[216,256]{1,0:T(8,128)(2,1)S(1)}, u32[]{:S(2)}, u32[]{:S(2)}) collective-permute-start(bf16[216,256]{1,0:T(8,128)(2,1)S(1)} %get-tuple-element.101), channel_id=1, source_target_pairs={{0,4},{4,0},{8,12},{12,8},{16,20},{20,16},{24,28},{28,24},{1,5},{5... | collective-permute-start | bytes 331784 | tf_op jit(solution)/shard_map/ppermute | solution.py:665
  44.7 5.2 %collective-permute-start.16 = (bf16[2,16,1152]{2,1,0:T(8,128)(2,1)S(1)}, bf16[2,16,1152]{2,1,0:T(8,128)(2,1)S(1)}, u32[]{:S(2)}, u32[]{:S(2)}) collective-permute-start(bf16[2,16,1152]{2,1,0:T(8,128)(2,1)S(1)} %get-tuple-element.91.refs_1_), channel_id=1, source_target_pairs={{0,8},{4,12},{8,0},{12,4},{16,24},{20,28},{24,16},{28,20},{1,9},{5... | collective-permute-start | bytes 221192 | tf_op jit(solution)/shard_map/ppermute | solution.py:665
  47.6 6.4 %collective-permute-start.23 = (bf16[216,256]{1,0:T(8,128)(2,1)S(1)}, bf16[216,256]{1,0:T(8,128)(2,1)S(1)}, u32[]{:S(2)}, u32[]{:S(2)}) collective-permute-start(bf16[216,256]{1,0:T(8,128)(2,1)S(1)} %shard_map.121), channel_id=1, source_target_pairs={{0,8},{4,12},{8,0},{12,4},{16,24},{20,28},{24,16},{28,20},{1,9},{5... | collective-permute-start | bytes 331784 | tf_op jit(solution)/shard_map/ppermute | solution.py:665
  49.9 5.6 %collective-permute-start.17 = (bf16[16,1152]{1,0:T(8,128)(2,1)S(1)}, bf16[16,1152]{1,0:T(8,128)(2,1)S(1)}, u32[]{:S(2)}, u32[]{:S(2)}) collective-permute-start(bf16[16,1152]{1,0:T(8,128)(2,1)S(1)} %get-tuple-element.93.refs_1_), channel_id=1, source_target_pairs={{0,16},{4,20},{8,24},{12,28},{16,0},{20,4},{24,8},{28,12},{1,17},{... | collective-permute-start | bytes 110600 | tf_op jit(solution)/shard_map/ppermute | solution.py:665
  50.9 9.1 %collective-permute-start.18 = (bf16[216,256]{1,0:T(8,128)(2,1)S(1)}, bf16[216,256]{1,0:T(8,128)(2,1)S(1)}, u32[]{:S(2)}, u32[]{:S(2)}) collective-permute-start(bf16[216,256]{1,0:T(8,128)(2,1)S(1)} %get-tuple-element.97), channel_id=1, source_target_pairs={{0,4},{4,0},{8,12},{12,8},{16,20},{20,16},{24,28},{28,24},{1,5},{5... | collective-permute-start | bytes 331784 | tf_op jit(solution)/shard_map/ppermute | solution.py:665
  51.7 8.3 %collective-permute-start.20 = (bf16[216,256]{1,0:T(8,128)(2,1)S(1)}, bf16[216,256]{1,0:T(8,128)(2,1)S(1)}, u32[]{:S(2)}, u32[]{:S(2)}) collective-permute-start(bf16[216,256]{1,0:T(8,128)(2,1)S(1)} %shard_map.120.refs_2_), channel_id=1, source_target_pairs={{0,8},{4,12},{8,0},{12,4},{16,24},{20,28},{24,16},{28,20},{1,9},{5... | collective-permute-start | bytes 331784 | tf_op jit(solution)/shard_map/ppermute | solution.py:665
  54.1 6.5 %collective-permute-start.24 = (bf16[216,256]{1,0:T(8,128)(2,1)S(1)}, bf16[216,256]{1,0:T(8,128)(2,1)S(1)}, u32[]{:S(2)}, u32[]{:S(2)}) collective-permute-start(bf16[216,256]{1,0:T(8,128)(2,1)S(1)} %shard_map.122), channel_id=1, source_target_pairs={{0,16},{4,20},{8,24},{12,28},{16,0},{20,4},{24,8},{28,12},{1,17},{... | collective-permute-start | bytes 331784 | tf_op jit(solution)/shard_map/ppermute | solution.py:665
  60.6 6.8 %collective-permute-start.30 = (bf16[256,256]{1,0:T(8,128)(2,1)S(1)}, bf16[256,256]{1,0:T(8,128)(2,1)S(1)}, u32[]{:S(2)}, u32[]{:S(2)}) collective-permute-start(bf16[256,256]{1,0:T(8,128)(2,1)S(1)} %shard_map.123.refs_0_), channel_id=1, source_target_pairs={{0,8},{4,12},{8,0},{12,4},{16,24},{20,28},{24,16},{28,20},{1,9},{5... | collective-permute-start | bytes 393224 | tf_op jit(solution)/shard_map/ppermute | solution.py:665
  60.9 10.3 %collective-permute-start.28 = (bf16[256,256]{1,0:T(8,128)(2,1)S(1)}, bf16[256,256]{1,0:T(8,128)(2,1)S(1)}, u32[]{:S(2)}, u32[]{:S(2)}) collective-permute-start(bf16[256,256]{1,0:T(8,128)(2,1)S(1)} %shard_map.123.refs_0_), channel_id=1, source_target_pairs={{0,16},{4,20},{8,24},{12,28},{16,0},{20,4},{24,8},{28,12},{1,17},{... | collective-permute-start | bytes 393224 | tf_op jit(solution)/shard_map/ppermute | solution.py:665
  63.2 8.5 %collective-permute-start.26 = (bf16[256,256]{1,0:T(8,128)(2,1)S(1)}, bf16[256,256]{1,0:T(8,128)(2,1)S(1)}, u32[]{:S(2)}, u32[]{:S(2)}) collective-permute-start(bf16[256,256]{1,0:T(8,128)(2,1)S(1)} %shard_map.123.refs_0_), channel_id=1, source_target_pairs={{0,24},{4,28},{8,16},{12,20},{16,8},{20,12},{24,0},{28,4},{1,25},{... | collective-permute-start | bytes 393224 | tf_op jit(solution)/shard_map/ppermute | solution.py:665
  65.1 8.1 %collective-permute-start.32 = (bf16[256,256]{1,0:T(8,128)(2,1)S(1)}, bf16[256,256]{1,0:T(8,128)(2,1)S(1)}, u32[]{:S(2)}, u32[]{:S(2)}) collective-permute-start(bf16[256,256]{1,0:T(8,128)(2,1)S(1)} %shard_map.123.refs_0_), channel_id=1, source_target_pairs={{0,4},{4,0},{8,12},{12,8},{16,20},{20,16},{24,28},{28,24},{1,5},{5... | collective-permute-start | bytes 393224 | tf_op jit(solution)/shard_map/ppermute | solution.py:665
  67.4 6.6 %collective-permute-start.31 = (bf16[256,256]{1,0:T(8,128)(2,1)S(1)}, bf16[256,256]{1,0:T(8,128)(2,1)S(1)}, u32[]{:S(2)}, u32[]{:S(2)}) collective-permute-start(bf16[256,256]{1,0:T(8,128)(2,1)S(1)} %collective-permute-done.30.refs_0_), channel_id=1, source_target_pairs={{0,4},{4,0},{8,12},{12,8},{16,20},{20,16},{24,28},{28,24},{1,5},{5... | collective-permute-start | bytes 393224 | tf_op jit(solution)/shard_map/ppermute | solution.py:665
  71.1 5.0 %collective-permute-start.29 = (bf16[256,256]{1,0:T(8,128)(2,1)S(1)}, bf16[256,256]{1,0:T(8,128)(2,1)S(1)}, u32[]{:S(2)}, u32[]{:S(2)}) collective-permute-start(bf16[256,256]{1,0:T(8,128)(2,1)S(1)} %collective-permute-done.28.refs_0_), channel_id=1, source_target_pairs={{0,4},{4,0},{8,12},{12,8},{16,20},{20,16},{24,28},{28,24},{1,5},{5... | collective-permute-start | bytes 393224 | tf_op jit(solution)/shard_map/ppermute | solution.py:665
  71.7 5.8 %collective-permute-start.27 = (bf16[256,256]{1,0:T(8,128)(2,1)S(1)}, bf16[256,256]{1,0:T(8,128)(2,1)S(1)}, u32[]{:S(2)}, u32[]{:S(2)}) collective-permute-start(bf16[256,256]{1,0:T(8,128)(2,1)S(1)} %collective-permute-done.26.refs_2_), channel_id=1, source_target_pairs={{0,4},{4,0},{8,12},{12,8},{16,20},{20,16},{24,28},{28,24},{1,5},{5... | collective-permute-start | bytes 393224 | tf_op jit(solution)/shard_map/ppermute | solution.py:665
  (16 other events, 56.2 us)
